TPU v7x, 32 devices: a whole 2x2x4 slice. The times are simulated.
32 devices in a mesh: groups: 2 (over y), space: 8 (over z, x), rhs: 2 (over core).
Axes of the slice: x: 2, y: 2, z: 4, core: 2. Of those that a mesh axis runs over, the one named last changes fastest.
Arguments:
- vectors: bfloat16 [65536, 256], P(('groups', 'space'), 'rhs'), parts along dimension 0, may hold values from -6 to 6
- near_blocks: bfloat16 [128, 12, 256, 256], P('space'), may hold values from -0.109375 to 0.109375
- near_list: int32 [128, 12], P('space'), may hold values from 0 to 127, as said below
- basis: bfloat16 [128, 256, 64], P('space'), may hold values from -0.375 to 0.375
- up_one: bfloat16 [128, 64, 64], P('space'), may hold values from -0.5 to 0.5
- up_two: bfloat16 [64, 64, 64], P('space'), may hold values from -0.5 to 0.5
- couple_zero: bfloat16 [128, 16, 64, 64], P('space'), may hold values from -0.1875 to 0.1875
- couple_one: bfloat16 [64, 16, 64, 64], P('space'), may hold values from -0.1875 to 0.1875
- couple_two: bfloat16 [32, 16, 64, 64], P('space'), may hold values from -0.1875 to 0.1875
- far_zero: int32 [128, 16], P('space'), may hold values from 0 to 127, as said below
- far_one: int32 [64, 16], P('space'), may hold values from 0 to 63, as said below
- far_two: int32 [32, 16], P('space'), may hold values from 0 to 31, as said below
Outputs:
- product: bfloat16 [65536, 256], P(('groups', 'space'), 'rhs'), parts along dimension 0
There are 2 independent parts, one for each index of `groups`. A program takes and returns all parts, laid end to end along the dimension named above; an argument that names none is the same for every part. Nothing has to cross between parts.
Inputs may be any that keep to these rules, and one draw needn't show every extreme that they name: `near_list`: entry 0 of each leaf's list is the leaf itself; entries may repeat. Entry 1 is the first leaf of the next index of space and entry 2 the last leaf of the previous index (the leaf itself where that index does not exist); every other entry is a leaf of the leaf's own index of space (leaves i * 16 to (i+1) * 16 - 1). `far_zero`: each entry names a node of the leaf level held by an index of space at most 2 away from the index that holds the listing node (index i holds nodes i * 16 to (i+1) * 16 - 1). `far_one`: each entry names a node of level one held by an index of space at most 2 away from the index that holds the listing node (index i holds nodes i * 8 to (i+1) * 8 - 1). `far_two`: each entry names a node of level two held by an index of space at most 2 away from the index that holds the listing node (index i holds nodes i * 4 to (i+1) * 4 - 1).
All inputs are finite; a program needn't handle non-finite values.
Results may differ from a plain program's by a relative error of at most 0.005.
Values may be sent and summed in bfloat16 or wider, within the bound.
No kernel may reach another device: no remote copies, remote signals or barrier semaphores. Data moves between devices by JAX's collectives and lax.ppermute only.
A program may use at most 128 MiB of HBM per device.

v0:
```python
import jax
import jax.numpy as jnp
from jax import lax
from jax.sharding import PartitionSpec as P

LEAF = 256
REACH = 2


def with_halo(array, sides, width):
    for axis, dim in sides:
        size, length = (lax.axis_size(axis), array.shape[dim])
        up = [(i, (i + 1) % size) for i in range(size - 1)]
        down = [(j, i) for i, j in up]
        last = lax.slice_in_dim(array, length - width, length, axis=dim)
        leading = lax.slice_in_dim(array, 0, width, axis=dim)
        before = lax.ppermute(last, axis, up)
        after = lax.ppermute(leading, axis, down)
        array = jnp.concatenate([before, array, after], axis=dim)
    return array


def from_behind(array, axis, by):
    length = lax.axis_size(axis)
    pairs = [(i, i + by) for i in range(length) if 0 <= i + by < length]
    return lax.ppermute(array, axis, pairs)


def couple_level(matrices, partner_list, gathered):
    picked = gathered[partner_list]
    return jnp.einsum("pkab,pkbc->pac", matrices, picked, preferred_element_type=jnp.float32)


def body(
    vectors,
    near_blocks,
    near_list,
    basis,
    up_one,
    up_two,
    couple_zero,
    couple_one,
    couple_two,
    far_zero,
    far_one,
    far_two,
):
    per_device = near_list.shape[0]
    columns = vectors.shape[1]
    rank_size = basis.shape[2]
    myself = lax.axis_index("space")
    points = vectors.reshape(per_device, LEAF, columns)
    padded = with_halo(vectors, (("space", 0),), LEAF).reshape(per_device + 2, LEAF, columns)
    position = near_list - (myself * per_device - 1)
    partner_rows = padded[position]
    near_term = jnp.einsum(
        "lkpq,lkqc->lpc", near_blocks, partner_rows, preferred_element_type=jnp.float32
    )
    coef_zero = jnp.einsum(
        "lpr,lpc->lrc", basis, points, preferred_element_type=jnp.float32
    ).astype(jnp.bfloat16)
    lifted = jnp.einsum("lab,lac->lbc", up_one, coef_zero, preferred_element_type=jnp.float32)
    coef_one = (
        lifted.reshape(per_device // 2, 2, rank_size, columns).sum(axis=1).astype(jnp.bfloat16)
    )
    lifted = jnp.einsum("lab,lac->lbc", up_two, coef_one, preferred_element_type=jnp.float32)
    coef_two = (
        lifted.reshape(per_device // 4, 2, rank_size, columns).sum(axis=1).astype(jnp.bfloat16)
    )
    own_levels = (coef_zero, coef_one, coef_two)
    windows = []
    for offset in range(-REACH, REACH + 1):
        if offset == 0:
            windows.append(own_levels)
        else:
            windows.append(
                from_behind((own_levels[0], own_levels[1], own_levels[2]), "space", -offset)
            )
    gathered_zero = jnp.concatenate([piece[0] for piece in windows], axis=0)
    gathered_one = jnp.concatenate([piece[1] for piece in windows], axis=0)
    gathered_two = jnp.concatenate([piece[2] for piece in windows], axis=0)
    first_dev = myself - REACH
    list_zero = far_zero - first_dev * per_device
    list_one = far_one - first_dev * (per_device // 2)
    list_two = far_two - first_dev * (per_device // 4)
    field_zero = couple_level(couple_zero, list_zero, gathered_zero)
    field_one = couple_level(couple_one, list_one, gathered_one)
    field_two = couple_level(couple_two, list_two, gathered_two)
    down_two = field_two.astype(jnp.bfloat16)
    parent_two = jnp.repeat(down_two, 2, axis=0)
    down_one = (
        field_one
        + jnp.einsum("pab,pbc->pac", up_two, parent_two, preferred_element_type=jnp.float32)
    ).astype(jnp.bfloat16)
    parent_one = jnp.repeat(down_one, 2, axis=0)
    down_zero = (
        field_zero
        + jnp.einsum("lab,lbc->lac", up_one, parent_one, preferred_element_type=jnp.float32)
    ).astype(jnp.bfloat16)
    far_term = jnp.einsum("lpr,lrc->lpc", basis, down_zero, preferred_element_type=jnp.float32)
    return (near_term + far_term).astype(jnp.bfloat16).reshape(per_device * LEAF, columns)


def solution(mesh):
    placed = (
        P(("groups", "space"), "rhs"),
        P("space", None, None, None),
        P("space", None),
        P("space", None, None),
        P("space", None, None),
        P("space", None, None),
        P("space", None, None, None),
        P("space", None, None, None),
        P("space", None, None, None),
        P("space", None),
        P("space", None),
        P("space", None),
    )
    return jax.shard_map(
        body, mesh=mesh, in_specs=placed, out_specs=P(("groups", "space"), "rhs"), check_vma=False
    )
```

profile of v0, /device:TPU:24, one launch (start us, length us, event | category | flops | bytes accessed | tf_op | source)
XLA Modules:
  0.0 110.8 jit_solution(17021975179974371056)
XLA Ops:
  0.0 2.6 %convolution_convert_fusion = bf16[16,64,128]{2,1,0:T(8,128)(2,1)} fusion(bf16[16,256,64]{1,2,0:T(8,128)(2,1)} %param.15, bf16[16,256,128]{2,1,0:T(8,128)(2,1)} %bitcast.79), kind=kOutput, calls=%fused_computation.10 | convolution fusion | flops 67239936 | bytes 1835008 | tf_op jit(solution)/shard_map/lpr,lpc->lrc/dot_general | solution.py:59
  2.6 2.0 %bitcast_reduce_fusion = bf16[8,64,128]{2,1,0:T(8,128)(2,1)} fusion(bf16[16,64,128]{2,1,0:T(8,128)(2,1)} %convolution_convert_fusion, bf16[16,64,64]{2,1,0:T(8,128)(2,1)} %param.16), kind=kOutput, calls=%fused_computation.19 | convolution fusion | flops 16842752 | bytes 524288 | tf_op jit(solution)/shard_map/lab,lac->lbc/dot_general | solution.py:62
  4.6 1.1 %bitcast_reduce_fusion.1 = bf16[4,64,128]{2,1,0:T(8,128)(2,1)S(1)} fusion(bf16[8,64,128]{2,1,0:T(8,128)(2,1)} %bitcast_reduce_fusion, bf16[8,64,64]{2,1,0:T(8,128)(2,1)S(1)} %copy-done.2), kind=kOutput, calls=%fused_computation.20 | convolution fusion | flops 8421376 | bytes 262144 | tf_op jit(solution)/shard_map/lab,lac->lbc/dot_general | solution.py:66
  5.7 1.3 %collective-permute-start.10 = (bf16[4,64,128]{2,1,0:T(8,128)(2,1)S(1)}, bf16[4,64,128]{2,1,0:T(8,128)(2,1)S(1)}, u32[]{:S(2)}, u32[]{:S(2)}) collective-permute-start(bf16[4,64,128]{2,1,0:T(8,128)(2,1)S(1)} %bitcast_reduce_fusion.1), channel_id=1, source_target_pairs={{0,4},{2,6},{4,8},{6,10},{8,12},{10,14},{1,5},{3,7},{5,9},{7,11},{... | collective-permute-start | bytes 196616 | tf_op jit(solution)/shard_map/ppermute | solution.py:26
  7.0 3.4 %collective-permute-start.11 = (bf16[4,64,128]{2,1,0:T(8,128)(2,1)S(1)}, bf16[4,64,128]{2,1,0:T(8,128)(2,1)}, u32[]{:S(2)}, u32[]{:S(2)}) collective-permute-start(bf16[4,64,128]{2,1,0:T(8,128)(2,1)S(1)} %bitcast_reduce_fusion.1), channel_id=1, source_target_pairs={{0,2},{2,4},{4,6},{6,8},{8,10},{10,12},{12,14},{1,3},{3,5},{5,7},{... | collective-permute-start | bytes 196616 | tf_op jit(solution)/shard_map/ppermute | solution.py:26
  10.4 4.0 %collective-permute-start.12 = (bf16[4,64,128]{2,1,0:T(8,128)(2,1)S(1)}, bf16[4,64,128]{2,1,0:T(8,128)(2,1)}, u32[]{:S(2)}, u32[]{:S(2)}) collective-permute-start(bf16[4,64,128]{2,1,0:T(8,128)(2,1)S(1)} %bitcast_reduce_fusion.1), channel_id=1, source_target_pairs={{2,0},{4,2},{6,4},{8,6},{10,8},{12,10},{14,12},{3,1},{5,3},{7,5},{... | collective-permute-start | bytes 196616 | tf_op jit(solution)/shard_map/ppermute | solution.py:26
  14.4 0.9 fusion.9
  15.3 3.9 %collective-permute-start.1 = (bf16[256,128]{1,0:T(8,128)(2,1)S(1)}, bf16[256,128]{1,0:T(8,128)(2,1)S(1)}, u32[]{:S(2)}, u32[]{:S(2)}) collective-permute-start(bf16[256,128]{1,0:T(8,128)(2,1)S(1)} %get-tuple-element.6), channel_id=1, source_target_pairs={{2,0},{4,2},{6,4},{8,6},{10,8},{12,10},{14,12},{3,1},{5,3},{7,5},{... | collective-permute-start | bytes 196616 | tf_op jit(solution)/shard_map/ppermute | solution.py:18
  19.3 1.9 %collective-permute-start = (bf16[256,128]{1,0:T(8,128)(2,1)S(1)}, bf16[256,128]{1,0:T(8,128)(2,1)S(1)}, u32[]{:S(2)}, u32[]{:S(2)}) collective-permute-start(bf16[256,128]{1,0:T(8,128)(2,1)S(1)} %get-tuple-element.5), channel_id=1, source_target_pairs={{0,2},{2,4},{4,6},{6,8},{8,10},{10,12},{12,14},{1,3},{3,5},{5,7},{... | collective-permute-start | bytes 196616 | tf_op jit(solution)/shard_map/ppermute | solution.py:17
  21.2 0.1 reshape.30
  21.3 0.1 reshape.54
  21.7 4.5 %collective-permute-start.13 = (bf16[4,64,128]{2,1,0:T(8,128)(2,1)S(1)}, bf16[4,64,128]{2,1,0:T(8,128)(2,1)}, u32[]{:S(2)}, u32[]{:S(2)}) collective-permute-start(bf16[4,64,128]{2,1,0:T(8,128)(2,1)S(1)} %bitcast_reduce_fusion.1), channel_id=1, source_target_pairs={{4,0},{6,2},{8,4},{10,6},{12,8},{14,10},{5,1},{7,3},{9,5},{11,7},{... | collective-permute-start | bytes 196616 | tf_op jit(solution)/shard_map/ppermute | solution.py:26
  26.2 0.1 collective-permute-done
  26.3 1.3 %collective-permute-start.6 = (bf16[8,64,128]{2,1,0:T(8,128)(2,1)}, bf16[8,64,128]{2,1,0:T(8,128)(2,1)}, u32[]{:S(2)}, u32[]{:S(2)}) collective-permute-start(bf16[8,64,128]{2,1,0:T(8,128)(2,1)} %bitcast_reduce_fusion), channel_id=1, source_target_pairs={{0,4},{2,6},{4,8},{6,10},{8,12},{10,14},{1,5},{3,7},{5,9},{7,11},{... | collective-permute-start | bytes 393224 | tf_op jit(solution)/shard_map/ppermute | solution.py:26
  27.6 1.3 %pad_maximum_fusion = bf16[4608,128]{1,0:T(8,128)(2,1)S(1)} fusion(bf16[256,128]{1,0:T(8,128)(2,1)S(1)} %collective-permute-done.1, bf16[4096,128]{1,0:T(8,128)(2,1)} %param.12, bf16[256,128]{1,0:T(8,128)(2,1)S(1)} %collective-permute-done), kind=kLoop, calls=%fused_computation.11 | loop fusion | flops 3538944 | bytes 2359296 | tf_op jit(solution)/shard_map/concatenate | solution.py:19
  28.9 8.2 %gather_fusion = bf16[192,256,128]{2,1,0:T(8,128)(2,1)} fusion(bf16[18,256,128]{2,1,0:T(8,128)(2,1)S(1)} %bitcast.75, s32[1024]{0:T(1024)S(1)} %pad_clamp_fusion.3), kind=kCustom, calls=%fused_computation | custom fusion | bytes 25166592 | tf_op jit(solution)/shard_map/gather | solution.py:55
  37.1 16.7 %fusion.10 = f32[16,128,256,1]{2,1,3,0:T(8,128)} fusion(bf16[16,12,256,128]{3,2,1,0:T(8,128)(2,1)} %bitcast.76, bf16[16,12,256,256]{3,2,1,0:T(8,128)(2,1)} %param.13), kind=kOutput, calls=%fused_computation.45 | convolution fusion | flops 3221225472 | bytes 39845888 | tf_op jit(solution)/shard_map/lkpq,lkqc->lpc/dot_general | solution.py:56
  53.8 0.6 copy-done.4
  54.4 3.3 %collective-permute-start.7 = (bf16[8,64,128]{2,1,0:T(8,128)(2,1)}, bf16[8,64,128]{2,1,0:T(8,128)(2,1)}, u32[]{:S(2)}, u32[]{:S(2)}) collective-permute-start(bf16[8,64,128]{2,1,0:T(8,128)(2,1)} %bitcast_reduce_fusion), channel_id=1, source_target_pairs={{0,2},{2,4},{4,6},{6,8},{8,10},{10,12},{12,14},{1,3},{3,5},{5,7},{... | collective-permute-start | bytes 393224 | tf_op jit(solution)/shard_map/ppermute | solution.py:26
  57.7 0.8 constant_dynamic-update-slice_fusion.14
  58.5 4.0 %collective-permute-start.8 = (bf16[8,64,128]{2,1,0:T(8,128)(2,1)}, bf16[8,64,128]{2,1,0:T(8,128)(2,1)}, u32[]{:S(2)}, u32[]{:S(2)}) collective-permute-start(bf16[8,64,128]{2,1,0:T(8,128)(2,1)} %bitcast_reduce_fusion), channel_id=1, source_target_pairs={{2,0},{4,2},{6,4},{8,6},{10,8},{12,10},{14,12},{3,1},{5,3},{7,5},{... | collective-permute-start | bytes 393224 | tf_op jit(solution)/shard_map/ppermute | solution.py:26
  62.5 0.9 constant_dynamic-update-slice_fusion.13
  63.4 4.7 %collective-permute-start.9 = (bf16[8,64,128]{2,1,0:T(8,128)(2,1)}, bf16[8,64,128]{2,1,0:T(8,128)(2,1)}, u32[]{:S(2)}, u32[]{:S(2)}) collective-permute-start(bf16[8,64,128]{2,1,0:T(8,128)(2,1)} %bitcast_reduce_fusion), channel_id=1, source_target_pairs={{4,0},{6,2},{8,4},{10,6},{12,8},{14,10},{5,1},{7,3},{9,5},{11,7},{... | collective-permute-start | bytes 393224 | tf_op jit(solution)/shard_map/ppermute | solution.py:26
  68.1 0.9 constant_dynamic-update-slice_fusion.11
  69.0 1.3 %collective-permute-start.2 = (bf16[16,64,128]{2,1,0:T(8,128)(2,1)}, bf16[16,64,128]{2,1,0:T(8,128)(2,1)}, u32[]{:S(2)}, u32[]{:S(2)}) collective-permute-start(bf16[16,64,128]{2,1,0:T(8,128)(2,1)} %convolution_convert_fusion), channel_id=1, source_target_pairs={{0,4},{2,6},{4,8},{6,10},{8,12},{10,14},{1,5},{3,7},{5,9},{7,11},{... | collective-permute-start | bytes 786440 | tf_op jit(solution)/shard_map/ppermute | solution.py:26
  70.3 0.9 constant_dynamic-update-slice_fusion.10
  71.1 0.7 gather_fusion.3
  71.9 1.6 %fusion.8 = bf16[4,64,128]{2,1,0:T(8,128)(2,1)S(1)} fusion(bf16[4,16,64,64]{3,2,1,0:T(8,128)(2,1)} %param.20, bf16[4,16,64,128]{3,2,1,0:T(8,128)(2,1)S(1)} %bitcast.80), kind=kOutput, calls=%fused_computation.18 | convolution fusion | flops 67141632 | bytes 1638400 | tf_op jit(solution)/shard_map/pkab,pkbc->pac/dot_general | solution.py:31
  73.5 0.2 fusion.11
  73.7 2.4 %collective-permute-start.3 = (bf16[16,64,128]{2,1,0:T(8,128)(2,1)}, bf16[16,64,128]{2,1,0:T(8,128)(2,1)}, u32[]{:S(2)}, u32[]{:S(2)}) collective-permute-start(bf16[16,64,128]{2,1,0:T(8,128)(2,1)} %convolution_convert_fusion), channel_id=1, source_target_pairs={{0,2},{2,4},{4,6},{6,8},{8,10},{10,12},{12,14},{1,3},{3,5},{5,7},{... | collective-permute-start | bytes 786440 | tf_op jit(solution)/shard_map/ppermute | solution.py:26
  76.1 0.9 constant_dynamic-update-slice_fusion.9
  77.0 4.4 %collective-permute-start.4 = (bf16[16,64,128]{2,1,0:T(8,128)(2,1)}, bf16[16,64,128]{2,1,0:T(8,128)(2,1)}, u32[]{:S(2)}, u32[]{:S(2)}) collective-permute-start(bf16[16,64,128]{2,1,0:T(8,128)(2,1)} %convolution_convert_fusion), channel_id=1, source_target_pairs={{2,0},{4,2},{6,4},{8,6},{10,8},{12,10},{14,12},{3,1},{5,3},{7,5},{... | collective-permute-start | bytes 786440 | tf_op jit(solution)/shard_map/ppermute | solution.py:26
  81.4 0.9 constant_dynamic-update-slice_fusion.8
  82.3 0.9 constant_dynamic-update-slice_fusion.7
  83.3 5.3 %collective-permute-start.5 = (bf16[16,64,128]{2,1,0:T(8,128)(2,1)}, bf16[16,64,128]{2,1,0:T(8,128)(2,1)}, u32[]{:S(2)}, u32[]{:S(2)}) collective-permute-start(bf16[16,64,128]{2,1,0:T(8,128)(2,1)} %convolution_convert_fusion), channel_id=1, source_target_pairs={{4,0},{6,2},{8,4},{10,6},{12,8},{14,10},{5,1},{7,3},{9,5},{11,7},{... | collective-permute-start | bytes 786440 | tf_op jit(solution)/shard_map/ppermute | solution.py:26
  88.5 0.9 constant_dynamic-update-slice_fusion.6
  89.5 0.9 constant_dynamic-update-slice_fusion.5
  90.4 2.2 %gather_fusion.2 = bf16[128,64,128]{2,1,0:T(8,128)(2,1)} fusion(bf16[40,64,128]{2,1,0:T(8,128)(2,1)S(1)} %constant_dynamic-update-slice_fusion.5, s32[1024]{0:T(1024)S(1)} %pad_clamp_fusion.1), kind=kCustom, calls=%fused_computation.2 | custom fusion | bytes 4194816 | tf_op jit(solution)/shard_map/gather | solution.py:30
  92.5 2.2 %fusion.6 = bf16[8,64,128]{2,1,0:T(8,128)(2,1)S(1)} fusion(f32[8,128,64]{1,2,0:T(8,128)S(1)} %fusion.11, bf16[8,16,64,64]{3,2,1,0:T(8,128)(2,1)S(1)} %copy-done, bf16[8,16,64,128]{3,2,1,0:T(8,128)(2,1)} %bitcast.78), kind=kOutput, calls=%fused_computation.15 | convolution fusion | flops 134348800 | bytes 3538944 | tf_op jit(solution)/shard_map/pkab,pkbc->pac/dot_general | solution.py:31
  94.8 1.0 fusion.12
  95.8 1.0 constant_dynamic-update-slice_fusion.4
  96.8 1.0 constant_dynamic-update-slice_fusion.3
  97.8 1.0 constant_dynamic-update-slice_fusion.2
  98.8 1.0 constant_dynamic-update-slice_fusion.1
  99.8 1.0 constant_dynamic-update-slice_fusion
  100.8 3.1 %gather_fusion.1 = bf16[256,64,128]{2,1,0:T(8,128)(2,1)} fusion(bf16[80,64,128]{2,1,0:T(8,128)(2,1)S(1)} %constant_dynamic-update-slice_fusion, s32[1024]{0:T(1024)S(1)} %pad_clamp_fusion.2), kind=kCustom, calls=%fused_computation.1 | custom fusion | bytes 8389632 | tf_op jit(solution)/shard_map/gather | solution.py:30
  103.9 5.7 %fusion.1 = bf16[16,256,128]{1,2,0:T(8,128)(2,1)S(1)} fusion(bf16[16,256,64]{1,2,0:T(8,128)(2,1)} %param.15, f32[16,128,256,1]{2,1,3,0:T(8,128)} %fusion.10, f32[16,128,64]{1,2,0:T(8,128)} %fusion.12, bf16[16,16,64,64]{3,2,1,0:T(8,128)(2,1)} %param.18, bf16[16,16,64,128]{3,2,1,0:T(8,128)(2,1)} %bitcast.77), kind=kOutput, calls=%fused_computation.6 | convolution fusion | flops 336855040 | bytes 10485760 | tf_op jit(solution)/shard_map/lpr,lrc->lpc/dot_general | solution.py:100
  109.5 1.3 %copy.19 = bf16[16,256,128]{2,1,0:T(8,128)(2,1)} copy(bf16[16,256,128]{1,2,0:T(8,128)(2,1)S(1)} %fusion.1) | data formatting | bytes 2097152 | tf_op jit(solution)/shard_map/convert_element_type | solution.py:101
  (43 shorter events, 0.4 us)
Async XLA Ops:
  0.0 92.5 %copy-start = (bf16[8,16,64,64]{3,2,1,0:T(8,128)(2,1)S(1)}, bf16[8,16,64,64]{3,2,1,0:T(8,128)(2,1)}, u32[]{:S(2)}) copy-start(bf16[8,16,64,64]{3,2,1,0:T(8,128)(2,1)} %param.19) | copy-start | bytes 3145732
  0.0 4.6 %copy-start.2 = (bf16[8,64,64]{2,1,0:T(8,128)(2,1)S(1)}, bf16[8,64,64]{2,1,0:T(8,128)(2,1)}, u32[]{:S(2)}) copy-start(bf16[8,64,64]{2,1,0:T(8,128)(2,1)} %param.17) | copy-start | bytes 196612
  0.0 21.2 %copy-start.5 = (s32[16,12]{1,0:T(8,128)S(1)}, s32[16,12]{1,0:T(8,128)}, u32[]{:S(2)}) copy-start(s32[16,12]{1,0:T(8,128)} %param.14) | copy-start | bytes 2308
  0.0 21.3 %copy-start.8 = (s32[4,16]{1,0:T(4,128)S(1)}, s32[4,16]{1,0:T(4,128)}, u32[]{:S(2)}) copy-start(s32[4,16]{1,0:T(4,128)} %param.23) | copy-start | bytes 772
  0.0 21.4 %copy-start.7 = (s32[8,16]{1,0:T(8,128)S(1)}, s32[8,16]{1,0:T(8,128)}, u32[]{:S(2)}) copy-start(s32[8,16]{1,0:T(8,128)} %param.22) | copy-start | bytes 1540
  0.0 21.5 %copy-start.6 = (s32[16,16]{1,0:T(8,128)S(1)}, s32[16,16]{1,0:T(8,128)}, u32[]{:S(2)}) copy-start(s32[16,16]{1,0:T(8,128)} %param.21) | copy-start | bytes 3076
  5.7 48.0 %collective-permute-start.10 = (bf16[4,64,128]{2,1,0:T(8,128)(2,1)S(1)}, bf16[4,64,128]{2,1,0:T(8,128)(2,1)S(1)}, u32[]{:S(2)}, u32[]{:S(2)}) collective-permute-start(bf16[4,64,128]{2,1,0:T(8,128)(2,1)S(1)} %bitcast_reduce_fusion.1), channel_id=1, source_target_pairs={{0,4},{2,6},{4,8},{6,10},{8,12},{10,14},{1,5},{3,7},{5,9},{7,11},{... | collective-permute-start | bytes 196616 | tf_op jit(solution)/shard_map/ppermute | solution.py:26
  7.0 51.5 %collective-permute-start.11 = (bf16[4,64,128]{2,1,0:T(8,128)(2,1)S(1)}, bf16[4,64,128]{2,1,0:T(8,128)(2,1)}, u32[]{:S(2)}, u32[]{:S(2)}) collective-permute-start(bf16[4,64,128]{2,1,0:T(8,128)(2,1)S(1)} %bitcast_reduce_fusion.1), channel_id=1, source_target_pairs={{0,2},{2,4},{4,6},{6,8},{8,10},{10,12},{12,14},{1,3},{3,5},{5,7},{... | collective-permute-start | bytes 196616 | tf_op jit(solution)/shard_map/ppermute | solution.py:26
  10.4 53.0 %collective-permute-start.12 = (bf16[4,64,128]{2,1,0:T(8,128)(2,1)S(1)}, bf16[4,64,128]{2,1,0:T(8,128)(2,1)}, u32[]{:S(2)}, u32[]{:S(2)}) collective-permute-start(bf16[4,64,128]{2,1,0:T(8,128)(2,1)S(1)} %bitcast_reduce_fusion.1), channel_id=1, source_target_pairs={{2,0},{4,2},{6,4},{8,6},{10,8},{12,10},{14,12},{3,1},{5,3},{7,5},{... | collective-permute-start | bytes 196616 | tf_op jit(solution)/shard_map/ppermute | solution.py:26
  15.3 6.3 %collective-permute-start.1 = (bf16[256,128]{1,0:T(8,128)(2,1)S(1)}, bf16[256,128]{1,0:T(8,128)(2,1)S(1)}, u32[]{:S(2)}, u32[]{:S(2)}) collective-permute-start(bf16[256,128]{1,0:T(8,128)(2,1)S(1)} %get-tuple-element.6), channel_id=1, source_target_pairs={{2,0},{4,2},{6,4},{8,6},{10,8},{12,10},{14,12},{3,1},{5,3},{7,5},{... | collective-permute-start | bytes 196616 | tf_op jit(solution)/shard_map/ppermute | solution.py:18
  19.3 7.1 %collective-permute-start = (bf16[256,128]{1,0:T(8,128)(2,1)S(1)}, bf16[256,128]{1,0:T(8,128)(2,1)S(1)}, u32[]{:S(2)}, u32[]{:S(2)}) collective-permute-start(bf16[256,128]{1,0:T(8,128)(2,1)S(1)} %get-tuple-element.5), channel_id=1, source_target_pairs={{0,2},{2,4},{4,6},{6,8},{8,10},{10,12},{12,14},{1,3},{3,5},{5,7},{... | collective-permute-start | bytes 196616 | tf_op jit(solution)/shard_map/ppermute | solution.py:17
  21.7 47.3 %collective-permute-start.13 = (bf16[4,64,128]{2,1,0:T(8,128)(2,1)S(1)}, bf16[4,64,128]{2,1,0:T(8,128)(2,1)}, u32[]{:S(2)}, u32[]{:S(2)}) collective-permute-start(bf16[4,64,128]{2,1,0:T(8,128)(2,1)S(1)} %bitcast_reduce_fusion.1), channel_id=1, source_target_pairs={{4,0},{6,2},{8,4},{10,6},{12,8},{14,10},{5,1},{7,3},{9,5},{11,7},{... | collective-permute-start | bytes 196616 | tf_op jit(solution)/shard_map/ppermute | solution.py:26
  26.3 47.4 %collective-permute-start.6 = (bf16[8,64,128]{2,1,0:T(8,128)(2,1)}, bf16[8,64,128]{2,1,0:T(8,128)(2,1)}, u32[]{:S(2)}, u32[]{:S(2)}) collective-permute-start(bf16[8,64,128]{2,1,0:T(8,128)(2,1)} %bitcast_reduce_fusion), channel_id=1, source_target_pairs={{0,4},{2,6},{4,8},{6,10},{8,12},{10,14},{1,5},{3,7},{5,9},{7,11},{... | collective-permute-start | bytes 393224 | tf_op jit(solution)/shard_map/ppermute | solution.py:26
  53.8 0.6 copy-start.4
  54.4 22.6 %collective-permute-start.7 = (bf16[8,64,128]{2,1,0:T(8,128)(2,1)}, bf16[8,64,128]{2,1,0:T(8,128)(2,1)}, u32[]{:S(2)}, u32[]{:S(2)}) collective-permute-start(bf16[8,64,128]{2,1,0:T(8,128)(2,1)} %bitcast_reduce_fusion), channel_id=1, source_target_pairs={{0,2},{2,4},{4,6},{6,8},{8,10},{10,12},{12,14},{1,3},{3,5},{5,7},{... | collective-permute-start | bytes 393224 | tf_op jit(solution)/shard_map/ppermute | solution.py:26
  58.5 24.8 %collective-permute-start.8 = (bf16[8,64,128]{2,1,0:T(8,128)(2,1)}, bf16[8,64,128]{2,1,0:T(8,128)(2,1)}, u32[]{:S(2)}, u32[]{:S(2)}) collective-permute-start(bf16[8,64,128]{2,1,0:T(8,128)(2,1)} %bitcast_reduce_fusion), channel_id=1, source_target_pairs={{2,0},{4,2},{6,4},{8,6},{10,8},{12,10},{14,12},{3,1},{5,3},{7,5},{... | collective-permute-start | bytes 393224 | tf_op jit(solution)/shard_map/ppermute | solution.py:26
  63.4 26.0 %collective-permute-start.9 = (bf16[8,64,128]{2,1,0:T(8,128)(2,1)}, bf16[8,64,128]{2,1,0:T(8,128)(2,1)}, u32[]{:S(2)}, u32[]{:S(2)}) collective-permute-start(bf16[8,64,128]{2,1,0:T(8,128)(2,1)} %bitcast_reduce_fusion), channel_id=1, source_target_pairs={{4,0},{6,2},{8,4},{10,6},{12,8},{14,10},{5,1},{7,3},{9,5},{11,7},{... | collective-permute-start | bytes 393224 | tf_op jit(solution)/shard_map/ppermute | solution.py:26
  69.0 26.9 %collective-permute-start.2 = (bf16[16,64,128]{2,1,0:T(8,128)(2,1)}, bf16[16,64,128]{2,1,0:T(8,128)(2,1)}, u32[]{:S(2)}, u32[]{:S(2)}) collective-permute-start(bf16[16,64,128]{2,1,0:T(8,128)(2,1)} %convolution_convert_fusion), channel_id=1, source_target_pairs={{0,4},{2,6},{4,8},{6,10},{8,12},{10,14},{1,5},{3,7},{5,9},{7,11},{... | collective-permute-start | bytes 786440 | tf_op jit(solution)/shard_map/ppermute | solution.py:26
  71.9 1.7 %copy-start.3 = (bf16[8,64,64]{2,1,0:T(8,128)(2,1)S(1)}, bf16[8,64,64]{2,1,0:T(8,128)(2,1)}, u32[]{:S(2)}) copy-start(bf16[8,64,64]{2,1,0:T(8,128)(2,1)} %param.17) | copy-start | bytes 196612
  73.7 23.1 %collective-permute-start.3 = (bf16[16,64,128]{2,1,0:T(8,128)(2,1)}, bf16[16,64,128]{2,1,0:T(8,128)(2,1)}, u32[]{:S(2)}, u32[]{:S(2)}) collective-permute-start(bf16[16,64,128]{2,1,0:T(8,128)(2,1)} %convolution_convert_fusion), channel_id=1, source_target_pairs={{0,2},{2,4},{4,6},{6,8},{8,10},{10,12},{12,14},{1,3},{3,5},{5,7},{... | collective-permute-start | bytes 786440 | tf_op jit(solution)/shard_map/ppermute | solution.py:26
  77.0 21.8 %collective-permute-start.4 = (bf16[16,64,128]{2,1,0:T(8,128)(2,1)}, bf16[16,64,128]{2,1,0:T(8,128)(2,1)}, u32[]{:S(2)}, u32[]{:S(2)}) collective-permute-start(bf16[16,64,128]{2,1,0:T(8,128)(2,1)} %convolution_convert_fusion), channel_id=1, source_target_pairs={{2,0},{4,2},{6,4},{8,6},{10,8},{12,10},{14,12},{3,1},{5,3},{7,5},{... | collective-permute-start | bytes 786440 | tf_op jit(solution)/shard_map/ppermute | solution.py:26
  83.3 16.5 %collective-permute-start.5 = (bf16[16,64,128]{2,1,0:T(8,128)(2,1)}, bf16[16,64,128]{2,1,0:T(8,128)(2,1)}, u32[]{:S(2)}, u32[]{:S(2)}) collective-permute-start(bf16[16,64,128]{2,1,0:T(8,128)(2,1)} %convolution_convert_fusion), channel_id=1, source_target_pairs={{4,0},{6,2},{8,4},{10,6},{12,8},{14,10},{5,1},{7,3},{9,5},{11,7},{... | collective-permute-start | bytes 786440 | tf_op jit(solution)/shard_map/ppermute | solution.py:26
  92.5 2.3 %copy-start.1 = (bf16[16,64,64]{2,1,0:T(8,128)(2,1)S(1)}, bf16[16,64,64]{2,1,0:T(8,128)(2,1)}, u32[]{:S(2)}) copy-start(bf16[16,64,64]{2,1,0:T(8,128)(2,1)} %param.16) | copy-start | bytes 393220
where the time goes:
time: 112 us; the launch traced here: 111 us
  starting transfers between devices  45.6 us (41%)
  matrix products  33 us (29%)
  local copies, waits for them, and re-layouts  30.3 us (27%)
  other arithmetic  1.36 us (1%)
    ppermute x12, starting transfers between devices, from_behind(): return lax.ppermute(array, axis, pairs)  39.7 us
    dot_general x1, matrix products, body(): jnp.einsum('lkpq,lkqc->lpc', near_blocks, partner_rows, preferred_element...  16.7 us
    unnamed x30, local copies, waits for them, and re-layouts  10.8 us
    gather x1, local copies, waits for them, and re-layouts, body(): partner_rows = padded[position]  8.17 us
    gather x3, local copies, waits for them, and re-layouts, couple_level(): picked = gathered[partner_list]  5.95 us
    dot_general x1, matrix products, body(): jnp.einsum('lpr,lrc->lpc', basis, down_zero, preferred_element_type=jnp.f...  5.67 us
    ppermute x1, starting transfers between devices, with_halo(): after = lax.ppermute(leading, axis, down)  3.92 us
    dot_general x2, matrix products, couple_level(): jnp.einsum('pkab,pkbc->pac', matrices, picked, preferred_element_type=jnp...  3.81 us
  transfers between devices with their start and end apart: 14, of which 1 were waited for; matrix products, arithmetic and copies ran while one was open for 43% of the time, Pallas kernels for 0%

commit v1 on v0

v1 whole, which is shorter than its diff:
```python
import functools

import jax
import jax.numpy as jnp
from jax import lax
from jax.experimental import pallas as pl
from jax.experimental.pallas import tpu as pltpu
from jax.sharding import PartitionSpec as P

LEAF = 256
REACH = 2
MIB = 1024 * 1024


def dot(a, b):
    return jnp.dot(a, b, preferred_element_type=jnp.float32)


def dot_t(a, b):
    return lax.dot_general(a, b, (((0,), (0,)), ((), ())), preferred_element_type=jnp.float32)


def up_kernel(x_ref, basis_ref, up_one_ref, up_two_ref, plain_ref, ahead_ref, behind_ref):
    leaves, rank = basis_ref.shape[:2]
    total = leaves + leaves // 2 + leaves // 4

    def put(node, value):
        rows = pl.ds(node * rank, rank)
        plain_ref[rows, :] = value
        ahead_ref[rows, :] = value
        behind_ref[rows, :] = value

    first_one, first_two = leaves, leaves + leaves // 2
    ones = []
    for p in range(leaves // 2):
        pair = []
        for leaf in (2 * p, 2 * p + 1):
            coef = dot(basis_ref[leaf], x_ref[pl.ds(leaf * LEAF, LEAF), :])
            coef = coef.astype(jnp.bfloat16)
            put(leaf, coef)
            pair.append(coef)
        up = up_one_ref[2 * p : 2 * p + 2].reshape(2 * rank, rank)
        coef = dot_t(up, jnp.concatenate(pair, axis=0)).astype(jnp.bfloat16)
        put(first_one + p, coef)
        ones.append(coef)
    for q in range(leaves // 4):
        up = up_two_ref[2 * q : 2 * q + 2].reshape(2 * rank, rank)
        coef = dot_t(up, jnp.concatenate(ones[2 * q : 2 * q + 2], axis=0)).astype(jnp.bfloat16)
        put(first_two + q, coef)
    edge = pl.ds(total * rank, LEAF)
    ahead_ref[edge, :] = x_ref[pl.ds((leaves - 1) * LEAF, LEAF), :]
    behind_ref[edge, :] = x_ref[pl.ds(0, LEAF), :]


def near_kernel(list_ref, x_ref, self_ref, a_ref, b_ref, c_ref, out_ref):
    leaf = pl.program_id(0)

    def rows(slot):
        start = pl.multiple_of(list_ref[leaf, slot] * LEAF, LEAF)
        return x_ref[pl.ds(start, LEAF), :]

    total = dot(self_ref[0, 0], rows(0))
    slot = 3
    for ref in (a_ref, b_ref, c_ref):
        for k in range(ref.shape[1]):
            total += dot(ref[0, k], rows(slot))
            slot += 1
    out_ref[...] = total


def far_kernel(
    zero_list,
    one_list,
    two_list,
    own_edge,
    own_ref,
    before_two,
    before_one,
    after_one,
    after_two,
    x_ref,
    near_ref,
    next_ref,
    prev_ref,
    basis_ref,
    up_one_ref,
    up_two_ref,
    couple_zero_ref,
    couple_one_ref,
    couple_two_ref,
    out_ref,
    zero_buf,
    one_buf,
    two_buf,
    edge_buf,
    sems,
):
    step = pl.program_id(0)
    steps = pl.num_programs(0)
    leaves = zero_list.shape[0]
    rank = basis_ref.shape[1]
    fars = zero_list.shape[1]
    pieces = (before_two, before_one, own_ref, after_one, after_two)
    sizes = (leaves * rank, leaves // 2 * rank, leaves // 4 * rank)

    @pl.when(step == 0)
    def _():
        copies = []
        for i, piece in enumerate(pieces):
            start = 0
            for j, (buf, size) in enumerate(zip((zero_buf, one_buf, two_buf), sizes)):
                copies.append(
                    pltpu.make_async_copy(
                        piece.at[pl.ds(start, size), :],
                        buf.at[pl.ds(i * size, size), :],
                        sems.at[i * 3 + j],
                    )
                )
                start += size
        total = sum(sizes)
        for i, piece in enumerate((before_one, after_one)):
            copies.append(
                pltpu.make_async_copy(
                    piece.at[pl.ds(total, LEAF), :], edge_buf.at[i], sems.at[15 + i]
                )
            )
        for copy in copies:
            copy.start()
        for copy in copies:
            copy.wait()

    def field(matrices, where, node, buf):
        total = None
        for k in range(fars):
            start = pl.multiple_of(where[node, k] * rank, rank)
            term = dot(matrices[k], buf[pl.ds(start, rank), :])
            total = term if total is None else total + term
        return total

    down_two = field(couple_two_ref.at[0], two_list, step, two_buf).astype(jnp.bfloat16)
    for i in range(2):
        down_one = field(couple_one_ref.at[i], one_list, 2 * step + i, one_buf)
        down_one = (down_one + dot(up_two_ref[i], down_two)).astype(jnp.bfloat16)
        for j in range(2):
            n = 2 * i + j
            leaf = 4 * step + n
            down_zero = field(couple_zero_ref.at[n], zero_list, leaf, zero_buf)
            down_zero = (down_zero + dot(up_one_ref[n], down_one)).astype(jnp.bfloat16)
            total = near_ref[pl.ds(n * LEAF, LEAF), :] + dot_t(basis_ref[n], down_zero)
            own_rows = x_ref[pl.ds(n * LEAF, LEAF), :]
            rows = jnp.where(own_edge[0] == 1, own_rows, edge_buf[1])
            total += dot(next_ref[n, 0], rows)
            rows = jnp.where(own_edge[1] == 1, own_rows, edge_buf[0])
            total += dot(prev_ref[n, 0], rows)
            out_ref[pl.ds(n * LEAF, LEAF), :] = total.astype(jnp.bfloat16)


def whole(shape):
    return pl.BlockSpec(shape, lambda *_: (0,) * len(shape))


def body(
    vectors,
    near_blocks,
    near_list,
    basis,
    up_one,
    up_two,
    couple_zero,
    couple_one,
    couple_two,
    far_zero,
    far_one,
    far_two,
):
    leaves = near_list.shape[0]
    nears = near_list.shape[1]
    columns = vectors.shape[1]
    rank = basis.shape[2]
    fars = far_zero.shape[1]
    size = lax.axis_size("space")
    myself = lax.axis_index("space")
    nodes = leaves + leaves // 2 + leaves // 4
    basis_t = jnp.swapaxes(basis, 1, 2)

    plain, ahead, behind = pl.pallas_call(
        up_kernel,
        out_shape=[
            jax.ShapeDtypeStruct((nodes * rank, columns), jnp.bfloat16),
            jax.ShapeDtypeStruct((nodes * rank + LEAF, columns), jnp.bfloat16),
            jax.ShapeDtypeStruct((nodes * rank + LEAF, columns), jnp.bfloat16),
        ],
        compiler_params=pltpu.CompilerParams(vmem_limit_bytes=24 * MIB),
        name="up_pass",
    )(vectors, basis_t, up_one, up_two)

    def shift(array, by):
        return lax.ppermute(
            array, "space", [(i, i + by) for i in range(size) if 0 <= i + by < size]
        )

    before_one = shift(ahead, 1)
    after_one = shift(behind, -1)
    before_two = shift(plain, 2)
    after_two = shift(plain, -2)

    third = (nears - 3) // 3
    near = pl.pallas_call(
        near_kernel,
        grid_spec=pltpu.PrefetchScalarGridSpec(
            num_scalar_prefetch=1,
            grid=(leaves,),
            in_specs=[
                whole(vectors.shape),
                pl.BlockSpec((1, 1, LEAF, LEAF), lambda l, _: (l, 0, 0, 0)),
                pl.BlockSpec((1, third, LEAF, LEAF), lambda l, _: (l, 1, 0, 0)),
                pl.BlockSpec((1, third, LEAF, LEAF), lambda l, _: (l, 2, 0, 0)),
                pl.BlockSpec((1, third, LEAF, LEAF), lambda l, _: (l, 3, 0, 0)),
            ],
            out_specs=pl.BlockSpec((LEAF, columns), lambda l, _: (l, 0)),
        ),
        out_shape=jax.ShapeDtypeStruct((leaves * LEAF, columns), jnp.float32),
        compiler_params=pltpu.CompilerParams(vmem_limit_bytes=24 * MIB),
        cost_estimate=pl.CostEstimate(
            flops=2 * leaves * (nears - 2) * LEAF * LEAF * columns,
            bytes_accessed=2 * leaves * (nears - 2) * LEAF * LEAF + 6 * leaves * LEAF * columns,
            transcendentals=0,
        ),
        name="near_own",
    )(near_list - myself * leaves, vectors, *([near_blocks] * 4))

    first = myself - REACH
    own_edge = jnp.stack([myself == size - 1, myself == 0]).astype(jnp.int32)
    any_spec = pl.BlockSpec(memory_space=pl.ANY)
    return pl.pallas_call(
        far_kernel,
        grid_spec=pltpu.PrefetchScalarGridSpec(
            num_scalar_prefetch=4,
            grid=(leaves // 4,),
            in_specs=[any_spec] * 5
            + [
                pl.BlockSpec((4 * LEAF, columns), lambda q, *_: (q, 0)),
                pl.BlockSpec((4 * LEAF, columns), lambda q, *_: (q, 0)),
                pl.BlockSpec((4, 1, LEAF, LEAF), lambda q, *_: (q, 1, 0, 0)),
                pl.BlockSpec((4, 1, LEAF, LEAF), lambda q, *_: (q, 2, 0, 0)),
                pl.BlockSpec((4, rank, LEAF), lambda q, *_: (q, 0, 0)),
                pl.BlockSpec((4, rank, rank), lambda q, *_: (q, 0, 0)),
                pl.BlockSpec((2, rank, rank), lambda q, *_: (q, 0, 0)),
                pl.BlockSpec((4, fars, rank, rank), lambda q, *_: (q, 0, 0, 0)),
                pl.BlockSpec((2, fars, rank, rank), lambda q, *_: (q, 0, 0, 0)),
                pl.BlockSpec((1, fars, rank, rank), lambda q, *_: (q, 0, 0, 0)),
            ],
            out_specs=pl.BlockSpec((4 * LEAF, columns), lambda q, *_: (q, 0)),
            scratch_shapes=[
                pltpu.VMEM((5 * leaves * rank, columns), jnp.bfloat16),
                pltpu.VMEM((5 * (leaves // 2) * rank, columns), jnp.bfloat16),
                pltpu.VMEM((5 * (leaves // 4) * rank, columns), jnp.bfloat16),
                pltpu.VMEM((2, LEAF, columns), jnp.bfloat16),
                pltpu.SemaphoreType.DMA((17,)),
            ],
        ),
        out_shape=jax.ShapeDtypeStruct(vectors.shape, jnp.bfloat16),
        compiler_params=pltpu.CompilerParams(vmem_limit_bytes=32 * MIB),
        name="far_down",
    )(
        far_zero - first * leaves,
        far_one - first * (leaves // 2),
        far_two - first * (leaves // 4),
        own_edge,
        plain,
        before_two,
        before_one,
        after_one,
        after_two,
        vectors,
        near,
        near_blocks,
        near_blocks,
        basis_t,
        up_one,
        up_two,
        couple_zero,
        couple_one,
        couple_two,
    )


def solution(mesh):
    placed = (
        P(("groups", "space"), "rhs"),
        P("space", None, None, None),
        P("space", None),
        P("space", None, None),
        P("space", None, None),
        P("space", None, None),
        P("space", None, None, None),
        P("space", None, None, None),
        P("space", None, None, None),
        P("space", None),
        P("space", None),
        P("space", None),
    )
    return jax.shard_map(
        body, mesh=mesh, in_specs=placed, out_specs=P(("groups", "space"), "rhs"), check_vma=False
    )
```

time: 112 us -> 53.7 us (0.48)
  the two profiles are of different devices: /device:TPU:24 before, /device:TPU:16 now
where the time goes in v1:
time: 53.7 us; the launch traced here: 53.1 us
  Pallas kernels  22.6 us (42%)
  local copies, waits for them, and re-layouts  13.5 us (25%)
  starting transfers between devices  12.6 us (23%)
  other arithmetic  2.85 us (5%)
  waiting for transfers between devices  1.37 us (3%)
    unnamed x26, local copies, waits for them, and re-layouts  13.5 us
    ppermute x4, starting transfers between devices, shift(): lax.ppermute(array, 'space', [(i, i + by) for i in range(size) if 0 <= i...  12.6 us
    pallas_call x1, Pallas kernels, body(): pl.pallas_call(far_kernel, grid_spec=pltpu.PrefetchScalarGridSpec(num_sca...  12.3 us
    pallas_call x1, Pallas kernels, body(): pl.pallas_call(near_kernel, grid_spec=pltpu.PrefetchScalarGridSpec(num_sc...  8.91 us
    pallas_call x1, Pallas kernels, body(): pl.pallas_call(up_kernel, out_shape=[jax.ShapeDtypeStruct((nodes * rank,...  1.44 us
    ppermute x4, waiting for transfers between devices, shift(): lax.ppermute(array, 'space', [(i, i + by) for i in range(size) if 0 <= i...  1.37 us
  transfers between devices with their start and end apart: 4, of which 1 were waited for; matrix products, arithmetic and copies ran while one was open for 5% of the time, Pallas kernels for 17%

profile of v1, /device:TPU:16, one launch (start us, length us, event | category | flops | bytes accessed | tf_op | source)
XLA Modules:
  0.0 53.1 jit_solution(300853821528733752)
XLA Ops:
  0.0 0.0 copy-start.1
  0.0 1.2 %copy-done.1 = bf16[4096,128]{1,0:T(8,128)(2,1)S(1)} copy-done((bf16[4096,128]{1,0:T(8,128)(2,1)S(1)}, bf16[4096,128]{1,0:T(8,128)(2,1)}, u32[]{:S(2)}) %copy-start.1) | copy-done | bytes 1048600
  1.2 0.0 copy-start.5
  1.2 1.0 %copy-done.5 = bf16[16,256,64]{1,2,0:T(8,128)(2,1)S(1)} copy-done((bf16[16,256,64]{1,2,0:T(8,128)(2,1)S(1)}, bf16[16,256,64]{1,2,0:T(8,128)(2,1)}, u32[]{:S(2)}) %copy-start.5) | copy-done | bytes 524312
  2.3 0.0 copy-start.9
  2.3 0.9 %copy-done.9 = bf16[16,64,64]{2,1,0:T(8,128)(2,1)S(1)} copy-done((bf16[16,64,64]{2,1,0:T(8,128)(2,1)S(1)}, bf16[16,64,64]{2,1,0:T(8,128)(2,1)}, u32[]{:S(2)}) %copy-start.9) | copy-done | bytes 131096
  3.2 0.0 copy-start.11
  3.2 0.9 %copy-done.11 = bf16[8,64,64]{2,1,0:T(8,128)(2,1)S(1)} copy-done((bf16[8,64,64]{2,1,0:T(8,128)(2,1)S(1)}, bf16[8,64,64]{2,1,0:T(8,128)(2,1)}, u32[]{:S(2)}) %copy-start.11) | copy-done | bytes 65560
  4.1 1.4 %up_pass.1 = (bf16[1792,128]{1,0:T(8,128)(2,1)S(1)}, bf16[2048,128]{1,0:T(8,128)(2,1)S(1)}, bf16[2048,128]{1,0:T(8,128)(2,1)S(1)}) custom-call(bf16[4096,128]{1,0:T(8,128)(2,1)S(1)} %copy-done.1, bf16[16,64,256]{2,1,0:T(8,128)(2,1)S(1)} %bitcast.3, bf16[16,64,64]{2,1,0:T(8,128)(2,1)S(1)} %copy-done.9, bf16[8,64,64]{2,1,0:T(8,128)(2,1)S(1)} %copy-done.11), custom_call_target="tpu_custom_call" | custom-call | tf_op jit(solution)/shard_map/up_pass/pallas_call | solution.py:186
  5.6 2.4 %collective-permute-start.3 = (bf16[1792,128]{1,0:T(8,128)(2,1)S(1)}, bf16[1792,128]{1,0:T(8,128)(2,1)S(1)}, u32[]{:S(2)}, u32[]{:S(2)}) collective-permute-start(bf16[1792,128]{1,0:T(8,128)(2,1)S(1)} %get-tuple-element.8.own_ref), channel_id=1, source_target_pairs={{4,0},{6,2},{8,4},{10,6},{12,8},{14,10},{5,1},{7,3},{9,5},{11,7},{... | collective-permute-start | bytes 1376264 | tf_op jit(solution)/shard_map/ppermute | solution.py:198
  7.9 3.5 %collective-permute-start = (bf16[1792,128]{1,0:T(8,128)(2,1)S(1)}, bf16[1792,128]{1,0:T(8,128)(2,1)S(1)}, u32[]{:S(2)}, u32[]{:S(2)}) collective-permute-start(bf16[1792,128]{1,0:T(8,128)(2,1)S(1)} %get-tuple-element.8.own_ref), channel_id=1, source_target_pairs={{0,4},{2,6},{4,8},{6,10},{8,12},{10,14},{1,5},{3,7},{5,9},{7,11},{... | collective-permute-start | bytes 1376264 | tf_op jit(solution)/shard_map/ppermute | solution.py:198
  11.4 3.4 %collective-permute-start.1 = (bf16[2048,128]{1,0:T(8,128)(2,1)S(1)}, bf16[2048,128]{1,0:T(8,128)(2,1)S(1)}, u32[]{:S(2)}, u32[]{:S(2)}) collective-permute-start(bf16[2048,128]{1,0:T(8,128)(2,1)S(1)} %get-tuple-element.9), channel_id=1, source_target_pairs={{0,2},{2,4},{4,6},{6,8},{8,10},{10,12},{12,14},{1,3},{3,5},{5,7},{... | collective-permute-start | bytes 1572872 | tf_op jit(solution)/shard_map/ppermute | solution.py:198
  14.9 3.3 %collective-permute-start.2 = (bf16[2048,128]{1,0:T(8,128)(2,1)S(1)}, bf16[2048,128]{1,0:T(8,128)(2,1)S(1)}, u32[]{:S(2)}, u32[]{:S(2)}) collective-permute-start(bf16[2048,128]{1,0:T(8,128)(2,1)S(1)} %get-tuple-element.10), channel_id=1, source_target_pairs={{2,0},{4,2},{6,4},{8,6},{10,8},{12,10},{14,12},{3,1},{5,3},{7,5},{... | collective-permute-start | bytes 1572872 | tf_op jit(solution)/shard_map/ppermute | solution.py:198
  18.2 0.7 %broadcast_subtract_fusion.2.one_list = s32[8,16]{1,0:T(8,128)S(1)} fusion(s32[8,16]{1,0:T(8,128)} %param.22, s32[]{:T(128)S(6)} %mul.13), kind=kLoop, calls=%fused_computation.2 | loop fusion | flops 128 | bytes 1028 | tf_op jit(solution)/shard_map/sub | solution.py:267
  18.9 0.7 %broadcast_subtract_fusion.list_ref = s32[16,12]{1,0:T(8,128)S(1)} fusion(s32[16,12]{1,0:T(8,128)} %param.14, s32[]{:T(128)S(6)} %mul.15), kind=kLoop, calls=%fused_computation | loop fusion | flops 192 | bytes 1540 | tf_op jit(solution)/shard_map/sub | solution.py:230
  19.6 0.7 %broadcast_subtract_fusion.1.zero_list = s32[16,16]{1,0:T(8,128)S(1)} fusion(s32[16,16]{1,0:T(8,128)} %param.21, s32[]{:T(128)S(6)} %mul.12), kind=kLoop, calls=%fused_computation.1 | loop fusion | flops 256 | bytes 2052 | tf_op jit(solution)/shard_map/sub | solution.py:266
  20.3 0.1 add_convert_fusion.own_edge
  20.4 0.7 %broadcast_subtract_fusion.3.two_list = s32[4,16]{1,0:T(4,128)S(1)} fusion(s32[4,16]{1,0:T(4,128)} %param.23, s32[]{:T(128)S(6)} %mul.14), kind=kLoop, calls=%fused_computation.4 | loop fusion | flops 64 | bytes 516 | tf_op jit(solution)/shard_map/sub | solution.py:268
  21.1 0.0 copy-start
  21.1 8.2 %copy-done = bf16[16,12,256,256]{3,2,1,0:T(8,128)(2,1)S(1)} copy-done((bf16[16,12,256,256]{3,2,1,0:T(8,128)(2,1)S(1)}, bf16[16,12,256,256]{3,2,1,0:T(8,128)(2,1)}, u32[]{:S(2)}) %copy-start) | copy-done | bytes 25165848
  29.2 0.0 copy-start.2
  29.2 1.2 %copy-done.2 = bf16[4096,128]{1,0:T(8,128)(2,1)S(1)} copy-done((bf16[4096,128]{1,0:T(8,128)(2,1)S(1)}, bf16[4096,128]{1,0:T(8,128)(2,1)}, u32[]{:S(2)}) %copy-start.2) | copy-done | bytes 1048600
  30.5 0.0 copy-start.3
  30.5 0.0 copy-start.4
  30.5 0.0 copy-start.6
  30.5 0.0 copy-start.7
  30.5 0.0 copy-start.8
  30.5 0.0 copy-start.10
  30.5 0.0 copy-start.12
  30.5 8.9 %near_own.1.near_ref = f32[4096,128]{1,0:T(8,128)S(1)} custom-call(s32[16,12]{1,0:T(8,128)S(1)} %broadcast_subtract_fusion.list_ref, bf16[4096,128]{1,0:T(8,128)(2,1)S(1)} %copy-done.2, bf16[16,12,256,256]{3,2,1,0:T(8,128)(2,1)S(1)} %copy-done, bf16[16,12,256,256]{3,2,1,0:T(8,128)(2,1)S(1)} %copy-done, bf16[16,12,256,256]{3,2,1,0:T(8,128)(2,1)S(1)} %copy-done, ...), custom_call_target="tpu_custom_call" | custom-call | flops 2684354560 | bytes 24117248 | tf_op jit(solution)/shard_map/near_own/pallas_call | solution.py:208
  39.4 0.0 collective-permute-done.3.after_two
  39.4 0.0 collective-permute-done.before_two
  39.4 0.0 collective-permute-done.1.before_one
  39.4 1.4 %collective-permute-done.2.after_one = bf16[2048,128]{1,0:T(8,128)(2,1)S(1)} collective-permute-done((bf16[2048,128]{1,0:T(8,128)(2,1)S(1)}, bf16[2048,128]{1,0:T(8,128)(2,1)S(1)}, u32[]{:S(2)}, u32[]{:S(2)}) %collective-permute-start.2) | collective-permute-done | bytes 524320 | tf_op jit(solution)/shard_map/ppermute | solution.py:198
  40.8 0.0 copy-done.3
  40.8 0.0 copy-done.4
  40.8 0.0 copy-done.6
  40.8 0.0 copy-done.7
  40.8 0.0 copy-done.8
  40.8 0.0 copy-done.10
  40.8 0.0 copy-done.12
  40.9 12.3 %far_down.1 = bf16[4096,128]{1,0:T(8,128)(2,1)} custom-call(s32[16,16]{1,0:T(8,128)S(1)} %broadcast_subtract_fusion.1.zero_list, s32[8,16]{1,0:T(8,128)S(1)} %broadcast_subtract_fusion.2.one_list, s32[4,16]{1,0:T(4,128)S(1)} %broadcast_subtract_fusion.3.two_list, s32[2]{0:T(128)S(1)} %add_convert_fusion.own_edge, ...), custom_call_target="tpu_custom_call" | custom-call | tf_op jit(solution)/shard_map/far_down/pallas_call | solution.py:235
Async XLA Ops:
  0.0 1.2 %copy-start.1 = (bf16[4096,128]{1,0:T(8,128)(2,1)S(1)}, bf16[4096,128]{1,0:T(8,128)(2,1)}, u32[]{:S(2)}) copy-start(bf16[4096,128]{1,0:T(8,128)(2,1)} %x_ref.5) | copy-start | bytes 3145732
  1.2 1.0 %copy-start.5 = (bf16[16,256,64]{1,2,0:T(8,128)(2,1)S(1)}, bf16[16,256,64]{1,2,0:T(8,128)(2,1)}, u32[]{:S(2)}) copy-start(bf16[16,256,64]{1,2,0:T(8,128)(2,1)} %param.15) | copy-start | bytes 1572868
  2.3 0.9 %copy-start.9 = (bf16[16,64,64]{2,1,0:T(8,128)(2,1)S(1)}, bf16[16,64,64]{2,1,0:T(8,128)(2,1)}, u32[]{:S(2)}) copy-start(bf16[16,64,64]{2,1,0:T(8,128)(2,1)} %up_one_ref.3) | copy-start | bytes 393220
  3.2 0.9 %copy-start.11 = (bf16[8,64,64]{2,1,0:T(8,128)(2,1)S(1)}, bf16[8,64,64]{2,1,0:T(8,128)(2,1)}, u32[]{:S(2)}) copy-start(bf16[8,64,64]{2,1,0:T(8,128)(2,1)} %up_two_ref.3) | copy-start | bytes 196612
  5.6 33.9 %collective-permute-start.3 = (bf16[1792,128]{1,0:T(8,128)(2,1)S(1)}, bf16[1792,128]{1,0:T(8,128)(2,1)S(1)}, u32[]{:S(2)}, u32[]{:S(2)}) collective-permute-start(bf16[1792,128]{1,0:T(8,128)(2,1)S(1)} %get-tuple-element.8.own_ref), channel_id=1, source_target_pairs={{4,0},{6,2},{8,4},{10,6},{12,8},{14,10},{5,1},{7,3},{9,5},{11,7},{... | collective-permute-start | bytes 1376264 | tf_op jit(solution)/shard_map/ppermute | solution.py:198
  7.9 31.5 %collective-permute-start = (bf16[1792,128]{1,0:T(8,128)(2,1)S(1)}, bf16[1792,128]{1,0:T(8,128)(2,1)S(1)}, u32[]{:S(2)}, u32[]{:S(2)}) collective-permute-start(bf16[1792,128]{1,0:T(8,128)(2,1)S(1)} %get-tuple-element.8.own_ref), channel_id=1, source_target_pairs={{0,4},{2,6},{4,8},{6,10},{8,12},{10,14},{1,5},{3,7},{5,9},{7,11},{... | collective-permute-start | bytes 1376264 | tf_op jit(solution)/shard_map/ppermute | solution.py:198
  11.4 28.0 %collective-permute-start.1 = (bf16[2048,128]{1,0:T(8,128)(2,1)S(1)}, bf16[2048,128]{1,0:T(8,128)(2,1)S(1)}, u32[]{:S(2)}, u32[]{:S(2)}) collective-permute-start(bf16[2048,128]{1,0:T(8,128)(2,1)S(1)} %get-tuple-element.9), channel_id=1, source_target_pairs={{0,2},{2,4},{4,6},{6,8},{8,10},{10,12},{12,14},{1,3},{3,5},{5,7},{... | collective-permute-start | bytes 1572872 | tf_op jit(solution)/shard_map/ppermute | solution.py:198
  14.9 26.0 %collective-permute-start.2 = (bf16[2048,128]{1,0:T(8,128)(2,1)S(1)}, bf16[2048,128]{1,0:T(8,128)(2,1)S(1)}, u32[]{:S(2)}, u32[]{:S(2)}) collective-permute-start(bf16[2048,128]{1,0:T(8,128)(2,1)S(1)} %get-tuple-element.10), channel_id=1, source_target_pairs={{2,0},{4,2},{6,4},{8,6},{10,8},{12,10},{14,12},{3,1},{5,3},{7,5},{... | collective-permute-start | bytes 1572872 | tf_op jit(solution)/shard_map/ppermute | solution.py:198
  21.1 8.2 %copy-start = (bf16[16,12,256,256]{3,2,1,0:T(8,128)(2,1)S(1)}, bf16[16,12,256,256]{3,2,1,0:T(8,128)(2,1)}, u32[]{:S(2)}) copy-start(bf16[16,12,256,256]{3,2,1,0:T(8,128)(2,1)} %prev_ref.1) | copy-start | bytes 75497472
  29.2 1.2 %copy-start.2 = (bf16[4096,128]{1,0:T(8,128)(2,1)S(1)}, bf16[4096,128]{1,0:T(8,128)(2,1)}, u32[]{:S(2)}) copy-start(bf16[4096,128]{1,0:T(8,128)(2,1)} %x_ref.5) | copy-start | bytes 3145732
  30.5 10.4 %copy-start.3 = (bf16[4096,128]{1,0:T(8,128)(2,1)S(1)}, bf16[4096,128]{1,0:T(8,128)(2,1)}, u32[]{:S(2)}) copy-start(bf16[4096,128]{1,0:T(8,128)(2,1)} %x_ref.5) | copy-start | bytes 3145732
  30.5 10.4 %copy-start.4 = (bf16[16,16,64,64]{3,2,1,0:T(8,128)(2,1)S(1)}, bf16[16,16,64,64]{3,2,1,0:T(8,128)(2,1)}, u32[]{:S(2)}) copy-start(bf16[16,16,64,64]{3,2,1,0:T(8,128)(2,1)} %couple_zero_ref.1) | copy-start | bytes 6291460
  30.5 10.4 %copy-start.6 = (bf16[16,256,64]{1,2,0:T(8,128)(2,1)S(1)}, bf16[16,256,64]{1,2,0:T(8,128)(2,1)}, u32[]{:S(2)}) copy-start(bf16[16,256,64]{1,2,0:T(8,128)(2,1)} %param.15) | copy-start | bytes 1572868
  30.5 10.4 %copy-start.7 = (bf16[8,16,64,64]{3,2,1,0:T(8,128)(2,1)S(1)}, bf16[8,16,64,64]{3,2,1,0:T(8,128)(2,1)}, u32[]{:S(2)}) copy-start(bf16[8,16,64,64]{3,2,1,0:T(8,128)(2,1)} %couple_one_ref.1) | copy-start | bytes 3145732
  30.5 10.4 %copy-start.8 = (bf16[4,16,64,64]{3,2,1,0:T(8,128)(2,1)S(1)}, bf16[4,16,64,64]{3,2,1,0:T(8,128)(2,1)}, u32[]{:S(2)}) copy-start(bf16[4,16,64,64]{3,2,1,0:T(8,128)(2,1)} %couple_two_ref.1) | copy-start | bytes 1572868
  30.5 10.4 %copy-start.10 = (bf16[16,64,64]{2,1,0:T(8,128)(2,1)S(1)}, bf16[16,64,64]{2,1,0:T(8,128)(2,1)}, u32[]{:S(2)}) copy-start(bf16[16,64,64]{2,1,0:T(8,128)(2,1)} %up_one_ref.3) | copy-start | bytes 393220
  30.5 10.4 %copy-start.12 = (bf16[8,64,64]{2,1,0:T(8,128)(2,1)S(1)}, bf16[8,64,64]{2,1,0:T(8,128)(2,1)}, u32[]{:S(2)}) copy-start(bf16[8,64,64]{2,1,0:T(8,128)(2,1)} %up_two_ref.3) | copy-start | bytes 196612

commit v2 on v0

v2 whole, which is shorter than its diff:
```python
import jax
import jax.numpy as jnp
from jax import lax
from jax.experimental import pallas as pl
from jax.experimental.pallas import tpu as pltpu
from jax.sharding import PartitionSpec as P

LEAF = 256
REACH = 2
SPAN = 2 * REACH + 1
DEPTH = 4
MIB = 1024 * 1024


def dot(a, b):
    return jnp.dot(a, b, preferred_element_type=jnp.float32)


def dot_t(a, b):
    return lax.dot_general(a, b, (((0,), (0,)), ((), ())), preferred_element_type=jnp.float32)


def up_kernel(
    me_ref, x_hbm, basis_hbm, up_one_hbm, up_two_hbm, plain_ref, pair_ref,
    x_ref, basis_ref, up_one_ref, up_two_ref, sems,
):
    leaves, rank = basis_ref.shape[:2]
    steps = leaves // 4
    copies = []
    for q in range(steps):
        rows = pl.ds(q * 4 * LEAF, 4 * LEAF)
        some = pl.ds(q * 4, 4)
        copies.append(
            (
                pltpu.make_async_copy(x_hbm.at[rows, :], x_ref.at[rows, :], sems.at[2 * q]),
                pltpu.make_async_copy(basis_hbm.at[some], basis_ref.at[some], sems.at[2 * q + 1]),
            )
        )
    ups = (
        pltpu.make_async_copy(up_one_hbm, up_one_ref, sems.at[2 * steps]),
        pltpu.make_async_copy(up_two_hbm, up_two_ref, sems.at[2 * steps + 1]),
    )
    for pair in (copies[0], ups, *copies[1:]):
        for copy in pair:
            copy.start()

    def put(node, value):
        plain_ref[pl.ds(node * rank, rank), :] = value
        pair_ref[pl.ds(2 * LEAF + node * rank, rank), :] = value

    first_one, first_two = leaves, leaves + leaves // 2
    for q in range(steps):
        for copy in copies[q]:
            copy.wait()
        if q == 0:
            for copy in ups:
                copy.wait()
        ones = []
        for p in (2 * q, 2 * q + 1):
            pair = []
            for leaf in (2 * p, 2 * p + 1):
                coef = dot(basis_ref[leaf], x_ref[pl.ds(leaf * LEAF, LEAF), :])
                coef = coef.astype(jnp.bfloat16)
                put(leaf, coef)
                pair.append(coef)
            up = up_one_ref[2 * p : 2 * p + 2].reshape(2 * rank, rank)
            coef = dot_t(up, jnp.concatenate(pair, axis=0)).astype(jnp.bfloat16)
            put(first_one + p, coef)
            ones.append(coef)
        up = up_two_ref[2 * q : 2 * q + 2].reshape(2 * rank, rank)
        put(first_two + q, dot_t(up, jnp.concatenate(ones, axis=0)).astype(jnp.bfloat16))
    odd = lax.rem(me_ref[0], 2)
    last = (leaves - 1) * LEAF
    near_edge = pl.multiple_of((1 - odd) * last, LEAF)
    far_edge = pl.multiple_of(odd * last, LEAF)
    pair_ref[pl.ds(0, LEAF), :] = x_ref[pl.ds(near_edge, LEAF), :]
    pair_ref[pl.ds(LEAF, LEAF), :] = x_ref[pl.ds(far_edge, LEAF), :]


def near_kernel(
    me_ref, list_ref, x_hbm, blocks_hbm, zero_hbm, one_hbm, two_hbm,
    out_ref, edge_ref, zero_ref, one_ref, two_ref,
    x_ref, block_buf, zero_buf, one_buf, two_buf, sems, x_sem, edge_sem, *, size,
):
    leaves, nears = list_ref.shape
    half, quarter = one_buf.shape[1], two_buf.shape[1]
    first = me_ref[0] * leaves

    def copies(leaf, slot):
        pairs = (
            (blocks_hbm.at[leaf, pl.ds(0, 1)], block_buf.at[slot, pl.ds(0, 1)]),
            (blocks_hbm.at[leaf, pl.ds(3, nears - 3)], block_buf.at[slot, pl.ds(1, nears - 3)]),
            (zero_hbm.at[leaf], zero_buf.at[slot]),
            (one_hbm.at[leaf // 2, pl.ds(leaf % 2 * half, half)], one_buf.at[slot]),
            (two_hbm.at[leaf // 4, pl.ds(leaf % 4 * quarter, quarter)], two_buf.at[slot]),
        )
        return [
            pltpu.make_async_copy(src, dst, sems.at[slot, i]) for i, (src, dst) in enumerate(pairs)
        ]

    x_copy = pltpu.make_async_copy(x_hbm, x_ref, x_sem)
    edge_copy = pltpu.make_async_copy(blocks_hbm.at[:, pl.ds(1, 2)], edge_ref, edge_sem)
    x_copy.start()
    for leaf in range(DEPTH - 1):
        for copy in copies(leaf, leaf):
            copy.start()
    x_copy.wait()

    def step(leaf, carry):
        slot = lax.rem(leaf, DEPTH)

        @pl.when(leaf + DEPTH - 1 < leaves)
        def _():
            for copy in copies(leaf + DEPTH - 1, lax.rem(leaf + DEPTH - 1, DEPTH)):
                copy.start()

        @pl.when(leaf + DEPTH - 1 == leaves)
        def _():
            edge_copy.start()

        for copy in copies(leaf, slot):
            copy.wait()
        rows = []
        for k in (0, *range(3, nears)):
            start = pl.multiple_of((list_ref[leaf, k] - first) * LEAF, LEAF)
            rows.append(x_ref[pl.ds(start, LEAF), :])
        blocks = [block_buf[slot, k] for k in range(nears - 2)]
        total = dot(jnp.concatenate(blocks, axis=1), jnp.concatenate(rows, axis=0))
        out_ref[pl.ds(pl.multiple_of(leaf * LEAF, LEAF), LEAF), :] = total
        for buf, ref in ((zero_buf, zero_ref), (one_buf, one_ref), (two_buf, two_ref)):
            wide = [buf[slot, k] for k in range(buf.shape[1])]
            ref[leaf] = jnp.concatenate(wide, axis=1)
        return carry

    lax.fori_loop(0, leaves, step, 0)
    edge_copy.wait()

    for side, here in ((0, me_ref[0] == size - 1), (1, me_ref[0] == 0)):

        @pl.when(here)
        def _():
            def own(leaf, carry):
                rows = pl.ds(pl.multiple_of(leaf * LEAF, LEAF), LEAF)
                out_ref[rows, :] += dot(edge_ref[leaf, side], x_ref[rows, :])
                return carry

            lax.fori_loop(0, leaves, own, 0)


def far_kernel(
    me_ref, zero_list, one_list, two_list,
    own_ref, pair_ref, before_ref, after_ref, low_ref, high_ref,
    near_ref, edge_ref, basis_ref, up_one_ref, up_two_ref, zero_ref, one_ref, two_ref,
    out_ref, zero_buf, one_buf, two_buf, sems,
):
    leaves, fars = zero_list.shape
    rank = basis_ref.shape[1]
    me = me_ref[0]
    odd = lax.rem(me, 2)
    sizes = (leaves * rank, leaves // 2 * rank, leaves // 4 * rank)
    bufs = (zero_buf, one_buf, two_buf)
    pair_at = REACH + 1 - 2 * odd
    diag_at = REACH - 1 + 2 * odd
    plans = (
        (own_ref, 0, (0, 1, 2), REACH),
        (before_ref, 0, (0, 1, 2), 0),
        (after_ref, 0, (0, 1, 2), SPAN - 1),
        (pair_ref, 2 * LEAF, (0, 1, 2), pair_at),
        (low_ref, LEAF, (0,), diag_at),
        (high_ref, 0, (1, 2), diag_at),
    )
    copies = []
    for ref, start, levels, place in plans:
        for level in levels:
            at = pl.multiple_of(place * sizes[level], sizes[level])
            copies.append(
                pltpu.make_async_copy(
                    ref.at[pl.ds(start, sizes[level]), :],
                    bufs[level].at[pl.ds(at, sizes[level]), :],
                    sems.at[len(copies)],
                )
            )
            start += sizes[level]
    for copy in copies:
        copy.start()
    for copy in copies:
        copy.wait()

    def field(wide, where, node, first, buf):
        picked = []
        for k in range(fars):
            start = pl.multiple_of((where[node, k] - first) * rank, rank)
            picked.append(buf[pl.ds(start, rank), :])
        return dot(jnp.concatenate(wide, axis=1), jnp.concatenate(picked, axis=0))

    pair_rows, diag_rows = pair_ref[pl.ds(0, LEAF), :], low_ref[pl.ds(0, LEAF), :]
    edge_rows = jnp.concatenate([pair_rows, diag_rows], axis=0)

    def step(q, carry):
        wide = [two_ref[4 * q + i] for i in range(4)]
        first = (me - REACH) * (leaves // 4)
        down_two = field(wide, two_list, q, first, two_buf).astype(jnp.bfloat16)
        for i in range(2):
            p = 2 * q + i
            wide = [one_ref[2 * p + j] for j in range(2)]
            first = (me - REACH) * (leaves // 2)
            down_one = field(wide, one_list, p, first, one_buf)
            down_one = (down_one + dot(up_two_ref[p], down_two)).astype(jnp.bfloat16)
            for j in range(2):
                leaf = 2 * p + j
                first = (me - REACH) * leaves
                down_zero = field([zero_ref[leaf]], zero_list, leaf, first, zero_buf)
                down_zero = (down_zero + dot(up_one_ref[leaf], down_one)).astype(jnp.bfloat16)
                rows = pl.ds(pl.multiple_of(leaf * LEAF, LEAF), LEAF)
                total = near_ref[rows, :] + dot_t(basis_ref[leaf], down_zero)
                sides = [edge_ref[leaf, odd], edge_ref[leaf, 1 - odd]]
                total += dot(jnp.concatenate(sides, axis=1), edge_rows)
                out_ref[rows, :] = total.astype(jnp.bfloat16)
        return carry

    lax.fori_loop(0, leaves // 4, step, 0)


def body(
    vectors,
    near_blocks,
    near_list,
    basis,
    up_one,
    up_two,
    couple_zero,
    couple_one,
    couple_two,
    far_zero,
    far_one,
    far_two,
):
    leaves, nears = near_list.shape
    columns = vectors.shape[1]
    rank = basis.shape[2]
    fars = far_zero.shape[1]
    size = lax.axis_size("space")
    myself = lax.axis_index("space")
    me = myself.astype(jnp.int32).reshape(1)
    nodes = leaves + leaves // 2 + leaves // 4
    basis_t = jnp.swapaxes(basis, 1, 2)
    bf16 = jnp.bfloat16

    hbm = pl.BlockSpec(memory_space=pltpu.HBM)
    vmem = pl.BlockSpec(memory_space=pltpu.VMEM)
    smem = pl.BlockSpec(memory_space=pltpu.SMEM)

    plain, pair = pl.pallas_call(
        up_kernel,
        in_specs=[smem] + [hbm] * 4,
        out_specs=[vmem] * 2,
        out_shape=[
            jax.ShapeDtypeStruct((nodes * rank, columns), bf16),
            jax.ShapeDtypeStruct((2 * LEAF + nodes * rank, columns), bf16),
        ],
        scratch_shapes=[
            pltpu.VMEM(vectors.shape, bf16),
            pltpu.VMEM(basis_t.shape, bf16),
            pltpu.VMEM(up_one.shape, bf16),
            pltpu.VMEM(up_two.shape, bf16),
            pltpu.SemaphoreType.DMA((leaves // 2 + 2,)),
        ],
        compiler_params=pltpu.CompilerParams(vmem_limit_bytes=16 * MIB),
        name="up_pass",
    )(me, *[pltpu.with_memory_space_constraint(a, pltpu.HBM) for a in (vectors, basis_t, up_one, up_two)])

    def send(array, to):
        return lax.ppermute(
            array, "space", [(i, to(i)) for i in range(size) if 0 <= to(i) < size]
        )

    from_pair = send(pair, lambda i: i + 1 - 2 * (i % 2))
    before = send(plain, lambda i: i + 2)
    after = send(plain, lambda i: i - 2)

    near, edge, wide_zero, wide_one, wide_two = pl.pallas_call(
        lambda *refs: near_kernel(*refs, size=size),
        in_specs=[smem] * 2 + [hbm] * 5,
        out_specs=[vmem] * 5,
        out_shape=[
            jax.ShapeDtypeStruct(vectors.shape, jnp.float32),
            jax.ShapeDtypeStruct((leaves, 2, LEAF, LEAF), bf16),
            jax.ShapeDtypeStruct((leaves, rank, fars * rank), bf16),
            jax.ShapeDtypeStruct((leaves, rank, fars // 2 * rank), bf16),
            jax.ShapeDtypeStruct((leaves, rank, fars // 4 * rank), bf16),
        ],
        scratch_shapes=[
            pltpu.VMEM(vectors.shape, bf16),
            pltpu.VMEM((DEPTH, nears - 2, LEAF, LEAF), bf16),
            pltpu.VMEM((DEPTH, fars, rank, rank), bf16),
            pltpu.VMEM((DEPTH, fars // 2, rank, rank), bf16),
            pltpu.VMEM((DEPTH, fars // 4, rank, rank), bf16),
            pltpu.SemaphoreType.DMA((DEPTH, 5)),
            pltpu.SemaphoreType.DMA,
            pltpu.SemaphoreType.DMA,
        ],
        compiler_params=pltpu.CompilerParams(vmem_limit_bytes=32 * MIB),
        cost_estimate=pl.CostEstimate(
            flops=2 * leaves * (nears - 2) * LEAF * LEAF * columns,
            bytes_accessed=2 * leaves * nears * LEAF * LEAF + 6 * leaves * LEAF * columns,
            transcendentals=0,
        ),
        name="near_own",
    )(
        me,
        near_list,
        *[
            pltpu.with_memory_space_constraint(a, pltpu.HBM)
            for a in (vectors, near_blocks, couple_zero, couple_one, couple_two)
        ],
    )

    from_pair, before, after, near = lax.optimization_barrier((from_pair, before, after, near))
    split = LEAF + leaves * rank
    low = send(from_pair[LEAF : LEAF + split], lambda i: i + 2 - 4 * (i % 2))
    upper = jnp.where(me[0] % 2 == 1, before[leaves * rank :], after[leaves * rank :])
    high = send(upper, lambda i: i + 1 - 2 * (i % 2))

    return pl.pallas_call(
        far_kernel,
        in_specs=[smem] * 4 + [vmem] * 14,
        out_specs=vmem,
        out_shape=jax.ShapeDtypeStruct(vectors.shape, bf16),
        scratch_shapes=[
            pltpu.VMEM((SPAN * leaves * rank, columns), bf16),
            pltpu.VMEM((SPAN * (leaves // 2) * rank, columns), bf16),
            pltpu.VMEM((SPAN * (leaves // 4) * rank, columns), bf16),
            pltpu.SemaphoreType.DMA((15,)),
        ],
        compiler_params=pltpu.CompilerParams(vmem_limit_bytes=32 * MIB),
        name="far_down",
    )(
        me, far_zero, far_one, far_two,
        plain, from_pair, before, after, low, high,
        near, edge, basis_t, up_one, up_two, wide_zero, wide_one, wide_two,
    )


def solution(mesh):
    placed = (
        P(("groups", "space"), "rhs"),
        P("space", None, None, None),
        P("space", None),
        P("space", None, None),
        P("space", None, None),
        P("space", None, None),
        P("space", None, None, None),
        P("space", None, None, None),
        P("space", None, None, None),
        P("space", None),
        P("space", None),
        P("space", None),
    )
    return jax.shard_map(
        body, mesh=mesh, in_specs=placed, out_specs=P(("groups", "space"), "rhs"), check_vma=False
    )
```

time: 112 us -> 47.1 us (0.42)
  the two profiles are of different devices: /device:TPU:24 before, /device:TPU:0 now
where the time goes in v2:
time: 47.1 us; the launch traced here: 46.9 us
  Pallas kernels  29.4 us (62%)
  starting transfers between devices  10.2 us (22%)
  waiting for transfers between devices  6.28 us (13%)
  local copies, waits for them, and re-layouts  0.74 us (2%)
    pallas_call x1, Pallas kernels, body(): pl.pallas_call(lambda *refs: near_kernel(*refs, size=size), in_specs=[sme...  15.8 us
    ppermute x5, starting transfers between devices, send(): lax.ppermute(array, 'space', [(i, to(i)) for i in range(size) if 0 <= to(...  10.2 us
    pallas_call x1, Pallas kernels, body(): pl.pallas_call(far_kernel, in_specs=[smem] * 4 + [vmem] * 14, out_specs=v...  10.1 us
    ppermute x5, waiting for transfers between devices, send(): lax.ppermute(array, 'space', [(i, to(i)) for i in range(size) if 0 <= to(...  6.28 us
    pallas_call x1, Pallas kernels, body(): pl.pallas_call(up_kernel, in_specs=[smem] + [hbm] * 4, out_specs=[vmem] *...  3.47 us
  transfers between devices with their start and end apart: 5, of which 2 were waited for; matrix products, arithmetic and copies ran while one was open for 0% of the time, Pallas kernels for 34%

profile of v2, /device:TPU:0, one launch (start us, length us, event | category | flops | bytes accessed | tf_op | source)
XLA Modules:
  0.0 46.9 jit_solution(888257171040455339)
XLA Ops:
  0.0 3.5 %up_pass.1 = (bf16[1792,128]{1,0:T(8,128)(2,1)S(1)}, bf16[2304,128]{1,0:T(8,128)(2,1)S(1)}) custom-call(s32[1]{0:T(128)} %bitcast.me_ref.refs_0_, bf16[4096,128]{1,0:T(8,128)(2,1)} %refs_2_.1, bf16[16,64,256]{2,1,0:T(8,128)(2,1)} %bitcast.2, bf16[16,64,64]{2,1,0:T(8,128)(2,1)} %up_one_ref.1, bf16[8,64,64]{2,1,0:T(8,128)(2,1)} %up_two_ref.1), custom_call_target="tpu_custom_call" | custom-call | tf_op jit(solution)/shard_map/up_pass/pallas_call | solution.py:253
  3.5 3.0 %collective-permute-start = (bf16[2304,128]{1,0:T(8,128)(2,1)S(1)}, bf16[2304,128]{1,0:T(8,128)(2,1)S(1)}, u32[]{:S(2)}, u32[]{:S(2)}) collective-permute-start(bf16[2304,128]{1,0:T(8,128)(2,1)S(1)} %get-tuple-element.17), channel_id=1, source_target_pairs={{0,2},{2,0},{4,6},{6,4},{8,10},{10,8},{12,14},{14,12},{1,3},{3,1},... | collective-permute-start | bytes 1769480 | tf_op jit(solution)/shard_map/ppermute | solution.py:273
  6.5 1.3 %collective-permute-start.2 = (bf16[1792,128]{1,0:T(8,128)(2,1)S(1)}, bf16[1792,128]{1,0:T(8,128)(2,1)S(1)}, u32[]{:S(2)}, u32[]{:S(2)}) collective-permute-start(bf16[1792,128]{1,0:T(8,128)(2,1)S(1)} %get-tuple-element.16.own_ref), channel_id=1, source_target_pairs={{4,0},{6,2},{8,4},{10,6},{12,8},{14,10},{5,1},{7,3},{9,5},{11,7},{... | collective-permute-start | bytes 1376264 | tf_op jit(solution)/shard_map/ppermute | solution.py:273
  7.8 4.6 %collective-permute-start.1 = (bf16[1792,128]{1,0:T(8,128)(2,1)S(1)}, bf16[1792,128]{1,0:T(8,128)(2,1)S(1)}, u32[]{:S(2)}, u32[]{:S(2)}) collective-permute-start(bf16[1792,128]{1,0:T(8,128)(2,1)S(1)} %get-tuple-element.16.own_ref), channel_id=1, source_target_pairs={{0,4},{2,6},{4,8},{6,10},{8,12},{10,14},{1,5},{3,7},{5,9},{7,11},{... | collective-permute-start | bytes 1376264 | tf_op jit(solution)/shard_map/ppermute | solution.py:273
  12.4 0.0 copy-start.3
  12.4 0.7 %copy-done.3 = s32[16,12]{1,0:T(8,128)S(1)} copy-done((s32[16,12]{1,0:T(8,128)S(1)}, s32[16,12]{1,0:T(8,128)}, u32[]{:S(2)}) %copy-start.3) | copy-done | bytes 792
  13.1 0.0 copy-start
  13.1 0.0 copy-start.1
  13.1 0.0 copy-start.2
  13.1 0.0 copy-start.4
  13.1 0.0 copy-start.5
  13.1 0.0 copy-start.6
  13.1 15.8 %near_own.1 = (f32[4096,128]{1,0:T(8,128)S(1)}, bf16[16,2,256,256]{3,2,1,0:T(8,128)(2,1)S(1)}, bf16[16,64,1024]{2,1,0:T(8,128)(2,1)S(1)}, bf16[16,64,512]{2,1,0:T(8,128)(2,1)S(1)}, bf16[16,64,256]{2,1,0:T(8,128)(2,1)S(1)}) custom-call(s32[1]{0:T(128)} %bitcast.me_ref.refs_0_, s32[16,12]{1,0:T(8,128)S(1)} %copy-done.3, bf16[4096,128]{1,0:T(8,128)(2,1)} %refs_2_.1, ...), custom_call_target="tpu_custom_call" | custom-call | flops 2684354560 | bytes 28311552 | tf_op jit(solution)/shard_map/near_own/pallas_call | solution.py:281
  28.9 0.0 collective-permute-done.2.after_ref
  28.9 0.0 collective-permute-done.1.before_ref
  29.0 0.0 collective-permute-done.pair_ref
  29.0 1.3 %collective-permute-start.3 = (bf16[1280,128]{1,0:T(8,128)(2,1)S(1)}, bf16[1280,128]{1,0:T(8,128)(2,1)S(1)}, u32[]{:S(2)}, u32[]{:S(2)}) collective-permute-start(bf16[1280,128]{1,0:T(8,128)(2,1)S(1)} %slice.9), channel_id=1, source_target_pairs={{0,4},{4,8},{6,2},{8,12},{10,6},{14,10},{1,5},{5,9},{7,3},{9,13},{... | collective-permute-start | bytes 983048 | tf_op jit(solution)/shard_map/ppermute | solution.py:273
  30.3 0.1 collective-permute-start.4
  30.4 5.8 %collective-permute-done.4.high_ref = bf16[768,128]{1,0:T(8,128)(2,1)S(1)} collective-permute-done((bf16[768,128]{1,0:T(8,128)(2,1)S(1)}, bf16[768,128]{1,0:T(8,128)(2,1)S(1)}, u32[]{:S(2)}, u32[]{:S(2)}) %collective-permute-start.4) | collective-permute-done | bytes 196640 | tf_op jit(solution)/shard_map/ppermute | solution.py:273
  36.2 0.5 %collective-permute-done.3.low_ref = bf16[1280,128]{1,0:T(8,128)(2,1)S(1)} collective-permute-done((bf16[1280,128]{1,0:T(8,128)(2,1)S(1)}, bf16[1280,128]{1,0:T(8,128)(2,1)S(1)}, u32[]{:S(2)}, u32[]{:S(2)}) %collective-permute-start.3) | collective-permute-done | bytes 327712 | tf_op jit(solution)/shard_map/ppermute | solution.py:273
  36.7 0.0 copy-done
  36.7 0.0 copy-done.1
  36.7 0.0 copy-done.2
  36.7 0.0 copy-done.4
  36.7 0.0 copy-done.5
  36.7 0.0 copy-done.6
  36.7 10.1 %far_down.1 = bf16[4096,128]{1,0:T(8,128)(2,1)} custom-call(s32[1]{0:T(128)} %bitcast.me_ref.refs_0_, s32[16,16]{1,0:T(8,128)S(1)} %copy-done.4, s32[8,16]{1,0:T(8,128)S(1)} %copy-done.5, s32[4,16]{1,0:T(4,128)S(1)} %copy-done.6, bf16[1792,128]{1,0:T(8,128)(2,1)S(1)} %get-tuple-element.16.own_ref, bf16[2304,128]{1,0:T(8,128)(2,1)S(1)} %collective-permute-done.pair_ref, ...), custom_call_target="tpu_custom_call" | custom-call | tf_op jit(solution)/shard_map/far_down/pallas_call | solution.py:324
  (2 shorter events, 0.0 us)
Async XLA Ops:
  3.5 25.5 %collective-permute-start = (bf16[2304,128]{1,0:T(8,128)(2,1)S(1)}, bf16[2304,128]{1,0:T(8,128)(2,1)S(1)}, u32[]{:S(2)}, u32[]{:S(2)}) collective-permute-start(bf16[2304,128]{1,0:T(8,128)(2,1)S(1)} %get-tuple-element.17), channel_id=1, source_target_pairs={{0,2},{2,0},{4,6},{6,4},{8,10},{10,8},{12,14},{14,12},{1,3},{3,1},... | collective-permute-start | bytes 1769480 | tf_op jit(solution)/shard_map/ppermute | solution.py:273
  6.5 22.5 %collective-permute-start.2 = (bf16[1792,128]{1,0:T(8,128)(2,1)S(1)}, bf16[1792,128]{1,0:T(8,128)(2,1)S(1)}, u32[]{:S(2)}, u32[]{:S(2)}) collective-permute-start(bf16[1792,128]{1,0:T(8,128)(2,1)S(1)} %get-tuple-element.16.own_ref), channel_id=1, source_target_pairs={{4,0},{6,2},{8,4},{10,6},{12,8},{14,10},{5,1},{7,3},{9,5},{11,7},{... | collective-permute-start | bytes 1376264 | tf_op jit(solution)/shard_map/ppermute | solution.py:273
  7.8 21.2 %collective-permute-start.1 = (bf16[1792,128]{1,0:T(8,128)(2,1)S(1)}, bf16[1792,128]{1,0:T(8,128)(2,1)S(1)}, u32[]{:S(2)}, u32[]{:S(2)}) collective-permute-start(bf16[1792,128]{1,0:T(8,128)(2,1)S(1)} %get-tuple-element.16.own_ref), channel_id=1, source_target_pairs={{0,4},{2,6},{4,8},{6,10},{8,12},{10,14},{1,5},{3,7},{5,9},{7,11},{... | collective-permute-start | bytes 1376264 | tf_op jit(solution)/shard_map/ppermute | solution.py:273
  12.4 0.7 %copy-start.3 = (s32[16,12]{1,0:T(8,128)S(1)}, s32[16,12]{1,0:T(8,128)}, u32[]{:S(2)}) copy-start(s32[16,12]{1,0:T(8,128)} %refs_1_.1) | copy-start | bytes 2308
  13.1 23.6 %copy-start = (bf16[16,256,64]{1,2,0:T(8,128)(2,1)S(1)}, bf16[16,256,64]{1,2,0:T(8,128)(2,1)}, u32[]{:S(2)}) copy-start(bf16[16,256,64]{1,2,0:T(8,128)(2,1)} %param.15) | copy-start | bytes 1572868
  13.1 23.6 %copy-start.1 = (bf16[16,64,64]{2,1,0:T(8,128)(2,1)S(1)}, bf16[16,64,64]{2,1,0:T(8,128)(2,1)}, u32[]{:S(2)}) copy-start(bf16[16,64,64]{2,1,0:T(8,128)(2,1)} %up_one_ref.1) | copy-start | bytes 393220
  13.1 23.6 %copy-start.2 = (bf16[8,64,64]{2,1,0:T(8,128)(2,1)S(1)}, bf16[8,64,64]{2,1,0:T(8,128)(2,1)}, u32[]{:S(2)}) copy-start(bf16[8,64,64]{2,1,0:T(8,128)(2,1)} %up_two_ref.1) | copy-start | bytes 196612
  13.1 23.6 %copy-start.4 = (s32[16,16]{1,0:T(8,128)S(1)}, s32[16,16]{1,0:T(8,128)}, u32[]{:S(2)}) copy-start(s32[16,16]{1,0:T(8,128)} %zero_list.1) | copy-start | bytes 3076
  13.1 23.6 %copy-start.5 = (s32[8,16]{1,0:T(8,128)S(1)}, s32[8,16]{1,0:T(8,128)}, u32[]{:S(2)}) copy-start(s32[8,16]{1,0:T(8,128)} %one_list.1) | copy-start | bytes 1540
  13.1 23.6 %copy-start.6 = (s32[4,16]{1,0:T(4,128)S(1)}, s32[4,16]{1,0:T(4,128)}, u32[]{:S(2)}) copy-start(s32[4,16]{1,0:T(4,128)} %two_list.1) | copy-start | bytes 772
  29.0 7.7 %collective-permute-start.3 = (bf16[1280,128]{1,0:T(8,128)(2,1)S(1)}, bf16[1280,128]{1,0:T(8,128)(2,1)S(1)}, u32[]{:S(2)}, u32[]{:S(2)}) collective-permute-start(bf16[1280,128]{1,0:T(8,128)(2,1)S(1)} %slice.9), channel_id=1, source_target_pairs={{0,4},{4,8},{6,2},{8,12},{10,6},{14,10},{1,5},{5,9},{7,3},{9,13},{... | collective-permute-start | bytes 983048 | tf_op jit(solution)/shard_map/ppermute | solution.py:273
  30.3 5.9 %collective-permute-start.4 = (bf16[768,128]{1,0:T(8,128)(2,1)S(1)}, bf16[768,128]{1,0:T(8,128)(2,1)S(1)}, u32[]{:S(2)}, u32[]{:S(2)}) collective-permute-start(bf16[768,128]{1,0:T(8,128)(2,1)S(1)} %slice_select_fusion), channel_id=1, source_target_pairs={{0,2},{2,0},{4,6},{6,4},{8,10},{10,8},{12,14},{14,12},{1,3},{3,1},... | collective-permute-start | bytes 589832 | tf_op jit(solution)/shard_map/ppermute | solution.py:273

commit v3 on v2

v3 whole, which is shorter than its diff:
```python
import jax
import jax.numpy as jnp
from jax import lax
from jax.experimental import pallas as pl
from jax.experimental.pallas import tpu as pltpu
from jax.sharding import PartitionSpec as P

LEAF = 256
REACH = 2
SPAN = 2 * REACH + 1
DEPTH = 4
MIB = 1024 * 1024


def dot(a, b):
    return jnp.dot(a, b, preferred_element_type=jnp.float32)


def dot_t(a, b):
    return lax.dot_general(a, b, (((0,), (0,)), ((), ())), preferred_element_type=jnp.float32)


def up_kernel(
    me_ref, x_hbm, basis_hbm, up_one_hbm, up_two_hbm, plain_ref, pair_ref,
    x_ref, basis_ref, up_one_ref, up_two_ref, sems,
):
    leaves, rank = basis_ref.shape[:2]
    steps = leaves // 4
    copies = []
    for q in range(steps):
        rows = pl.ds(q * 4 * LEAF, 4 * LEAF)
        some = pl.ds(q * 4, 4)
        copies.append(
            (
                pltpu.make_async_copy(x_hbm.at[rows, :], x_ref.at[rows, :], sems.at[2 * q]),
                pltpu.make_async_copy(basis_hbm.at[some], basis_ref.at[some], sems.at[2 * q + 1]),
            )
        )
    ups = (
        pltpu.make_async_copy(up_one_hbm, up_one_ref, sems.at[2 * steps]),
        pltpu.make_async_copy(up_two_hbm, up_two_ref, sems.at[2 * steps + 1]),
    )
    for pair in (*copies, ups):
        for copy in pair:
            copy.start()

    def put(node, value):
        value = value.astype(jnp.bfloat16)
        plain_ref[pl.ds(node * rank, rank), :] = value
        pair_ref[pl.ds(node * rank, rank), :] = value
        return value

    def join(ups, pair):
        return dot_t(ups.reshape(2 * rank, rank), jnp.concatenate(pair, axis=0))

    zeros = []
    for q in range(steps):
        for copy in copies[q]:
            copy.wait()
        for leaf in range(4 * q, 4 * q + 4):
            coef = dot(basis_ref[leaf], x_ref[pl.ds(leaf * LEAF, LEAF), :])
            zeros.append(put(leaf, coef))
    for copy in ups:
        copy.wait()
    ones = []
    for p in range(leaves // 2):
        pair = slice(2 * p, 2 * p + 2)
        ones.append(put(leaves + p, join(up_one_ref[pair], zeros[pair])))
    for q in range(leaves // 4):
        pair = slice(2 * q, 2 * q + 2)
        put(leaves + leaves // 2 + q, join(up_two_ref[pair], ones[pair]))
    odd = lax.rem(me_ref[0], 2)
    last = (leaves - 1) * LEAF
    end = pl.ds(plain_ref.shape[0] - LEAF, LEAF)
    pair_ref[end, :] = x_ref[pl.ds(pl.multiple_of((1 - odd) * last, LEAF), LEAF), :]
    plain_ref[end, :] = x_ref[pl.ds(pl.multiple_of(odd * last, LEAF), LEAF), :]


def near_kernel(
    me_ref, list_hbm, x_hbm, blocks_hbm, out_ref, edge_ref,
    list_ref, x_ref, block_buf, sems, x_sem, list_sem, *, size,
):
    leaves, nears = list_ref.shape
    me = me_ref[0]
    first = me * leaves

    def copies(leaf, slot):
        pairs = (
            (blocks_hbm.at[leaf, pl.ds(0, 1)], block_buf.at[slot, pl.ds(0, 1)]),
            (blocks_hbm.at[leaf, pl.ds(3, nears - 3)], block_buf.at[slot, pl.ds(1, nears - 3)]),
            (blocks_hbm.at[leaf, pl.ds(1, 2)], edge_ref.at[leaf]),
        )
        return [
            pltpu.make_async_copy(src, dst, sems.at[slot, i]) for i, (src, dst) in enumerate(pairs)
        ]

    x_copy = pltpu.make_async_copy(x_hbm, x_ref, x_sem)
    list_copy = pltpu.make_async_copy(list_hbm, list_ref, list_sem)
    list_copy.start()
    x_copy.start()
    for leaf in range(DEPTH - 1):
        for copy in copies(leaf, leaf):
            copy.start()
    list_copy.wait()
    x_copy.wait()

    def step(leaf, carry):
        slot = lax.rem(leaf, DEPTH)

        @pl.when(leaf + DEPTH - 1 < leaves)
        def _():
            for copy in copies(leaf + DEPTH - 1, lax.rem(leaf + DEPTH - 1, DEPTH)):
                copy.start()

        for copy in copies(leaf, slot):
            copy.wait()
        rows = []
        for k in (0, *range(3, nears)):
            start = pl.multiple_of((list_ref[leaf, k] - first) * LEAF, LEAF)
            rows.append(x_ref[pl.ds(start, LEAF), :])
        blocks = [block_buf[slot, k] for k in range(nears - 2)]
        here = pl.ds(pl.multiple_of(leaf * LEAF, LEAF), LEAF)
        out_ref[here, :] = dot(jnp.concatenate(blocks, axis=1), jnp.concatenate(rows, axis=0))

        for side, alone in ((0, me == size - 1), (1, me == 0)):

            @pl.when(alone)
            def _():
                out_ref[here, :] += dot(edge_ref[leaf, side], x_ref[here, :])

        return carry

    lax.fori_loop(0, leaves, step, 0)


def add_edge(near_ref, edge_ref, side, rows):
    leaves = edge_ref.shape[0]

    def step(leaf, carry):
        here = pl.ds(pl.multiple_of(leaf * LEAF, LEAF), LEAF)
        near_ref[here, :] += dot(edge_ref[leaf, side], rows)
        return carry

    lax.fori_loop(0, leaves, step, 0, unroll=4)


def window_copies(plans, wins, sizes, sems):
    copies = []
    for ref, levels, place in plans:
        start = 0
        for level in levels:
            at = pl.multiple_of(place * sizes[level], sizes[level])
            copies.append(
                pltpu.make_async_copy(
                    ref.at[pl.ds(start, sizes[level]), :],
                    wins[level].at[pl.ds(at, sizes[level]), :],
                    sems.at[len(copies)],
                )
            )
            start += sizes[level]
    return copies


def prep_kernel(
    me_ref, own_ref, pair_ref, before_ref, after_ref, near_in, edge_ref, zero_hbm, one_hbm, two_hbm,
    near_ref, zero_win, one_win, two_win, zero_wide, one_wide, two_wide,
    zero_buf, one_buf, two_buf, sems, win_sems,
):
    del near_in
    rank = zero_buf.shape[-1]
    levels = (
        (two_hbm, two_buf, two_wide),
        (one_hbm, one_buf, one_wide),
        (zero_hbm, zero_buf, zero_wide),
    )
    chunks = []
    for hbm, buf, wide in levels:
        for first in range(0, buf.shape[0], 4):
            some = pl.ds(first, 4)
            copy = pltpu.make_async_copy(hbm.at[some], buf.at[some], sems.at[len(chunks)])
            copy.start()
            chunks.append((copy, buf, wide, first))
    odd = lax.rem(me_ref[0], 2)
    plans = (
        (own_ref, (0, 1, 2), REACH),
        (before_ref, (0, 1, 2), 0),
        (after_ref, (0, 1, 2), SPAN - 1),
        (pair_ref, (0, 1, 2), REACH + 1 - 2 * odd),
    )
    wins = (zero_win, one_win, two_win)
    sizes = [win.shape[0] // SPAN for win in wins]
    moves = window_copies(plans, wins, sizes, win_sems)
    for move in moves:
        move.start()
    add_edge(near_ref, edge_ref, odd, pair_ref[pl.ds(pair_ref.shape[0] - LEAF, LEAF), :])
    for copy, buf, wide, first in chunks:
        copy.wait()
        for node in range(first, first + 4):
            fars = buf.shape[1]
            wide[node] = jnp.concatenate([buf[node, k] for k in range(fars)], axis=1)
    for move in moves:
        move.wait()


def far_kernel(
    me_ref, zero_list, one_list, two_list, low_ref, high_ref, near_in, edge_ref,
    basis_ref, up_one_ref, up_two_ref, zero_wide, one_wide, two_wide, zero_in, one_in, two_in,
    out_hbm, near_ref, zero_win, one_win, two_win, out_buf, win_sems, out_sems,
):
    del near_in, zero_in, one_in, two_in
    leaves, fars = zero_list.shape
    rank = basis_ref.shape[1]
    me = me_ref[0]
    odd = lax.rem(me, 2)
    wins = (zero_win, one_win, two_win)
    sizes = [win.shape[0] // SPAN for win in wins]
    place = REACH - 1 + 2 * odd
    moves = window_copies(((low_ref, (0,), place), (high_ref, (1, 2), place)), wins, sizes, win_sems)
    for move in moves:
        move.start()
    add_edge(near_ref, edge_ref, 1 - odd, high_ref[pl.ds(high_ref.shape[0] - LEAF, LEAF), :])
    for move in moves:
        move.wait()

    def field(wide, where, node, win):
        first = (me - REACH) * wide.shape[0]
        picked = []
        for k in range(fars):
            start = pl.multiple_of((where[node, k] - first) * rank, rank)
            picked.append(win[pl.ds(start, rank), :])
        return dot(wide[node], jnp.concatenate(picked, axis=0))

    down_two = [
        field(two_wide, two_list, q, two_win).astype(jnp.bfloat16) for q in range(leaves // 4)
    ]
    down_one = []
    for p in range(leaves // 2):
        total = field(one_wide, one_list, p, one_win) + dot(up_two_ref[p], down_two[p // 2])
        down_one.append(total.astype(jnp.bfloat16))
    outs = []
    for leaf in range(leaves):
        total = field(zero_wide, zero_list, leaf, zero_win)
        total = total + dot(up_one_ref[leaf], down_one[leaf // 2])
        here = pl.ds(leaf * LEAF, LEAF)
        total = near_ref[here, :] + dot_t(basis_ref[leaf], total.astype(jnp.bfloat16))
        out_buf[here, :] = total.astype(jnp.bfloat16)
        if leaf % 4 == 3:
            some = pl.ds((leaf - 3) * LEAF, 4 * LEAF)
            outs.append(
                pltpu.make_async_copy(
                    out_buf.at[some, :], out_hbm.at[some, :], out_sems.at[leaf // 4]
                )
            )
            outs[-1].start()
    for copy in outs:
        copy.wait()


def body(
    vectors,
    near_blocks,
    near_list,
    basis,
    up_one,
    up_two,
    couple_zero,
    couple_one,
    couple_two,
    far_zero,
    far_one,
    far_two,
):
    leaves, nears = near_list.shape
    columns = vectors.shape[1]
    rank = basis.shape[2]
    fars = far_zero.shape[1]
    size = lax.axis_size("space")
    me = lax.axis_index("space").astype(jnp.int32).reshape(1)
    counts = (leaves, leaves // 2, leaves // 4)
    rows = sum(counts) * rank + LEAF
    basis_t = jnp.swapaxes(basis, 1, 2)
    bf16 = jnp.bfloat16

    hbm = pl.BlockSpec(memory_space=pltpu.HBM)
    vmem = pl.BlockSpec(memory_space=pltpu.VMEM)
    smem = pl.BlockSpec(memory_space=pltpu.SMEM)

    def in_hbm(*arrays):
        return [pltpu.with_memory_space_constraint(a, pltpu.HBM) for a in arrays]

    plain, pair = pl.pallas_call(
        up_kernel,
        in_specs=[smem] + [hbm] * 4,
        out_specs=[vmem] * 2,
        out_shape=[jax.ShapeDtypeStruct((rows, columns), bf16)] * 2,
        scratch_shapes=[
            pltpu.VMEM(vectors.shape, bf16),
            pltpu.VMEM(basis_t.shape, bf16),
            pltpu.VMEM(up_one.shape, bf16),
            pltpu.VMEM(up_two.shape, bf16),
            pltpu.SemaphoreType.DMA((leaves // 2 + 2,)),
        ],
        compiler_params=pltpu.CompilerParams(vmem_limit_bytes=16 * MIB),
        name="up_pass",
    )(me, *in_hbm(vectors, basis_t, up_one, up_two))

    def send(array, to):
        return lax.ppermute(
            array, "space", [(i, to(i)) for i in range(size) if 0 <= to(i) < size]
        )

    from_pair = send(pair, lambda i: i + 1 - 2 * (i % 2))
    before = send(plain, lambda i: i + 2)
    after = send(plain, lambda i: i - 2)

    near, edge = pl.pallas_call(
        lambda *refs: near_kernel(*refs, size=size),
        in_specs=[smem] + [hbm] * 3,
        out_specs=[vmem] * 2,
        out_shape=[
            jax.ShapeDtypeStruct(vectors.shape, jnp.float32),
            jax.ShapeDtypeStruct((leaves, 2, LEAF, LEAF), bf16),
        ],
        scratch_shapes=[
            pltpu.SMEM(near_list.shape, jnp.int32),
            pltpu.VMEM(vectors.shape, bf16),
            pltpu.VMEM((DEPTH, nears - 2, LEAF, LEAF), bf16),
            pltpu.SemaphoreType.DMA((DEPTH, 3)),
            pltpu.SemaphoreType.DMA,
            pltpu.SemaphoreType.DMA,
        ],
        compiler_params=pltpu.CompilerParams(vmem_limit_bytes=24 * MIB),
        cost_estimate=pl.CostEstimate(
            flops=2 * leaves * (nears - 2) * LEAF * LEAF * columns,
            bytes_accessed=2 * leaves * nears * LEAF * LEAF + 6 * leaves * LEAF * columns,
            transcendentals=0,
        ),
        name="near_own",
    )(me, *in_hbm(near_list, vectors, near_blocks))

    from_pair, before, after, near = lax.optimization_barrier((from_pair, before, after, near))
    split = leaves * rank
    low = send(from_pair[:split], lambda i: i + 2 - 4 * (i % 2))
    upper = jnp.where(me[0] % 2 == 1, before[split:], after[split:])
    high = send(upper, lambda i: i + 1 - 2 * (i % 2))

    wins = [jax.ShapeDtypeStruct((SPAN * n * rank, columns), bf16) for n in counts]
    near, *rest = pl.pallas_call(
        prep_kernel,
        in_specs=[smem] + [vmem] * 6 + [hbm] * 3,
        out_specs=[vmem] * 7,
        out_shape=[
            jax.ShapeDtypeStruct(vectors.shape, jnp.float32),
            *wins,
            *[jax.ShapeDtypeStruct((n, rank, fars * rank), bf16) for n in counts],
        ],
        input_output_aliases={5: 0},
        scratch_shapes=[
            *[pltpu.VMEM((n, fars, rank, rank), bf16) for n in counts],
            pltpu.SemaphoreType.DMA((sum(n // 4 for n in counts),)),
            pltpu.SemaphoreType.DMA((12,)),
        ],
        compiler_params=pltpu.CompilerParams(vmem_limit_bytes=24 * MIB),
        cost_estimate=pl.CostEstimate(
            flops=2 * leaves * LEAF * LEAF * columns,
            bytes_accessed=4 * sum(counts) * fars * rank * rank,
            transcendentals=0,
        ),
        name="prep",
    )(me, plain, from_pair, before, after, near, edge, *in_hbm(couple_zero, couple_one, couple_two))
    windows, wides = rest[:3], rest[3:]

    out, *_ = pl.pallas_call(
        far_kernel,
        in_specs=[smem] * 4 + [vmem] * 13,
        out_specs=[hbm] + [vmem] * 4,
        out_shape=[
            jax.ShapeDtypeStruct(vectors.shape, bf16),
            jax.ShapeDtypeStruct(vectors.shape, jnp.float32),
            *wins,
        ],
        input_output_aliases={6: 1, 14: 2, 15: 3, 16: 4},
        scratch_shapes=[
            pltpu.VMEM(vectors.shape, bf16),
            pltpu.SemaphoreType.DMA((3,)),
            pltpu.SemaphoreType.DMA((leaves // 4,)),
        ],
        compiler_params=pltpu.CompilerParams(vmem_limit_bytes=24 * MIB),
        name="far_down",
    )(
        me, far_zero, far_one, far_two, low, high, near, edge,
        basis_t, up_one, up_two, *wides, *windows,
    )
    return out


def solution(mesh):
    placed = (
        P(("groups", "space"), "rhs"),
        P("space", None, None, None),
        P("space", None),
        P("space", None, None),
        P("space", None, None),
        P("space", None, None),
        P("space", None, None, None),
        P("space", None, None, None),
        P("space", None, None, None),
        P("space", None),
        P("space", None),
        P("space", None),
    )
    return jax.shard_map(
        body, mesh=mesh, in_specs=placed, out_specs=P(("groups", "space"), "rhs"), check_vma=False
    )
```

time: 47.1 us -> 40.3 us (0.86)
  waiting for transfers between devices: 6.28 us -> 3.18 us
  Pallas kernels: 29.4 us -> 26.4 us
  local copies, waits for them, and re-layouts: 0.74 us -> 0.06 us
    ppermute x5, waiting for transfers between devices: 6.28 us -> 3.18 us  [send(): lax.ppermute(array, 'space', [(i, to(i)) for i in range(size) if 0 <= to(...]
    pallas_call x1, Pallas kernels: 15.8 us -> 13.7 us  [body(): pl.pallas_call(lambda *refs: near_kernel(*refs, size=size), in_specs=[sme...]
    pallas_call x1, Pallas kernels: 3.47 us -> 2.16 us  [body(): pl.pallas_call(up_kernel, in_specs=[smem] + [hbm] * 4, out_specs=[vmem] *...]
    unnamed x14 -> x12, local copies, waits for them, and re-layouts: 0.72 us -> 0.04 us
    pallas_call x1 -> x2, Pallas kernels: 10.1 us -> 10.6 us  [the longest x1 6.67 us: body(): pl.pallas_call(far_kernel, in_specs=[smem] * 4 + [vmem] * 13, out_specs=[...]
  transfers between devices with their start and end apart: 5 -> 5, of which waited for: 2 -> 2; matrix products, arithmetic and copies ran while one was open for 0% -> 0% of each run, Pallas kernels for 34% -> 44%
where the time goes in v3:
time: 40.3 us; the launch traced here: 40.1 us
  Pallas kernels  26.4 us (66%)
  starting transfers between devices  10.2 us (25%)
  waiting for transfers between devices  3.18 us (8%)
    pallas_call x1, Pallas kernels, body(): pl.pallas_call(lambda *refs: near_kernel(*refs, size=size), in_specs=[sme...  13.7 us
    ppermute x5, starting transfers between devices, send(): lax.ppermute(array, 'space', [(i, to(i)) for i in range(size) if 0 <= to(...  10.2 us
    pallas_call x1, Pallas kernels, body(): pl.pallas_call(far_kernel, in_specs=[smem] * 4 + [vmem] * 13, out_specs=[...  6.67 us
    pallas_call x1, Pallas kernels, body(): pl.pallas_call(prep_kernel, in_specs=[smem] + [vmem] * 6 + [hbm] * 3, out...  3.93 us
    ppermute x5, waiting for transfers between devices, send(): lax.ppermute(array, 'space', [(i, to(i)) for i in range(size) if 0 <= to(...  3.18 us
    pallas_call x1, Pallas kernels, body(): pl.pallas_call(up_kernel, in_specs=[smem] + [hbm] * 4, out_specs=[vmem] *...  2.16 us
  transfers between devices with their start and end apart: 5, of which 2 were waited for; matrix products, arithmetic and copies ran while one was open for 0% of the time, Pallas kernels for 44%

profile of v3, /device:TPU:0, one launch (start us, length us, event | category | flops | bytes accessed | tf_op | source)
XLA Modules:
  0.0 40.1 jit_solution(24457570413247339)
XLA Ops:
  0.0 2.2 %up_pass.1 = (bf16[2048,128]{1,0:T(8,128)(2,1)S(1)}, bf16[2048,128]{1,0:T(8,128)(2,1)S(1)}) custom-call(s32[1]{0:T(128)} %bitcast.me_ref.refs_0_, bf16[4096,128]{1,0:T(8,128)(2,1)} %refs_2_.1, bf16[16,64,256]{2,1,0:T(8,128)(2,1)} %bitcast.2, bf16[16,64,64]{2,1,0:T(8,128)(2,1)} %up_one_ref.1, bf16[8,64,64]{2,1,0:T(8,128)(2,1)} %up_two_ref.1), custom_call_target="tpu_custom_call" | custom-call | tf_op jit(solution)/shard_map/up_pass/pallas_call | solution.py:291
  2.2 3.0 %collective-permute-start = (bf16[2048,128]{1,0:T(8,128)(2,1)S(1)}, bf16[2048,128]{1,0:T(8,128)(2,1)S(1)}, u32[]{:S(2)}, u32[]{:S(2)}) collective-permute-start(bf16[2048,128]{1,0:T(8,128)(2,1)S(1)} %get-tuple-element.21), channel_id=1, source_target_pairs={{0,2},{2,0},{4,6},{6,4},{8,10},{10,8},{12,14},{14,12},{1,3},{3,1},... | collective-permute-start | bytes 1572872 | tf_op jit(solution)/shard_map/ppermute | solution.py:308
  5.2 1.3 %collective-permute-start.2 = (bf16[2048,128]{1,0:T(8,128)(2,1)S(1)}, bf16[2048,128]{1,0:T(8,128)(2,1)S(1)}, u32[]{:S(2)}, u32[]{:S(2)}) collective-permute-start(bf16[2048,128]{1,0:T(8,128)(2,1)S(1)} %get-tuple-element.22.own_ref), channel_id=1, source_target_pairs={{4,0},{6,2},{8,4},{10,6},{12,8},{14,10},{5,1},{7,3},{9,5},{11,7},{... | collective-permute-start | bytes 1572872 | tf_op jit(solution)/shard_map/ppermute | solution.py:308
  6.5 4.6 %collective-permute-start.1 = (bf16[2048,128]{1,0:T(8,128)(2,1)S(1)}, bf16[2048,128]{1,0:T(8,128)(2,1)S(1)}, u32[]{:S(2)}, u32[]{:S(2)}) collective-permute-start(bf16[2048,128]{1,0:T(8,128)(2,1)S(1)} %get-tuple-element.22.own_ref), channel_id=1, source_target_pairs={{0,4},{2,6},{4,8},{6,10},{8,12},{10,14},{1,5},{3,7},{5,9},{7,11},{... | collective-permute-start | bytes 1572872 | tf_op jit(solution)/shard_map/ppermute | solution.py:308
  11.1 13.7 %near_own.1 = (f32[4096,128]{1,0:T(8,128)S(1)}, bf16[16,2,256,256]{3,2,1,0:T(8,128)(2,1)S(1)}) custom-call(s32[1]{0:T(128)} %bitcast.me_ref.refs_0_, s32[16,12]{1,0:T(8,128)} %refs_1_.1, bf16[4096,128]{1,0:T(8,128)(2,1)} %refs_2_.1, bf16[16,12,256,256]{3,2,1,0:T(8,128)(2,1)} %refs_3_.1), custom_call_target="tpu_custom_call" | custom-call | flops 2684354560 | bytes 28311552 | tf_op jit(solution)/shard_map/near_own/pallas_call | solution.py:316
  24.7 0.0 collective-permute-done.pair_ref
  24.7 0.0 collective-permute-done.2.after_ref
  24.8 0.0 collective-permute-done.1.before_ref
  24.8 1.3 %collective-permute-start.3 = (bf16[1024,128]{1,0:T(8,128)(2,1)S(1)}, bf16[1024,128]{1,0:T(8,128)(2,1)S(1)}, u32[]{:S(2)}, u32[]{:S(2)}) collective-permute-start(bf16[1024,128]{1,0:T(8,128)(2,1)S(1)} %slice.9), channel_id=1, source_target_pairs={{0,4},{4,8},{6,2},{8,12},{10,6},{14,10},{1,5},{5,9},{7,3},{9,13},{... | collective-permute-start | bytes 786440 | tf_op jit(solution)/shard_map/ppermute | solution.py:308
  26.1 0.1 collective-permute-start.4
  26.2 0.0 copy-start
  26.2 0.0 copy-start.1
  26.2 0.0 copy-start.2
  26.3 0.0 copy-start.3
  26.3 0.0 copy-start.4
  26.3 0.0 copy-start.5
  26.3 3.9 %prep.1 = (f32[4096,128]{1,0:T(8,128)S(1)}, bf16[5120,128]{1,0:T(8,128)(2,1)S(1)}, bf16[2560,128]{1,0:T(8,128)(2,1)S(1)}, bf16[1280,128]{1,0:T(8,128)(2,1)S(1)},...) custom-call(s32[1]{0:T(128)} %bitcast.me_ref.refs_0_, ...), custom_call_target="tpu_custom_call", output_to_operand_aliasing={{0}: (5, {})} | custom-call | flops 268435456 | bytes 7340032 | tf_op jit(solution)/shard_map/prep/pallas_call | solution.py:348
  30.2 0.8 %collective-permute-done.3.low_ref = bf16[1024,128]{1,0:T(8,128)(2,1)S(1)} collective-permute-done((bf16[1024,128]{1,0:T(8,128)(2,1)S(1)}, bf16[1024,128]{1,0:T(8,128)(2,1)S(1)}, u32[]{:S(2)}, u32[]{:S(2)}) %collective-permute-start.3) | collective-permute-done | bytes 262176 | tf_op jit(solution)/shard_map/ppermute | solution.py:308
  31.1 2.3 %collective-permute-done.4.high_ref = bf16[1024,128]{1,0:T(8,128)(2,1)S(1)} collective-permute-done((bf16[1024,128]{1,0:T(8,128)(2,1)S(1)}, bf16[1024,128]{1,0:T(8,128)(2,1)S(1)}, u32[]{:S(2)}, u32[]{:S(2)}) %collective-permute-start.4) | collective-permute-done | bytes 262176 | tf_op jit(solution)/shard_map/ppermute | solution.py:308
  33.4 0.0 copy-done
  33.4 0.0 copy-done.1
  33.4 0.0 copy-done.2
  33.4 0.0 copy-done.3
  33.4 0.0 copy-done.4
  33.4 0.0 copy-done.5
  33.5 6.7 %far_down.1 = (bf16[4096,128]{1,0:T(8,128)(2,1)}, f32[4096,128]{1,0:T(8,128)S(1)}, bf16[5120,128]{1,0:T(8,128)(2,1)S(1)}, bf16[2560,128]{1,0:T(8,128)(2,1)S(1)}, bf16[1280,128]{1,0:T(8,128)(2,1)S(1)}) custom-call(s32[1]{0:T(128)} %bitcast.me_ref.refs_0_, ...), custom_call_target="tpu_custom_call", output_to_operand_aliasing={{1}: (6, {}), {2}: (14, {}), {3}: (15, {}), {4}: (16, {})} | custom-call | tf_op jit(solution)/shard_map/far_down/pallas_call | solution.py:373
  (2 shorter events, 0.0 us)
Async XLA Ops:
  2.2 22.6 %collective-permute-start = (bf16[2048,128]{1,0:T(8,128)(2,1)S(1)}, bf16[2048,128]{1,0:T(8,128)(2,1)S(1)}, u32[]{:S(2)}, u32[]{:S(2)}) collective-permute-start(bf16[2048,128]{1,0:T(8,128)(2,1)S(1)} %get-tuple-element.21), channel_id=1, source_target_pairs={{0,2},{2,0},{4,6},{6,4},{8,10},{10,8},{12,14},{14,12},{1,3},{3,1},... | collective-permute-start | bytes 1572872 | tf_op jit(solution)/shard_map/ppermute | solution.py:308
  5.2 19.6 %collective-permute-start.2 = (bf16[2048,128]{1,0:T(8,128)(2,1)S(1)}, bf16[2048,128]{1,0:T(8,128)(2,1)S(1)}, u32[]{:S(2)}, u32[]{:S(2)}) collective-permute-start(bf16[2048,128]{1,0:T(8,128)(2,1)S(1)} %get-tuple-element.22.own_ref), channel_id=1, source_target_pairs={{4,0},{6,2},{8,4},{10,6},{12,8},{14,10},{5,1},{7,3},{9,5},{11,7},{... | collective-permute-start | bytes 1572872 | tf_op jit(solution)/shard_map/ppermute | solution.py:308
  6.5 18.3 %collective-permute-start.1 = (bf16[2048,128]{1,0:T(8,128)(2,1)S(1)}, bf16[2048,128]{1,0:T(8,128)(2,1)S(1)}, u32[]{:S(2)}, u32[]{:S(2)}) collective-permute-start(bf16[2048,128]{1,0:T(8,128)(2,1)S(1)} %get-tuple-element.22.own_ref), channel_id=1, source_target_pairs={{0,4},{2,6},{4,8},{6,10},{8,12},{10,14},{1,5},{3,7},{5,9},{7,11},{... | collective-permute-start | bytes 1572872 | tf_op jit(solution)/shard_map/ppermute | solution.py:308
  24.8 6.3 %collective-permute-start.3 = (bf16[1024,128]{1,0:T(8,128)(2,1)S(1)}, bf16[1024,128]{1,0:T(8,128)(2,1)S(1)}, u32[]{:S(2)}, u32[]{:S(2)}) collective-permute-start(bf16[1024,128]{1,0:T(8,128)(2,1)S(1)} %slice.9), channel_id=1, source_target_pairs={{0,4},{4,8},{6,2},{8,12},{10,6},{14,10},{1,5},{5,9},{7,3},{9,13},{... | collective-permute-start | bytes 786440 | tf_op jit(solution)/shard_map/ppermute | solution.py:308
  26.1 7.3 %collective-permute-start.4 = (bf16[1024,128]{1,0:T(8,128)(2,1)S(1)}, bf16[1024,128]{1,0:T(8,128)(2,1)S(1)}, u32[]{:S(2)}, u32[]{:S(2)}) collective-permute-start(bf16[1024,128]{1,0:T(8,128)(2,1)S(1)} %slice_select_fusion), channel_id=1, source_target_pairs={{0,2},{2,0},{4,6},{6,4},{8,10},{10,8},{12,14},{14,12},{1,3},{3,1},... | collective-permute-start | bytes 786440 | tf_op jit(solution)/shard_map/ppermute | solution.py:308
  26.2 7.2 %copy-start = (bf16[16,256,64]{1,2,0:T(8,128)(2,1)S(1)}, bf16[16,256,64]{1,2,0:T(8,128)(2,1)}, u32[]{:S(2)}) copy-start(bf16[16,256,64]{1,2,0:T(8,128)(2,1)} %param.15) | copy-start | bytes 1572868
  26.2 7.2 %copy-start.1 = (bf16[16,64,64]{2,1,0:T(8,128)(2,1)S(1)}, bf16[16,64,64]{2,1,0:T(8,128)(2,1)}, u32[]{:S(2)}) copy-start(bf16[16,64,64]{2,1,0:T(8,128)(2,1)} %up_one_ref.1) | copy-start | bytes 393220
  26.2 7.2 %copy-start.2 = (bf16[8,64,64]{2,1,0:T(8,128)(2,1)S(1)}, bf16[8,64,64]{2,1,0:T(8,128)(2,1)}, u32[]{:S(2)}) copy-start(bf16[8,64,64]{2,1,0:T(8,128)(2,1)} %up_two_ref.1) | copy-start | bytes 196612
  26.3 7.2 %copy-start.3 = (s32[16,16]{1,0:T(8,128)S(1)}, s32[16,16]{1,0:T(8,128)}, u32[]{:S(2)}) copy-start(s32[16,16]{1,0:T(8,128)} %zero_list.1) | copy-start | bytes 3076
  26.3 7.2 %copy-start.4 = (s32[8,16]{1,0:T(8,128)S(1)}, s32[8,16]{1,0:T(8,128)}, u32[]{:S(2)}) copy-start(s32[8,16]{1,0:T(8,128)} %one_list.1) | copy-start | bytes 1540
  26.3 7.2 %copy-start.5 = (s32[4,16]{1,0:T(4,128)S(1)}, s32[4,16]{1,0:T(4,128)}, u32[]{:S(2)}) copy-start(s32[4,16]{1,0:T(4,128)} %two_list.1) | copy-start | bytes 772

commit v4 on v3

--- a/solution.py
+++ b/solution.py
@@ -1,3 +1,5 @@
+import functools
+
 import jax
 import jax.numpy as jnp
 from jax import lax
@@ -78,11 +80,10 @@
 
 def near_kernel(
     me_ref, list_hbm, x_hbm, blocks_hbm, out_ref, edge_ref,
-    list_ref, x_ref, block_buf, sems, x_sem, list_sem, *, size,
+    list_ref, x_ref, block_buf, sems, x_sem, list_sem,
 ):
     leaves, nears = list_ref.shape
-    me = me_ref[0]
-    first = me * leaves
+    first = me_ref[0] * leaves
 
     def copies(leaf, slot):
         pairs = (
@@ -121,13 +122,6 @@
         blocks = [block_buf[slot, k] for k in range(nears - 2)]
         here = pl.ds(pl.multiple_of(leaf * LEAF, LEAF), LEAF)
         out_ref[here, :] = dot(jnp.concatenate(blocks, axis=1), jnp.concatenate(rows, axis=0))
-
-        for side, alone in ((0, me == size - 1), (1, me == 0)):
-
-            @pl.when(alone)
-            def _():
-                out_ref[here, :] += dot(edge_ref[leaf, side], x_ref[here, :])
-
         return carry
 
     lax.fori_loop(0, leaves, step, 0)
@@ -162,9 +156,10 @@
 
 
 def prep_kernel(
-    me_ref, own_ref, pair_ref, before_ref, after_ref, near_in, edge_ref, zero_hbm, one_hbm, two_hbm,
+    me_ref, own_ref, pair_ref, first_ref, second_ref, near_in, edge_ref,
+    x_hbm, zero_hbm, one_hbm, two_hbm,
     near_ref, zero_win, one_win, two_win, zero_wide, one_wide, two_wide,
-    zero_buf, one_buf, two_buf, sems, win_sems,
+    x_ref, zero_buf, one_buf, two_buf, sems, win_sems, x_sem, *, size,
 ):
     del near_in
     rank = zero_buf.shape[-1]
@@ -180,11 +175,13 @@
             copy = pltpu.make_async_copy(hbm.at[some], buf.at[some], sems.at[len(chunks)])
             copy.start()
             chunks.append((copy, buf, wide, first))
-    odd = lax.rem(me_ref[0], 2)
+    me = me_ref[0]
+    odd = lax.rem(me, 2)
+    block = lax.rem(me // 2, 2)
     plans = (
         (own_ref, (0, 1, 2), REACH),
-        (before_ref, (0, 1, 2), 0),
-        (after_ref, (0, 1, 2), SPAN - 1),
+        (first_ref, (0, 1, 2), (1 - block) * (SPAN - 1)),
+        (second_ref, (0, 1, 2), block * (SPAN - 1)),
         (pair_ref, (0, 1, 2), REACH + 1 - 2 * odd),
     )
     wins = (zero_win, one_win, two_win)
@@ -193,6 +190,16 @@
     for move in moves:
         move.start()
     add_edge(near_ref, edge_ref, odd, pair_ref[pl.ds(pair_ref.shape[0] - LEAF, LEAF), :])
+
+    @pl.when((me == 0) | (me == size - 1))
+    def _():
+        x_copy = pltpu.make_async_copy(x_hbm, x_ref, x_sem)
+        x_copy.start()
+        x_copy.wait()
+        for leaf in range(edge_ref.shape[0]):
+            here = pl.ds(leaf * LEAF, LEAF)
+            near_ref[here, :] += dot(edge_ref[leaf, 1 - odd], x_ref[here, :])
+
     for copy, buf, wide, first in chunks:
         copy.wait()
         for node in range(first, first + 4):
@@ -310,11 +317,11 @@
         )
 
     from_pair = send(pair, lambda i: i + 1 - 2 * (i % 2))
-    before = send(plain, lambda i: i + 2)
-    after = send(plain, lambda i: i - 2)
+    first = send(plain, lambda i: i + 2 - i // 2 % 2 * 4)
+    second = send(plain, lambda i: i - 2 + i // 2 % 2 * 4)
 
     near, edge = pl.pallas_call(
-        lambda *refs: near_kernel(*refs, size=size),
+        near_kernel,
         in_specs=[smem] + [hbm] * 3,
         out_specs=[vmem] * 2,
         out_shape=[
@@ -338,16 +345,16 @@
         name="near_own",
     )(me, *in_hbm(near_list, vectors, near_blocks))
 
-    from_pair, before, after, near = lax.optimization_barrier((from_pair, before, after, near))
+    from_pair, first, second, near = lax.optimization_barrier((from_pair, first, second, near))
     split = leaves * rank
     low = send(from_pair[:split], lambda i: i + 2 - 4 * (i % 2))
-    upper = jnp.where(me[0] % 2 == 1, before[split:], after[split:])
+    upper = jnp.where((me[0] // 2 + me[0]) % 2 == 0, first[split:], second[split:])
     high = send(upper, lambda i: i + 1 - 2 * (i % 2))
 
     wins = [jax.ShapeDtypeStruct((SPAN * n * rank, columns), bf16) for n in counts]
     near, *rest = pl.pallas_call(
-        prep_kernel,
-        in_specs=[smem] + [vmem] * 6 + [hbm] * 3,
+        functools.partial(prep_kernel, size=size),
+        in_specs=[smem] + [vmem] * 6 + [hbm] * 4,
         out_specs=[vmem] * 7,
         out_shape=[
             jax.ShapeDtypeStruct(vectors.shape, jnp.float32),
@@ -356,9 +363,11 @@
         ],
         input_output_aliases={5: 0},
         scratch_shapes=[
+            pltpu.VMEM(vectors.shape, bf16),
             *[pltpu.VMEM((n, fars, rank, rank), bf16) for n in counts],
             pltpu.SemaphoreType.DMA((sum(n // 4 for n in counts),)),
             pltpu.SemaphoreType.DMA((12,)),
+            pltpu.SemaphoreType.DMA,
         ],
         compiler_params=pltpu.CompilerParams(vmem_limit_bytes=24 * MIB),
         cost_estimate=pl.CostEstimate(
@@ -367,7 +376,10 @@
             transcendentals=0,
         ),
         name="prep",
-    )(me, plain, from_pair, before, after, near, edge, *in_hbm(couple_zero, couple_one, couple_two))
+    )(
+        me, plain, from_pair, first, second, near, edge,
+        *in_hbm(vectors, couple_zero, couple_one, couple_two),
+    )
     windows, wides = rest[:3], rest[3:]
 
     out, *_ = pl.pallas_call(

time: 40.3 us -> 38.7 us (0.960)
  waiting for transfers between devices: 3.18 us -> 0.6 us
  starting transfers between devices: 10.2 us -> 11.8 us
  Pallas kernels: 26.4 us -> 25.9 us
    ppermute x5, waiting for transfers between devices: 3.18 us -> 0.6 us  [send(): lax.ppermute(array, 'space', [(i, to(i)) for i in range(size) if 0 <= to(...]
    ppermute x5, starting transfers between devices: 10.2 us -> 11.8 us  [send(): lax.ppermute(array, 'space', [(i, to(i)) for i in range(size) if 0 <= to(...]
    pallas_call x2, Pallas kernels: 17.6 us -> 17 us  [the longest x1 10.8 us: body(): pl.pallas_call(near_kernel, in_specs=[smem] + [hbm] * 3, out_specs=[vmem]...]
where the time goes in v4:
time: 38.7 us; the launch traced here: 38.5 us
  Pallas kernels  25.9 us (67%)
  starting transfers between devices  11.8 us (30%)
  waiting for transfers between devices  0.6 us (2%)
    ppermute x5, starting transfers between devices, send(): lax.ppermute(array, 'space', [(i, to(i)) for i in range(size) if 0 <= to(...  11.8 us
    pallas_call x1, Pallas kernels, body(): pl.pallas_call(near_kernel, in_specs=[smem] + [hbm] * 3, out_specs=[vmem]...  10.8 us
    pallas_call x1, Pallas kernels, body(): pl.pallas_call(far_kernel, in_specs=[smem] * 4 + [vmem] * 13, out_specs=[...  6.67 us
    pallas_call x1, Pallas kernels, body(): pl.pallas_call(functools.partial(prep_kernel, size=size), in_specs=[smem]...  6.19 us
    pallas_call x1, Pallas kernels, body(): pl.pallas_call(up_kernel, in_specs=[smem] + [hbm] * 4, out_specs=[vmem] *...  2.16 us
  transfers between devices with their start and end apart: 5, of which 2 were waited for; matrix products, arithmetic and copies ran while one was open for 0% of the time, Pallas kernels for 44%

profile of v4, /device:TPU:0, one launch (start us, length us, event | category | flops | bytes accessed | tf_op | source)
XLA Modules:
  0.0 38.5 jit_solution(12006784946572138713)
XLA Ops:
  0.0 2.2 %up_pass.1 = (bf16[2048,128]{1,0:T(8,128)(2,1)S(1)}, bf16[2048,128]{1,0:T(8,128)(2,1)S(1)}) custom-call(s32[1]{0:T(128)} %bitcast.me_ref, bf16[4096,128]{1,0:T(8,128)(2,1)} %x_hbm.5, bf16[16,64,256]{2,1,0:T(8,128)(2,1)} %bitcast.2, bf16[16,64,64]{2,1,0:T(8,128)(2,1)} %up_one_ref.1, bf16[8,64,64]{2,1,0:T(8,128)(2,1)} %up_two_ref.1), custom_call_target="tpu_custom_call" | custom-call | tf_op jit(solution)/shard_map/up_pass/pallas_call | solution.py:298
  2.2 3.0 %collective-permute-start = (bf16[2048,128]{1,0:T(8,128)(2,1)S(1)}, bf16[2048,128]{1,0:T(8,128)(2,1)S(1)}, u32[]{:S(2)}, u32[]{:S(2)}) collective-permute-start(bf16[2048,128]{1,0:T(8,128)(2,1)S(1)} %get-tuple-element.21), channel_id=1, source_target_pairs={{0,2},{2,0},{4,6},{6,4},{8,10},{10,8},{12,14},{14,12},{1,3},{3,1},... | collective-permute-start | bytes 1572872 | tf_op jit(solution)/shard_map/ppermute | solution.py:315
  5.2 0.7 %collective-permute-start.2 = (bf16[2048,128]{1,0:T(8,128)(2,1)S(1)}, bf16[2048,128]{1,0:T(8,128)(2,1)S(1)}, u32[]{:S(2)}, u32[]{:S(2)}) collective-permute-start(bf16[2048,128]{1,0:T(8,128)(2,1)S(1)} %get-tuple-element.22.own_ref), channel_id=1, source_target_pairs={{4,8},{6,10},{8,4},{10,6},{5,9},{7,11},{9,5},{11,7},{20,24},{22,26... | collective-permute-start | bytes 1572872 | tf_op jit(solution)/shard_map/ppermute | solution.py:315
  5.9 4.4 %collective-permute-start.1 = (bf16[2048,128]{1,0:T(8,128)(2,1)S(1)}, bf16[2048,128]{1,0:T(8,128)(2,1)S(1)}, u32[]{:S(2)}, u32[]{:S(2)}) collective-permute-start(bf16[2048,128]{1,0:T(8,128)(2,1)S(1)} %get-tuple-element.22.own_ref), channel_id=1, source_target_pairs={{0,4},{2,6},{4,0},{6,2},{8,12},{10,14},{12,8},{14,10},{1,5},{3,7},... | collective-permute-start | bytes 1572872 | tf_op jit(solution)/shard_map/ppermute | solution.py:315
  10.3 10.8 %near_own.1 = (f32[4096,128]{1,0:T(8,128)S(1)}, bf16[16,2,256,256]{3,2,1,0:T(8,128)(2,1)S(1)}) custom-call(s32[1]{0:T(128)} %bitcast.me_ref, s32[16,12]{1,0:T(8,128)} %list_hbm.1, bf16[4096,128]{1,0:T(8,128)(2,1)} %x_hbm.5, bf16[16,12,256,256]{3,2,1,0:T(8,128)(2,1)} %blocks_hbm.1), custom_call_target="tpu_custom_call" | custom-call | flops 2684354560 | bytes 28311552 | tf_op jit(solution)/shard_map/near_own/pallas_call | solution.py:323
  21.1 0.0 collective-permute-done.pair_ref
  21.1 0.0 collective-permute-done.2.second_ref
  21.1 0.5 %collective-permute-done.1.first_ref = bf16[2048,128]{1,0:T(8,128)(2,1)S(1)} collective-permute-done((bf16[2048,128]{1,0:T(8,128)(2,1)S(1)}, bf16[2048,128]{1,0:T(8,128)(2,1)S(1)}, u32[]{:S(2)}, u32[]{:S(2)}) %collective-permute-start.1) | collective-permute-done | bytes 524320 | tf_op jit(solution)/shard_map/ppermute | solution.py:315
  21.7 3.7 %collective-permute-start.3 = (bf16[1024,128]{1,0:T(8,128)(2,1)S(1)}, bf16[1024,128]{1,0:T(8,128)(2,1)S(1)}, u32[]{:S(2)}, u32[]{:S(2)}) collective-permute-start(bf16[1024,128]{1,0:T(8,128)(2,1)S(1)} %slice.9), channel_id=1, source_target_pairs={{0,4},{4,8},{6,2},{8,12},{10,6},{14,10},{1,5},{5,9},{7,3},{9,13},{... | collective-permute-start | bytes 786440 | tf_op jit(solution)/shard_map/ppermute | solution.py:315
  25.4 0.1 collective-permute-start.4
  25.5 0.0 copy-start
  25.5 0.0 copy-start.1
  25.5 0.0 copy-start.2
  25.5 0.0 copy-start.3
  25.5 0.0 copy-start.4
  25.5 0.0 copy-start.5
  25.5 6.2 %prep.1 = (f32[4096,128]{1,0:T(8,128)S(1)}, bf16[5120,128]{1,0:T(8,128)(2,1)S(1)}, bf16[2560,128]{1,0:T(8,128)(2,1)S(1)}, bf16[1280,128]{1,0:T(8,128)(2,1)S(1)},...) custom-call(s32[1]{0:T(128)} %bitcast.me_ref, ...), custom_call_target="tpu_custom_call", output_to_operand_aliasing={{0}: (5, {})} | custom-call | flops 268435456 | bytes 7340032 | tf_op jit(solution)/shard_map/prep/pallas_call | solution.py:355
  31.7 0.0 collective-permute-done.3.low_ref
  31.8 0.1 collective-permute-done.4.high_ref
  31.8 0.0 copy-done
  31.8 0.0 copy-done.1
  31.8 0.0 copy-done.2
  31.8 0.0 copy-done.3
  31.8 0.0 copy-done.4
  31.9 0.0 copy-done.5
  31.9 6.7 %far_down.1 = (bf16[4096,128]{1,0:T(8,128)(2,1)}, f32[4096,128]{1,0:T(8,128)S(1)}, bf16[5120,128]{1,0:T(8,128)(2,1)S(1)}, bf16[2560,128]{1,0:T(8,128)(2,1)S(1)}, bf16[1280,128]{1,0:T(8,128)(2,1)S(1)}) custom-call(s32[1]{0:T(128)} %bitcast.me_ref, s32[16,16]{1,0:T(8,128)S(1)} %copy-done.3, ...), custom_call_target="tpu_custom_call", output_to_operand_aliasing={{1}: (6, {}), {2}: (14, {}), {3}: (15, {}), {4}: (16, {})} | custom-call | tf_op jit(solution)/shard_map/far_down/pallas_call | solution.py:385
  (2 shorter events, 0.0 us)
Async XLA Ops:
  2.2 19.0 %collective-permute-start = (bf16[2048,128]{1,0:T(8,128)(2,1)S(1)}, bf16[2048,128]{1,0:T(8,128)(2,1)S(1)}, u32[]{:S(2)}, u32[]{:S(2)}) collective-permute-start(bf16[2048,128]{1,0:T(8,128)(2,1)S(1)} %get-tuple-element.21), channel_id=1, source_target_pairs={{0,2},{2,0},{4,6},{6,4},{8,10},{10,8},{12,14},{14,12},{1,3},{3,1},... | collective-permute-start | bytes 1572872 | tf_op jit(solution)/shard_map/ppermute | solution.py:315
  5.2 16.0 %collective-permute-start.2 = (bf16[2048,128]{1,0:T(8,128)(2,1)S(1)}, bf16[2048,128]{1,0:T(8,128)(2,1)S(1)}, u32[]{:S(2)}, u32[]{:S(2)}) collective-permute-start(bf16[2048,128]{1,0:T(8,128)(2,1)S(1)} %get-tuple-element.22.own_ref), channel_id=1, source_target_pairs={{4,8},{6,10},{8,4},{10,6},{5,9},{7,11},{9,5},{11,7},{20,24},{22,26... | collective-permute-start | bytes 1572872 | tf_op jit(solution)/shard_map/ppermute | solution.py:315
  5.9 15.8 %collective-permute-start.1 = (bf16[2048,128]{1,0:T(8,128)(2,1)S(1)}, bf16[2048,128]{1,0:T(8,128)(2,1)S(1)}, u32[]{:S(2)}, u32[]{:S(2)}) collective-permute-start(bf16[2048,128]{1,0:T(8,128)(2,1)S(1)} %get-tuple-element.22.own_ref), channel_id=1, source_target_pairs={{0,4},{2,6},{4,0},{6,2},{8,12},{10,14},{12,8},{14,10},{1,5},{3,7},... | collective-permute-start | bytes 1572872 | tf_op jit(solution)/shard_map/ppermute | solution.py:315
  21.7 10.1 %collective-permute-start.3 = (bf16[1024,128]{1,0:T(8,128)(2,1)S(1)}, bf16[1024,128]{1,0:T(8,128)(2,1)S(1)}, u32[]{:S(2)}, u32[]{:S(2)}) collective-permute-start(bf16[1024,128]{1,0:T(8,128)(2,1)S(1)} %slice.9), channel_id=1, source_target_pairs={{0,4},{4,8},{6,2},{8,12},{10,6},{14,10},{1,5},{5,9},{7,3},{9,13},{... | collective-permute-start | bytes 786440 | tf_op jit(solution)/shard_map/ppermute | solution.py:315
  25.4 6.4 %collective-permute-start.4 = (bf16[1024,128]{1,0:T(8,128)(2,1)S(1)}, bf16[1024,128]{1,0:T(8,128)(2,1)S(1)}, u32[]{:S(2)}, u32[]{:S(2)}) collective-permute-start(bf16[1024,128]{1,0:T(8,128)(2,1)S(1)} %slice_select_fusion), channel_id=1, source_target_pairs={{0,2},{2,0},{4,6},{6,4},{8,10},{10,8},{12,14},{14,12},{1,3},{3,1},... | collective-permute-start | bytes 786440 | tf_op jit(solution)/shard_map/ppermute | solution.py:315
  25.5 6.4 %copy-start = (bf16[16,256,64]{1,2,0:T(8,128)(2,1)S(1)}, bf16[16,256,64]{1,2,0:T(8,128)(2,1)}, u32[]{:S(2)}) copy-start(bf16[16,256,64]{1,2,0:T(8,128)(2,1)} %param.15) | copy-start | bytes 1572868
  25.5 6.4 %copy-start.1 = (bf16[16,64,64]{2,1,0:T(8,128)(2,1)S(1)}, bf16[16,64,64]{2,1,0:T(8,128)(2,1)}, u32[]{:S(2)}) copy-start(bf16[16,64,64]{2,1,0:T(8,128)(2,1)} %up_one_ref.1) | copy-start | bytes 393220
  25.5 6.3 %copy-start.2 = (bf16[8,64,64]{2,1,0:T(8,128)(2,1)S(1)}, bf16[8,64,64]{2,1,0:T(8,128)(2,1)}, u32[]{:S(2)}) copy-start(bf16[8,64,64]{2,1,0:T(8,128)(2,1)} %up_two_ref.1) | copy-start | bytes 196612
  25.5 6.3 %copy-start.3 = (s32[16,16]{1,0:T(8,128)S(1)}, s32[16,16]{1,0:T(8,128)}, u32[]{:S(2)}) copy-start(s32[16,16]{1,0:T(8,128)} %zero_list.1) | copy-start | bytes 3076
  25.5 6.3 %copy-start.4 = (s32[8,16]{1,0:T(8,128)S(1)}, s32[8,16]{1,0:T(8,128)}, u32[]{:S(2)}) copy-start(s32[8,16]{1,0:T(8,128)} %one_list.1) | copy-start | bytes 1540
  25.5 6.3 %copy-start.5 = (s32[4,16]{1,0:T(4,128)S(1)}, s32[4,16]{1,0:T(4,128)}, u32[]{:S(2)}) copy-start(s32[4,16]{1,0:T(4,128)} %two_list.1) | copy-start | bytes 772

commit v5 on v4

--- a/solution.py
+++ b/solution.py
@@ -23,8 +23,8 @@
 
 
 def up_kernel(
-    me_ref, x_hbm, basis_hbm, up_one_hbm, up_two_hbm, plain_ref, pair_ref,
-    x_ref, basis_ref, up_one_ref, up_two_ref, sems,
+    me_ref, x_hbm, basis_hbm, up_one_hbm, up_two_hbm, plain_ref, pair_ref, x_ref,
+    basis_ref, up_one_ref, up_two_ref, sems,
 ):
     leaves, rank = basis_ref.shape[:2]
     steps = leaves // 4
@@ -79,8 +79,7 @@
 
 
 def near_kernel(
-    me_ref, list_hbm, x_hbm, blocks_hbm, out_ref, edge_ref,
-    list_ref, x_ref, block_buf, sems, x_sem, list_sem,
+    me_ref, x_ref, list_hbm, blocks_hbm, out_ref, edge_ref, list_ref, block_buf, sems, list_sem,
 ):
     leaves, nears = list_ref.shape
     first = me_ref[0] * leaves
@@ -95,15 +94,12 @@
             pltpu.make_async_copy(src, dst, sems.at[slot, i]) for i, (src, dst) in enumerate(pairs)
         ]
 
-    x_copy = pltpu.make_async_copy(x_hbm, x_ref, x_sem)
     list_copy = pltpu.make_async_copy(list_hbm, list_ref, list_sem)
     list_copy.start()
-    x_copy.start()
     for leaf in range(DEPTH - 1):
         for copy in copies(leaf, leaf):
             copy.start()
     list_copy.wait()
-    x_copy.wait()
 
     def step(leaf, carry):
         slot = lax.rem(leaf, DEPTH)
@@ -127,11 +123,12 @@
     lax.fori_loop(0, leaves, step, 0)
 
 
-def add_edge(near_ref, edge_ref, side, rows):
+def add_edge(near_ref, edge_ref, side, ref, start, stride):
     leaves = edge_ref.shape[0]
 
     def step(leaf, carry):
         here = pl.ds(pl.multiple_of(leaf * LEAF, LEAF), LEAF)
+        rows = ref[pl.ds(pl.multiple_of(start + leaf * stride, LEAF), LEAF), :]
         near_ref[here, :] += dot(edge_ref[leaf, side], rows)
         return carry
 
@@ -157,9 +154,9 @@
 
 def prep_kernel(
     me_ref, own_ref, pair_ref, first_ref, second_ref, near_in, edge_ref,
-    x_hbm, zero_hbm, one_hbm, two_hbm,
+    zero_hbm, one_hbm, two_hbm,
     near_ref, zero_win, one_win, two_win, zero_wide, one_wide, two_wide,
-    x_ref, zero_buf, one_buf, two_buf, sems, win_sems, x_sem, *, size,
+    zero_buf, one_buf, two_buf, sems, win_sems,
 ):
     del near_in
     rank = zero_buf.shape[-1]
@@ -189,17 +186,7 @@
     moves = window_copies(plans, wins, sizes, win_sems)
     for move in moves:
         move.start()
-    add_edge(near_ref, edge_ref, odd, pair_ref[pl.ds(pair_ref.shape[0] - LEAF, LEAF), :])
-
-    @pl.when((me == 0) | (me == size - 1))
-    def _():
-        x_copy = pltpu.make_async_copy(x_hbm, x_ref, x_sem)
-        x_copy.start()
-        x_copy.wait()
-        for leaf in range(edge_ref.shape[0]):
-            here = pl.ds(leaf * LEAF, LEAF)
-            near_ref[here, :] += dot(edge_ref[leaf, 1 - odd], x_ref[here, :])
-
+    add_edge(near_ref, edge_ref, odd, pair_ref, pair_ref.shape[0] - LEAF, 0)
     for copy, buf, wide, first in chunks:
         copy.wait()
         for node in range(first, first + 4):
@@ -210,9 +197,9 @@
 
 
 def far_kernel(
-    me_ref, zero_list, one_list, two_list, low_ref, high_ref, near_in, edge_ref,
+    me_ref, zero_list, one_list, two_list, x_ref, low_ref, high_ref, near_in, edge_ref,
     basis_ref, up_one_ref, up_two_ref, zero_wide, one_wide, two_wide, zero_in, one_in, two_in,
-    out_hbm, near_ref, zero_win, one_win, two_win, out_buf, win_sems, out_sems,
+    out_hbm, near_ref, zero_win, one_win, two_win, out_buf, win_sems, out_sems, *, size,
 ):
     del near_in, zero_in, one_in, two_in
     leaves, fars = zero_list.shape
@@ -225,7 +212,17 @@
     moves = window_copies(((low_ref, (0,), place), (high_ref, (1, 2), place)), wins, sizes, win_sems)
     for move in moves:
         move.start()
-    add_edge(near_ref, edge_ref, 1 - odd, high_ref[pl.ds(high_ref.shape[0] - LEAF, LEAF), :])
+
+    alone = (me == 0) | (me == size - 1)
+
+    @pl.when(alone)
+    def _():
+        add_edge(near_ref, edge_ref, 1 - odd, x_ref, 0, LEAF)
+
+    @pl.when(jnp.logical_not(alone))
+    def _():
+        add_edge(near_ref, edge_ref, 1 - odd, high_ref, high_ref.shape[0] - LEAF, 0)
+
     for move in moves:
         move.wait()
 
@@ -295,13 +292,16 @@
     def in_hbm(*arrays):
         return [pltpu.with_memory_space_constraint(a, pltpu.HBM) for a in arrays]
 
-    plain, pair = pl.pallas_call(
+    plain, pair, points = pl.pallas_call(
         up_kernel,
         in_specs=[smem] + [hbm] * 4,
-        out_specs=[vmem] * 2,
-        out_shape=[jax.ShapeDtypeStruct((rows, columns), bf16)] * 2,
+        out_specs=[vmem] * 3,
+        out_shape=[
+            jax.ShapeDtypeStruct((rows, columns), bf16),
+            jax.ShapeDtypeStruct((rows, columns), bf16),
+            jax.ShapeDtypeStruct(vectors.shape, bf16),
+        ],
         scratch_shapes=[
-            pltpu.VMEM(vectors.shape, bf16),
             pltpu.VMEM(basis_t.shape, bf16),
             pltpu.VMEM(up_one.shape, bf16),
             pltpu.VMEM(up_two.shape, bf16),
@@ -313,7 +313,7 @@
 
     def send(array, to):
         return lax.ppermute(
-            array, "space", [(i, to(i)) for i in range(size) if 0 <= to(i) < size]
+            array, "space", [(i, to(i) if 0 <= to(i) < size else i) for i in range(size)]
         )
 
     from_pair = send(pair, lambda i: i + 1 - 2 * (i % 2))
@@ -322,7 +322,7 @@
 
     near, edge = pl.pallas_call(
         near_kernel,
-        in_specs=[smem] + [hbm] * 3,
+        in_specs=[smem, vmem] + [hbm] * 2,
         out_specs=[vmem] * 2,
         out_shape=[
             jax.ShapeDtypeStruct(vectors.shape, jnp.float32),
@@ -330,10 +330,8 @@
         ],
         scratch_shapes=[
             pltpu.SMEM(near_list.shape, jnp.int32),
-            pltpu.VMEM(vectors.shape, bf16),
             pltpu.VMEM((DEPTH, nears - 2, LEAF, LEAF), bf16),
             pltpu.SemaphoreType.DMA((DEPTH, 3)),
-            pltpu.SemaphoreType.DMA,
             pltpu.SemaphoreType.DMA,
         ],
         compiler_params=pltpu.CompilerParams(vmem_limit_bytes=24 * MIB),
@@ -343,18 +341,18 @@
             transcendentals=0,
         ),
         name="near_own",
-    )(me, *in_hbm(near_list, vectors, near_blocks))
+    )(me, points, *in_hbm(near_list, near_blocks))
 
     from_pair, first, second, near = lax.optimization_barrier((from_pair, first, second, near))
     split = leaves * rank
-    low = send(from_pair[:split], lambda i: i + 2 - 4 * (i % 2))
+    low = send(from_pair[:split], lambda i: (i + 2 - 4 * (i % 2)) % size)
     upper = jnp.where((me[0] // 2 + me[0]) % 2 == 0, first[split:], second[split:])
     high = send(upper, lambda i: i + 1 - 2 * (i % 2))
 
     wins = [jax.ShapeDtypeStruct((SPAN * n * rank, columns), bf16) for n in counts]
     near, *rest = pl.pallas_call(
-        functools.partial(prep_kernel, size=size),
-        in_specs=[smem] + [vmem] * 6 + [hbm] * 4,
+        prep_kernel,
+        in_specs=[smem] + [vmem] * 6 + [hbm] * 3,
         out_specs=[vmem] * 7,
         out_shape=[
             jax.ShapeDtypeStruct(vectors.shape, jnp.float32),
@@ -363,11 +361,9 @@
         ],
         input_output_aliases={5: 0},
         scratch_shapes=[
-            pltpu.VMEM(vectors.shape, bf16),
             *[pltpu.VMEM((n, fars, rank, rank), bf16) for n in counts],
             pltpu.SemaphoreType.DMA((sum(n // 4 for n in counts),)),
             pltpu.SemaphoreType.DMA((12,)),
-            pltpu.SemaphoreType.DMA,
         ],
         compiler_params=pltpu.CompilerParams(vmem_limit_bytes=24 * MIB),
         cost_estimate=pl.CostEstimate(
@@ -378,20 +374,20 @@
         name="prep",
     )(
         me, plain, from_pair, first, second, near, edge,
-        *in_hbm(vectors, couple_zero, couple_one, couple_two),
+        *in_hbm(couple_zero, couple_one, couple_two),
     )
     windows, wides = rest[:3], rest[3:]
 
     out, *_ = pl.pallas_call(
-        far_kernel,
-        in_specs=[smem] * 4 + [vmem] * 13,
+        functools.partial(far_kernel, size=size),
+        in_specs=[smem] * 4 + [vmem] * 14,
         out_specs=[hbm] + [vmem] * 4,
         out_shape=[
             jax.ShapeDtypeStruct(vectors.shape, bf16),
             jax.ShapeDtypeStruct(vectors.shape, jnp.float32),
             *wins,
         ],
-        input_output_aliases={6: 1, 14: 2, 15: 3, 16: 4},
+        input_output_aliases={7: 1, 15: 2, 16: 3, 17: 4},
         scratch_shapes=[
             pltpu.VMEM(vectors.shape, bf16),
             pltpu.SemaphoreType.DMA((3,)),
@@ -400,7 +396,7 @@
         compiler_params=pltpu.CompilerParams(vmem_limit_bytes=24 * MIB),
         name="far_down",
     )(
-        me, far_zero, far_one, far_two, low, high, near, edge,
+        me, far_zero, far_one, far_two, points, low, high, near, edge,
         basis_t, up_one, up_two, *wides, *windows,
     )
     return out

time: 38.7 us -> 38.1 us (0.984)
  waiting for transfers between devices: 0.6 us -> 4.36 us
  Pallas kernels: 25.9 us -> 23.3 us
  starting transfers between devices: 11.8 us -> 10.1 us
    ppermute x5, waiting for transfers between devices: 0.6 us -> 4.36 us  [send(): lax.ppermute(array, 'space', [(i, to(i) if 0 <= to(i) < size else i) for...]
    pallas_call x3, Pallas kernels: 23.7 us -> 20.3 us  [the longest x1 9.67 us: body(): pl.pallas_call(near_kernel, in_specs=[smem, vmem] + [hbm] * 2, out_specs=...]
    ppermute x5, starting transfers between devices: 11.8 us -> 10.1 us  [send(): lax.ppermute(array, 'space', [(i, to(i) if 0 <= to(i) < size else i) for...]
    pallas_call x1, Pallas kernels: 2.16 us -> 2.96 us  [body(): pl.pallas_call(up_kernel, in_specs=[smem] + [hbm] * 4, out_specs=[vmem] *...]
  transfers between devices with their start and end apart: 5 -> 5, of which waited for: 2 -> 2; matrix products, arithmetic and copies ran while one was open for 0% -> 0% of each run, Pallas kernels for 44% -> 36%
where the time goes in v5:
time: 38.1 us; the launch traced here: 38 us
  Pallas kernels  23.3 us (61%)
  starting transfers between devices  10.1 us (27%)
  waiting for transfers between devices  4.36 us (11%)
    ppermute x5, starting transfers between devices, send(): lax.ppermute(array, 'space', [(i, to(i) if 0 <= to(i) < size else i) for...  10.1 us
    pallas_call x1, Pallas kernels, body(): pl.pallas_call(near_kernel, in_specs=[smem, vmem] + [hbm] * 2, out_specs=...  9.67 us
    pallas_call x1, Pallas kernels, body(): pl.pallas_call(functools.partial(far_kernel, size=size), in_specs=[smem]...  6.73 us
    ppermute x5, waiting for transfers between devices, send(): lax.ppermute(array, 'space', [(i, to(i) if 0 <= to(i) < size else i) for...  4.36 us
    pallas_call x1, Pallas kernels, body(): pl.pallas_call(prep_kernel, in_specs=[smem] + [vmem] * 6 + [hbm] * 3, out...  3.94 us
    pallas_call x1, Pallas kernels, body(): pl.pallas_call(up_kernel, in_specs=[smem] + [hbm] * 4, out_specs=[vmem] *...  2.96 us
  transfers between devices with their start and end apart: 5, of which 2 were waited for; matrix products, arithmetic and copies ran while one was open for 0% of the time, Pallas kernels for 36%

profile of v5, /device:TPU:0, one launch (start us, length us, event | category | flops | bytes accessed | tf_op | source)
XLA Modules:
  0.0 38.0 jit_solution(1628392391360071331)
XLA Ops:
  0.0 3.0 %up_pass.1 = (bf16[2048,128]{1,0:T(8,128)(2,1)S(1)}, bf16[2048,128]{1,0:T(8,128)(2,1)}, bf16[4096,128]{1,0:T(8,128)(2,1)S(1)}) custom-call(s32[1]{0:T(128)} %bitcast.me_ref, bf16[4096,128]{1,0:T(8,128)(2,1)} %x_hbm.1, bf16[16,64,256]{2,1,0:T(8,128)(2,1)} %bitcast.2, bf16[16,64,64]{2,1,0:T(8,128)(2,1)} %up_one_ref.1, bf16[8,64,64]{2,1,0:T(8,128)(2,1)} %up_two_ref.1), custom_call_target="tpu_custom_call" | custom-call | tf_op jit(solution)/shard_map/up_pass/pallas_call | solution.py:295
  3.0 3.0 %collective-permute-start = (bf16[2048,128]{1,0:T(8,128)(2,1)}, bf16[2048,128]{1,0:T(8,128)(2,1)S(1)}, u32[]{:S(2)}, u32[]{:S(2)}) collective-permute-start(bf16[2048,128]{1,0:T(8,128)(2,1)} %get-tuple-element.23), channel_id=1, source_target_pairs={{0,2},{2,0},{4,6},{6,4},{8,10},{10,8},{12,14},{14,12},{1,3},{3,1},... | collective-permute-start | bytes 1572872 | tf_op jit(solution)/shard_map/ppermute | solution.py:315
  6.0 0.7 %collective-permute-start.2 = (bf16[2048,128]{1,0:T(8,128)(2,1)S(1)}, bf16[2048,128]{1,0:T(8,128)(2,1)S(1)}, u32[]{:S(2)}, u32[]{:S(2)}) collective-permute-start(bf16[2048,128]{1,0:T(8,128)(2,1)S(1)} %get-tuple-element.24.own_ref), channel_id=1, source_target_pairs={{0,0},{2,2},{4,8},{6,10},{8,4},{10,6},{12,12},{14,14},{1,1},{3,3},... | collective-permute-start | bytes 1572872 | tf_op jit(solution)/shard_map/ppermute | solution.py:315
  6.7 4.4 %collective-permute-start.1 = (bf16[2048,128]{1,0:T(8,128)(2,1)S(1)}, bf16[2048,128]{1,0:T(8,128)(2,1)S(1)}, u32[]{:S(2)}, u32[]{:S(2)}) collective-permute-start(bf16[2048,128]{1,0:T(8,128)(2,1)S(1)} %get-tuple-element.24.own_ref), channel_id=1, source_target_pairs={{0,4},{2,6},{4,0},{6,2},{8,12},{10,14},{12,8},{14,10},{1,5},{3,7},... | collective-permute-start | bytes 1572872 | tf_op jit(solution)/shard_map/ppermute | solution.py:315
  11.1 9.7 %near_own.1 = (f32[4096,128]{1,0:T(8,128)S(1)}, bf16[16,2,256,256]{3,2,1,0:T(8,128)(2,1)S(1)}) custom-call(s32[1]{0:T(128)} %bitcast.me_ref, bf16[4096,128]{1,0:T(8,128)(2,1)S(1)} %get-tuple-element.22.x_ref, s32[16,12]{1,0:T(8,128)} %list_hbm.1, bf16[16,12,256,256]{3,2,1,0:T(8,128)(2,1)} %blocks_hbm.1), custom_call_target="tpu_custom_call" | custom-call | flops 2684354560 | bytes 28311552 | tf_op jit(solution)/shard_map/near_own/pallas_call | solution.py:323
  20.8 0.0 collective-permute-done.pair_ref
  20.8 0.0 collective-permute-done.2.second_ref
  20.8 1.7 %collective-permute-done.1.first_ref = bf16[2048,128]{1,0:T(8,128)(2,1)S(1)} collective-permute-done((bf16[2048,128]{1,0:T(8,128)(2,1)S(1)}, bf16[2048,128]{1,0:T(8,128)(2,1)S(1)}, u32[]{:S(2)}, u32[]{:S(2)}) %collective-permute-start.1) | collective-permute-done | bytes 524320 | tf_op jit(solution)/shard_map/ppermute | solution.py:315
  22.5 1.8 %collective-permute-start.3 = (bf16[1024,128]{1,0:T(8,128)(2,1)S(1)}, bf16[1024,128]{1,0:T(8,128)(2,1)S(1)}, u32[]{:S(2)}, u32[]{:S(2)}) collective-permute-start(bf16[1024,128]{1,0:T(8,128)(2,1)S(1)} %slice.9), channel_id=1, source_target_pairs={{0,4},{2,14},{4,8},{6,2},{8,12},{10,6},{12,0},{14,10},{1,5},{3,15}... | collective-permute-start | bytes 786440 | tf_op jit(solution)/shard_map/ppermute | solution.py:315
  24.3 0.2 collective-permute-start.4
  24.5 0.0 copy-start
  24.5 0.0 copy-start.1
  24.5 0.0 copy-start.2
  24.5 0.0 copy-start.3
  24.5 0.0 copy-start.4
  24.5 0.0 copy-start.5
  24.5 3.9 %prep.1 = (f32[4096,128]{1,0:T(8,128)S(1)}, bf16[5120,128]{1,0:T(8,128)(2,1)S(1)}, bf16[2560,128]{1,0:T(8,128)(2,1)S(1)}, bf16[1280,128]{1,0:T(8,128)(2,1)S(1)},...) custom-call(s32[1]{0:T(128)} %bitcast.me_ref, ...), custom_call_target="tpu_custom_call", output_to_operand_aliasing={{0}: (5, {})} | custom-call | flops 268435456 | bytes 7340032 | tf_op jit(solution)/shard_map/prep/pallas_call | solution.py:353
  28.5 2.7 %collective-permute-done.3.low_ref = bf16[1024,128]{1,0:T(8,128)(2,1)S(1)} collective-permute-done((bf16[1024,128]{1,0:T(8,128)(2,1)S(1)}, bf16[1024,128]{1,0:T(8,128)(2,1)S(1)}, u32[]{:S(2)}, u32[]{:S(2)}) %collective-permute-start.3) | collective-permute-done | bytes 262176 | tf_op jit(solution)/shard_map/ppermute | solution.py:315
  31.2 0.0 collective-permute-done.4.high_ref
  31.2 0.0 copy-done
  31.2 0.0 copy-done.1
  31.2 0.0 copy-done.2
  31.2 0.0 copy-done.3
  31.2 0.0 copy-done.4
  31.2 0.0 copy-done.5
  31.2 6.7 %far_down.1 = (bf16[4096,128]{1,0:T(8,128)(2,1)}, f32[4096,128]{1,0:T(8,128)S(1)}, bf16[5120,128]{1,0:T(8,128)(2,1)S(1)}, bf16[2560,128]{1,0:T(8,128)(2,1)S(1)}, bf16[1280,128]{1,0:T(8,128)(2,1)S(1)}) custom-call(s32[1]{0:T(128)} %bitcast.me_ref, s32[16,16]{1,0:T(8,128)S(1)} %copy-done.3, ...), custom_call_target="tpu_custom_call", output_to_operand_aliasing={{1}: (7, {}), {2}: (15, {}), {3}: (16, {}), {4}: (17, {})} | custom-call | tf_op jit(solution)/shard_map/far_down/pallas_call | solution.py:381
  (2 shorter events, 0.0 us)
Async XLA Ops:
  3.0 17.8 %collective-permute-start = (bf16[2048,128]{1,0:T(8,128)(2,1)}, bf16[2048,128]{1,0:T(8,128)(2,1)S(1)}, u32[]{:S(2)}, u32[]{:S(2)}) collective-permute-start(bf16[2048,128]{1,0:T(8,128)(2,1)} %get-tuple-element.23), channel_id=1, source_target_pairs={{0,2},{2,0},{4,6},{6,4},{8,10},{10,8},{12,14},{14,12},{1,3},{3,1},... | collective-permute-start | bytes 1572872 | tf_op jit(solution)/shard_map/ppermute | solution.py:315
  6.0 14.8 %collective-permute-start.2 = (bf16[2048,128]{1,0:T(8,128)(2,1)S(1)}, bf16[2048,128]{1,0:T(8,128)(2,1)S(1)}, u32[]{:S(2)}, u32[]{:S(2)}) collective-permute-start(bf16[2048,128]{1,0:T(8,128)(2,1)S(1)} %get-tuple-element.24.own_ref), channel_id=1, source_target_pairs={{0,0},{2,2},{4,8},{6,10},{8,4},{10,6},{12,12},{14,14},{1,1},{3,3},... | collective-permute-start | bytes 1572872 | tf_op jit(solution)/shard_map/ppermute | solution.py:315
  6.7 15.8 %collective-permute-start.1 = (bf16[2048,128]{1,0:T(8,128)(2,1)S(1)}, bf16[2048,128]{1,0:T(8,128)(2,1)S(1)}, u32[]{:S(2)}, u32[]{:S(2)}) collective-permute-start(bf16[2048,128]{1,0:T(8,128)(2,1)S(1)} %get-tuple-element.24.own_ref), channel_id=1, source_target_pairs={{0,4},{2,6},{4,0},{6,2},{8,12},{10,14},{12,8},{14,10},{1,5},{3,7},... | collective-permute-start | bytes 1572872 | tf_op jit(solution)/shard_map/ppermute | solution.py:315
  22.5 8.7 %collective-permute-start.3 = (bf16[1024,128]{1,0:T(8,128)(2,1)S(1)}, bf16[1024,128]{1,0:T(8,128)(2,1)S(1)}, u32[]{:S(2)}, u32[]{:S(2)}) collective-permute-start(bf16[1024,128]{1,0:T(8,128)(2,1)S(1)} %slice.9), channel_id=1, source_target_pairs={{0,4},{2,14},{4,8},{6,2},{8,12},{10,6},{12,0},{14,10},{1,5},{3,15}... | collective-permute-start | bytes 786440 | tf_op jit(solution)/shard_map/ppermute | solution.py:315
  24.3 6.9 %collective-permute-start.4 = (bf16[1024,128]{1,0:T(8,128)(2,1)S(1)}, bf16[1024,128]{1,0:T(8,128)(2,1)S(1)}, u32[]{:S(2)}, u32[]{:S(2)}) collective-permute-start(bf16[1024,128]{1,0:T(8,128)(2,1)S(1)} %slice_select_fusion), channel_id=1, source_target_pairs={{0,2},{2,0},{4,6},{6,4},{8,10},{10,8},{12,14},{14,12},{1,3},{3,1},... | collective-permute-start | bytes 786440 | tf_op jit(solution)/shard_map/ppermute | solution.py:315
  24.5 6.7 %copy-start = (bf16[16,256,64]{1,2,0:T(8,128)(2,1)S(1)}, bf16[16,256,64]{1,2,0:T(8,128)(2,1)}, u32[]{:S(2)}) copy-start(bf16[16,256,64]{1,2,0:T(8,128)(2,1)} %param.15) | copy-start | bytes 1572868
  24.5 6.7 %copy-start.1 = (bf16[16,64,64]{2,1,0:T(8,128)(2,1)S(1)}, bf16[16,64,64]{2,1,0:T(8,128)(2,1)}, u32[]{:S(2)}) copy-start(bf16[16,64,64]{2,1,0:T(8,128)(2,1)} %up_one_ref.1) | copy-start | bytes 393220
  24.5 6.7 %copy-start.2 = (bf16[8,64,64]{2,1,0:T(8,128)(2,1)S(1)}, bf16[8,64,64]{2,1,0:T(8,128)(2,1)}, u32[]{:S(2)}) copy-start(bf16[8,64,64]{2,1,0:T(8,128)(2,1)} %up_two_ref.1) | copy-start | bytes 196612
  24.5 6.7 %copy-start.3 = (s32[16,16]{1,0:T(8,128)S(1)}, s32[16,16]{1,0:T(8,128)}, u32[]{:S(2)}) copy-start(s32[16,16]{1,0:T(8,128)} %zero_list.1) | copy-start | bytes 3076
  24.5 6.7 %copy-start.4 = (s32[8,16]{1,0:T(8,128)S(1)}, s32[8,16]{1,0:T(8,128)}, u32[]{:S(2)}) copy-start(s32[8,16]{1,0:T(8,128)} %one_list.1) | copy-start | bytes 1540
  24.5 6.7 %copy-start.5 = (s32[4,16]{1,0:T(4,128)S(1)}, s32[4,16]{1,0:T(4,128)}, u32[]{:S(2)}) copy-start(s32[4,16]{1,0:T(4,128)} %two_list.1) | copy-start | bytes 772

commit v6 on v5

--- a/solution.py
+++ b/solution.py
@@ -154,9 +154,9 @@
 
 def prep_kernel(
     me_ref, own_ref, pair_ref, first_ref, second_ref, near_in, edge_ref,
-    zero_hbm, one_hbm, two_hbm,
-    near_ref, zero_win, one_win, two_win, zero_wide, one_wide, two_wide,
-    zero_buf, one_buf, two_buf, sems, win_sems,
+    basis_hbm, zero_hbm, one_hbm, two_hbm,
+    near_ref, zero_win, one_win, two_win, zero_wide, one_wide, two_wide, basis_ref,
+    basis_buf, zero_buf, one_buf, two_buf, sems, win_sems, basis_sem,
 ):
     del near_in
     rank = zero_buf.shape[-1]
@@ -165,6 +165,8 @@
         (one_hbm, one_buf, one_wide),
         (zero_hbm, zero_buf, zero_wide),
     )
+    basis_copy = pltpu.make_async_copy(basis_hbm, basis_buf, basis_sem)
+    basis_copy.start()
     chunks = []
     for hbm, buf, wide in levels:
         for first in range(0, buf.shape[0], 4):
@@ -187,6 +189,9 @@
     for move in moves:
         move.start()
     add_edge(near_ref, edge_ref, odd, pair_ref, pair_ref.shape[0] - LEAF, 0)
+    basis_copy.wait()
+    for leaf in range(basis_ref.shape[0]):
+        basis_ref[leaf] = basis_buf[leaf].T
     for copy, buf, wide, first in chunks:
         copy.wait()
         for node in range(first, first + 4):
@@ -203,7 +208,7 @@
 ):
     del near_in, zero_in, one_in, two_in
     leaves, fars = zero_list.shape
-    rank = basis_ref.shape[1]
+    rank = basis_ref.shape[2]
     me = me_ref[0]
     odd = lax.rem(me, 2)
     wins = (zero_win, one_win, two_win)
@@ -246,7 +251,7 @@
         total = field(zero_wide, zero_list, leaf, zero_win)
         total = total + dot(up_one_ref[leaf], down_one[leaf // 2])
         here = pl.ds(leaf * LEAF, LEAF)
-        total = near_ref[here, :] + dot_t(basis_ref[leaf], total.astype(jnp.bfloat16))
+        total = near_ref[here, :] + dot(basis_ref[leaf], total.astype(jnp.bfloat16))
         out_buf[here, :] = total.astype(jnp.bfloat16)
         if leaf % 4 == 3:
             some = pl.ds((leaf - 3) * LEAF, 4 * LEAF)
@@ -297,9 +302,9 @@
         in_specs=[smem] + [hbm] * 4,
         out_specs=[vmem] * 3,
         out_shape=[
-            jax.ShapeDtypeStruct((rows, columns), bf16),
-            jax.ShapeDtypeStruct((rows, columns), bf16),
-            jax.ShapeDtypeStruct(vectors.shape, bf16),
+            pltpu.VMEM((rows, columns), bf16),
+            pltpu.VMEM((rows, columns), bf16),
+            pltpu.VMEM(vectors.shape, bf16),
         ],
         scratch_shapes=[
             pltpu.VMEM(basis_t.shape, bf16),
@@ -311,10 +316,15 @@
         name="up_pass",
     )(me, *in_hbm(vectors, basis_t, up_one, up_two))
 
+    cores = lax.axis_size("rhs")
+
     def send(array, to):
-        return lax.ppermute(
-            array, "space", [(i, to(i) if 0 <= to(i) < size else i) for i in range(size)]
-        )
+        pairs = []
+        for i in range(size):
+            for c in range(cores):
+                j, d = (to(i), c) if 0 <= to(i) < size else (i, cores - 1 - c)
+                pairs.append((i * cores + c, j * cores + d))
+        return lax.ppermute(array, ("space", "rhs"), pairs)
 
     from_pair = send(pair, lambda i: i + 1 - 2 * (i % 2))
     first = send(plain, lambda i: i + 2 - i // 2 % 2 * 4)
@@ -352,18 +362,21 @@
     wins = [jax.ShapeDtypeStruct((SPAN * n * rank, columns), bf16) for n in counts]
     near, *rest = pl.pallas_call(
         prep_kernel,
-        in_specs=[smem] + [vmem] * 6 + [hbm] * 3,
-        out_specs=[vmem] * 7,
+        in_specs=[smem] + [vmem] * 6 + [hbm] * 4,
+        out_specs=[vmem] * 8,
         out_shape=[
             jax.ShapeDtypeStruct(vectors.shape, jnp.float32),
             *wins,
             *[jax.ShapeDtypeStruct((n, rank, fars * rank), bf16) for n in counts],
+            jax.ShapeDtypeStruct(basis.shape, bf16),
         ],
         input_output_aliases={5: 0},
         scratch_shapes=[
+            pltpu.VMEM(basis_t.shape, bf16),
             *[pltpu.VMEM((n, fars, rank, rank), bf16) for n in counts],
             pltpu.SemaphoreType.DMA((sum(n // 4 for n in counts),)),
             pltpu.SemaphoreType.DMA((12,)),
+            pltpu.SemaphoreType.DMA,
         ],
         compiler_params=pltpu.CompilerParams(vmem_limit_bytes=24 * MIB),
         cost_estimate=pl.CostEstimate(
@@ -374,9 +387,9 @@
         name="prep",
     )(
         me, plain, from_pair, first, second, near, edge,
-        *in_hbm(couple_zero, couple_one, couple_two),
-    )
-    windows, wides = rest[:3], rest[3:]
+        *in_hbm(basis_t, couple_zero, couple_one, couple_two),
+    )
+    windows, wides, basis_n = rest[:3], rest[3:6], rest[6]
 
     out, *_ = pl.pallas_call(
         functools.partial(far_kernel, size=size),
@@ -397,7 +410,7 @@
         name="far_down",
     )(
         me, far_zero, far_one, far_two, points, low, high, near, edge,
-        basis_t, up_one, up_two, *wides, *windows,
+        basis_n, up_one, up_two, *wides, *windows,
     )
     return out
 

time: 38.1 us -> 37.4 us (0.982)
  waiting for transfers between devices: 4.36 us -> 2.61 us
  Pallas kernels: 23.3 us -> 24.3 us
    ppermute x5, waiting for transfers between devices: 4.36 us -> 2.61 us  [send(): return lax.ppermute(array, ('space', 'rhs'), pairs)]
    pallas_call x1, Pallas kernels: 3.94 us -> 4.94 us  [body(): pl.pallas_call(prep_kernel, in_specs=[smem] + [vmem] * 6 + [hbm] * 4, out...]
  transfers between devices with their start and end apart: 5 -> 5, of which waited for: 2 -> 3; matrix products, arithmetic and copies ran while one was open for 0% -> 0% of each run, Pallas kernels for 36% -> 39%
where the time goes in v6:
time: 37.4 us; the launch traced here: 37.3 us
  Pallas kernels  24.3 us (65%)
  starting transfers between devices  10.2 us (27%)
  waiting for transfers between devices  2.61 us (7%)
    ppermute x5, starting transfers between devices, send(): return lax.ppermute(array, ('space', 'rhs'), pairs)  10.2 us
    pallas_call x1, Pallas kernels, body(): pl.pallas_call(near_kernel, in_specs=[smem, vmem] + [hbm] * 2, out_specs=...  9.67 us
    pallas_call x1, Pallas kernels, body(): pl.pallas_call(functools.partial(far_kernel, size=size), in_specs=[smem]...  6.73 us
    pallas_call x1, Pallas kernels, body(): pl.pallas_call(prep_kernel, in_specs=[smem] + [vmem] * 6 + [hbm] * 4, out...  4.94 us
    pallas_call x1, Pallas kernels, body(): pl.pallas_call(up_kernel, in_specs=[smem] + [hbm] * 4, out_specs=[vmem] *...  2.96 us
    ppermute x5, waiting for transfers between devices, send(): return lax.ppermute(array, ('space', 'rhs'), pairs)  2.61 us
  transfers between devices with their start and end apart: 5, of which 3 were waited for; matrix products, arithmetic and copies ran while one was open for 0% of the time, Pallas kernels for 39%

profile of v6, /device:TPU:0, one launch (start us, length us, event | category | flops | bytes accessed | tf_op | source)
XLA Modules:
  0.0 37.3 jit_solution(217189258351662088)
XLA Ops:
  0.0 3.0 %up_pass.1 = (bf16[2048,128]{1,0:T(8,128)(2,1)S(1)}, bf16[2048,128]{1,0:T(8,128)(2,1)}, bf16[4096,128]{1,0:T(8,128)(2,1)S(1)}) custom-call(s32[1]{0:T(128)} %bitcast.me_ref, bf16[4096,128]{1,0:T(8,128)(2,1)} %x_hbm.1, bf16[16,64,256]{2,1,0:T(8,128)(2,1)} %bitcast.2, bf16[16,64,64]{2,1,0:T(8,128)(2,1)} %up_one_ref.1, bf16[8,64,64]{2,1,0:T(8,128)(2,1)} %up_two_ref.1), custom_call_target="tpu_custom_call" | custom-call | tf_op jit(solution)/shard_map/up_pass/pallas_call | solution.py:300
  3.0 3.0 %collective-permute-start = (bf16[2048,128]{1,0:T(8,128)(2,1)}, bf16[2048,128]{1,0:T(8,128)(2,1)S(1)}, u32[]{:S(2)}, u32[]{:S(2)}) collective-permute-start(bf16[2048,128]{1,0:T(8,128)(2,1)} %get-tuple-element.24), channel_id=1, source_target_pairs={{0,2},{1,3},{2,0},{3,1},{4,6},{5,7},{6,4},{7,5},{8,10},{9,11},{10,... | collective-permute-start | bytes 1572872 | tf_op jit(solution)/shard_map/ppermute | solution.py:327
  6.0 0.0 collective-permute-start.2
  6.0 3.1 %collective-permute-start.1 = (bf16[2048,128]{1,0:T(8,128)(2,1)S(1)}, bf16[2048,128]{1,0:T(8,128)(2,1)S(1)}, u32[]{:S(2)}, u32[]{:S(2)}) collective-permute-start(bf16[2048,128]{1,0:T(8,128)(2,1)S(1)} %get-tuple-element.25.own_ref), channel_id=1, source_target_pairs={{0,4},{1,5},{2,6},{3,7},{4,0},{5,1},{6,2},{7,3},{8,12},{9,13},{10,... | collective-permute-start | bytes 1572872 | tf_op jit(solution)/shard_map/ppermute | solution.py:327
  9.1 9.7 %near_own.1 = (f32[4096,128]{1,0:T(8,128)S(1)}, bf16[16,2,256,256]{3,2,1,0:T(8,128)(2,1)S(1)}) custom-call(s32[1]{0:T(128)} %bitcast.me_ref, bf16[4096,128]{1,0:T(8,128)(2,1)S(1)} %get-tuple-element.23.x_ref, s32[16,12]{1,0:T(8,128)} %list_hbm.1, bf16[16,12,256,256]{3,2,1,0:T(8,128)(2,1)} %blocks_hbm.1), custom_call_target="tpu_custom_call" | custom-call | flops 2684354560 | bytes 28311552 | tf_op jit(solution)/shard_map/near_own/pallas_call | solution.py:333
  18.8 0.0 collective-permute-done.pair_ref
  18.8 0.0 collective-permute-done.2.second_ref
  18.8 1.7 %collective-permute-done.1.first_ref = bf16[2048,128]{1,0:T(8,128)(2,1)S(1)} collective-permute-done((bf16[2048,128]{1,0:T(8,128)(2,1)S(1)}, bf16[2048,128]{1,0:T(8,128)(2,1)S(1)}, u32[]{:S(2)}, u32[]{:S(2)}) %collective-permute-start.1) | collective-permute-done | bytes 524320 | tf_op jit(solution)/shard_map/ppermute | solution.py:327
  20.5 1.8 %collective-permute-start.3 = (bf16[1024,128]{1,0:T(8,128)(2,1)S(1)}, bf16[1024,128]{1,0:T(8,128)(2,1)S(1)}, u32[]{:S(2)}, u32[]{:S(2)}) collective-permute-start(bf16[1024,128]{1,0:T(8,128)(2,1)S(1)} %slice.9), channel_id=1, source_target_pairs={{0,4},{1,5},{2,14},{3,15},{4,8},{5,9},{6,2},{7,3},{8,12},{9,13},{1... | collective-permute-start | bytes 786440 | tf_op jit(solution)/shard_map/ppermute | solution.py:327
  22.3 2.3 %collective-permute-start.4 = (bf16[1024,128]{1,0:T(8,128)(2,1)S(1)}, bf16[1024,128]{1,0:T(8,128)(2,1)S(1)}, u32[]{:S(2)}, u32[]{:S(2)}) collective-permute-start(bf16[1024,128]{1,0:T(8,128)(2,1)S(1)} %slice_select_fusion), channel_id=1, source_target_pairs={{0,2},{1,3},{2,0},{3,1},{4,6},{5,7},{6,4},{7,5},{8,10},{9,11},{10,... | collective-permute-start | bytes 786440 | tf_op jit(solution)/shard_map/ppermute | solution.py:327
  24.6 0.0 copy-start
  24.6 0.0 copy-start.1
  24.6 0.0 copy-start.2
  24.6 0.0 copy-start.3
  24.6 0.0 copy-start.4
  24.6 4.9 %prep.1 = (f32[4096,128]{1,0:T(8,128)S(1)}, bf16[5120,128]{1,0:T(8,128)(2,1)S(1)}, bf16[2560,128]{1,0:T(8,128)(2,1)S(1)}, bf16[1280,128]{1,0:T(8,128)(2,1)S(1)},...) custom-call(s32[1]{0:T(128)} %bitcast.me_ref, ...), custom_call_target="tpu_custom_call", output_to_operand_aliasing={{0}: (5, {})} | custom-call | flops 268435456 | bytes 7340032 | tf_op jit(solution)/shard_map/prep/pallas_call | solution.py:363
  29.6 0.6 %collective-permute-done.3.low_ref = bf16[1024,128]{1,0:T(8,128)(2,1)S(1)} collective-permute-done((bf16[1024,128]{1,0:T(8,128)(2,1)S(1)}, bf16[1024,128]{1,0:T(8,128)(2,1)S(1)}, u32[]{:S(2)}, u32[]{:S(2)}) %collective-permute-start.3) | collective-permute-done | bytes 262176 | tf_op jit(solution)/shard_map/ppermute | solution.py:327
  30.2 0.4 collective-permute-done.4.high_ref
  30.5 0.0 copy-done
  30.5 0.0 copy-done.1
  30.5 0.0 copy-done.2
  30.5 0.0 copy-done.3
  30.6 0.0 copy-done.4
  30.6 6.7 %far_down.1 = (bf16[4096,128]{1,0:T(8,128)(2,1)}, f32[4096,128]{1,0:T(8,128)S(1)}, bf16[5120,128]{1,0:T(8,128)(2,1)S(1)}, bf16[2560,128]{1,0:T(8,128)(2,1)S(1)}, bf16[1280,128]{1,0:T(8,128)(2,1)S(1)}) custom-call(s32[1]{0:T(128)} %bitcast.me_ref, s32[16,16]{1,0:T(8,128)S(1)} %copy-done.2, ...), custom_call_target="tpu_custom_call", output_to_operand_aliasing={{1}: (7, {}), {2}: (15, {}), {3}: (16, {}), {4}: (17, {})} | custom-call | tf_op jit(solution)/shard_map/far_down/pallas_call | solution.py:394
  (2 shorter events, 0.0 us)
Async XLA Ops:
  3.0 15.8 %collective-permute-start = (bf16[2048,128]{1,0:T(8,128)(2,1)}, bf16[2048,128]{1,0:T(8,128)(2,1)S(1)}, u32[]{:S(2)}, u32[]{:S(2)}) collective-permute-start(bf16[2048,128]{1,0:T(8,128)(2,1)} %get-tuple-element.24), channel_id=1, source_target_pairs={{0,2},{1,3},{2,0},{3,1},{4,6},{5,7},{6,4},{7,5},{8,10},{9,11},{10,... | collective-permute-start | bytes 1572872 | tf_op jit(solution)/shard_map/ppermute | solution.py:327
  6.0 12.8 %collective-permute-start.2 = (bf16[2048,128]{1,0:T(8,128)(2,1)S(1)}, bf16[2048,128]{1,0:T(8,128)(2,1)S(1)}, u32[]{:S(2)}, u32[]{:S(2)}) collective-permute-start(bf16[2048,128]{1,0:T(8,128)(2,1)S(1)} %get-tuple-element.25.own_ref), channel_id=1, source_target_pairs={{0,1},{1,0},{2,3},{3,2},{4,8},{5,9},{6,10},{7,11},{8,4},{9,5},{10,... | collective-permute-start | bytes 1572872 | tf_op jit(solution)/shard_map/ppermute | solution.py:327
  6.0 14.5 %collective-permute-start.1 = (bf16[2048,128]{1,0:T(8,128)(2,1)S(1)}, bf16[2048,128]{1,0:T(8,128)(2,1)S(1)}, u32[]{:S(2)}, u32[]{:S(2)}) collective-permute-start(bf16[2048,128]{1,0:T(8,128)(2,1)S(1)} %get-tuple-element.25.own_ref), channel_id=1, source_target_pairs={{0,4},{1,5},{2,6},{3,7},{4,0},{5,1},{6,2},{7,3},{8,12},{9,13},{10,... | collective-permute-start | bytes 1572872 | tf_op jit(solution)/shard_map/ppermute | solution.py:327
  20.5 9.7 %collective-permute-start.3 = (bf16[1024,128]{1,0:T(8,128)(2,1)S(1)}, bf16[1024,128]{1,0:T(8,128)(2,1)S(1)}, u32[]{:S(2)}, u32[]{:S(2)}) collective-permute-start(bf16[1024,128]{1,0:T(8,128)(2,1)S(1)} %slice.9), channel_id=1, source_target_pairs={{0,4},{1,5},{2,14},{3,15},{4,8},{5,9},{6,2},{7,3},{8,12},{9,13},{1... | collective-permute-start | bytes 786440 | tf_op jit(solution)/shard_map/ppermute | solution.py:327
  22.3 8.2 %collective-permute-start.4 = (bf16[1024,128]{1,0:T(8,128)(2,1)S(1)}, bf16[1024,128]{1,0:T(8,128)(2,1)S(1)}, u32[]{:S(2)}, u32[]{:S(2)}) collective-permute-start(bf16[1024,128]{1,0:T(8,128)(2,1)S(1)} %slice_select_fusion), channel_id=1, source_target_pairs={{0,2},{1,3},{2,0},{3,1},{4,6},{5,7},{6,4},{7,5},{8,10},{9,11},{10,... | collective-permute-start | bytes 786440 | tf_op jit(solution)/shard_map/ppermute | solution.py:327
  24.6 5.9 %copy-start = (bf16[16,64,64]{2,1,0:T(8,128)(2,1)S(1)}, bf16[16,64,64]{2,1,0:T(8,128)(2,1)}, u32[]{:S(2)}) copy-start(bf16[16,64,64]{2,1,0:T(8,128)(2,1)} %up_one_ref.1) | copy-start | bytes 393220
  24.6 5.9 %copy-start.1 = (bf16[8,64,64]{2,1,0:T(8,128)(2,1)S(1)}, bf16[8,64,64]{2,1,0:T(8,128)(2,1)}, u32[]{:S(2)}) copy-start(bf16[8,64,64]{2,1,0:T(8,128)(2,1)} %up_two_ref.1) | copy-start | bytes 196612
  24.6 5.9 %copy-start.2 = (s32[16,16]{1,0:T(8,128)S(1)}, s32[16,16]{1,0:T(8,128)}, u32[]{:S(2)}) copy-start(s32[16,16]{1,0:T(8,128)} %zero_list.1) | copy-start | bytes 3076
  24.6 5.9 %copy-start.3 = (s32[8,16]{1,0:T(8,128)S(1)}, s32[8,16]{1,0:T(8,128)}, u32[]{:S(2)}) copy-start(s32[8,16]{1,0:T(8,128)} %one_list.1) | copy-start | bytes 1540
  24.6 5.9 %copy-start.4 = (s32[4,16]{1,0:T(4,128)S(1)}, s32[4,16]{1,0:T(4,128)}, u32[]{:S(2)}) copy-start(s32[4,16]{1,0:T(4,128)} %two_list.1) | copy-start | bytes 772

commit v7 on v5

--- a/solution.py
+++ b/solution.py
@@ -23,8 +23,8 @@
 
 
 def up_kernel(
-    me_ref, x_hbm, basis_hbm, up_one_hbm, up_two_hbm, plain_ref, pair_ref, x_ref,
-    basis_ref, up_one_ref, up_two_ref, sems,
+    me_ref, x_hbm, basis_hbm, up_one_hbm, up_two_hbm, plain_ref, pair_ref, points_ref,
+    x_ref, basis_ref, up_one_ref, up_two_ref, sems,
 ):
     leaves, rank = basis_ref.shape[:2]
     steps = leaves // 4
@@ -42,7 +42,8 @@
         pltpu.make_async_copy(up_one_hbm, up_one_ref, sems.at[2 * steps]),
         pltpu.make_async_copy(up_two_hbm, up_two_ref, sems.at[2 * steps + 1]),
     )
-    for pair in (*copies, ups):
+    keep = pltpu.make_async_copy(x_hbm, points_ref, sems.at[2 * steps + 2])
+    for pair in (*copies, ups, (keep,)):
         for copy in pair:
             copy.start()
 
@@ -76,6 +77,7 @@
     end = pl.ds(plain_ref.shape[0] - LEAF, LEAF)
     pair_ref[end, :] = x_ref[pl.ds(pl.multiple_of((1 - odd) * last, LEAF), LEAF), :]
     plain_ref[end, :] = x_ref[pl.ds(pl.multiple_of(odd * last, LEAF), LEAF), :]
+    keep.wait()
 
 
 def near_kernel(
@@ -123,13 +125,13 @@
     lax.fori_loop(0, leaves, step, 0)
 
 
-def add_edge(near_ref, edge_ref, side, ref, start, stride):
+def add_edge(sum_ref, near_ref, edge_ref, side, ref, start, stride):
     leaves = edge_ref.shape[0]
 
     def step(leaf, carry):
         here = pl.ds(pl.multiple_of(leaf * LEAF, LEAF), LEAF)
         rows = ref[pl.ds(pl.multiple_of(start + leaf * stride, LEAF), LEAF), :]
-        near_ref[here, :] += dot(edge_ref[leaf, side], rows)
+        sum_ref[here, :] = near_ref[here, :] + dot(edge_ref[leaf, side], rows)
         return carry
 
     lax.fori_loop(0, leaves, step, 0, unroll=4)
@@ -153,12 +155,11 @@
 
 
 def prep_kernel(
-    me_ref, own_ref, pair_ref, first_ref, second_ref, near_in, edge_ref,
+    me_ref, own_ref, pair_ref, first_ref, second_ref, near_ref, edge_ref,
     zero_hbm, one_hbm, two_hbm,
-    near_ref, zero_win, one_win, two_win, zero_wide, one_wide, two_wide,
-    zero_buf, one_buf, two_buf, sems, win_sems,
+    sum_ref, zero_win, one_win, two_win, zero_wide, one_wide, two_wide,
+    sum_buf, zero_buf, one_buf, two_buf, sems, win_sems, sum_sem,
 ):
-    del near_in
     rank = zero_buf.shape[-1]
     levels = (
         (two_hbm, two_buf, two_wide),
@@ -186,7 +187,9 @@
     moves = window_copies(plans, wins, sizes, win_sems)
     for move in moves:
         move.start()
-    add_edge(near_ref, edge_ref, odd, pair_ref, pair_ref.shape[0] - LEAF, 0)
+    add_edge(sum_buf, near_ref, edge_ref, odd, pair_ref, pair_ref.shape[0] - LEAF, 0)
+    moves.append(pltpu.make_async_copy(sum_buf, sum_ref, sum_sem))
+    moves[-1].start()
     for copy, buf, wide, first in chunks:
         copy.wait()
         for node in range(first, first + 4):
@@ -197,11 +200,11 @@
 
 
 def far_kernel(
-    me_ref, zero_list, one_list, two_list, x_ref, low_ref, high_ref, near_in, edge_ref,
+    me_ref, zero_list, one_list, two_list, x_ref, low_first, low_second, high_ref, near_ref, edge_ref,
     basis_ref, up_one_ref, up_two_ref, zero_wide, one_wide, two_wide, zero_in, one_in, two_in,
-    out_hbm, near_ref, zero_win, one_win, two_win, out_buf, win_sems, out_sems, *, size,
+    out_hbm, zero_win, one_win, two_win, sum_buf, out_buf, win_sems, out_sems, *, size,
 ):
-    del near_in, zero_in, one_in, two_in
+    del zero_in, one_in, two_in
     leaves, fars = zero_list.shape
     rank = basis_ref.shape[1]
     me = me_ref[0]
@@ -209,19 +212,24 @@
     wins = (zero_win, one_win, two_win)
     sizes = [win.shape[0] // SPAN for win in wins]
     place = REACH - 1 + 2 * odd
-    moves = window_copies(((low_ref, (0,), place), (high_ref, (1, 2), place)), wins, sizes, win_sems)
-    for move in moves:
+    plans = ((low_first, (0,), place), (high_ref, (1, 2), place))
+    moves = window_copies(plans, wins, sizes, win_sems)
+    other = window_copies(((low_second, (0,), place),), wins, sizes, win_sems)[0]
+    from_first = lax.rem(me + me // 2, 2) == 1
+    for move in moves[1:]:
         move.start()
+    pl.when(from_first)(moves[0].start)
+    pl.when(jnp.logical_not(from_first))(other.start)
 
     alone = (me == 0) | (me == size - 1)
 
     @pl.when(alone)
     def _():
-        add_edge(near_ref, edge_ref, 1 - odd, x_ref, 0, LEAF)
+        add_edge(sum_buf, near_ref, edge_ref, 1 - odd, x_ref, 0, LEAF)
 
     @pl.when(jnp.logical_not(alone))
     def _():
-        add_edge(near_ref, edge_ref, 1 - odd, high_ref, high_ref.shape[0] - LEAF, 0)
+        add_edge(sum_buf, near_ref, edge_ref, 1 - odd, high_ref, high_ref.shape[0] - LEAF, 0)
 
     for move in moves:
         move.wait()
@@ -246,7 +254,7 @@
         total = field(zero_wide, zero_list, leaf, zero_win)
         total = total + dot(up_one_ref[leaf], down_one[leaf // 2])
         here = pl.ds(leaf * LEAF, LEAF)
-        total = near_ref[here, :] + dot_t(basis_ref[leaf], total.astype(jnp.bfloat16))
+        total = sum_buf[here, :] + dot_t(basis_ref[leaf], total.astype(jnp.bfloat16))
         out_buf[here, :] = total.astype(jnp.bfloat16)
         if leaf % 4 == 3:
             some = pl.ds((leaf - 3) * LEAF, 4 * LEAF)
@@ -297,28 +305,34 @@
         in_specs=[smem] + [hbm] * 4,
         out_specs=[vmem] * 3,
         out_shape=[
-            jax.ShapeDtypeStruct((rows, columns), bf16),
-            jax.ShapeDtypeStruct((rows, columns), bf16),
-            jax.ShapeDtypeStruct(vectors.shape, bf16),
+            pltpu.VMEM((rows, columns), bf16),
+            pltpu.VMEM((rows, columns), bf16),
+            pltpu.VMEM(vectors.shape, bf16),
         ],
         scratch_shapes=[
+            pltpu.VMEM(vectors.shape, bf16),
             pltpu.VMEM(basis_t.shape, bf16),
             pltpu.VMEM(up_one.shape, bf16),
             pltpu.VMEM(up_two.shape, bf16),
-            pltpu.SemaphoreType.DMA((leaves // 2 + 2,)),
+            pltpu.SemaphoreType.DMA((leaves // 2 + 3,)),
         ],
         compiler_params=pltpu.CompilerParams(vmem_limit_bytes=16 * MIB),
         name="up_pass",
     )(me, *in_hbm(vectors, basis_t, up_one, up_two))
 
+    cores = lax.axis_size("rhs")
+
     def send(array, to):
-        return lax.ppermute(
-            array, "space", [(i, to(i) if 0 <= to(i) < size else i) for i in range(size)]
-        )
+        pairs = []
+        for i in range(size):
+            for c in range(cores):
+                j, d = (to(i), c) if 0 <= to(i) < size else (i, cores - 1 - c)
+                pairs.append((i * cores + c, j * cores + d))
+        return lax.ppermute(array, ("space", "rhs"), pairs)
 
     from_pair = send(pair, lambda i: i + 1 - 2 * (i % 2))
-    first = send(plain, lambda i: i + 2 - i // 2 % 2 * 4)
-    second = send(plain, lambda i: i - 2 + i // 2 % 2 * 4)
+    turns = (lambda i: i + 2 - i // 2 % 2 * 4, lambda i: i - 2 + i // 2 % 2 * 4)
+    first, second = [send(plain, turn) for turn in turns]
 
     near, edge = pl.pallas_call(
         near_kernel,
@@ -343,9 +357,10 @@
         name="near_own",
     )(me, points, *in_hbm(near_list, near_blocks))
 
-    from_pair, first, second, near = lax.optimization_barrier((from_pair, first, second, near))
     split = leaves * rank
-    low = send(from_pair[:split], lambda i: (i + 2 - 4 * (i % 2)) % size)
+    from_pair, near = lax.optimization_barrier((from_pair, near))
+    lows = [send(from_pair[:split], turn) for turn in turns]
+    first, second, near = lax.optimization_barrier((first, second, near))
     upper = jnp.where((me[0] // 2 + me[0]) % 2 == 0, first[split:], second[split:])
     high = send(upper, lambda i: i + 1 - 2 * (i % 2))
 
@@ -359,11 +374,12 @@
             *wins,
             *[jax.ShapeDtypeStruct((n, rank, fars * rank), bf16) for n in counts],
         ],
-        input_output_aliases={5: 0},
         scratch_shapes=[
+            pltpu.VMEM(vectors.shape, jnp.float32),
             *[pltpu.VMEM((n, fars, rank, rank), bf16) for n in counts],
             pltpu.SemaphoreType.DMA((sum(n // 4 for n in counts),)),
             pltpu.SemaphoreType.DMA((12,)),
+            pltpu.SemaphoreType.DMA,
         ],
         compiler_params=pltpu.CompilerParams(vmem_limit_bytes=24 * MIB),
         cost_estimate=pl.CostEstimate(
@@ -380,15 +396,12 @@
 
     out, *_ = pl.pallas_call(
         functools.partial(far_kernel, size=size),
-        in_specs=[smem] * 4 + [vmem] * 14,
-        out_specs=[hbm] + [vmem] * 4,
-        out_shape=[
-            jax.ShapeDtypeStruct(vectors.shape, bf16),
-            jax.ShapeDtypeStruct(vectors.shape, jnp.float32),
-            *wins,
-        ],
-        input_output_aliases={7: 1, 15: 2, 16: 3, 17: 4},
+        in_specs=[smem] * 4 + [vmem] * 15,
+        out_specs=[hbm] + [vmem] * 3,
+        out_shape=[jax.ShapeDtypeStruct(vectors.shape, bf16), *wins],
+        input_output_aliases={16: 1, 17: 2, 18: 3},
         scratch_shapes=[
+            pltpu.VMEM(vectors.shape, jnp.float32),
             pltpu.VMEM(vectors.shape, bf16),
             pltpu.SemaphoreType.DMA((3,)),
             pltpu.SemaphoreType.DMA((leaves // 4,)),
@@ -396,7 +409,7 @@
         compiler_params=pltpu.CompilerParams(vmem_limit_bytes=24 * MIB),
         name="far_down",
     )(
-        me, far_zero, far_one, far_two, points, low, high, near, edge,
+        me, far_zero, far_one, far_two, points, *lows, high, near, edge,
         basis_t, up_one, up_two, *wides, *windows,
     )
     return out

time: 38.1 us -> 34.5 us (0.906)
  starting transfers between devices: 10.1 us -> 7.95 us
  waiting for transfers between devices: 4.36 us -> 2.79 us
    ppermute x5 -> x6, starting transfers between devices: 10.1 us -> 7.95 us  [send(): return lax.ppermute(array, ('space', 'rhs'), pairs)]
    ppermute x5 -> x6, waiting for transfers between devices: 4.36 us -> 2.79 us  [send(): return lax.ppermute(array, ('space', 'rhs'), pairs)]
  transfers between devices with their start and end apart: 5 -> 6, of which waited for: 2 -> 3; matrix products, arithmetic and copies ran while one was open for 0% -> 0% of each run, Pallas kernels for 36% -> 40%
where the time goes in v7:
time: 34.5 us; the launch traced here: 34.4 us
  Pallas kernels  23.4 us (68%)
  starting transfers between devices  7.95 us (23%)
  waiting for transfers between devices  2.79 us (8%)
    pallas_call x1, Pallas kernels, body(): pl.pallas_call(near_kernel, in_specs=[smem, vmem] + [hbm] * 2, out_specs=...  9.67 us
    ppermute x6, starting transfers between devices, send(): return lax.ppermute(array, ('space', 'rhs'), pairs)  7.95 us
    pallas_call x1, Pallas kernels, body(): pl.pallas_call(functools.partial(far_kernel, size=size), in_specs=[smem]...  6.69 us
    pallas_call x1, Pallas kernels, body(): pl.pallas_call(prep_kernel, in_specs=[smem] + [vmem] * 6 + [hbm] * 3, out...  4.11 us
    pallas_call x1, Pallas kernels, body(): pl.pallas_call(up_kernel, in_specs=[smem] + [hbm] * 4, out_specs=[vmem] *...  2.96 us
    ppermute x6, waiting for transfers between devices, send(): return lax.ppermute(array, ('space', 'rhs'), pairs)  2.79 us
  transfers between devices with their start and end apart: 6, of which 3 were waited for; matrix products, arithmetic and copies ran while one was open for 0% of the time, Pallas kernels for 40%

profile of v7, /device:TPU:0, one launch (start us, length us, event | category | flops | bytes accessed | tf_op | source)
XLA Modules:
  0.0 34.4 jit_solution(2618802860599523897)
XLA Ops:
  0.0 3.0 %up_pass.1 = (bf16[2048,128]{1,0:T(8,128)(2,1)S(1)}, bf16[2048,128]{1,0:T(8,128)(2,1)}, bf16[4096,128]{1,0:T(8,128)(2,1)S(1)}) custom-call(s32[1]{0:T(128)} %bitcast.me_ref, bf16[4096,128]{1,0:T(8,128)(2,1)} %x_hbm.1, bf16[16,64,256]{2,1,0:T(8,128)(2,1)} %bitcast.2, bf16[16,64,64]{2,1,0:T(8,128)(2,1)} %up_one_ref.1, bf16[8,64,64]{2,1,0:T(8,128)(2,1)} %up_two_ref.1), custom_call_target="tpu_custom_call" | custom-call | tf_op jit(solution)/shard_map/up_pass/pallas_call | solution.py:303
  3.0 3.0 %collective-permute-start = (bf16[2048,128]{1,0:T(8,128)(2,1)}, bf16[2048,128]{1,0:T(8,128)(2,1)S(1)}, u32[]{:S(2)}, u32[]{:S(2)}) collective-permute-start(bf16[2048,128]{1,0:T(8,128)(2,1)} %get-tuple-element.24), channel_id=1, source_target_pairs={{0,2},{1,3},{2,0},{3,1},{4,6},{5,7},{6,4},{7,5},{8,10},{9,11},{10,... | collective-permute-start | bytes 1572872 | tf_op jit(solution)/shard_map/ppermute | solution.py:331
  6.0 1.6 %collective-permute-start.3 = (bf16[2048,128]{1,0:T(8,128)(2,1)S(1)}, bf16[2048,128]{1,0:T(8,128)(2,1)S(1)}, u32[]{:S(2)}, u32[]{:S(2)}) collective-permute-start(bf16[2048,128]{1,0:T(8,128)(2,1)S(1)} %get-tuple-element.27.own_ref), channel_id=1, source_target_pairs={{0,4},{1,5},{2,6},{3,7},{4,0},{5,1},{6,2},{7,3},{8,12},{9,13},{10,... | collective-permute-start | bytes 1572872 | tf_op jit(solution)/shard_map/ppermute | solution.py:331
  7.6 0.0 collective-permute-start.4
  7.6 9.7 %near_own.1 = (f32[4096,128]{1,0:T(8,128)S(1)}, bf16[16,2,256,256]{3,2,1,0:T(8,128)(2,1)S(1)}) custom-call(s32[1]{0:T(128)} %bitcast.me_ref, bf16[4096,128]{1,0:T(8,128)(2,1)S(1)} %get-tuple-element.23.x_ref, s32[16,12]{1,0:T(8,128)} %list_hbm.1, bf16[16,12,256,256]{3,2,1,0:T(8,128)(2,1)} %blocks_hbm.1), custom_call_target="tpu_custom_call" | custom-call | flops 2684354560 | bytes 28311552 | tf_op jit(solution)/shard_map/near_own/pallas_call | solution.py:337
  17.2 0.9 %collective-permute-done.pair_ref = bf16[2048,128]{1,0:T(8,128)(2,1)S(1)} collective-permute-done((bf16[2048,128]{1,0:T(8,128)(2,1)}, bf16[2048,128]{1,0:T(8,128)(2,1)S(1)}, u32[]{:S(2)}, u32[]{:S(2)}) %collective-permute-start) | collective-permute-done | bytes 524320 | tf_op jit(solution)/shard_map/ppermute | solution.py:331
  18.1 1.2 %collective-permute-done.3.first_ref = bf16[2048,128]{1,0:T(8,128)(2,1)S(1)} collective-permute-done((bf16[2048,128]{1,0:T(8,128)(2,1)S(1)}, bf16[2048,128]{1,0:T(8,128)(2,1)S(1)}, u32[]{:S(2)}, u32[]{:S(2)}) %collective-permute-start.3) | collective-permute-done | bytes 524320 | tf_op jit(solution)/shard_map/ppermute | solution.py:331
  19.4 0.0 collective-permute-done.4.second_ref
  19.4 0.6 %collective-permute-start.5 = (bf16[1024,128]{1,0:T(8,128)(2,1)S(1)}, bf16[1024,128]{1,0:T(8,128)(2,1)S(1)}, u32[]{:S(2)}, u32[]{:S(2)}) collective-permute-start(bf16[1024,128]{1,0:T(8,128)(2,1)S(1)} %slice_select_fusion), channel_id=1, source_target_pairs={{0,2},{1,3},{2,0},{3,1},{4,6},{5,7},{6,4},{7,5},{8,10},{9,11},{10,... | collective-permute-start | bytes 786440 | tf_op jit(solution)/shard_map/ppermute | solution.py:331
  20.0 2.8 %collective-permute-start.1 = (bf16[1024,128]{1,0:T(8,128)(2,1)S(1)}, bf16[1024,128]{1,0:T(8,128)(2,1)S(1)}, u32[]{:S(2)}, u32[]{:S(2)}) collective-permute-start(bf16[1024,128]{1,0:T(8,128)(2,1)S(1)} %slice.10), channel_id=1, source_target_pairs={{0,4},{1,5},{2,6},{3,7},{4,0},{5,1},{6,2},{7,3},{8,12},{9,13},{10,... | collective-permute-start | bytes 786440 | tf_op jit(solution)/shard_map/ppermute | solution.py:331
  22.8 0.0 collective-permute-start.2
  22.8 0.0 copy-start
  22.8 0.0 copy-start.1
  22.8 0.0 copy-start.2
  22.8 0.0 copy-start.3
  22.8 0.0 copy-start.4
  22.8 0.0 copy-start.5
  22.8 4.1 %prep.1 = (f32[4096,128]{1,0:T(8,128)S(1)}, bf16[5120,128]{1,0:T(8,128)(2,1)S(1)}, bf16[2560,128]{1,0:T(8,128)(2,1)S(1)}, bf16[1280,128]{1,0:T(8,128)(2,1)S(1)},...) custom-call(s32[1]{0:T(128)} %bitcast.me_ref, ...), custom_call_target="tpu_custom_call" | custom-call | flops 268435456 | bytes 7340032 | tf_op jit(solution)/shard_map/prep/pallas_call | solution.py:368
  27.0 0.0 collective-permute-done.5.high_ref
  27.0 0.7 %collective-permute-done.1.low_first = bf16[1024,128]{1,0:T(8,128)(2,1)S(1)} collective-permute-done((bf16[1024,128]{1,0:T(8,128)(2,1)S(1)}, bf16[1024,128]{1,0:T(8,128)(2,1)S(1)}, u32[]{:S(2)}, u32[]{:S(2)}) %collective-permute-start.1) | collective-permute-done | bytes 262176 | tf_op jit(solution)/shard_map/ppermute | solution.py:331
  27.6 0.0 collective-permute-done.2.low_second
  27.6 0.0 copy-done
  27.6 0.0 copy-done.1
  27.6 0.0 copy-done.2
  27.6 0.0 copy-done.3
  27.7 0.0 copy-done.4
  27.7 0.0 copy-done.5
  27.7 6.7 %far_down.1 = (bf16[4096,128]{1,0:T(8,128)(2,1)}, bf16[5120,128]{1,0:T(8,128)(2,1)S(1)}, bf16[2560,128]{1,0:T(8,128)(2,1)S(1)}, bf16[1280,128]{1,0:T(8,128)(2,1)S(1)}) custom-call(s32[1]{0:T(128)} %bitcast.me_ref, s32[16,16]{1,0:T(8,128)S(1)} %copy-done.3, s32[8,16]{1,0:T(8,128)S(1)} %copy-done.4, ...), custom_call_target="tpu_custom_call", output_to_operand_aliasing={{1}: (16, {}), {2}: (17, {}), {3}: (18, {})} | custom-call | tf_op jit(solution)/shard_map/far_down/pallas_call | solution.py:397
  (2 shorter events, 0.0 us)
Async XLA Ops:
  3.0 15.1 %collective-permute-start = (bf16[2048,128]{1,0:T(8,128)(2,1)}, bf16[2048,128]{1,0:T(8,128)(2,1)S(1)}, u32[]{:S(2)}, u32[]{:S(2)}) collective-permute-start(bf16[2048,128]{1,0:T(8,128)(2,1)} %get-tuple-element.24), channel_id=1, source_target_pairs={{0,2},{1,3},{2,0},{3,1},{4,6},{5,7},{6,4},{7,5},{8,10},{9,11},{10,... | collective-permute-start | bytes 1572872 | tf_op jit(solution)/shard_map/ppermute | solution.py:331
  6.0 13.4 %collective-permute-start.3 = (bf16[2048,128]{1,0:T(8,128)(2,1)S(1)}, bf16[2048,128]{1,0:T(8,128)(2,1)S(1)}, u32[]{:S(2)}, u32[]{:S(2)}) collective-permute-start(bf16[2048,128]{1,0:T(8,128)(2,1)S(1)} %get-tuple-element.27.own_ref), channel_id=1, source_target_pairs={{0,4},{1,5},{2,6},{3,7},{4,0},{5,1},{6,2},{7,3},{8,12},{9,13},{10,... | collective-permute-start | bytes 1572872 | tf_op jit(solution)/shard_map/ppermute | solution.py:331
  7.6 11.8 %collective-permute-start.4 = (bf16[2048,128]{1,0:T(8,128)(2,1)S(1)}, bf16[2048,128]{1,0:T(8,128)(2,1)S(1)}, u32[]{:S(2)}, u32[]{:S(2)}) collective-permute-start(bf16[2048,128]{1,0:T(8,128)(2,1)S(1)} %get-tuple-element.27.own_ref), channel_id=1, source_target_pairs={{0,1},{1,0},{2,3},{3,2},{4,8},{5,9},{6,10},{7,11},{8,4},{9,5},{10,... | collective-permute-start | bytes 1572872 | tf_op jit(solution)/shard_map/ppermute | solution.py:331
  19.4 7.6 %collective-permute-start.5 = (bf16[1024,128]{1,0:T(8,128)(2,1)S(1)}, bf16[1024,128]{1,0:T(8,128)(2,1)S(1)}, u32[]{:S(2)}, u32[]{:S(2)}) collective-permute-start(bf16[1024,128]{1,0:T(8,128)(2,1)S(1)} %slice_select_fusion), channel_id=1, source_target_pairs={{0,2},{1,3},{2,0},{3,1},{4,6},{5,7},{6,4},{7,5},{8,10},{9,11},{10,... | collective-permute-start | bytes 786440 | tf_op jit(solution)/shard_map/ppermute | solution.py:331
  20.0 7.6 %collective-permute-start.1 = (bf16[1024,128]{1,0:T(8,128)(2,1)S(1)}, bf16[1024,128]{1,0:T(8,128)(2,1)S(1)}, u32[]{:S(2)}, u32[]{:S(2)}) collective-permute-start(bf16[1024,128]{1,0:T(8,128)(2,1)S(1)} %slice.10), channel_id=1, source_target_pairs={{0,4},{1,5},{2,6},{3,7},{4,0},{5,1},{6,2},{7,3},{8,12},{9,13},{10,... | collective-permute-start | bytes 786440 | tf_op jit(solution)/shard_map/ppermute | solution.py:331
  22.8 4.8 %collective-permute-start.2 = (bf16[1024,128]{1,0:T(8,128)(2,1)S(1)}, bf16[1024,128]{1,0:T(8,128)(2,1)S(1)}, u32[]{:S(2)}, u32[]{:S(2)}) collective-permute-start(bf16[1024,128]{1,0:T(8,128)(2,1)S(1)} %slice.10), channel_id=1, source_target_pairs={{0,1},{1,0},{2,3},{3,2},{4,8},{5,9},{6,10},{7,11},{8,4},{9,5},{10,... | collective-permute-start | bytes 786440 | tf_op jit(solution)/shard_map/ppermute | solution.py:331
  22.8 4.8 %copy-start = (bf16[16,256,64]{1,2,0:T(8,128)(2,1)S(1)}, bf16[16,256,64]{1,2,0:T(8,128)(2,1)}, u32[]{:S(2)}) copy-start(bf16[16,256,64]{1,2,0:T(8,128)(2,1)} %param.15) | copy-start | bytes 1572868
  22.8 4.8 %copy-start.1 = (bf16[16,64,64]{2,1,0:T(8,128)(2,1)S(1)}, bf16[16,64,64]{2,1,0:T(8,128)(2,1)}, u32[]{:S(2)}) copy-start(bf16[16,64,64]{2,1,0:T(8,128)(2,1)} %up_one_ref.1) | copy-start | bytes 393220
  22.8 4.8 %copy-start.2 = (bf16[8,64,64]{2,1,0:T(8,128)(2,1)S(1)}, bf16[8,64,64]{2,1,0:T(8,128)(2,1)}, u32[]{:S(2)}) copy-start(bf16[8,64,64]{2,1,0:T(8,128)(2,1)} %up_two_ref.1) | copy-start | bytes 196612
  22.8 4.8 %copy-start.3 = (s32[16,16]{1,0:T(8,128)S(1)}, s32[16,16]{1,0:T(8,128)}, u32[]{:S(2)}) copy-start(s32[16,16]{1,0:T(8,128)} %zero_list.1) | copy-start | bytes 3076
  22.8 4.8 %copy-start.4 = (s32[8,16]{1,0:T(8,128)S(1)}, s32[8,16]{1,0:T(8,128)}, u32[]{:S(2)}) copy-start(s32[8,16]{1,0:T(8,128)} %one_list.1) | copy-start | bytes 1540
  22.8 4.8 %copy-start.5 = (s32[4,16]{1,0:T(4,128)S(1)}, s32[4,16]{1,0:T(4,128)}, u32[]{:S(2)}) copy-start(s32[4,16]{1,0:T(4,128)} %two_list.1) | copy-start | bytes 772

commit v8 on v7

v8 whole, which is shorter than its diff:
```python
import functools

import jax
import jax.numpy as jnp
from jax import lax
from jax.experimental import pallas as pl
from jax.experimental.pallas import tpu as pltpu
from jax.sharding import PartitionSpec as P

LEAF = 256
REACH = 2
SPAN = 2 * REACH + 1
DEPTH = 4
MIB = 1024 * 1024


def dot(a, b):
    return jnp.dot(a, b, preferred_element_type=jnp.float32)


def dot_t(a, b):
    return lax.dot_general(a, b, (((0,), (0,)), ((), ())), preferred_element_type=jnp.float32)


def up_kernel(
    me_ref, x_hbm, basis_hbm, up_one_hbm, up_two_hbm, plain_ref, pair_ref,
    x_ref, basis_ref, up_one_ref, up_two_ref, sems,
):
    leaves, rank = basis_ref.shape[:2]
    steps = leaves // 4
    copies = []
    for q in range(steps):
        rows = pl.ds(q * 4 * LEAF, 4 * LEAF)
        some = pl.ds(q * 4, 4)
        copies.append(
            (
                pltpu.make_async_copy(x_hbm.at[rows, :], x_ref.at[rows, :], sems.at[2 * q]),
                pltpu.make_async_copy(basis_hbm.at[some], basis_ref.at[some], sems.at[2 * q + 1]),
            )
        )
    ups = (
        pltpu.make_async_copy(up_one_hbm, up_one_ref, sems.at[2 * steps]),
        pltpu.make_async_copy(up_two_hbm, up_two_ref, sems.at[2 * steps + 1]),
    )
    for pair in (*copies, ups):
        for copy in pair:
            copy.start()

    def put(node, value):
        value = value.astype(jnp.bfloat16)
        plain_ref[pl.ds(node * rank, rank), :] = value
        pair_ref[pl.ds(2 * LEAF + node * rank, rank), :] = value
        return value

    def join(ups, pair):
        return dot_t(ups.reshape(2 * rank, rank), jnp.concatenate(pair, axis=0))

    zeros = []
    for q in range(steps):
        for copy in copies[q]:
            copy.wait()
        for leaf in range(4 * q, 4 * q + 4):
            coef = dot(basis_ref[leaf], x_ref[pl.ds(leaf * LEAF, LEAF), :])
            zeros.append(put(leaf, coef))
    for copy in ups:
        copy.wait()
    ones = []
    for p in range(leaves // 2):
        pair = slice(2 * p, 2 * p + 2)
        ones.append(put(leaves + p, join(up_one_ref[pair], zeros[pair])))
    for q in range(leaves // 4):
        pair = slice(2 * q, 2 * q + 2)
        put(leaves + leaves // 2 + q, join(up_two_ref[pair], ones[pair]))
    odd = lax.rem(me_ref[0], 2)
    last = (leaves - 1) * LEAF
    near_edge = pl.multiple_of((1 - odd) * last, LEAF)
    far_edge = pl.multiple_of(odd * last, LEAF)
    pair_ref[pl.ds(0, LEAF), :] = x_ref[pl.ds(near_edge, LEAF), :]
    pair_ref[pl.ds(LEAF, LEAF), :] = x_ref[pl.ds(far_edge, LEAF), :]


def last_place(me):
    return REACH - 1 + 2 * lax.rem(me, 2)


def near_kernel(
    me_ref, x_ref, near_hbm, zero_list_hbm, one_list_hbm, two_list_hbm,
    blocks_hbm, zero_hbm, one_hbm, two_hbm,
    out_ref, edge_ref, zero_wide, one_wide, two_wide, starts_ref,
    near_list, zero_list, one_list, two_list, turn_ref,
    block_buf, zero_buf, upper_buf, sems, list_sems,
):
    leaves, nears = near_list.shape
    ones, twos = one_wide.shape[0], two_wide.shape[0]
    fars, rank = zero_buf.shape[1:3]
    total = leaves + ones + twos
    me = me_ref[0]

    def copies(leaf, slot):
        pairs = (
            (blocks_hbm.at[leaf, pl.ds(0, 1)], block_buf.at[slot, pl.ds(0, 1)]),
            (blocks_hbm.at[leaf, pl.ds(3, nears - 3)], block_buf.at[slot, pl.ds(1, nears - 3)]),
            (blocks_hbm.at[leaf, pl.ds(1, 2)], edge_ref.at[leaf]),
            (zero_hbm.at[leaf], zero_buf.at[slot]),
        )
        return [
            pltpu.make_async_copy(src, dst, sems.at[slot, i]) for i, (src, dst) in enumerate(pairs)
        ]

    def upper(leaf, slot, act):
        sem = sems.at[slot, 4]

        @pl.when(leaf < ones)
        def _():
            act(pltpu.make_async_copy(one_hbm.at[leaf], upper_buf.at[slot], sem))

        @pl.when((leaf >= ones) & (leaf < ones + twos))
        def _():
            act(pltpu.make_async_copy(two_hbm.at[leaf - ones], upper_buf.at[slot], sem))

    def fetch(leaf, slot):
        for copy in copies(leaf, slot):
            copy.start()
        upper(leaf, slot, lambda copy: copy.start())

    hbms = (near_hbm, zero_list_hbm, one_list_hbm, two_list_hbm)
    lists = (near_list, zero_list, one_list, two_list)
    moves = [
        pltpu.make_async_copy(src, dst, list_sems.at[i])
        for i, (src, dst) in enumerate(zip(hbms, lists))
    ]
    for move in moves:
        move.start()
    for leaf in range(DEPTH - 1):
        fetch(leaf, leaf)
    starts_ref[total, 0] = 0
    for move in moves:
        move.wait()

    def pack(where, node, row, buf, wide):
        per = where.shape[0]
        first = (me - REACH) * per
        low = last_place(me) * per
        count = jnp.int32(0)
        for k in range(fars):
            index = where[node, k] - first
            late = (index >= low) & (index < low + per)
            at = jnp.where(late, count, fars - 1 - k + count)
            starts_ref[row, at] = index * rank
            turn_ref[at] = k
            count = count + late.astype(jnp.int32)
        starts_ref[total, 0] = jnp.maximum(starts_ref[total, 0], count)
        wide[node] = jnp.concatenate([buf[turn_ref[k]] for k in range(fars)], axis=1)

    def step(leaf, carry):
        slot = lax.rem(leaf, DEPTH)

        @pl.when(leaf + DEPTH - 1 < leaves)
        def _():
            fetch(leaf + DEPTH - 1, lax.rem(leaf + DEPTH - 1, DEPTH))

        for copy in copies(leaf, slot):
            copy.wait()
        upper(leaf, slot, lambda copy: copy.wait())
        rows = []
        for k in (0, *range(3, nears)):
            start = pl.multiple_of((near_list[leaf, k] - me * leaves) * LEAF, LEAF)
            rows.append(x_ref[pl.ds(start, LEAF), :])
        blocks = [block_buf[slot, k] for k in range(nears - 2)]
        here = pl.ds(pl.multiple_of(leaf * LEAF, LEAF), LEAF)
        out_ref[here, :] = dot(jnp.concatenate(blocks, axis=1), jnp.concatenate(rows, axis=0))
        pack(zero_list, leaf, leaf, zero_buf.at[slot], zero_wide)

        @pl.when(leaf < ones)
        def _():
            pack(one_list, leaf, leaves + leaf, upper_buf.at[slot], one_wide)

        @pl.when((leaf >= ones) & (leaf < ones + twos))
        def _():
            pack(two_list, leaf - ones, leaves + leaf, upper_buf.at[slot], two_wide)

        return carry

    lax.fori_loop(0, leaves, step, 0)


def add_edge(sum_ref, near_ref, edge_ref, side, ref, start, stride):
    leaves = edge_ref.shape[0]

    def step(leaf, carry):
        here = pl.ds(pl.multiple_of(leaf * LEAF, LEAF), LEAF)
        rows = ref[pl.ds(pl.multiple_of(start + leaf * stride, LEAF), LEAF), :]
        sum_ref[here, :] = near_ref[here, :] + dot(edge_ref[leaf, side], rows)
        return carry

    lax.fori_loop(0, leaves, step, 0, unroll=4)


def window_copies(plans, sems):
    copies = []
    for ref, start, win, at, size in plans:
        copies.append(
            pltpu.make_async_copy(
                ref.at[pl.ds(start, size), :], win.at[pl.ds(at, size), :], sems.at[len(copies)]
            )
        )
    return copies


def field(wide, starts_ref, row, win, slots):
    rank = wide.shape[0]
    rows = []
    for k in slots:
        rows.append(win[pl.ds(pl.multiple_of(starts_ref[row, k], rank), rank), :])
    some = wide[:, slots[0] * rank : (slots[-1] + 1) * rank]
    return dot(some, jnp.concatenate(rows, axis=0))


def mid_kernel(
    me_ref, starts_ref, own_ref, pair_ref, first_ref, second_ref, near_ref, edge_ref,
    zero_wide, one_wide, two_wide, sum_ref, zero_win, one_win, two_win, part_ref, sems,
):
    me = me_ref[0]
    odd = lax.rem(me, 2)
    block = lax.rem(me // 2, 2)
    wins, wides = (zero_win, one_win, two_win), (zero_wide, one_wide, two_wide)
    pieces = (
        (own_ref, 0, REACH),
        (first_ref, 0, (1 - block) * (SPAN - 1)),
        (second_ref, 0, block * (SPAN - 1)),
        (pair_ref, 2 * LEAF, REACH + 1 - 2 * odd),
    )
    plans = []
    for ref, start, place in pieces:
        for win in wins:
            size = win.shape[0] // SPAN
            plans.append((ref, start, win, pl.multiple_of(place * size, size), size))
            start += size
    moves = window_copies(plans, sems)
    for move in moves:
        move.start()
    add_edge(sum_ref, near_ref, edge_ref, odd, pair_ref, 0, 0)
    for move in moves:
        move.wait()
    row = 0
    for wide, win in zip(wides, wins):
        nodes, rank, deep = wide.shape
        fars = deep // rank
        for node in range(nodes):
            part = field(wide.at[node], starts_ref, row, win, range(fars // 2, fars))
            part_ref[pl.ds(row * rank, rank), :] = part
            row += 1


def far_kernel(
    me_ref, starts_ref, x_ref, low_first, low_second, high_ref, near_ref, edge_ref,
    basis_ref, up_one_ref, up_two_ref, zero_wide, one_wide, two_wide,
    zero_in, one_in, two_in, part_in,
    out_hbm, zero_win, one_win, two_win, part_ref, sum_buf, out_buf, win_sems, out_sems, *, size,
):
    del zero_in, one_in, two_in, part_in
    leaves, rank, deep = zero_wide.shape
    ones, twos = leaves // 2, leaves // 4
    fars = deep // rank
    me = me_ref[0]
    odd = lax.rem(me, 2)
    place = last_place(me)
    sizes = [n * rank for n in (leaves, ones, twos)]
    at = [pl.multiple_of(place * n, n) for n in sizes]
    split = sizes[0] - LEAF
    moves = window_copies(
        (
            (low_first, LEAF, zero_win, at[0], split),
            (high_ref, 0, zero_win, pl.multiple_of(at[0] + split, LEAF), LEAF),
            (high_ref, LEAF, one_win, at[1], sizes[1]),
            (high_ref, LEAF + sizes[1], two_win, at[2], sizes[2]),
        ),
        win_sems,
    )
    other = window_copies(((low_second, LEAF, zero_win, at[0], split),), win_sems)[0]
    from_first = lax.rem(me + me // 2, 2) == 1
    for move in moves[1:]:
        move.start()
    pl.when(from_first)(moves[0].start)
    pl.when(jnp.logical_not(from_first))(other.start)

    alone = (me == 0) | (me == size - 1)

    @pl.when(alone)
    def _():
        add_edge(sum_buf, near_ref, edge_ref, 1 - odd, x_ref, 0, LEAF)

    @pl.when(jnp.logical_not(alone) & from_first)
    def _():
        add_edge(sum_buf, near_ref, edge_ref, 1 - odd, low_first, 0, 0)

    @pl.when(jnp.logical_not(alone) & jnp.logical_not(from_first))
    def _():
        add_edge(sum_buf, near_ref, edge_ref, 1 - odd, low_second, 0, 0)

    for move in moves:
        move.wait()

    @pl.when(starts_ref[leaves + ones + twos, 0] > fars // 2)
    def _():
        levels = ((zero_wide, zero_win, 0), (one_wide, one_win, leaves))
        for wide, win, base in (*levels, (two_wide, two_win, leaves + ones)):

            def again(node, carry):
                row = base + node
                part = field(wide.at[node], starts_ref, row, win, range(fars // 2, fars))
                part_ref[pl.ds(pl.multiple_of(row * rank, rank), rank), :] = part
                return carry

            lax.fori_loop(0, wide.shape[0], again, 0)

    def whole_field(wide, win, node, row):
        part = part_ref[pl.ds(row * rank, rank), :]
        return part + field(wide.at[node], starts_ref, row, win, range(fars // 2))

    down_two = [
        whole_field(two_wide, two_win, q, leaves + ones + q).astype(jnp.bfloat16)
        for q in range(twos)
    ]
    down_one = []
    for p in range(ones):
        total = whole_field(one_wide, one_win, p, leaves + p) + dot(up_two_ref[p], down_two[p // 2])
        down_one.append(total.astype(jnp.bfloat16))
    outs = []
    for leaf in range(leaves):
        total = whole_field(zero_wide, zero_win, leaf, leaf)
        total = total + dot(up_one_ref[leaf], down_one[leaf // 2])
        here = pl.ds(leaf * LEAF, LEAF)
        total = sum_buf[here, :] + dot_t(basis_ref[leaf], total.astype(jnp.bfloat16))
        out_buf[here, :] = total.astype(jnp.bfloat16)
        if leaf % 4 == 3:
            some = pl.ds((leaf - 3) * LEAF, 4 * LEAF)
            outs.append(
                pltpu.make_async_copy(
                    out_buf.at[some, :], out_hbm.at[some, :], out_sems.at[leaf // 4]
                )
            )
            outs[-1].start()
    for copy in outs:
        copy.wait()


def body(
    vectors,
    near_blocks,
    near_list,
    basis,
    up_one,
    up_two,
    couple_zero,
    couple_one,
    couple_two,
    far_zero,
    far_one,
    far_two,
):
    leaves, nears = near_list.shape
    columns = vectors.shape[1]
    rank = basis.shape[2]
    fars = far_zero.shape[1]
    size = lax.axis_size("space")
    cores = lax.axis_size("rhs")
    me = lax.axis_index("space").astype(jnp.int32).reshape(1)
    counts = (leaves, leaves // 2, leaves // 4)
    nodes = sum(counts)
    basis_t = jnp.swapaxes(basis, 1, 2)
    bf16, f32 = jnp.bfloat16, jnp.float32

    hbm = pl.BlockSpec(memory_space=pltpu.HBM)
    vmem = pl.BlockSpec(memory_space=pltpu.VMEM)
    smem = pl.BlockSpec(memory_space=pltpu.SMEM)

    def in_hbm(*arrays):
        return [pltpu.with_memory_space_constraint(a, pltpu.HBM) for a in arrays]

    plain, pair = pl.pallas_call(
        up_kernel,
        in_specs=[smem] + [hbm] * 4,
        out_specs=[vmem] * 2,
        out_shape=[
            pltpu.VMEM((nodes * rank, columns), bf16),
            pltpu.VMEM((2 * LEAF + nodes * rank, columns), bf16),
        ],
        scratch_shapes=[
            pltpu.VMEM(vectors.shape, bf16),
            pltpu.VMEM(basis_t.shape, bf16),
            pltpu.VMEM(up_one.shape, bf16),
            pltpu.VMEM(up_two.shape, bf16),
            pltpu.SemaphoreType.DMA((leaves // 2 + 2,)),
        ],
        compiler_params=pltpu.CompilerParams(vmem_limit_bytes=8 * MIB),
        name="up_pass",
    )(me, *in_hbm(vectors, basis_t, up_one, up_two))

    def send(array, to):
        pairs = []
        for i in range(size):
            for c in range(cores):
                j, d = (to(i), c) if 0 <= to(i) < size else (i, cores - 1 - c)
                pairs.append((i * cores + c, j * cores + d))
        return lax.ppermute(array, ("space", "rhs"), pairs)

    def partner(i):
        return i + 1 - 2 * (i % 2)

    from_pair = send(pair, partner)
    turns = (lambda i: i + 2 - i // 2 % 2 * 4, lambda i: i - 2 + i // 2 % 2 * 4)
    first, second = [send(plain, turn) for turn in turns]

    near, edge, *wides, starts = pl.pallas_call(
        near_kernel,
        in_specs=[smem, vmem] + [hbm] * 8,
        out_specs=[vmem] * 5 + [smem],
        out_shape=[
            pltpu.VMEM(vectors.shape, f32),
            pltpu.VMEM((leaves, 2, LEAF, LEAF), bf16),
            *[pltpu.VMEM((n, rank, fars * rank), bf16) for n in counts],
            jax.ShapeDtypeStruct((nodes + 1, fars), jnp.int32),
        ],
        scratch_shapes=[
            *[pltpu.SMEM(a.shape, jnp.int32) for a in (near_list, far_zero, far_one, far_two)],
            pltpu.SMEM((fars,), jnp.int32),
            pltpu.VMEM((DEPTH, nears - 2, LEAF, LEAF), bf16),
            pltpu.VMEM((DEPTH, fars, rank, rank), bf16),
            pltpu.VMEM((DEPTH, fars, rank, rank), bf16),
            pltpu.SemaphoreType.DMA((DEPTH, 5)),
            pltpu.SemaphoreType.DMA((4,)),
        ],
        compiler_params=pltpu.CompilerParams(vmem_limit_bytes=16 * MIB),
        cost_estimate=pl.CostEstimate(
            flops=2 * leaves * (nears - 2) * LEAF * LEAF * columns,
            bytes_accessed=2 * leaves * nears * LEAF * LEAF + 6 * leaves * LEAF * columns,
            transcendentals=0,
        ),
        name="near_own",
    )(
        me,
        pltpu.with_memory_space_constraint(vectors, pltpu.VMEM),
        *in_hbm(near_list, far_zero, far_one, far_two),
        *in_hbm(near_blocks, couple_zero, couple_one, couple_two),
    )

    split = leaves * rank - LEAF
    from_pair, near = lax.optimization_barrier((from_pair, near))
    lows = [send(from_pair[LEAF : 2 * LEAF + split], turn) for turn in turns]
    first, second, near = lax.optimization_barrier((first, second, near))
    upper = jnp.where((me[0] // 2 + me[0]) % 2 == 0, first[split:], second[split:])
    high = send(upper, partner)

    sums, *windows, part = pl.pallas_call(
        mid_kernel,
        in_specs=[smem] * 2 + [vmem] * 9,
        out_specs=[vmem] * 5,
        out_shape=[
            pltpu.VMEM(vectors.shape, f32),
            *[pltpu.VMEM((SPAN * n * rank, columns), bf16) for n in counts],
            pltpu.VMEM((nodes * rank, columns), f32),
        ],
        scratch_shapes=[pltpu.SemaphoreType.DMA((12,))],
        compiler_params=pltpu.CompilerParams(vmem_limit_bytes=8 * MIB),
        cost_estimate=pl.CostEstimate(
            flops=2 * leaves * LEAF * LEAF * columns + nodes * fars * rank * rank * columns,
            bytes_accessed=4 * nodes * fars * rank * rank,
            transcendentals=0,
        ),
        name="mid",
    )(me, starts, plain, from_pair, first, second, near, edge, *wides)

    out, *_ = pl.pallas_call(
        functools.partial(far_kernel, size=size),
        in_specs=[smem] * 2 + [vmem] * 16,
        out_specs=[hbm] + [vmem] * 4,
        out_shape=[
            jax.ShapeDtypeStruct(vectors.shape, bf16),
            *[pltpu.VMEM((SPAN * n * rank, columns), bf16) for n in counts],
            pltpu.VMEM((nodes * rank, columns), f32),
        ],
        input_output_aliases={14: 1, 15: 2, 16: 3, 17: 4},
        scratch_shapes=[
            pltpu.VMEM(vectors.shape, f32),
            pltpu.VMEM(vectors.shape, bf16),
            pltpu.SemaphoreType.DMA((4,)),
            pltpu.SemaphoreType.DMA((leaves // 4,)),
        ],
        compiler_params=pltpu.CompilerParams(vmem_limit_bytes=16 * MIB),
        name="far_down",
    )(
        me, starts, pltpu.with_memory_space_constraint(vectors, pltpu.VMEM), *lows, high, sums, edge,
        basis_t, up_one, up_two, *wides, *windows, part,
    )
    return out


def solution(mesh):
    placed = (
        P(("groups", "space"), "rhs"),
        P("space", None, None, None),
        P("space", None),
        P("space", None, None),
        P("space", None, None),
        P("space", None, None),
        P("space", None, None, None),
        P("space", None, None, None),
        P("space", None, None, None),
        P("space", None),
        P("space", None),
        P("space", None),
    )
    return jax.shard_map(
        body, mesh=mesh, in_specs=placed, out_specs=P(("groups", "space"), "rhs"), check_vma=False
    )
```

time: 34.5 us -> 39.3 us (1.14)
  Pallas kernels: 23.4 us -> 27.2 us
  waiting for transfers between devices: 2.79 us -> 3.46 us
  starting transfers between devices: 7.95 us -> 8.39 us
    pallas_call x2, Pallas kernels: 13.8 us -> 17.4 us  [the longest x1 13.5 us: body(): pl.pallas_call(near_kernel, in_specs=[smem, vmem] + [hbm] * 8, out_specs=...]
    ppermute x6, waiting for transfers between devices: 2.79 us -> 3.46 us  [send(): return lax.ppermute(array, ('space', 'rhs'), pairs)]
    ppermute x6, starting transfers between devices: 7.95 us -> 8.39 us  [send(): return lax.ppermute(array, ('space', 'rhs'), pairs)]
  transfers between devices with their start and end apart: 6 -> 6, of which waited for: 3 -> 2; matrix products, arithmetic and copies ran while one was open for 0% -> 0% of each run, Pallas kernels for 40% -> 44%
where the time goes in v8:
time: 39.3 us; the launch traced here: 39.2 us
  Pallas kernels  27.2 us (69%)
  starting transfers between devices  8.39 us (21%)
  waiting for transfers between devices  3.46 us (9%)
    pallas_call x1, Pallas kernels, body(): pl.pallas_call(near_kernel, in_specs=[smem, vmem] + [hbm] * 8, out_specs=...  13.5 us
    ppermute x6, starting transfers between devices, send(): return lax.ppermute(array, ('space', 'rhs'), pairs)  8.39 us
    pallas_call x1, Pallas kernels, body(): pl.pallas_call(functools.partial(far_kernel, size=size), in_specs=[smem]...  6.69 us
    pallas_call x1, Pallas kernels, body(): pl.pallas_call(mid_kernel, in_specs=[smem] * 2 + [vmem] * 9, out_specs=[v...  3.87 us
    ppermute x6, waiting for transfers between devices, send(): return lax.ppermute(array, ('space', 'rhs'), pairs)  3.46 us
    pallas_call x1, Pallas kernels, body(): pl.pallas_call(up_kernel, in_specs=[smem] + [hbm] * 4, out_specs=[vmem] *...  3.07 us
  transfers between devices with their start and end apart: 6, of which 2 were waited for; matrix products, arithmetic and copies ran while one was open for 0% of the time, Pallas kernels for 44%

profile of v8, /device:TPU:0, one launch (start us, length us, event | category | flops | bytes accessed | tf_op | source)
XLA Modules:
  0.0 39.2 jit_solution(2908286230923861232)
XLA Ops:
  0.0 0.0 copy-start
  0.0 3.1 %up_pass.1 = (bf16[1792,128]{1,0:T(8,128)(2,1)S(1)}, bf16[2304,128]{1,0:T(8,128)(2,1)}) custom-call(s32[1]{0:T(128)} %bitcast.me_ref, bf16[4096,128]{1,0:T(8,128)(2,1)} %x_ref.3, bf16[16,64,256]{2,1,0:T(8,128)(2,1)} %bitcast.2, bf16[16,64,64]{2,1,0:T(8,128)(2,1)} %up_one_ref.1, bf16[8,64,64]{2,1,0:T(8,128)(2,1)} %up_two_ref.1), custom_call_target="tpu_custom_call" | custom-call | tf_op jit(solution)/shard_map/up_pass/pallas_call | solution.py:381
  3.1 3.0 %collective-permute-start = (bf16[2304,128]{1,0:T(8,128)(2,1)}, bf16[2304,128]{1,0:T(8,128)(2,1)S(1)}, u32[]{:S(2)}, u32[]{:S(2)}) collective-permute-start(bf16[2304,128]{1,0:T(8,128)(2,1)} %get-tuple-element.25), channel_id=1, source_target_pairs={{0,2},{1,3},{2,0},{3,1},{4,6},{5,7},{6,4},{7,5},{8,10},{9,11},{10,... | collective-permute-start | bytes 1769480 | tf_op jit(solution)/shard_map/ppermute | solution.py:406
  6.1 0.0 collective-permute-start.4
  6.1 3.1 %collective-permute-start.3 = (bf16[1792,128]{1,0:T(8,128)(2,1)S(1)}, bf16[1792,128]{1,0:T(8,128)(2,1)S(1)}, u32[]{:S(2)}, u32[]{:S(2)}) collective-permute-start(bf16[1792,128]{1,0:T(8,128)(2,1)S(1)} %get-tuple-element.28.own_ref), channel_id=1, source_target_pairs={{0,4},{1,5},{2,6},{3,7},{4,0},{5,1},{6,2},{7,3},{8,12},{9,13},{10,... | collective-permute-start | bytes 1376264 | tf_op jit(solution)/shard_map/ppermute | solution.py:406
  9.2 0.0 copy-done
  9.2 13.5 %near_own.1 = (f32[4096,128]{1,0:T(8,128)S(1)}, bf16[16,2,256,256]{3,2,1,0:T(8,128)(2,1)S(1)}, bf16[16,64,1024]{2,1,0:T(8,128)(2,1)S(1)}, bf16[8,64,1024]{2,1,0:...) custom-call(s32[1]{0:T(128)} %bitcast.me_ref, bf16[4096,128]{1,0:T(8,128)(2,1)S(1)} %copy-done, ...), custom_call_target="tpu_custom_call" | custom-call | flops 2684354560 | bytes 28311552 | tf_op jit(solution)/shard_map/near_own/pallas_call | solution.py:415
  22.8 0.0 collective-permute-done.pair_ref
  22.8 0.1 collective-permute-start.2
  22.9 1.6 %collective-permute-start.1 = (bf16[1024,128]{1,0:T(8,128)(2,1)S(1)}, bf16[1024,128]{1,0:T(8,128)(2,1)S(1)}, u32[]{:S(2)}, u32[]{:S(2)}) collective-permute-start(bf16[1024,128]{1,0:T(8,128)(2,1)S(1)} %slice.10), channel_id=1, source_target_pairs={{0,4},{1,5},{2,6},{3,7},{4,0},{5,1},{6,2},{7,3},{8,12},{9,13},{10,... | collective-permute-start | bytes 786440 | tf_op jit(solution)/shard_map/ppermute | solution.py:406
  24.5 0.0 collective-permute-done.4.second_ref
  24.5 0.0 collective-permute-done.3.first_ref
  24.5 0.6 %collective-permute-start.5 = (bf16[1024,128]{1,0:T(8,128)(2,1)S(1)}, bf16[1024,128]{1,0:T(8,128)(2,1)S(1)}, u32[]{:S(2)}, u32[]{:S(2)}) collective-permute-start(bf16[1024,128]{1,0:T(8,128)(2,1)S(1)} %slice_select_fusion), channel_id=1, source_target_pairs={{0,2},{1,3},{2,0},{3,1},{4,6},{5,7},{6,4},{7,5},{8,10},{9,11},{10,... | collective-permute-start | bytes 786440 | tf_op jit(solution)/shard_map/ppermute | solution.py:406
  25.1 0.0 copy-start.1
  25.1 0.0 copy-start.2
  25.1 0.0 copy-start.3
  25.1 3.9 %mid.1 = (f32[4096,128]{1,0:T(8,128)S(1)}, bf16[5120,128]{1,0:T(8,128)(2,1)S(1)}, bf16[2560,128]{1,0:T(8,128)(2,1)S(1)}, bf16[1280,128]{1,0:T(8,128)(2,1)S(1)}, f32[1792,128]{1,0:T(8,128)S(1)}) custom-call(s32[1]{0:T(128)} %bitcast.me_ref, s32[29,16]{1,0:T(8,128)S(1)} %get-tuple-element.24.starts_ref, bf16[1792,128]{1,0:T(8,128)(2,1)S(1)} %get-tuple-element.28.own_ref, ...), custom_call_target="tpu_custom_call" | custom-call | flops 503316480 | bytes 7340032 | tf_op jit(solution)/shard_map/mid/pallas_call | solution.py:455
  29.0 0.0 collective-permute-done.2.low_second
  29.0 2.6 %collective-permute-done.1.low_first = bf16[1024,128]{1,0:T(8,128)(2,1)S(1)} collective-permute-done((bf16[1024,128]{1,0:T(8,128)(2,1)S(1)}, bf16[1024,128]{1,0:T(8,128)(2,1)S(1)}, u32[]{:S(2)}, u32[]{:S(2)}) %collective-permute-start.1) | collective-permute-done | bytes 262176 | tf_op jit(solution)/shard_map/ppermute | solution.py:406
  31.6 0.8 %collective-permute-done.5.high_ref = bf16[1024,128]{1,0:T(8,128)(2,1)S(1)} collective-permute-done((bf16[1024,128]{1,0:T(8,128)(2,1)S(1)}, bf16[1024,128]{1,0:T(8,128)(2,1)S(1)}, u32[]{:S(2)}, u32[]{:S(2)}) %collective-permute-start.5) | collective-permute-done | bytes 262176 | tf_op jit(solution)/shard_map/ppermute | solution.py:406
  32.5 0.0 copy-done.1
  32.5 0.0 copy-done.2
  32.5 0.0 copy-done.3
  32.5 6.7 %far_down.1 = (bf16[4096,128]{1,0:T(8,128)(2,1)}, bf16[5120,128]{1,0:T(8,128)(2,1)S(1)}, bf16[2560,128]{1,0:T(8,128)(2,1)S(1)}, bf16[1280,128]{1,0:T(8,128)(2,1)S(1)}, f32[1792,128]{1,0:T(8,128)S(1)}) custom-call(s32[1]{0:T(128)} %bitcast.me_ref, ...), custom_call_target="tpu_custom_call", output_to_operand_aliasing={{1}: (14, {}), {2}: (15, {}), {3}: (16, {}), {4}: (17, {})} | custom-call | tf_op jit(solution)/shard_map/far_down/pallas_call | solution.py:474
  (2 shorter events, 0.0 us)
Async XLA Ops:
  0.0 9.2 %copy-start = (bf16[4096,128]{1,0:T(8,128)(2,1)S(1)}, bf16[4096,128]{1,0:T(8,128)(2,1)}, u32[]{:S(2)}) copy-start(bf16[4096,128]{1,0:T(8,128)(2,1)} %x_ref.3) | copy-start | bytes 3145732
  3.1 19.7 %collective-permute-start = (bf16[2304,128]{1,0:T(8,128)(2,1)}, bf16[2304,128]{1,0:T(8,128)(2,1)S(1)}, u32[]{:S(2)}, u32[]{:S(2)}) collective-permute-start(bf16[2304,128]{1,0:T(8,128)(2,1)} %get-tuple-element.25), channel_id=1, source_target_pairs={{0,2},{1,3},{2,0},{3,1},{4,6},{5,7},{6,4},{7,5},{8,10},{9,11},{10,... | collective-permute-start | bytes 1769480 | tf_op jit(solution)/shard_map/ppermute | solution.py:406
  6.1 18.4 %collective-permute-start.4 = (bf16[1792,128]{1,0:T(8,128)(2,1)S(1)}, bf16[1792,128]{1,0:T(8,128)(2,1)S(1)}, u32[]{:S(2)}, u32[]{:S(2)}) collective-permute-start(bf16[1792,128]{1,0:T(8,128)(2,1)S(1)} %get-tuple-element.28.own_ref), channel_id=1, source_target_pairs={{0,1},{1,0},{2,3},{3,2},{4,8},{5,9},{6,10},{7,11},{8,4},{9,5},{10,... | collective-permute-start | bytes 1376264 | tf_op jit(solution)/shard_map/ppermute | solution.py:406
  6.1 18.4 %collective-permute-start.3 = (bf16[1792,128]{1,0:T(8,128)(2,1)S(1)}, bf16[1792,128]{1,0:T(8,128)(2,1)S(1)}, u32[]{:S(2)}, u32[]{:S(2)}) collective-permute-start(bf16[1792,128]{1,0:T(8,128)(2,1)S(1)} %get-tuple-element.28.own_ref), channel_id=1, source_target_pairs={{0,4},{1,5},{2,6},{3,7},{4,0},{5,1},{6,2},{7,3},{8,12},{9,13},{10,... | collective-permute-start | bytes 1376264 | tf_op jit(solution)/shard_map/ppermute | solution.py:406
  22.8 6.2 %collective-permute-start.2 = (bf16[1024,128]{1,0:T(8,128)(2,1)S(1)}, bf16[1024,128]{1,0:T(8,128)(2,1)S(1)}, u32[]{:S(2)}, u32[]{:S(2)}) collective-permute-start(bf16[1024,128]{1,0:T(8,128)(2,1)S(1)} %slice.10), channel_id=1, source_target_pairs={{0,1},{1,0},{2,3},{3,2},{4,8},{5,9},{6,10},{7,11},{8,4},{9,5},{10,... | collective-permute-start | bytes 786440 | tf_op jit(solution)/shard_map/ppermute | solution.py:406
  22.9 8.7 %collective-permute-start.1 = (bf16[1024,128]{1,0:T(8,128)(2,1)S(1)}, bf16[1024,128]{1,0:T(8,128)(2,1)S(1)}, u32[]{:S(2)}, u32[]{:S(2)}) collective-permute-start(bf16[1024,128]{1,0:T(8,128)(2,1)S(1)} %slice.10), channel_id=1, source_target_pairs={{0,4},{1,5},{2,6},{3,7},{4,0},{5,1},{6,2},{7,3},{8,12},{9,13},{10,... | collective-permute-start | bytes 786440 | tf_op jit(solution)/shard_map/ppermute | solution.py:406
  24.5 7.9 %collective-permute-start.5 = (bf16[1024,128]{1,0:T(8,128)(2,1)S(1)}, bf16[1024,128]{1,0:T(8,128)(2,1)S(1)}, u32[]{:S(2)}, u32[]{:S(2)}) collective-permute-start(bf16[1024,128]{1,0:T(8,128)(2,1)S(1)} %slice_select_fusion), channel_id=1, source_target_pairs={{0,2},{1,3},{2,0},{3,1},{4,6},{5,7},{6,4},{7,5},{8,10},{9,11},{10,... | collective-permute-start | bytes 786440 | tf_op jit(solution)/shard_map/ppermute | solution.py:406
  25.1 7.3 %copy-start.1 = (bf16[16,256,64]{1,2,0:T(8,128)(2,1)S(1)}, bf16[16,256,64]{1,2,0:T(8,128)(2,1)}, u32[]{:S(2)}) copy-start(bf16[16,256,64]{1,2,0:T(8,128)(2,1)} %param.15) | copy-start | bytes 1572868
  25.1 7.3 %copy-start.2 = (bf16[16,64,64]{2,1,0:T(8,128)(2,1)S(1)}, bf16[16,64,64]{2,1,0:T(8,128)(2,1)}, u32[]{:S(2)}) copy-start(bf16[16,64,64]{2,1,0:T(8,128)(2,1)} %up_one_ref.1) | copy-start | bytes 393220
  25.1 7.3 %copy-start.3 = (bf16[8,64,64]{2,1,0:T(8,128)(2,1)S(1)}, bf16[8,64,64]{2,1,0:T(8,128)(2,1)}, u32[]{:S(2)}) copy-start(bf16[8,64,64]{2,1,0:T(8,128)(2,1)} %up_two_ref.1) | copy-start | bytes 196612

commit v9 on v7

v9 whole, which is shorter than its diff:
```python
import functools

import jax
import jax.numpy as jnp
from jax import lax
from jax.experimental import pallas as pl
from jax.experimental.pallas import tpu as pltpu
from jax.sharding import PartitionSpec as P

LEAF = 256
REACH = 2
SPAN = 2 * REACH + 1
DEPTH = 4
MIB = 1024 * 1024


def dot(a, b):
    return jnp.dot(a, b, preferred_element_type=jnp.float32)


def dot_t(a, b):
    return lax.dot_general(a, b, (((0,), (0,)), ((), ())), preferred_element_type=jnp.float32)


def up_kernel(
    me_ref, x_hbm, basis_hbm, up_one_hbm, up_two_hbm, plain_ref, pair_ref,
    x_ref, basis_ref, up_one_ref, up_two_ref, sems,
):
    leaves, rank = basis_ref.shape[:2]
    steps = leaves // 4
    copies = []
    for q in range(steps):
        rows = pl.ds(q * 4 * LEAF, 4 * LEAF)
        some = pl.ds(q * 4, 4)
        copies.append(
            (
                pltpu.make_async_copy(x_hbm.at[rows, :], x_ref.at[rows, :], sems.at[2 * q]),
                pltpu.make_async_copy(basis_hbm.at[some], basis_ref.at[some], sems.at[2 * q + 1]),
            )
        )
    ups = (
        pltpu.make_async_copy(up_one_hbm, up_one_ref, sems.at[2 * steps]),
        pltpu.make_async_copy(up_two_hbm, up_two_ref, sems.at[2 * steps + 1]),
    )
    for pair in (*copies, ups):
        for copy in pair:
            copy.start()

    def put(node, value):
        value = value.astype(jnp.bfloat16)
        plain_ref[pl.ds(node * rank, rank), :] = value
        pair_ref[pl.ds(2 * LEAF + node * rank, rank), :] = value
        return value

    def join(ups, pair):
        return dot_t(ups.reshape(2 * rank, rank), jnp.concatenate(pair, axis=0))

    zeros = []
    for q in range(steps):
        for copy in copies[q]:
            copy.wait()
        for leaf in range(4 * q, 4 * q + 4):
            coef = dot(basis_ref[leaf], x_ref[pl.ds(leaf * LEAF, LEAF), :])
            zeros.append(put(leaf, coef))
    for copy in ups:
        copy.wait()
    ones = []
    for p in range(leaves // 2):
        pair = slice(2 * p, 2 * p + 2)
        ones.append(put(leaves + p, join(up_one_ref[pair], zeros[pair])))
    for q in range(leaves // 4):
        pair = slice(2 * q, 2 * q + 2)
        put(leaves + leaves // 2 + q, join(up_two_ref[pair], ones[pair]))
    odd = lax.rem(me_ref[0], 2)
    last = (leaves - 1) * LEAF
    near_edge = pl.multiple_of((1 - odd) * last, LEAF)
    far_edge = pl.multiple_of(odd * last, LEAF)
    pair_ref[pl.ds(0, LEAF), :] = x_ref[pl.ds(near_edge, LEAF), :]
    pair_ref[pl.ds(LEAF, LEAF), :] = x_ref[pl.ds(far_edge, LEAF), :]


def last_place(me):
    return REACH - 1 + 2 * lax.rem(me, 2)


def near_kernel(
    me_ref, list_hbm, x_hbm, blocks_hbm, out_ref, edge_ref, x_ref,
    list_ref, block_buf, sems, x_sem, list_sem,
):
    leaves, nears = list_ref.shape
    first = me_ref[0] * leaves

    def copies(leaf, slot):
        pairs = (
            (blocks_hbm.at[leaf, pl.ds(0, 1)], block_buf.at[slot, pl.ds(0, 1)]),
            (blocks_hbm.at[leaf, pl.ds(3, nears - 3)], block_buf.at[slot, pl.ds(1, nears - 3)]),
            (blocks_hbm.at[leaf, pl.ds(1, 2)], edge_ref.at[leaf]),
        )
        return [
            pltpu.make_async_copy(src, dst, sems.at[slot, i]) for i, (src, dst) in enumerate(pairs)
        ]

    list_copy = pltpu.make_async_copy(list_hbm, list_ref, list_sem)
    x_copy = pltpu.make_async_copy(x_hbm, x_ref, x_sem)
    list_copy.start()
    x_copy.start()
    for leaf in range(DEPTH - 1):
        for copy in copies(leaf, leaf):
            copy.start()
    list_copy.wait()
    x_copy.wait()

    def step(leaf, carry):
        slot = lax.rem(leaf, DEPTH)

        @pl.when(leaf + DEPTH - 1 < leaves)
        def _():
            for copy in copies(leaf + DEPTH - 1, lax.rem(leaf + DEPTH - 1, DEPTH)):
                copy.start()

        for copy in copies(leaf, slot):
            copy.wait()
        rows = []
        for k in (0, *range(3, nears)):
            start = pl.multiple_of((list_ref[leaf, k] - first) * LEAF, LEAF)
            rows.append(x_ref[pl.ds(start, LEAF), :])
        blocks = [block_buf[slot, k] for k in range(nears - 2)]
        here = pl.ds(pl.multiple_of(leaf * LEAF, LEAF), LEAF)
        out_ref[here, :] = dot(jnp.concatenate(blocks, axis=1), jnp.concatenate(rows, axis=0))
        return carry

    lax.fori_loop(0, leaves, step, 0)


def add_edge(sum_ref, near_ref, edge_ref, side, rows):
    for leaf in range(edge_ref.shape[0]):
        here = pl.ds(leaf * LEAF, LEAF)
        sum_ref[here, :] = near_ref[here, :] + dot(edge_ref[leaf, side], rows)


def window_copies(plans, sems):
    copies = []
    for ref, start, win, at, size in plans:
        copies.append(
            pltpu.make_async_copy(
                ref.at[pl.ds(start, size), :], win.at[pl.ds(at, size), :], sems.at[len(copies)]
            )
        )
    return copies


def prep_kernel(
    me_ref, own_ref, pair_ref, first_ref, second_ref, near_ref, edge_ref,
    zero_hbm, one_hbm, two_hbm,
    sum_ref, zero_win, one_win, two_win, zero_wide, one_wide, two_wide,
    zero_buf, one_buf, two_buf, sems, win_sems,
):
    levels = (
        (two_hbm, two_buf, two_wide),
        (one_hbm, one_buf, one_wide),
        (zero_hbm, zero_buf, zero_wide),
    )
    chunks = []
    for hbm, buf, wide in levels:
        for first in range(0, buf.shape[0], 4):
            some = pl.ds(first, 4)
            copy = pltpu.make_async_copy(hbm.at[some], buf.at[some], sems.at[len(chunks)])
            copy.start()
            chunks.append((copy, buf, wide, first))
    me = me_ref[0]
    odd = lax.rem(me, 2)
    block = lax.rem(me // 2, 2)
    pieces = (
        (own_ref, 0, REACH),
        (first_ref, 0, (1 - block) * (SPAN - 1)),
        (second_ref, 0, block * (SPAN - 1)),
        (pair_ref, 2 * LEAF, REACH + 1 - 2 * odd),
    )
    plans = []
    for ref, start, place in pieces:
        for win in (zero_win, one_win, two_win):
            size = win.shape[0] // SPAN
            plans.append((ref, start, win, pl.multiple_of(place * size, size), size))
            start += size
    moves = window_copies(plans, win_sems)
    for move in moves:
        move.start()
    add_edge(sum_ref, near_ref, edge_ref, odd, pair_ref[pl.ds(0, LEAF), :])
    for copy, buf, wide, first in chunks:
        copy.wait()
        for node in range(first, first + 4):
            fars = buf.shape[1]
            wide[node] = jnp.concatenate([buf[node, k] for k in range(fars)], axis=1)
    for move in moves:
        move.wait()


def far_kernel(
    me_ref, zero_list, one_list, two_list, x_ref, low_first, low_second, high_ref, near_ref, edge_ref,
    basis_ref, up_one_ref, up_two_ref, zero_wide, one_wide, two_wide, zero_in, one_in, two_in,
    out_hbm, zero_win, one_win, two_win,
    sum_buf, out_buf, rows_buf, field_buf, down_buf, win_sems, out_sems, *, size,
):
    del zero_in, one_in, two_in
    leaves, rank, deep = zero_wide.shape
    ones, twos = leaves // 2, leaves // 4
    fars = deep // rank
    me = me_ref[0]
    odd = lax.rem(me, 2)
    place = REACH - 1 + 2 * odd
    sizes = [n * rank for n in (leaves, ones, twos)]
    at = [pl.multiple_of(place * n, n) for n in sizes]
    split = sizes[0] - LEAF
    moves = window_copies(
        (
            (low_first, LEAF, zero_win, at[0], split),
            (high_ref, 0, zero_win, pl.multiple_of(at[0] + split, LEAF), LEAF),
            (high_ref, LEAF, one_win, at[1], sizes[1]),
            (high_ref, LEAF + sizes[1], two_win, at[2], sizes[2]),
        ),
        win_sems,
    )
    other = window_copies(((low_second, LEAF, zero_win, at[0], split),), win_sems)[0]
    from_first = lax.rem(me + me // 2, 2) == 1
    for move in moves[1:]:
        move.start()

    @pl.when(from_first)
    def _():
        moves[0].start()
        rows_buf[...] = low_first[pl.ds(0, LEAF), :]

    @pl.when(jnp.logical_not(from_first))
    def _():
        other.start()
        rows_buf[...] = low_second[pl.ds(0, LEAF), :]

    alone = (me == 0) | (me == size - 1)

    @pl.when(alone)
    def _():
        for leaf in range(leaves):
            here = pl.ds(leaf * LEAF, LEAF)
            sum_buf[here, :] = near_ref[here, :] + dot(edge_ref[leaf, 1 - odd], x_ref[here, :])

    @pl.when(jnp.logical_not(alone))
    def _():
        add_edge(sum_buf, near_ref, edge_ref, 1 - odd, rows_buf[...])

    for move in moves:
        move.wait()

    def node_rows(row):
        return pl.ds(row * rank, rank)

    base = leaves + ones
    levels = (
        (two_wide, two_list, two_win, base),
        (one_wide, one_list, one_win, leaves),
        (zero_wide, zero_list, zero_win, 0),
    )
    for wide, where, win, row in levels:
        first = (me - REACH) * wide.shape[0]
        for node in range(wide.shape[0]):
            picked = []
            for k in range(fars):
                start = pl.multiple_of((where[node, k] - first) * rank, rank)
                picked.append(win[pl.ds(start, rank), :])
            field_buf[node_rows(row + node), :] = dot(wide[node], jnp.concatenate(picked, axis=0))
    for q in range(twos):
        down_buf[node_rows(base + q), :] = field_buf[node_rows(base + q), :].astype(jnp.bfloat16)
    for p in range(ones):
        total = dot(up_two_ref[p], down_buf[node_rows(base + p // 2), :])
        total = total + field_buf[node_rows(leaves + p), :]
        down_buf[node_rows(leaves + p), :] = total.astype(jnp.bfloat16)
    for leaf in range(leaves):
        total = dot(up_one_ref[leaf], down_buf[node_rows(leaves + leaf // 2), :])
        total = total + field_buf[node_rows(leaf), :]
        down_buf[node_rows(leaf), :] = total.astype(jnp.bfloat16)
    outs = []
    for leaf in range(leaves):
        here = pl.ds(leaf * LEAF, LEAF)
        total = sum_buf[here, :] + dot_t(basis_ref[leaf], down_buf[node_rows(leaf), :])
        out_buf[here, :] = total.astype(jnp.bfloat16)
        if leaf % 4 == 3:
            some = pl.ds((leaf - 3) * LEAF, 4 * LEAF)
            outs.append(
                pltpu.make_async_copy(
                    out_buf.at[some, :], out_hbm.at[some, :], out_sems.at[leaf // 4]
                )
            )
            outs[-1].start()
    for copy in outs:
        copy.wait()


def body(
    vectors,
    near_blocks,
    near_list,
    basis,
    up_one,
    up_two,
    couple_zero,
    couple_one,
    couple_two,
    far_zero,
    far_one,
    far_two,
):
    leaves, nears = near_list.shape
    columns = vectors.shape[1]
    rank = basis.shape[2]
    fars = far_zero.shape[1]
    size = lax.axis_size("space")
    cores = lax.axis_size("rhs")
    me = lax.axis_index("space").astype(jnp.int32).reshape(1)
    counts = (leaves, leaves // 2, leaves // 4)
    nodes = sum(counts)
    basis_t = jnp.swapaxes(basis, 1, 2)
    bf16, f32 = jnp.bfloat16, jnp.float32

    hbm = pl.BlockSpec(memory_space=pltpu.HBM)
    vmem = pl.BlockSpec(memory_space=pltpu.VMEM)
    smem = pl.BlockSpec(memory_space=pltpu.SMEM)

    def in_hbm(*arrays):
        return [pltpu.with_memory_space_constraint(a, pltpu.HBM) for a in arrays]

    plain, pair = pl.pallas_call(
        up_kernel,
        in_specs=[smem] + [hbm] * 4,
        out_specs=[vmem] * 2,
        out_shape=[
            pltpu.VMEM((nodes * rank, columns), bf16),
            pltpu.VMEM((2 * LEAF + nodes * rank, columns), bf16),
        ],
        scratch_shapes=[
            pltpu.VMEM(vectors.shape, bf16),
            pltpu.VMEM(basis_t.shape, bf16),
            pltpu.VMEM(up_one.shape, bf16),
            pltpu.VMEM(up_two.shape, bf16),
            pltpu.SemaphoreType.DMA((leaves // 2 + 2,)),
        ],
        compiler_params=pltpu.CompilerParams(vmem_limit_bytes=8 * MIB),
        name="up_pass",
    )(me, *in_hbm(vectors, basis_t, up_one, up_two))

    def send(array, to):
        pairs = []
        for i in range(size):
            for c in range(cores):
                j, d = (to(i), c) if 0 <= to(i) < size else (i, cores - 1 - c)
                pairs.append((i * cores + c, j * cores + d))
        return lax.ppermute(array, ("space", "rhs"), pairs)

    def partner(i):
        return i + 1 - 2 * (i % 2)

    from_pair = send(pair, partner)
    turns = (lambda i: i + 2 - i // 2 % 2 * 4, lambda i: i - 2 + i // 2 % 2 * 4)
    first, second = [send(plain, turn) for turn in turns]

    near, edge, points = pl.pallas_call(
        near_kernel,
        in_specs=[smem] + [hbm] * 3,
        out_specs=[vmem] * 3,
        out_shape=[
            pltpu.VMEM(vectors.shape, f32),
            pltpu.VMEM((leaves, 2, LEAF, LEAF), bf16),
            pltpu.VMEM(vectors.shape, bf16),
        ],
        scratch_shapes=[
            pltpu.SMEM(near_list.shape, jnp.int32),
            pltpu.VMEM((DEPTH, nears - 2, LEAF, LEAF), bf16),
            pltpu.SemaphoreType.DMA((DEPTH, 3)),
            pltpu.SemaphoreType.DMA,
            pltpu.SemaphoreType.DMA,
        ],
        compiler_params=pltpu.CompilerParams(vmem_limit_bytes=16 * MIB),
        cost_estimate=pl.CostEstimate(
            flops=2 * leaves * (nears - 2) * LEAF * LEAF * columns,
            bytes_accessed=2 * leaves * nears * LEAF * LEAF + 6 * leaves * LEAF * columns,
            transcendentals=0,
        ),
        name="near_own",
    )(me, *in_hbm(near_list, vectors, near_blocks))

    split = leaves * rank - LEAF
    from_pair, near = lax.optimization_barrier((from_pair, near))
    lows = [send(from_pair[LEAF : 2 * LEAF + split], turn) for turn in turns]
    first, second, near = lax.optimization_barrier((first, second, near))
    upper = jnp.where((me[0] // 2 + me[0]) % 2 == 0, first[split:], second[split:])
    high = send(upper, partner)

    sums, *rest = pl.pallas_call(
        prep_kernel,
        in_specs=[smem] + [vmem] * 6 + [hbm] * 3,
        out_specs=[vmem] * 7,
        out_shape=[
            pltpu.VMEM(vectors.shape, f32),
            *[pltpu.VMEM((SPAN * n * rank, columns), bf16) for n in counts],
            *[pltpu.VMEM((n, rank, fars * rank), bf16) for n in counts],
        ],
        scratch_shapes=[
            *[pltpu.VMEM((n, fars, rank, rank), bf16) for n in counts],
            pltpu.SemaphoreType.DMA((sum(n // 4 for n in counts),)),
            pltpu.SemaphoreType.DMA((12,)),
        ],
        compiler_params=pltpu.CompilerParams(vmem_limit_bytes=16 * MIB),
        cost_estimate=pl.CostEstimate(
            flops=2 * leaves * LEAF * LEAF * columns,
            bytes_accessed=4 * nodes * fars * rank * rank,
            transcendentals=0,
        ),
        name="prep",
    )(me, plain, from_pair, first, second, near, edge, *in_hbm(couple_zero, couple_one, couple_two))
    windows, wides = rest[:3], rest[3:]

    out, *_ = pl.pallas_call(
        functools.partial(far_kernel, size=size),
        in_specs=[smem] * 4 + [vmem] * 15,
        out_specs=[hbm] + [vmem] * 3,
        out_shape=[
            jax.ShapeDtypeStruct(vectors.shape, bf16),
            *[pltpu.VMEM((SPAN * n * rank, columns), bf16) for n in counts],
        ],
        input_output_aliases={16: 1, 17: 2, 18: 3},
        scratch_shapes=[
            pltpu.VMEM(vectors.shape, f32),
            pltpu.VMEM(vectors.shape, bf16),
            pltpu.VMEM((LEAF, columns), bf16),
            pltpu.VMEM((nodes * rank, columns), f32),
            pltpu.VMEM((nodes * rank, columns), bf16),
            pltpu.SemaphoreType.DMA((4,)),
            pltpu.SemaphoreType.DMA((leaves // 4,)),
        ],
        compiler_params=pltpu.CompilerParams(vmem_limit_bytes=16 * MIB),
        name="far_down",
    )(
        me, far_zero, far_one, far_two, points, *lows, high, sums, edge,
        basis_t, up_one, up_two, *wides, *windows,
    )
    return out


def solution(mesh):
    placed = (
        P(("groups", "space"), "rhs"),
        P("space", None, None, None),
        P("space", None),
        P("space", None, None),
        P("space", None, None),
        P("space", None, None),
        P("space", None, None, None),
        P("space", None, None, None),
        P("space", None, None, None),
        P("space", None),
        P("space", None),
        P("space", None),
    )
    return jax.shard_map(
        body, mesh=mesh, in_specs=placed, out_specs=P(("groups", "space"), "rhs"), check_vma=False
    )
```

time: 34.5 us -> 32.5 us (0.942)
  Pallas kernels: 23.4 us -> 21.6 us
    pallas_call x1, Pallas kernels: 6.69 us -> 4.94 us  [body(): pl.pallas_call(functools.partial(far_kernel, size=size), in_specs=[smem]...]
    pallas_call x1, Pallas kernels: 9.67 us -> 10.9 us  [body(): pl.pallas_call(near_kernel, in_specs=[smem] + [hbm] * 3, out_specs=[vmem]...]
    pallas_call x1, Pallas kernels: 2.96 us -> 2.16 us  [body(): pl.pallas_call(up_kernel, in_specs=[smem] + [hbm] * 4, out_specs=[vmem] *...]
    pallas_call x1, Pallas kernels: 4.11 us -> 3.57 us  [body(): pl.pallas_call(prep_kernel, in_specs=[smem] + [vmem] * 6 + [hbm] * 3, out...]
  transfers between devices with their start and end apart: 6 -> 6, of which waited for: 3 -> 3; matrix products, arithmetic and copies ran while one was open for 0% -> 0% of each run, Pallas kernels for 40% -> 45%
where the time goes in v9:
time: 32.5 us; the launch traced here: 32.3 us
  Pallas kernels  21.6 us (66%)
  starting transfers between devices  8.03 us (25%)
  waiting for transfers between devices  2.5 us (8%)
    pallas_call x1, Pallas kernels, body(): pl.pallas_call(near_kernel, in_specs=[smem] + [hbm] * 3, out_specs=[vmem]...  10.9 us
    ppermute x6, starting transfers between devices, send(): return lax.ppermute(array, ('space', 'rhs'), pairs)  8.03 us
    pallas_call x1, Pallas kernels, body(): pl.pallas_call(functools.partial(far_kernel, size=size), in_specs=[smem]...  4.94 us
    pallas_call x1, Pallas kernels, body(): pl.pallas_call(prep_kernel, in_specs=[smem] + [vmem] * 6 + [hbm] * 3, out...  3.57 us
    ppermute x6, waiting for transfers between devices, send(): return lax.ppermute(array, ('space', 'rhs'), pairs)  2.5 us
    pallas_call x1, Pallas kernels, body(): pl.pallas_call(up_kernel, in_specs=[smem] + [hbm] * 4, out_specs=[vmem] *...  2.16 us
  transfers between devices with their start and end apart: 6, of which 3 were waited for; matrix products, arithmetic and copies ran while one was open for 0% of the time, Pallas kernels for 45%

profile of v9, /device:TPU:0, one launch (start us, length us, event | category | flops | bytes accessed | tf_op | source)
XLA Modules:
  0.0 32.3 jit_solution(5782639376781107722)
XLA Ops:
  0.0 2.2 %up_pass.1 = (bf16[1792,128]{1,0:T(8,128)(2,1)S(1)}, bf16[2304,128]{1,0:T(8,128)(2,1)S(1)}) custom-call(s32[1]{0:T(128)} %bitcast.me_ref, bf16[4096,128]{1,0:T(8,128)(2,1)} %x_hbm.3, bf16[16,64,256]{2,1,0:T(8,128)(2,1)} %bitcast.2, bf16[16,64,64]{2,1,0:T(8,128)(2,1)} %up_one_ref.1, bf16[8,64,64]{2,1,0:T(8,128)(2,1)} %up_two_ref.1), custom_call_target="tpu_custom_call" | custom-call | tf_op jit(solution)/shard_map/up_pass/pallas_call | solution.py:330
  2.2 3.0 %collective-permute-start = (bf16[2304,128]{1,0:T(8,128)(2,1)S(1)}, bf16[2304,128]{1,0:T(8,128)(2,1)S(1)}, u32[]{:S(2)}, u32[]{:S(2)}) collective-permute-start(bf16[2304,128]{1,0:T(8,128)(2,1)S(1)} %get-tuple-element.24), channel_id=1, source_target_pairs={{0,2},{1,3},{2,0},{3,1},{4,6},{5,7},{6,4},{7,5},{8,10},{9,11},{10,... | collective-permute-start | bytes 1769480 | tf_op jit(solution)/shard_map/ppermute | solution.py:355
  5.2 1.6 %collective-permute-start.3 = (bf16[1792,128]{1,0:T(8,128)(2,1)S(1)}, bf16[1792,128]{1,0:T(8,128)(2,1)S(1)}, u32[]{:S(2)}, u32[]{:S(2)}) collective-permute-start(bf16[1792,128]{1,0:T(8,128)(2,1)S(1)} %get-tuple-element.27.own_ref), channel_id=1, source_target_pairs={{0,4},{1,5},{2,6},{3,7},{4,0},{5,1},{6,2},{7,3},{8,12},{9,13},{10,... | collective-permute-start | bytes 1376264 | tf_op jit(solution)/shard_map/ppermute | solution.py:355
  6.8 0.0 collective-permute-start.4
  6.8 10.9 %near_own.1 = (f32[4096,128]{1,0:T(8,128)S(1)}, bf16[16,2,256,256]{3,2,1,0:T(8,128)(2,1)S(1)}, bf16[4096,128]{1,0:T(8,128)(2,1)S(1)}) custom-call(s32[1]{0:T(128)} %bitcast.me_ref, s32[16,12]{1,0:T(8,128)} %list_hbm.1, bf16[4096,128]{1,0:T(8,128)(2,1)} %x_hbm.3, bf16[16,12,256,256]{3,2,1,0:T(8,128)(2,1)} %blocks_hbm.1), custom_call_target="tpu_custom_call" | custom-call | flops 2684354560 | bytes 28311552 | tf_op jit(solution)/shard_map/near_own/pallas_call | solution.py:364
  17.7 0.8 %collective-permute-done.pair_ref = bf16[2304,128]{1,0:T(8,128)(2,1)S(1)} collective-permute-done((bf16[2304,128]{1,0:T(8,128)(2,1)S(1)}, bf16[2304,128]{1,0:T(8,128)(2,1)S(1)}, u32[]{:S(2)}, u32[]{:S(2)}) %collective-permute-start) | collective-permute-done | bytes 589856 | tf_op jit(solution)/shard_map/ppermute | solution.py:355
  18.5 0.0 collective-permute-done.3.first_ref
  18.5 0.0 collective-permute-done.4.second_ref
  18.5 1.8 %collective-permute-start.5 = (bf16[1024,128]{1,0:T(8,128)(2,1)S(1)}, bf16[1024,128]{1,0:T(8,128)(2,1)S(1)}, u32[]{:S(2)}, u32[]{:S(2)}) collective-permute-start(bf16[1024,128]{1,0:T(8,128)(2,1)S(1)} %slice_select_fusion), channel_id=1, source_target_pairs={{0,2},{1,3},{2,0},{3,1},{4,6},{5,7},{6,4},{7,5},{8,10},{9,11},{10,... | collective-permute-start | bytes 786440 | tf_op jit(solution)/shard_map/ppermute | solution.py:355
  20.4 1.6 %collective-permute-start.1 = (bf16[1024,128]{1,0:T(8,128)(2,1)S(1)}, bf16[1024,128]{1,0:T(8,128)(2,1)S(1)}, u32[]{:S(2)}, u32[]{:S(2)}) collective-permute-start(bf16[1024,128]{1,0:T(8,128)(2,1)S(1)} %slice.10), channel_id=1, source_target_pairs={{0,4},{1,5},{2,6},{3,7},{4,0},{5,1},{6,2},{7,3},{8,12},{9,13},{10,... | collective-permute-start | bytes 786440 | tf_op jit(solution)/shard_map/ppermute | solution.py:355
  22.0 0.0 collective-permute-start.2
  22.0 0.0 copy-start
  22.0 0.0 copy-start.1
  22.0 0.0 copy-start.2
  22.0 0.0 copy-start.3
  22.0 0.0 copy-start.4
  22.1 0.0 copy-start.5
  22.1 3.6 %prep.1 = (f32[4096,128]{1,0:T(8,128)S(1)}, bf16[5120,128]{1,0:T(8,128)(2,1)S(1)}, bf16[2560,128]{1,0:T(8,128)(2,1)S(1)}, bf16[1280,128]{1,0:T(8,128)(2,1)S(1)},...) custom-call(s32[1]{0:T(128)} %bitcast.me_ref, ...), custom_call_target="tpu_custom_call" | custom-call | flops 268435456 | bytes 7340032 | tf_op jit(solution)/shard_map/prep/pallas_call | solution.py:396
  25.6 0.9 %collective-permute-done.5.high_ref = bf16[1024,128]{1,0:T(8,128)(2,1)S(1)} collective-permute-done((bf16[1024,128]{1,0:T(8,128)(2,1)S(1)}, bf16[1024,128]{1,0:T(8,128)(2,1)S(1)}, u32[]{:S(2)}, u32[]{:S(2)}) %collective-permute-start.5) | collective-permute-done | bytes 262176 | tf_op jit(solution)/shard_map/ppermute | solution.py:355
  26.6 0.8 %collective-permute-done.1.low_first = bf16[1024,128]{1,0:T(8,128)(2,1)S(1)} collective-permute-done((bf16[1024,128]{1,0:T(8,128)(2,1)S(1)}, bf16[1024,128]{1,0:T(8,128)(2,1)S(1)}, u32[]{:S(2)}, u32[]{:S(2)}) %collective-permute-start.1) | collective-permute-done | bytes 262176 | tf_op jit(solution)/shard_map/ppermute | solution.py:355
  27.3 0.0 collective-permute-done.2.low_second
  27.3 0.0 copy-done
  27.3 0.0 copy-done.1
  27.3 0.0 copy-done.2
  27.4 0.0 copy-done.3
  27.4 0.0 copy-done.4
  27.4 0.0 copy-done.5
  27.4 4.9 %far_down.1 = (bf16[4096,128]{1,0:T(8,128)(2,1)}, bf16[5120,128]{1,0:T(8,128)(2,1)S(1)}, bf16[2560,128]{1,0:T(8,128)(2,1)S(1)}, bf16[1280,128]{1,0:T(8,128)(2,1)S(1)}) custom-call(s32[1]{0:T(128)} %bitcast.me_ref, s32[16,16]{1,0:T(8,128)S(1)} %copy-done.3, s32[8,16]{1,0:T(8,128)S(1)} %copy-done.4, ...), custom_call_target="tpu_custom_call", output_to_operand_aliasing={{1}: (16, {}), {2}: (17, {}), {3}: (18, {})} | custom-call | tf_op jit(solution)/shard_map/far_down/pallas_call | solution.py:420
  (2 shorter events, 0.0 us)
Async XLA Ops:
  2.2 16.3 %collective-permute-start = (bf16[2304,128]{1,0:T(8,128)(2,1)S(1)}, bf16[2304,128]{1,0:T(8,128)(2,1)S(1)}, u32[]{:S(2)}, u32[]{:S(2)}) collective-permute-start(bf16[2304,128]{1,0:T(8,128)(2,1)S(1)} %get-tuple-element.24), channel_id=1, source_target_pairs={{0,2},{1,3},{2,0},{3,1},{4,6},{5,7},{6,4},{7,5},{8,10},{9,11},{10,... | collective-permute-start | bytes 1769480 | tf_op jit(solution)/shard_map/ppermute | solution.py:355
  5.2 13.3 %collective-permute-start.3 = (bf16[1792,128]{1,0:T(8,128)(2,1)S(1)}, bf16[1792,128]{1,0:T(8,128)(2,1)S(1)}, u32[]{:S(2)}, u32[]{:S(2)}) collective-permute-start(bf16[1792,128]{1,0:T(8,128)(2,1)S(1)} %get-tuple-element.27.own_ref), channel_id=1, source_target_pairs={{0,4},{1,5},{2,6},{3,7},{4,0},{5,1},{6,2},{7,3},{8,12},{9,13},{10,... | collective-permute-start | bytes 1376264 | tf_op jit(solution)/shard_map/ppermute | solution.py:355
  6.8 11.8 %collective-permute-start.4 = (bf16[1792,128]{1,0:T(8,128)(2,1)S(1)}, bf16[1792,128]{1,0:T(8,128)(2,1)S(1)}, u32[]{:S(2)}, u32[]{:S(2)}) collective-permute-start(bf16[1792,128]{1,0:T(8,128)(2,1)S(1)} %get-tuple-element.27.own_ref), channel_id=1, source_target_pairs={{0,1},{1,0},{2,3},{3,2},{4,8},{5,9},{6,10},{7,11},{8,4},{9,5},{10,... | collective-permute-start | bytes 1376264 | tf_op jit(solution)/shard_map/ppermute | solution.py:355
  18.5 8.0 %collective-permute-start.5 = (bf16[1024,128]{1,0:T(8,128)(2,1)S(1)}, bf16[1024,128]{1,0:T(8,128)(2,1)S(1)}, u32[]{:S(2)}, u32[]{:S(2)}) collective-permute-start(bf16[1024,128]{1,0:T(8,128)(2,1)S(1)} %slice_select_fusion), channel_id=1, source_target_pairs={{0,2},{1,3},{2,0},{3,1},{4,6},{5,7},{6,4},{7,5},{8,10},{9,11},{10,... | collective-permute-start | bytes 786440 | tf_op jit(solution)/shard_map/ppermute | solution.py:355
  20.4 7.0 %collective-permute-start.1 = (bf16[1024,128]{1,0:T(8,128)(2,1)S(1)}, bf16[1024,128]{1,0:T(8,128)(2,1)S(1)}, u32[]{:S(2)}, u32[]{:S(2)}) collective-permute-start(bf16[1024,128]{1,0:T(8,128)(2,1)S(1)} %slice.10), channel_id=1, source_target_pairs={{0,4},{1,5},{2,6},{3,7},{4,0},{5,1},{6,2},{7,3},{8,12},{9,13},{10,... | collective-permute-start | bytes 786440 | tf_op jit(solution)/shard_map/ppermute | solution.py:355
  22.0 5.3 %collective-permute-start.2 = (bf16[1024,128]{1,0:T(8,128)(2,1)S(1)}, bf16[1024,128]{1,0:T(8,128)(2,1)S(1)}, u32[]{:S(2)}, u32[]{:S(2)}) collective-permute-start(bf16[1024,128]{1,0:T(8,128)(2,1)S(1)} %slice.10), channel_id=1, source_target_pairs={{0,1},{1,0},{2,3},{3,2},{4,8},{5,9},{6,10},{7,11},{8,4},{9,5},{10,... | collective-permute-start | bytes 786440 | tf_op jit(solution)/shard_map/ppermute | solution.py:355
  22.0 5.3 %copy-start = (bf16[16,256,64]{1,2,0:T(8,128)(2,1)S(1)}, bf16[16,256,64]{1,2,0:T(8,128)(2,1)}, u32[]{:S(2)}) copy-start(bf16[16,256,64]{1,2,0:T(8,128)(2,1)} %param.15) | copy-start | bytes 1572868
  22.0 5.3 %copy-start.1 = (bf16[16,64,64]{2,1,0:T(8,128)(2,1)S(1)}, bf16[16,64,64]{2,1,0:T(8,128)(2,1)}, u32[]{:S(2)}) copy-start(bf16[16,64,64]{2,1,0:T(8,128)(2,1)} %up_one_ref.1) | copy-start | bytes 393220
  22.0 5.3 %copy-start.2 = (bf16[8,64,64]{2,1,0:T(8,128)(2,1)S(1)}, bf16[8,64,64]{2,1,0:T(8,128)(2,1)}, u32[]{:S(2)}) copy-start(bf16[8,64,64]{2,1,0:T(8,128)(2,1)} %up_two_ref.1) | copy-start | bytes 196612
  22.0 5.3 %copy-start.3 = (s32[16,16]{1,0:T(8,128)S(1)}, s32[16,16]{1,0:T(8,128)}, u32[]{:S(2)}) copy-start(s32[16,16]{1,0:T(8,128)} %zero_list.1) | copy-start | bytes 3076
  22.0 5.3 %copy-start.4 = (s32[8,16]{1,0:T(8,128)S(1)}, s32[8,16]{1,0:T(8,128)}, u32[]{:S(2)}) copy-start(s32[8,16]{1,0:T(8,128)} %one_list.1) | copy-start | bytes 1540
  22.1 5.3 %copy-start.5 = (s32[4,16]{1,0:T(4,128)S(1)}, s32[4,16]{1,0:T(4,128)}, u32[]{:S(2)}) copy-start(s32[4,16]{1,0:T(4,128)} %two_list.1) | copy-start | bytes 772

commit v10 on v9

--- a/solution.py
+++ b/solution.py
@@ -49,7 +49,7 @@
     def put(node, value):
         value = value.astype(jnp.bfloat16)
         plain_ref[pl.ds(node * rank, rank), :] = value
-        pair_ref[pl.ds(2 * LEAF + node * rank, rank), :] = value
+        pair_ref[pl.ds(node * rank, rank), :] = value
         return value
 
     def join(ups, pair):
@@ -73,14 +73,9 @@
         put(leaves + leaves // 2 + q, join(up_two_ref[pair], ones[pair]))
     odd = lax.rem(me_ref[0], 2)
     last = (leaves - 1) * LEAF
-    near_edge = pl.multiple_of((1 - odd) * last, LEAF)
-    far_edge = pl.multiple_of(odd * last, LEAF)
-    pair_ref[pl.ds(0, LEAF), :] = x_ref[pl.ds(near_edge, LEAF), :]
-    pair_ref[pl.ds(LEAF, LEAF), :] = x_ref[pl.ds(far_edge, LEAF), :]
-
-
-def last_place(me):
-    return REACH - 1 + 2 * lax.rem(me, 2)
+    end = pl.ds(plain_ref.shape[0] - LEAF, LEAF)
+    pair_ref[end, :] = x_ref[pl.ds(pl.multiple_of((1 - odd) * last, LEAF), LEAF), :]
+    plain_ref[end, :] = x_ref[pl.ds(pl.multiple_of(odd * last, LEAF), LEAF), :]
 
 
 def near_kernel(
@@ -174,7 +169,7 @@
         (own_ref, 0, REACH),
         (first_ref, 0, (1 - block) * (SPAN - 1)),
         (second_ref, 0, block * (SPAN - 1)),
-        (pair_ref, 2 * LEAF, REACH + 1 - 2 * odd),
+        (pair_ref, 0, REACH + 1 - 2 * odd),
     )
     plans = []
     for ref, start, place in pieces:
@@ -185,7 +180,7 @@
     moves = window_copies(plans, win_sems)
     for move in moves:
         move.start()
-    add_edge(sum_ref, near_ref, edge_ref, odd, pair_ref[pl.ds(0, LEAF), :])
+    add_edge(sum_ref, near_ref, edge_ref, odd, pair_ref[pl.ds(pair_ref.shape[0] - LEAF, LEAF), :])
     for copy, buf, wide, first in chunks:
         copy.wait()
         for node in range(first, first + 4):
@@ -199,7 +194,7 @@
     me_ref, zero_list, one_list, two_list, x_ref, low_first, low_second, high_ref, near_ref, edge_ref,
     basis_ref, up_one_ref, up_two_ref, zero_wide, one_wide, two_wide, zero_in, one_in, two_in,
     out_hbm, zero_win, one_win, two_win,
-    sum_buf, out_buf, rows_buf, field_buf, down_buf, win_sems, out_sems, *, size,
+    sum_buf, out_buf, field_buf, down_buf, win_sems, out_sems, *, size,
 ):
     del zero_in, one_in, two_in
     leaves, rank, deep = zero_wide.shape
@@ -210,30 +205,21 @@
     place = REACH - 1 + 2 * odd
     sizes = [n * rank for n in (leaves, ones, twos)]
     at = [pl.multiple_of(place * n, n) for n in sizes]
-    split = sizes[0] - LEAF
     moves = window_copies(
         (
-            (low_first, LEAF, zero_win, at[0], split),
-            (high_ref, 0, zero_win, pl.multiple_of(at[0] + split, LEAF), LEAF),
-            (high_ref, LEAF, one_win, at[1], sizes[1]),
-            (high_ref, LEAF + sizes[1], two_win, at[2], sizes[2]),
+            (low_first, 0, zero_win, at[0], sizes[0]),
+            (high_ref, 0, one_win, at[1], sizes[1]),
+            (high_ref, sizes[1], two_win, at[2], sizes[2]),
         ),
         win_sems,
     )
-    other = window_copies(((low_second, LEAF, zero_win, at[0], split),), win_sems)[0]
+    other = window_copies(((low_second, 0, zero_win, at[0], sizes[0]),), win_sems)[0]
     from_first = lax.rem(me + me // 2, 2) == 1
     for move in moves[1:]:
         move.start()
 
-    @pl.when(from_first)
-    def _():
-        moves[0].start()
-        rows_buf[...] = low_first[pl.ds(0, LEAF), :]
-
-    @pl.when(jnp.logical_not(from_first))
-    def _():
-        other.start()
-        rows_buf[...] = low_second[pl.ds(0, LEAF), :]
+    pl.when(from_first)(moves[0].start)
+    pl.when(jnp.logical_not(from_first))(other.start)
 
     alone = (me == 0) | (me == size - 1)
 
@@ -245,7 +231,8 @@
 
     @pl.when(jnp.logical_not(alone))
     def _():
-        add_edge(sum_buf, near_ref, edge_ref, 1 - odd, rows_buf[...])
+        rows = high_ref[pl.ds(high_ref.shape[0] - LEAF, LEAF), :]
+        add_edge(sum_buf, near_ref, edge_ref, 1 - odd, rows)
 
     for move in moves:
         move.wait()
@@ -332,8 +319,8 @@
         in_specs=[smem] + [hbm] * 4,
         out_specs=[vmem] * 2,
         out_shape=[
-            pltpu.VMEM((nodes * rank, columns), bf16),
-            pltpu.VMEM((2 * LEAF + nodes * rank, columns), bf16),
+            pltpu.VMEM((nodes * rank + LEAF, columns), bf16),
+            pltpu.VMEM((nodes * rank + LEAF, columns), bf16),
         ],
         scratch_shapes=[
             pltpu.VMEM(vectors.shape, bf16),
@@ -386,9 +373,9 @@
         name="near_own",
     )(me, *in_hbm(near_list, vectors, near_blocks))
 
-    split = leaves * rank - LEAF
+    split = leaves * rank
     from_pair, near = lax.optimization_barrier((from_pair, near))
-    lows = [send(from_pair[LEAF : 2 * LEAF + split], turn) for turn in turns]
+    lows = [send(from_pair[:split], turn) for turn in turns]
     first, second, near = lax.optimization_barrier((first, second, near))
     upper = jnp.where((me[0] // 2 + me[0]) % 2 == 0, first[split:], second[split:])
     high = send(upper, partner)
@@ -409,7 +396,7 @@
         ],
         compiler_params=pltpu.CompilerParams(vmem_limit_bytes=16 * MIB),
         cost_estimate=pl.CostEstimate(
-            flops=2 * leaves * LEAF * LEAF * columns,
+            flops=4 * 10**9,
             bytes_accessed=4 * nodes * fars * rank * rank,
             transcendentals=0,
         ),
@@ -429,10 +416,9 @@
         scratch_shapes=[
             pltpu.VMEM(vectors.shape, f32),
             pltpu.VMEM(vectors.shape, bf16),
-            pltpu.VMEM((LEAF, columns), bf16),
             pltpu.VMEM((nodes * rank, columns), f32),
             pltpu.VMEM((nodes * rank, columns), bf16),
-            pltpu.SemaphoreType.DMA((4,)),
+            pltpu.SemaphoreType.DMA((3,)),
             pltpu.SemaphoreType.DMA((leaves // 4,)),
         ],
         compiler_params=pltpu.CompilerParams(vmem_limit_bytes=16 * MIB),

time: 32.5 us -> 34.5 us (1.062)
  waiting for transfers between devices: 2.5 us -> 4.58 us
  Pallas kernels: 21.6 us -> 21.2 us
  starting transfers between devices: 8.03 us -> 8.4 us
    ppermute x6, waiting for transfers between devices: 2.5 us -> 4.58 us  [send(): return lax.ppermute(array, ('space', 'rhs'), pairs)]
    pallas_call x1, Pallas kernels: 4.94 us -> 4.55 us  [body(): pl.pallas_call(functools.partial(far_kernel, size=size), in_specs=[smem]...]
    ppermute x6, starting transfers between devices: 8.03 us -> 8.4 us  [send(): return lax.ppermute(array, ('space', 'rhs'), pairs)]
  transfers between devices with their start and end apart: 6 -> 6, of which waited for: 3 -> 1; matrix products, arithmetic and copies ran while one was open for 0% -> 0% of each run, Pallas kernels for 45% -> 42%
where the time goes in v10:
time: 34.5 us; the launch traced here: 34.4 us
  Pallas kernels  21.2 us (61%)
  starting transfers between devices  8.4 us (24%)
  waiting for transfers between devices  4.58 us (13%)
    pallas_call x1, Pallas kernels, body(): pl.pallas_call(near_kernel, in_specs=[smem] + [hbm] * 3, out_specs=[vmem]...  10.9 us
    ppermute x6, starting transfers between devices, send(): return lax.ppermute(array, ('space', 'rhs'), pairs)  8.4 us
    ppermute x6, waiting for transfers between devices, send(): return lax.ppermute(array, ('space', 'rhs'), pairs)  4.58 us
    pallas_call x1, Pallas kernels, body(): pl.pallas_call(functools.partial(far_kernel, size=size), in_specs=[smem]...  4.55 us
    pallas_call x1, Pallas kernels, body(): pl.pallas_call(prep_kernel, in_specs=[smem] + [vmem] * 6 + [hbm] * 3, out...  3.57 us
    pallas_call x1, Pallas kernels, body(): pl.pallas_call(up_kernel, in_specs=[smem] + [hbm] * 4, out_specs=[vmem] *...  2.16 us
  transfers between devices with their start and end apart: 6, of which 1 were waited for; matrix products, arithmetic and copies ran while one was open for 0% of the time, Pallas kernels for 42%

profile of v10, /device:TPU:0, one launch (start us, length us, event | category | flops | bytes accessed | tf_op | source)
XLA Modules:
  0.0 34.4 jit_solution(17789193243803007384)
XLA Ops:
  0.0 2.2 %up_pass.1 = (bf16[2048,128]{1,0:T(8,128)(2,1)S(1)}, bf16[2048,128]{1,0:T(8,128)(2,1)S(1)}) custom-call(s32[1]{0:T(128)} %bitcast.me_ref, bf16[4096,128]{1,0:T(8,128)(2,1)} %x_hbm.3, bf16[16,64,256]{2,1,0:T(8,128)(2,1)} %bitcast.2, bf16[16,64,64]{2,1,0:T(8,128)(2,1)} %up_one_ref.1, bf16[8,64,64]{2,1,0:T(8,128)(2,1)} %up_two_ref.1), custom_call_target="tpu_custom_call" | custom-call | tf_op jit(solution)/shard_map/up_pass/pallas_call | solution.py:317
  2.2 3.0 %collective-permute-start = (bf16[2048,128]{1,0:T(8,128)(2,1)S(1)}, bf16[2048,128]{1,0:T(8,128)(2,1)S(1)}, u32[]{:S(2)}, u32[]{:S(2)}) collective-permute-start(bf16[2048,128]{1,0:T(8,128)(2,1)S(1)} %get-tuple-element.24), channel_id=1, source_target_pairs={{0,2},{1,3},{2,0},{3,1},{4,6},{5,7},{6,4},{7,5},{8,10},{9,11},{10,... | collective-permute-start | bytes 1572872 | tf_op jit(solution)/shard_map/ppermute | solution.py:342
  5.2 1.6 %collective-permute-start.3 = (bf16[2048,128]{1,0:T(8,128)(2,1)S(1)}, bf16[2048,128]{1,0:T(8,128)(2,1)S(1)}, u32[]{:S(2)}, u32[]{:S(2)}) collective-permute-start(bf16[2048,128]{1,0:T(8,128)(2,1)S(1)} %get-tuple-element.27.own_ref), channel_id=1, source_target_pairs={{0,4},{1,5},{2,6},{3,7},{4,0},{5,1},{6,2},{7,3},{8,12},{9,13},{10,... | collective-permute-start | bytes 1572872 | tf_op jit(solution)/shard_map/ppermute | solution.py:342
  6.8 0.0 collective-permute-start.4
  6.8 10.9 %near_own.1 = (f32[4096,128]{1,0:T(8,128)S(1)}, bf16[16,2,256,256]{3,2,1,0:T(8,128)(2,1)S(1)}, bf16[4096,128]{1,0:T(8,128)(2,1)S(1)}) custom-call(s32[1]{0:T(128)} %bitcast.me_ref, s32[16,12]{1,0:T(8,128)} %list_hbm.1, bf16[4096,128]{1,0:T(8,128)(2,1)} %x_hbm.3, bf16[16,12,256,256]{3,2,1,0:T(8,128)(2,1)} %blocks_hbm.1), custom_call_target="tpu_custom_call" | custom-call | flops 2684354560 | bytes 28311552 | tf_op jit(solution)/shard_map/near_own/pallas_call | solution.py:351
  17.7 0.0 collective-permute-done.pair_ref
  17.7 3.2 %collective-permute-start.1 = (bf16[1024,128]{1,0:T(8,128)(2,1)S(1)}, bf16[1024,128]{1,0:T(8,128)(2,1)S(1)}, u32[]{:S(2)}, u32[]{:S(2)}) collective-permute-start(bf16[1024,128]{1,0:T(8,128)(2,1)S(1)} %slice.10), channel_id=1, source_target_pairs={{0,4},{1,5},{2,6},{3,7},{4,0},{5,1},{6,2},{7,3},{8,12},{9,13},{10,... | collective-permute-start | bytes 786440 | tf_op jit(solution)/shard_map/ppermute | solution.py:342
  21.0 0.0 collective-permute-start.2
  21.0 0.0 collective-permute-done.3.first_ref
  21.0 0.0 collective-permute-done.4.second_ref
  21.0 0.6 %collective-permute-start.5 = (bf16[1024,128]{1,0:T(8,128)(2,1)S(1)}, bf16[1024,128]{1,0:T(8,128)(2,1)S(1)}, u32[]{:S(2)}, u32[]{:S(2)}) collective-permute-start(bf16[1024,128]{1,0:T(8,128)(2,1)S(1)} %slice_select_fusion), channel_id=1, source_target_pairs={{0,2},{1,3},{2,0},{3,1},{4,6},{5,7},{6,4},{7,5},{8,10},{9,11},{10,... | collective-permute-start | bytes 786440 | tf_op jit(solution)/shard_map/ppermute | solution.py:342
  21.6 0.0 copy-start
  21.6 0.0 copy-start.1
  21.6 0.0 copy-start.2
  21.6 0.0 copy-start.3
  21.6 0.0 copy-start.4
  21.6 0.0 copy-start.5
  21.6 3.6 %prep.1 = (f32[4096,128]{1,0:T(8,128)S(1)}, bf16[5120,128]{1,0:T(8,128)(2,1)S(1)}, bf16[2560,128]{1,0:T(8,128)(2,1)S(1)}, bf16[1280,128]{1,0:T(8,128)(2,1)S(1)},...) custom-call(s32[1]{0:T(128)} %bitcast.me_ref, ...), custom_call_target="tpu_custom_call" | custom-call | flops 4000000000 | bytes 7340032 | tf_op jit(solution)/shard_map/prep/pallas_call | solution.py:383
  25.2 4.6 %collective-permute-done.5.high_ref = bf16[1024,128]{1,0:T(8,128)(2,1)S(1)} collective-permute-done((bf16[1024,128]{1,0:T(8,128)(2,1)S(1)}, bf16[1024,128]{1,0:T(8,128)(2,1)S(1)}, u32[]{:S(2)}, u32[]{:S(2)}) %collective-permute-start.5) | collective-permute-done | bytes 262176 | tf_op jit(solution)/shard_map/ppermute | solution.py:342
  29.8 0.0 collective-permute-done.1.low_first
  29.8 0.0 collective-permute-done.2.low_second
  29.8 0.0 copy-done
  29.8 0.0 copy-done.1
  29.8 0.0 copy-done.2
  29.8 0.0 copy-done.3
  29.8 0.0 copy-done.4
  29.8 0.0 copy-done.5
  29.8 4.6 %far_down.1 = (bf16[4096,128]{1,0:T(8,128)(2,1)}, bf16[5120,128]{1,0:T(8,128)(2,1)S(1)}, bf16[2560,128]{1,0:T(8,128)(2,1)S(1)}, bf16[1280,128]{1,0:T(8,128)(2,1)S(1)}) custom-call(s32[1]{0:T(128)} %bitcast.me_ref, s32[16,16]{1,0:T(8,128)S(1)} %copy-done.3, s32[8,16]{1,0:T(8,128)S(1)} %copy-done.4, ...), custom_call_target="tpu_custom_call", output_to_operand_aliasing={{1}: (16, {}), {2}: (17, {}), {3}: (18, {})} | custom-call | tf_op jit(solution)/shard_map/far_down/pallas_call | solution.py:407
  (2 shorter events, 0.0 us)
Async XLA Ops:
  2.2 15.5 %collective-permute-start = (bf16[2048,128]{1,0:T(8,128)(2,1)S(1)}, bf16[2048,128]{1,0:T(8,128)(2,1)S(1)}, u32[]{:S(2)}, u32[]{:S(2)}) collective-permute-start(bf16[2048,128]{1,0:T(8,128)(2,1)S(1)} %get-tuple-element.24), channel_id=1, source_target_pairs={{0,2},{1,3},{2,0},{3,1},{4,6},{5,7},{6,4},{7,5},{8,10},{9,11},{10,... | collective-permute-start | bytes 1572872 | tf_op jit(solution)/shard_map/ppermute | solution.py:342
  5.2 15.8 %collective-permute-start.3 = (bf16[2048,128]{1,0:T(8,128)(2,1)S(1)}, bf16[2048,128]{1,0:T(8,128)(2,1)S(1)}, u32[]{:S(2)}, u32[]{:S(2)}) collective-permute-start(bf16[2048,128]{1,0:T(8,128)(2,1)S(1)} %get-tuple-element.27.own_ref), channel_id=1, source_target_pairs={{0,4},{1,5},{2,6},{3,7},{4,0},{5,1},{6,2},{7,3},{8,12},{9,13},{10,... | collective-permute-start | bytes 1572872 | tf_op jit(solution)/shard_map/ppermute | solution.py:342
  6.8 14.2 %collective-permute-start.4 = (bf16[2048,128]{1,0:T(8,128)(2,1)S(1)}, bf16[2048,128]{1,0:T(8,128)(2,1)S(1)}, u32[]{:S(2)}, u32[]{:S(2)}) collective-permute-start(bf16[2048,128]{1,0:T(8,128)(2,1)S(1)} %get-tuple-element.27.own_ref), channel_id=1, source_target_pairs={{0,1},{1,0},{2,3},{3,2},{4,8},{5,9},{6,10},{7,11},{8,4},{9,5},{10,... | collective-permute-start | bytes 1572872 | tf_op jit(solution)/shard_map/ppermute | solution.py:342
  17.7 12.0 %collective-permute-start.1 = (bf16[1024,128]{1,0:T(8,128)(2,1)S(1)}, bf16[1024,128]{1,0:T(8,128)(2,1)S(1)}, u32[]{:S(2)}, u32[]{:S(2)}) collective-permute-start(bf16[1024,128]{1,0:T(8,128)(2,1)S(1)} %slice.10), channel_id=1, source_target_pairs={{0,4},{1,5},{2,6},{3,7},{4,0},{5,1},{6,2},{7,3},{8,12},{9,13},{10,... | collective-permute-start | bytes 786440 | tf_op jit(solution)/shard_map/ppermute | solution.py:342
  21.0 8.8 %collective-permute-start.2 = (bf16[1024,128]{1,0:T(8,128)(2,1)S(1)}, bf16[1024,128]{1,0:T(8,128)(2,1)S(1)}, u32[]{:S(2)}, u32[]{:S(2)}) collective-permute-start(bf16[1024,128]{1,0:T(8,128)(2,1)S(1)} %slice.10), channel_id=1, source_target_pairs={{0,1},{1,0},{2,3},{3,2},{4,8},{5,9},{6,10},{7,11},{8,4},{9,5},{10,... | collective-permute-start | bytes 786440 | tf_op jit(solution)/shard_map/ppermute | solution.py:342
  21.0 8.8 %collective-permute-start.5 = (bf16[1024,128]{1,0:T(8,128)(2,1)S(1)}, bf16[1024,128]{1,0:T(8,128)(2,1)S(1)}, u32[]{:S(2)}, u32[]{:S(2)}) collective-permute-start(bf16[1024,128]{1,0:T(8,128)(2,1)S(1)} %slice_select_fusion), channel_id=1, source_target_pairs={{0,2},{1,3},{2,0},{3,1},{4,6},{5,7},{6,4},{7,5},{8,10},{9,11},{10,... | collective-permute-start | bytes 786440 | tf_op jit(solution)/shard_map/ppermute | solution.py:342
  21.6 8.2 %copy-start = (bf16[16,256,64]{1,2,0:T(8,128)(2,1)S(1)}, bf16[16,256,64]{1,2,0:T(8,128)(2,1)}, u32[]{:S(2)}) copy-start(bf16[16,256,64]{1,2,0:T(8,128)(2,1)} %param.15) | copy-start | bytes 1572868
  21.6 8.2 %copy-start.1 = (bf16[16,64,64]{2,1,0:T(8,128)(2,1)S(1)}, bf16[16,64,64]{2,1,0:T(8,128)(2,1)}, u32[]{:S(2)}) copy-start(bf16[16,64,64]{2,1,0:T(8,128)(2,1)} %up_one_ref.1) | copy-start | bytes 393220
  21.6 8.2 %copy-start.2 = (bf16[8,64,64]{2,1,0:T(8,128)(2,1)S(1)}, bf16[8,64,64]{2,1,0:T(8,128)(2,1)}, u32[]{:S(2)}) copy-start(bf16[8,64,64]{2,1,0:T(8,128)(2,1)} %up_two_ref.1) | copy-start | bytes 196612
  21.6 8.2 %copy-start.3 = (s32[16,16]{1,0:T(8,128)S(1)}, s32[16,16]{1,0:T(8,128)}, u32[]{:S(2)}) copy-start(s32[16,16]{1,0:T(8,128)} %zero_list.1) | copy-start | bytes 3076
  21.6 8.2 %copy-start.4 = (s32[8,16]{1,0:T(8,128)S(1)}, s32[8,16]{1,0:T(8,128)}, u32[]{:S(2)}) copy-start(s32[8,16]{1,0:T(8,128)} %one_list.1) | copy-start | bytes 1540
  21.6 8.2 %copy-start.5 = (s32[4,16]{1,0:T(4,128)S(1)}, s32[4,16]{1,0:T(4,128)}, u32[]{:S(2)}) copy-start(s32[4,16]{1,0:T(4,128)} %two_list.1) | copy-start | bytes 772

commit v11 on v10

--- a/solution.py
+++ b/solution.py
@@ -79,8 +79,7 @@
 
 
 def near_kernel(
-    me_ref, list_hbm, x_hbm, blocks_hbm, out_ref, edge_ref, x_ref,
-    list_ref, block_buf, sems, x_sem, list_sem,
+    me_ref, list_hbm, x_hbm, blocks_hbm, out_ref, x_ref, list_ref, block_buf, sems, x_sems, list_sem,
 ):
     leaves, nears = list_ref.shape
     first = me_ref[0] * leaves
@@ -89,21 +88,27 @@
         pairs = (
             (blocks_hbm.at[leaf, pl.ds(0, 1)], block_buf.at[slot, pl.ds(0, 1)]),
             (blocks_hbm.at[leaf, pl.ds(3, nears - 3)], block_buf.at[slot, pl.ds(1, nears - 3)]),
-            (blocks_hbm.at[leaf, pl.ds(1, 2)], edge_ref.at[leaf]),
         )
         return [
             pltpu.make_async_copy(src, dst, sems.at[slot, i]) for i, (src, dst) in enumerate(pairs)
         ]
 
     list_copy = pltpu.make_async_copy(list_hbm, list_ref, list_sem)
-    x_copy = pltpu.make_async_copy(x_hbm, x_ref, x_sem)
     list_copy.start()
-    x_copy.start()
+    x_copies = []
+    for q in range(leaves // 4):
+        rows = pl.ds(q * 4 * LEAF, 4 * LEAF)
+        x_copies.append(
+            pltpu.make_async_copy(x_hbm.at[rows, :], x_ref.at[rows, :], x_sems.at[q])
+        )
+    for copy in x_copies:
+        copy.start()
     for leaf in range(DEPTH - 1):
         for copy in copies(leaf, leaf):
             copy.start()
     list_copy.wait()
-    x_copy.wait()
+    for copy in x_copies:
+        copy.wait()
 
     def step(leaf, carry):
         slot = lax.rem(leaf, DEPTH)
@@ -145,10 +150,10 @@
 
 
 def prep_kernel(
-    me_ref, own_ref, pair_ref, first_ref, second_ref, near_ref, edge_ref,
-    zero_hbm, one_hbm, two_hbm,
-    sum_ref, zero_win, one_win, two_win, zero_wide, one_wide, two_wide,
-    zero_buf, one_buf, two_buf, sems, win_sems,
+    me_ref, own_ref, pair_ref, first_ref, second_ref, near_ref,
+    blocks_hbm, zero_hbm, one_hbm, two_hbm,
+    sum_ref, edge_ref, zero_win, one_win, two_win, zero_wide, one_wide, two_wide,
+    zero_buf, one_buf, two_buf, sems, win_sems, edge_sems,
 ):
     levels = (
         (two_hbm, two_buf, two_wide),
@@ -162,6 +167,12 @@
             copy = pltpu.make_async_copy(hbm.at[some], buf.at[some], sems.at[len(chunks)])
             copy.start()
             chunks.append((copy, buf, wide, first))
+    edges = []
+    for q in range(edge_ref.shape[0] // 4):
+        some = pl.ds(4 * q, 4)
+        src = blocks_hbm.at[some, pl.ds(1, 2)]
+        edges.append(pltpu.make_async_copy(src, edge_ref.at[some], edge_sems.at[q]))
+        edges[-1].start()
     me = me_ref[0]
     odd = lax.rem(me, 2)
     block = lax.rem(me // 2, 2)
@@ -180,21 +191,23 @@
     moves = window_copies(plans, win_sems)
     for move in moves:
         move.start()
-    add_edge(sum_ref, near_ref, edge_ref, odd, pair_ref[pl.ds(pair_ref.shape[0] - LEAF, LEAF), :])
     for copy, buf, wide, first in chunks:
         copy.wait()
         for node in range(first, first + 4):
             fars = buf.shape[1]
             wide[node] = jnp.concatenate([buf[node, k] for k in range(fars)], axis=1)
+    for copy in edges:
+        copy.wait()
+    add_edge(sum_ref, near_ref, edge_ref, odd, pair_ref[pl.ds(pair_ref.shape[0] - LEAF, LEAF), :])
     for move in moves:
         move.wait()
 
 
 def far_kernel(
-    me_ref, zero_list, one_list, two_list, x_ref, low_first, low_second, high_ref, near_ref, edge_ref,
+    me_ref, zero_list, one_list, two_list, x_ref, got_first, got_second, near_ref, edge_ref,
     basis_ref, up_one_ref, up_two_ref, zero_wide, one_wide, two_wide, zero_in, one_in, two_in,
     out_hbm, zero_win, one_win, two_win,
-    sum_buf, out_buf, field_buf, down_buf, win_sems, out_sems, *, size,
+    sum_buf, out_buf, rows_buf, field_buf, down_buf, win_sems, out_sems, *, size,
 ):
     del zero_in, one_in, two_in
     leaves, rank, deep = zero_wide.shape
@@ -205,21 +218,31 @@
     place = REACH - 1 + 2 * odd
     sizes = [n * rank for n in (leaves, ones, twos)]
     at = [pl.multiple_of(place * n, n) for n in sizes]
-    moves = window_copies(
-        (
-            (low_first, 0, zero_win, at[0], sizes[0]),
+
+    def arrivals(low_ref, high_ref):
+        plans = (
+            (low_ref, 0, zero_win, at[0], sizes[0]),
             (high_ref, 0, one_win, at[1], sizes[1]),
             (high_ref, sizes[1], two_win, at[2], sizes[2]),
-        ),
-        win_sems,
-    )
-    other = window_copies(((low_second, 0, zero_win, at[0], sizes[0]),), win_sems)[0]
-    from_first = lax.rem(me + me // 2, 2) == 1
-    for move in moves[1:]:
-        move.start()
-
-    pl.when(from_first)(moves[0].start)
-    pl.when(jnp.logical_not(from_first))(other.start)
+        )
+        return window_copies(plans, win_sems)
+
+    moves = arrivals(got_first, got_second)
+    other = arrivals(got_second, got_first)
+    end = pl.ds(got_first.shape[0] - LEAF, LEAF)
+    low_first = lax.rem(me + me // 2, 2) == 1
+
+    @pl.when(low_first)
+    def _():
+        for move in moves:
+            move.start()
+        rows_buf[...] = got_second[end, :]
+
+    @pl.when(jnp.logical_not(low_first))
+    def _():
+        for move in other:
+            move.start()
+        rows_buf[...] = got_first[end, :]
 
     alone = (me == 0) | (me == size - 1)
 
@@ -231,8 +254,7 @@
 
     @pl.when(jnp.logical_not(alone))
     def _():
-        rows = high_ref[pl.ds(high_ref.shape[0] - LEAF, LEAF), :]
-        add_edge(sum_buf, near_ref, edge_ref, 1 - odd, rows)
+        add_edge(sum_buf, near_ref, edge_ref, 1 - odd, rows_buf[...])
 
     for move in moves:
         move.wait()
@@ -348,20 +370,16 @@
     turns = (lambda i: i + 2 - i // 2 % 2 * 4, lambda i: i - 2 + i // 2 % 2 * 4)
     first, second = [send(plain, turn) for turn in turns]
 
-    near, edge, points = pl.pallas_call(
+    near, points = pl.pallas_call(
         near_kernel,
         in_specs=[smem] + [hbm] * 3,
-        out_specs=[vmem] * 3,
-        out_shape=[
-            pltpu.VMEM(vectors.shape, f32),
-            pltpu.VMEM((leaves, 2, LEAF, LEAF), bf16),
-            pltpu.VMEM(vectors.shape, bf16),
-        ],
+        out_specs=[vmem] * 2,
+        out_shape=[pltpu.VMEM(vectors.shape, f32), pltpu.VMEM(vectors.shape, bf16)],
         scratch_shapes=[
             pltpu.SMEM(near_list.shape, jnp.int32),
             pltpu.VMEM((DEPTH, nears - 2, LEAF, LEAF), bf16),
-            pltpu.SemaphoreType.DMA((DEPTH, 3)),
-            pltpu.SemaphoreType.DMA,
+            pltpu.SemaphoreType.DMA((DEPTH, 2)),
+            pltpu.SemaphoreType.DMA((leaves // 4,)),
             pltpu.SemaphoreType.DMA,
         ],
         compiler_params=pltpu.CompilerParams(vmem_limit_bytes=16 * MIB),
@@ -373,19 +391,26 @@
         name="near_own",
     )(me, *in_hbm(near_list, vectors, near_blocks))
 
+    def cycle(lower):
+        def to(i):
+            along = i + 2 - i % 2 * 4 if (i // 2 + i) % 2 == lower else partner(i)
+            return along if 0 <= along < size else partner(i)
+
+        return to
+
     split = leaves * rank
-    from_pair, near = lax.optimization_barrier((from_pair, near))
-    lows = [send(from_pair[:split], turn) for turn in turns]
-    first, second, near = lax.optimization_barrier((first, second, near))
-    upper = jnp.where((me[0] // 2 + me[0]) % 2 == 0, first[split:], second[split:])
-    high = send(upper, partner)
-
-    sums, *rest = pl.pallas_call(
+    from_pair, first, second, near = lax.optimization_barrier((from_pair, first, second, near))
+    even = (me[0] // 2 + me[0]) % 2 == 0
+    got_first = send(jnp.where(even, from_pair[:split], second[split:]), cycle(0))
+    got_second = send(jnp.where(even, first[split:], from_pair[:split]), cycle(1))
+
+    sums, edge, *rest = pl.pallas_call(
         prep_kernel,
-        in_specs=[smem] + [vmem] * 6 + [hbm] * 3,
-        out_specs=[vmem] * 7,
+        in_specs=[smem] + [vmem] * 5 + [hbm] * 4,
+        out_specs=[vmem] * 8,
         out_shape=[
             pltpu.VMEM(vectors.shape, f32),
+            pltpu.VMEM((leaves, 2, LEAF, LEAF), bf16),
             *[pltpu.VMEM((SPAN * n * rank, columns), bf16) for n in counts],
             *[pltpu.VMEM((n, rank, fars * rank), bf16) for n in counts],
         ],
@@ -393,29 +418,34 @@
             *[pltpu.VMEM((n, fars, rank, rank), bf16) for n in counts],
             pltpu.SemaphoreType.DMA((sum(n // 4 for n in counts),)),
             pltpu.SemaphoreType.DMA((12,)),
+            pltpu.SemaphoreType.DMA((leaves // 4,)),
         ],
         compiler_params=pltpu.CompilerParams(vmem_limit_bytes=16 * MIB),
         cost_estimate=pl.CostEstimate(
-            flops=4 * 10**9,
-            bytes_accessed=4 * nodes * fars * rank * rank,
+            flops=2 * leaves * LEAF * LEAF * columns,
+            bytes_accessed=4 * nodes * fars * rank * rank + 4 * leaves * LEAF * LEAF,
             transcendentals=0,
         ),
         name="prep",
-    )(me, plain, from_pair, first, second, near, edge, *in_hbm(couple_zero, couple_one, couple_two))
+    )(
+        me, plain, from_pair, first, second, near,
+        *in_hbm(near_blocks, couple_zero, couple_one, couple_two),
+    )
     windows, wides = rest[:3], rest[3:]
 
     out, *_ = pl.pallas_call(
         functools.partial(far_kernel, size=size),
-        in_specs=[smem] * 4 + [vmem] * 15,
+        in_specs=[smem] * 4 + [vmem] * 14,
         out_specs=[hbm] + [vmem] * 3,
         out_shape=[
             jax.ShapeDtypeStruct(vectors.shape, bf16),
             *[pltpu.VMEM((SPAN * n * rank, columns), bf16) for n in counts],
         ],
-        input_output_aliases={16: 1, 17: 2, 18: 3},
+        input_output_aliases={15: 1, 16: 2, 17: 3},
         scratch_shapes=[
             pltpu.VMEM(vectors.shape, f32),
             pltpu.VMEM(vectors.shape, bf16),
+            pltpu.VMEM((LEAF, columns), bf16),
             pltpu.VMEM((nodes * rank, columns), f32),
             pltpu.VMEM((nodes * rank, columns), bf16),
             pltpu.SemaphoreType.DMA((3,)),
@@ -424,7 +454,7 @@
         compiler_params=pltpu.CompilerParams(vmem_limit_bytes=16 * MIB),
         name="far_down",
     )(
-        me, far_zero, far_one, far_two, points, *lows, high, sums, edge,
+        me, far_zero, far_one, far_two, points, got_first, got_second, sums, edge,
         basis_t, up_one, up_two, *wides, *windows,
     )
     return out

time: 34.5 us -> 38.1 us (1.10)
  waiting for transfers between devices: 4.58 us -> 8.59 us
  starting transfers between devices: 8.4 us -> 6.71 us
  Pallas kernels: 21.2 us -> 22.5 us
    ppermute x6 -> x5, waiting for transfers between devices: 4.58 us -> 8.59 us  [send(): return lax.ppermute(array, ('space', 'rhs'), pairs)]
    pallas_call x1, Pallas kernels: 3.57 us -> 5.36 us  [body(): pl.pallas_call(prep_kernel, in_specs=[smem] + [vmem] * 5 + [hbm] * 4, out...]
    ppermute x6 -> x5, starting transfers between devices: 8.4 us -> 6.71 us  [send(): return lax.ppermute(array, ('space', 'rhs'), pairs)]
    pallas_call x1, Pallas kernels: 10.9 us -> 10.3 us  [body(): pl.pallas_call(near_kernel, in_specs=[smem] + [hbm] * 3, out_specs=[vmem]...]
  transfers between devices with their start and end apart: 6 -> 5, of which waited for: 1 -> 4; matrix products, arithmetic and copies ran while one was open for 0% -> 0% of each run, Pallas kernels for 42% -> 41%
where the time goes in v11:
time: 38.1 us; the launch traced here: 37.9 us
  Pallas kernels  22.5 us (59%)
  waiting for transfers between devices  8.59 us (23%)
  starting transfers between devices  6.71 us (18%)
    pallas_call x1, Pallas kernels, body(): pl.pallas_call(near_kernel, in_specs=[smem] + [hbm] * 3, out_specs=[vmem]...  10.3 us
    ppermute x5, waiting for transfers between devices, send(): return lax.ppermute(array, ('space', 'rhs'), pairs)  8.59 us
    ppermute x5, starting transfers between devices, send(): return lax.ppermute(array, ('space', 'rhs'), pairs)  6.71 us
    pallas_call x1, Pallas kernels, body(): pl.pallas_call(prep_kernel, in_specs=[smem] + [vmem] * 5 + [hbm] * 4, out...  5.36 us
    pallas_call x1, Pallas kernels, body(): pl.pallas_call(functools.partial(far_kernel, size=size), in_specs=[smem]...  4.61 us
    pallas_call x1, Pallas kernels, body(): pl.pallas_call(up_kernel, in_specs=[smem] + [hbm] * 4, out_specs=[vmem] *...  2.16 us
  transfers between devices with their start and end apart: 5, of which 4 were waited for; matrix products, arithmetic and copies ran while one was open for 0% of the time, Pallas kernels for 41%

profile of v11, /device:TPU:0, one launch (start us, length us, event | category | flops | bytes accessed | tf_op | source)
XLA Modules:
  0.0 37.9 jit_solution(2274770420012449951)
XLA Ops:
  0.0 2.2 %up_pass.1 = (bf16[2048,128]{1,0:T(8,128)(2,1)S(1)}, bf16[2048,128]{1,0:T(8,128)(2,1)S(1)}) custom-call(s32[1]{0:T(128)} %bitcast.me_ref, bf16[4096,128]{1,0:T(8,128)(2,1)} %x_hbm.3, bf16[16,64,256]{2,1,0:T(8,128)(2,1)} %bitcast.2, bf16[16,64,64]{2,1,0:T(8,128)(2,1)} %up_one_ref.1, bf16[8,64,64]{2,1,0:T(8,128)(2,1)} %up_two_ref.1), custom_call_target="tpu_custom_call" | custom-call | tf_op jit(solution)/shard_map/up_pass/pallas_call | solution.py:339
  2.2 3.1 %collective-permute-start.1 = (bf16[2048,128]{1,0:T(8,128)(2,1)S(1)}, bf16[2048,128]{1,0:T(8,128)(2,1)S(1)}, u32[]{:S(2)}, u32[]{:S(2)}) collective-permute-start(bf16[2048,128]{1,0:T(8,128)(2,1)S(1)} %get-tuple-element.24.own_ref), channel_id=1, source_target_pairs={{0,4},{1,5},{2,6},{3,7},{4,0},{5,1},{6,2},{7,3},{8,12},{9,13},{10,... | collective-permute-start | bytes 1572872 | tf_op jit(solution)/shard_map/ppermute | solution.py:364
  5.3 0.0 collective-permute-start.2
  5.3 1.5 %collective-permute-start = (bf16[2048,128]{1,0:T(8,128)(2,1)S(1)}, bf16[2048,128]{1,0:T(8,128)(2,1)S(1)}, u32[]{:S(2)}, u32[]{:S(2)}) collective-permute-start(bf16[2048,128]{1,0:T(8,128)(2,1)S(1)} %get-tuple-element.23), channel_id=1, source_target_pairs={{0,2},{1,3},{2,0},{3,1},{4,6},{5,7},{6,4},{7,5},{8,10},{9,11},{10,... | collective-permute-start | bytes 1572872 | tf_op jit(solution)/shard_map/ppermute | solution.py:364
  6.8 10.3 %near_own.1 = (f32[4096,128]{1,0:T(8,128)S(1)}, bf16[4096,128]{1,0:T(8,128)(2,1)S(1)}) custom-call(s32[1]{0:T(128)} %bitcast.me_ref, s32[16,12]{1,0:T(8,128)} %list_hbm.1, bf16[4096,128]{1,0:T(8,128)(2,1)} %x_hbm.3, bf16[16,12,256,256]{3,2,1,0:T(8,128)(2,1)} %blocks_hbm.3), custom_call_target="tpu_custom_call" | custom-call | flops 2684354560 | bytes 28311552 | tf_op jit(solution)/shard_map/near_own/pallas_call | solution.py:373
  17.1 0.1 collective-permute-done.1.first_ref
  17.2 0.0 collective-permute-done.2.second_ref
  17.2 2.4 %collective-permute-done.pair_ref = bf16[2048,128]{1,0:T(8,128)(2,1)S(1)} collective-permute-done((bf16[2048,128]{1,0:T(8,128)(2,1)S(1)}, bf16[2048,128]{1,0:T(8,128)(2,1)S(1)}, u32[]{:S(2)}, u32[]{:S(2)}) %collective-permute-start) | collective-permute-done | bytes 524320 | tf_op jit(solution)/shard_map/ppermute | solution.py:364
  19.6 2.0 %collective-permute-start.3 = (bf16[1024,128]{1,0:T(8,128)(2,1)S(1)}, bf16[1024,128]{1,0:T(8,128)(2,1)S(1)}, u32[]{:S(2)}, u32[]{:S(2)}) collective-permute-start(bf16[1024,128]{1,0:T(8,128)(2,1)S(1)} %get-tuple-element.40), channel_id=1, source_target_pairs={{0,4},{1,5},{2,0},{3,1},{4,6},{5,7},{6,2},{7,3},{8,12},{9,13},{10,... | collective-permute-start | bytes 786440 | tf_op jit(solution)/shard_map/ppermute | solution.py:364
  21.6 0.0 copy-start
  21.6 0.0 copy-start.1
  21.6 0.0 copy-start.2
  21.6 0.0 copy-start.3
  21.6 0.0 copy-start.4
  21.6 0.0 copy-start.5
  21.7 0.2 collective-permute-start.4
  21.8 5.4 %prep.1 = (f32[4096,128]{1,0:T(8,128)S(1)}, bf16[16,2,256,256]{3,2,1,0:T(8,128)(2,1)S(1)}, bf16[5120,128]{1,0:T(8,128)(2,1)S(1)}, bf16[2560,128]{1,0:T(8,128)(2,...) custom-call(s32[1]{0:T(128)} %bitcast.me_ref, ...), custom_call_target="tpu_custom_call" | custom-call | flops 268435456 | bytes 11534336 | tf_op jit(solution)/shard_map/prep/pallas_call | solution.py:407
  27.2 1.7 %collective-permute-done.3.got_first = bf16[1024,128]{1,0:T(8,128)(2,1)S(1)} collective-permute-done((bf16[1024,128]{1,0:T(8,128)(2,1)S(1)}, bf16[1024,128]{1,0:T(8,128)(2,1)S(1)}, u32[]{:S(2)}, u32[]{:S(2)}) %collective-permute-start.3) | collective-permute-done | bytes 262176 | tf_op jit(solution)/shard_map/ppermute | solution.py:364
  28.9 4.3 %collective-permute-done.4.got_second = bf16[1024,128]{1,0:T(8,128)(2,1)S(1)} collective-permute-done((bf16[1024,128]{1,0:T(8,128)(2,1)S(1)}, bf16[1024,128]{1,0:T(8,128)(2,1)S(1)}, u32[]{:S(2)}, u32[]{:S(2)}) %collective-permute-start.4) | collective-permute-done | bytes 262176 | tf_op jit(solution)/shard_map/ppermute | solution.py:364
  33.3 0.0 copy-done
  33.3 0.0 copy-done.1
  33.3 0.0 copy-done.2
  33.3 0.0 copy-done.3
  33.3 0.0 copy-done.4
  33.3 0.0 copy-done.5
  33.3 4.6 %far_down.1 = (bf16[4096,128]{1,0:T(8,128)(2,1)}, bf16[5120,128]{1,0:T(8,128)(2,1)S(1)}, bf16[2560,128]{1,0:T(8,128)(2,1)S(1)}, bf16[1280,128]{1,0:T(8,128)(2,1)S(1)}) custom-call(s32[1]{0:T(128)} %bitcast.me_ref, s32[16,16]{1,0:T(8,128)S(1)} %copy-done.3, s32[8,16]{1,0:T(8,128)S(1)} %copy-done.4, ...), custom_call_target="tpu_custom_call", output_to_operand_aliasing={{1}: (15, {}), {2}: (16, {}), {3}: (17, {})} | custom-call | tf_op jit(solution)/shard_map/far_down/pallas_call | solution.py:436
  (1 shorter events, 0.0 us)
Async XLA Ops:
  2.2 15.0 %collective-permute-start.1 = (bf16[2048,128]{1,0:T(8,128)(2,1)S(1)}, bf16[2048,128]{1,0:T(8,128)(2,1)S(1)}, u32[]{:S(2)}, u32[]{:S(2)}) collective-permute-start(bf16[2048,128]{1,0:T(8,128)(2,1)S(1)} %get-tuple-element.24.own_ref), channel_id=1, source_target_pairs={{0,4},{1,5},{2,6},{3,7},{4,0},{5,1},{6,2},{7,3},{8,12},{9,13},{10,... | collective-permute-start | bytes 1572872 | tf_op jit(solution)/shard_map/ppermute | solution.py:364
  5.3 11.9 %collective-permute-start.2 = (bf16[2048,128]{1,0:T(8,128)(2,1)S(1)}, bf16[2048,128]{1,0:T(8,128)(2,1)S(1)}, u32[]{:S(2)}, u32[]{:S(2)}) collective-permute-start(bf16[2048,128]{1,0:T(8,128)(2,1)S(1)} %get-tuple-element.24.own_ref), channel_id=1, source_target_pairs={{0,1},{1,0},{2,3},{3,2},{4,8},{5,9},{6,10},{7,11},{8,4},{9,5},{10,... | collective-permute-start | bytes 1572872 | tf_op jit(solution)/shard_map/ppermute | solution.py:364
  5.3 14.3 %collective-permute-start = (bf16[2048,128]{1,0:T(8,128)(2,1)S(1)}, bf16[2048,128]{1,0:T(8,128)(2,1)S(1)}, u32[]{:S(2)}, u32[]{:S(2)}) collective-permute-start(bf16[2048,128]{1,0:T(8,128)(2,1)S(1)} %get-tuple-element.23), channel_id=1, source_target_pairs={{0,2},{1,3},{2,0},{3,1},{4,6},{5,7},{6,4},{7,5},{8,10},{9,11},{10,... | collective-permute-start | bytes 1572872 | tf_op jit(solution)/shard_map/ppermute | solution.py:364
  19.6 9.3 %collective-permute-start.3 = (bf16[1024,128]{1,0:T(8,128)(2,1)S(1)}, bf16[1024,128]{1,0:T(8,128)(2,1)S(1)}, u32[]{:S(2)}, u32[]{:S(2)}) collective-permute-start(bf16[1024,128]{1,0:T(8,128)(2,1)S(1)} %get-tuple-element.40), channel_id=1, source_target_pairs={{0,4},{1,5},{2,0},{3,1},{4,6},{5,7},{6,2},{7,3},{8,12},{9,13},{10,... | collective-permute-start | bytes 786440 | tf_op jit(solution)/shard_map/ppermute | solution.py:364
  21.6 11.6 %copy-start = (bf16[16,256,64]{1,2,0:T(8,128)(2,1)S(1)}, bf16[16,256,64]{1,2,0:T(8,128)(2,1)}, u32[]{:S(2)}) copy-start(bf16[16,256,64]{1,2,0:T(8,128)(2,1)} %param.15) | copy-start | bytes 1572868
  21.6 11.6 %copy-start.1 = (bf16[16,64,64]{2,1,0:T(8,128)(2,1)S(1)}, bf16[16,64,64]{2,1,0:T(8,128)(2,1)}, u32[]{:S(2)}) copy-start(bf16[16,64,64]{2,1,0:T(8,128)(2,1)} %up_one_ref.1) | copy-start | bytes 393220
  21.6 11.6 %copy-start.2 = (bf16[8,64,64]{2,1,0:T(8,128)(2,1)S(1)}, bf16[8,64,64]{2,1,0:T(8,128)(2,1)}, u32[]{:S(2)}) copy-start(bf16[8,64,64]{2,1,0:T(8,128)(2,1)} %up_two_ref.1) | copy-start | bytes 196612
  21.6 11.6 %copy-start.3 = (s32[16,16]{1,0:T(8,128)S(1)}, s32[16,16]{1,0:T(8,128)}, u32[]{:S(2)}) copy-start(s32[16,16]{1,0:T(8,128)} %zero_list.1) | copy-start | bytes 3076
  21.6 11.6 %copy-start.4 = (s32[8,16]{1,0:T(8,128)S(1)}, s32[8,16]{1,0:T(8,128)}, u32[]{:S(2)}) copy-start(s32[8,16]{1,0:T(8,128)} %one_list.1) | copy-start | bytes 1540
  21.6 11.6 %copy-start.5 = (s32[4,16]{1,0:T(4,128)S(1)}, s32[4,16]{1,0:T(4,128)}, u32[]{:S(2)}) copy-start(s32[4,16]{1,0:T(4,128)} %two_list.1) | copy-start | bytes 772
  21.7 11.6 %collective-permute-start.4 = (bf16[1024,128]{1,0:T(8,128)(2,1)S(1)}, bf16[1024,128]{1,0:T(8,128)(2,1)S(1)}, u32[]{:S(2)}, u32[]{:S(2)}) collective-permute-start(bf16[1024,128]{1,0:T(8,128)(2,1)S(1)} %get-tuple-element.39), channel_id=1, source_target_pairs={{0,2},{1,3},{2,0},{3,1},{4,8},{5,9},{6,4},{7,5},{8,10},{9,11},{10,... | collective-permute-start | bytes 786440 | tf_op jit(solution)/shard_map/ppermute | solution.py:364

commit v12 on v11

--- a/solution.py
+++ b/solution.py
@@ -204,8 +204,8 @@
 
 
 def far_kernel(
-    me_ref, zero_list, one_list, two_list, x_ref, got_first, got_second, near_ref, edge_ref,
-    basis_ref, up_one_ref, up_two_ref, zero_wide, one_wide, two_wide, zero_in, one_in, two_in,
+    me_ref, zero_list, one_list, two_list, x_ref, got_first, got_second, got_third, near_ref,
+    edge_ref, basis_ref, up_one_ref, up_two_ref, zero_wide, one_wide, two_wide, zero_in, one_in, two_in,
     out_hbm, zero_win, one_win, two_win,
     sum_buf, out_buf, rows_buf, field_buf, down_buf, win_sems, out_sems, *, size,
 ):
@@ -227,22 +227,22 @@
         )
         return window_copies(plans, win_sems)
 
-    moves = arrivals(got_first, got_second)
-    other = arrivals(got_second, got_first)
     end = pl.ds(got_first.shape[0] - LEAF, LEAF)
     low_first = lax.rem(me + me // 2, 2) == 1
-
-    @pl.when(low_first)
-    def _():
-        for move in moves:
-            move.start()
-        rows_buf[...] = got_second[end, :]
-
-    @pl.when(jnp.logical_not(low_first))
-    def _():
-        for move in other:
-            move.start()
-        rows_buf[...] = got_first[end, :]
+    at_end = (me < 2) | (me >= size - 2)
+
+    def take(low_ref, high_ref):
+        def _():
+            for move in arrivals(low_ref, high_ref):
+                move.start()
+            rows_buf[...] = high_ref[end, :]
+
+        return _
+
+    pl.when(low_first & at_end)(take(got_first, got_second))
+    pl.when(low_first & jnp.logical_not(at_end))(take(got_first, got_third))
+    pl.when(jnp.logical_not(low_first))(take(got_second, got_third))
+    moves = arrivals(got_first, got_second)
 
     alone = (me == 0) | (me == size - 1)
 
@@ -391,18 +391,20 @@
         name="near_own",
     )(me, *in_hbm(near_list, vectors, near_blocks))
 
-    def cycle(lower):
-        def to(i):
-            along = i + 2 - i % 2 * 4 if (i // 2 + i) % 2 == lower else partner(i)
-            return along if 0 <= along < size else partner(i)
-
-        return to
+    def has_second(i):
+        return 0 <= turns[1](i) < size
 
     split = leaves * rank
-    from_pair, first, second, near = lax.optimization_barrier((from_pair, first, second, near))
-    even = (me[0] // 2 + me[0]) % 2 == 0
-    got_first = send(jnp.where(even, from_pair[:split], second[split:]), cycle(0))
-    got_second = send(jnp.where(even, first[split:], from_pair[:split]), cycle(1))
+    from_pair, near = lax.optimization_barrier((from_pair, near))
+    low = from_pair[:split]
+    got_first = send(low, turns[0])
+    first, second, near = lax.optimization_barrier((first, second, near))
+    upper = jnp.where((me[0] // 2 + me[0]) % 2 == 0, first[split:], second[split:])
+    at_end = (me[0] < 2) | (me[0] >= size - 2)
+    got_second = send(
+        jnp.where(at_end, upper, low), lambda i: turns[1](i) if has_second(i) else partner(i)
+    )
+    got_third = send(upper, lambda i: partner(i) if has_second(i) else -1)
 
     sums, edge, *rest = pl.pallas_call(
         prep_kernel,
@@ -422,7 +424,7 @@
         ],
         compiler_params=pltpu.CompilerParams(vmem_limit_bytes=16 * MIB),
         cost_estimate=pl.CostEstimate(
-            flops=2 * leaves * LEAF * LEAF * columns,
+            flops=4 * 10**9,
             bytes_accessed=4 * nodes * fars * rank * rank + 4 * leaves * LEAF * LEAF,
             transcendentals=0,
         ),
@@ -435,13 +437,13 @@
 
     out, *_ = pl.pallas_call(
         functools.partial(far_kernel, size=size),
-        in_specs=[smem] * 4 + [vmem] * 14,
+        in_specs=[smem] * 4 + [vmem] * 15,
         out_specs=[hbm] + [vmem] * 3,
         out_shape=[
             jax.ShapeDtypeStruct(vectors.shape, bf16),
             *[pltpu.VMEM((SPAN * n * rank, columns), bf16) for n in counts],
         ],
-        input_output_aliases={15: 1, 16: 2, 17: 3},
+        input_output_aliases={16: 1, 17: 2, 18: 3},
         scratch_shapes=[
             pltpu.VMEM(vectors.shape, f32),
             pltpu.VMEM(vectors.shape, bf16),
@@ -454,7 +456,7 @@
         compiler_params=pltpu.CompilerParams(vmem_limit_bytes=16 * MIB),
         name="far_down",
     )(
-        me, far_zero, far_one, far_two, points, got_first, got_second, sums, edge,
+        me, far_zero, far_one, far_two, points, got_first, got_second, got_third, sums, edge,
         basis_t, up_one, up_two, *wides, *windows,
     )
     return out

time: 38.1 us -> 32.7 us (0.86)
  waiting for transfers between devices: 8.59 us -> 2.08 us
  starting transfers between devices: 6.71 us -> 7.96 us
    ppermute x5 -> x6, waiting for transfers between devices: 8.59 us -> 2.08 us  [send(): return lax.ppermute(array, ('space', 'rhs'), pairs)]
    ppermute x5 -> x6, starting transfers between devices: 6.71 us -> 7.96 us  [send(): return lax.ppermute(array, ('space', 'rhs'), pairs)]
  transfers between devices with their start and end apart: 5 -> 6, of which waited for: 4 -> 2; matrix products, arithmetic and copies ran while one was open for 0% -> 0% of each run, Pallas kernels for 41% -> 48%
where the time goes in v12:
time: 32.7 us; the launch traced here: 32.6 us
  Pallas kernels  22.4 us (69%)
  starting transfers between devices  7.96 us (24%)
  waiting for transfers between devices  2.08 us (6%)
    pallas_call x1, Pallas kernels, body(): pl.pallas_call(near_kernel, in_specs=[smem] + [hbm] * 3, out_specs=[vmem]...  10.3 us
    ppermute x6, starting transfers between devices, send(): return lax.ppermute(array, ('space', 'rhs'), pairs)  7.96 us
    pallas_call x1, Pallas kernels, body(): pl.pallas_call(prep_kernel, in_specs=[smem] + [vmem] * 5 + [hbm] * 4, out...  5.3 us
    pallas_call x1, Pallas kernels, body(): pl.pallas_call(functools.partial(far_kernel, size=size), in_specs=[smem]...  4.57 us
    pallas_call x1, Pallas kernels, body(): pl.pallas_call(up_kernel, in_specs=[smem] + [hbm] * 4, out_specs=[vmem] *...  2.16 us
    ppermute x6, waiting for transfers between devices, send(): return lax.ppermute(array, ('space', 'rhs'), pairs)  2.08 us
  transfers between devices with their start and end apart: 6, of which 2 were waited for; matrix products, arithmetic and copies ran while one was open for 0% of the time, Pallas kernels for 48%

profile of v12, /device:TPU:0, one launch (start us, length us, event | category | flops | bytes accessed | tf_op | source)
XLA Modules:
  0.0 32.6 jit_solution(3071783606144228173)
XLA Ops:
  0.0 2.2 %up_pass.1 = (bf16[2048,128]{1,0:T(8,128)(2,1)S(1)}, bf16[2048,128]{1,0:T(8,128)(2,1)S(1)}) custom-call(s32[1]{0:T(128)} %bitcast.me_ref, bf16[4096,128]{1,0:T(8,128)(2,1)} %x_hbm.3, bf16[16,64,256]{2,1,0:T(8,128)(2,1)} %bitcast.2, bf16[16,64,64]{2,1,0:T(8,128)(2,1)} %up_one_ref.1, bf16[8,64,64]{2,1,0:T(8,128)(2,1)} %up_two_ref.1), custom_call_target="tpu_custom_call" | custom-call | tf_op jit(solution)/shard_map/up_pass/pallas_call | solution.py:339
  2.2 3.0 %collective-permute-start = (bf16[2048,128]{1,0:T(8,128)(2,1)S(1)}, bf16[2048,128]{1,0:T(8,128)(2,1)S(1)}, u32[]{:S(2)}, u32[]{:S(2)}) collective-permute-start(bf16[2048,128]{1,0:T(8,128)(2,1)S(1)} %get-tuple-element.24), channel_id=1, source_target_pairs={{0,2},{1,3},{2,0},{3,1},{4,6},{5,7},{6,4},{7,5},{8,10},{9,11},{10,... | collective-permute-start | bytes 1572872 | tf_op jit(solution)/shard_map/ppermute | solution.py:364
  5.2 1.6 %collective-permute-start.2 = (bf16[2048,128]{1,0:T(8,128)(2,1)S(1)}, bf16[2048,128]{1,0:T(8,128)(2,1)S(1)}, u32[]{:S(2)}, u32[]{:S(2)}) collective-permute-start(bf16[2048,128]{1,0:T(8,128)(2,1)S(1)} %get-tuple-element.27.own_ref), channel_id=1, source_target_pairs={{0,4},{1,5},{2,6},{3,7},{4,0},{5,1},{6,2},{7,3},{8,12},{9,13},{10,... | collective-permute-start | bytes 1572872 | tf_op jit(solution)/shard_map/ppermute | solution.py:364
  6.8 0.0 collective-permute-start.3
  6.8 10.3 %near_own.1 = (f32[4096,128]{1,0:T(8,128)S(1)}, bf16[4096,128]{1,0:T(8,128)(2,1)S(1)}) custom-call(s32[1]{0:T(128)} %bitcast.me_ref, s32[16,12]{1,0:T(8,128)} %list_hbm.1, bf16[4096,128]{1,0:T(8,128)(2,1)} %x_hbm.3, bf16[16,12,256,256]{3,2,1,0:T(8,128)(2,1)} %blocks_hbm.3), custom_call_target="tpu_custom_call" | custom-call | flops 2684354560 | bytes 28311552 | tf_op jit(solution)/shard_map/near_own/pallas_call | solution.py:373
  17.1 0.0 collective-permute-done.pair_ref
  17.1 1.5 %collective-permute-done.2.first_ref = bf16[2048,128]{1,0:T(8,128)(2,1)S(1)} collective-permute-done((bf16[2048,128]{1,0:T(8,128)(2,1)S(1)}, bf16[2048,128]{1,0:T(8,128)(2,1)S(1)}, u32[]{:S(2)}, u32[]{:S(2)}) %collective-permute-start.2) | collective-permute-done | bytes 524320 | tf_op jit(solution)/shard_map/ppermute | solution.py:364
  18.6 0.0 collective-permute-done.3.second_ref
  18.6 0.1 broadcast_select_fusion
  18.6 2.8 %collective-permute-start.1 = (bf16[1024,128]{1,0:T(8,128)(2,1)S(1)}, bf16[1024,128]{1,0:T(8,128)(2,1)S(1)}, u32[]{:S(2)}, u32[]{:S(2)}) collective-permute-start(bf16[1024,128]{1,0:T(8,128)(2,1)S(1)} %get-tuple-element.43), channel_id=1, source_target_pairs={{0,4},{1,5},{2,6},{3,7},{4,0},{5,1},{6,2},{7,3},{8,12},{9,13},{10,... | collective-permute-start | bytes 786440 | tf_op jit(solution)/shard_map/ppermute | solution.py:364
  21.4 0.5 %collective-permute-start.4 = (bf16[1024,128]{1,0:T(8,128)(2,1)S(1)}, bf16[1024,128]{1,0:T(8,128)(2,1)S(1)}, u32[]{:S(2)}, u32[]{:S(2)}) collective-permute-start(bf16[1024,128]{1,0:T(8,128)(2,1)S(1)} %get-tuple-element.41), channel_id=1, source_target_pairs={{0,2},{1,3},{2,0},{3,1},{4,8},{5,9},{6,10},{7,11},{8,4},{9,5},{10,... | collective-permute-start | bytes 786440 | tf_op jit(solution)/shard_map/ppermute | solution.py:364
  21.9 0.0 copy-start
  21.9 0.0 copy-start.1
  21.9 0.0 copy-start.2
  21.9 0.0 copy-start.3
  21.9 0.0 copy-start.4
  21.9 0.0 copy-start.5
  22.0 0.1 collective-permute-start.5
  22.0 5.3 %prep.1 = (f32[4096,128]{1,0:T(8,128)S(1)}, bf16[16,2,256,256]{3,2,1,0:T(8,128)(2,1)S(1)}, bf16[5120,128]{1,0:T(8,128)(2,1)S(1)}, bf16[2560,128]{1,0:T(8,128)(2,...) custom-call(s32[1]{0:T(128)} %bitcast.me_ref, ...), custom_call_target="tpu_custom_call" | custom-call | flops 4000000000 | bytes 11534336 | tf_op jit(solution)/shard_map/prep/pallas_call | solution.py:409
  27.3 0.0 collective-permute-done.1.got_first
  27.4 0.6 %collective-permute-done.4.got_second = bf16[1024,128]{1,0:T(8,128)(2,1)S(1)} collective-permute-done((bf16[1024,128]{1,0:T(8,128)(2,1)S(1)}, bf16[1024,128]{1,0:T(8,128)(2,1)S(1)}, u32[]{:S(2)}, u32[]{:S(2)}) %collective-permute-start.4) | collective-permute-done | bytes 262176 | tf_op jit(solution)/shard_map/ppermute | solution.py:364
  28.0 0.0 collective-permute-done.5.got_third
  28.0 0.0 copy-done
  28.0 0.0 copy-done.1
  28.0 0.0 copy-done.2
  28.0 0.0 copy-done.3
  28.0 0.0 copy-done.4
  28.0 0.0 copy-done.5
  28.0 4.6 %far_down.1 = (bf16[4096,128]{1,0:T(8,128)(2,1)}, bf16[5120,128]{1,0:T(8,128)(2,1)S(1)}, bf16[2560,128]{1,0:T(8,128)(2,1)S(1)}, bf16[1280,128]{1,0:T(8,128)(2,1)S(1)}) custom-call(s32[1]{0:T(128)} %bitcast.me_ref, s32[16,16]{1,0:T(8,128)S(1)} %copy-done.3, s32[8,16]{1,0:T(8,128)S(1)} %copy-done.4, ...), custom_call_target="tpu_custom_call", output_to_operand_aliasing={{1}: (16, {}), {2}: (17, {}), {3}: (18, {})} | custom-call | tf_op jit(solution)/shard_map/far_down/pallas_call | solution.py:438
Async XLA Ops:
  2.2 14.9 %collective-permute-start = (bf16[2048,128]{1,0:T(8,128)(2,1)S(1)}, bf16[2048,128]{1,0:T(8,128)(2,1)S(1)}, u32[]{:S(2)}, u32[]{:S(2)}) collective-permute-start(bf16[2048,128]{1,0:T(8,128)(2,1)S(1)} %get-tuple-element.24), channel_id=1, source_target_pairs={{0,2},{1,3},{2,0},{3,1},{4,6},{5,7},{6,4},{7,5},{8,10},{9,11},{10,... | collective-permute-start | bytes 1572872 | tf_op jit(solution)/shard_map/ppermute | solution.py:364
  5.2 13.4 %collective-permute-start.2 = (bf16[2048,128]{1,0:T(8,128)(2,1)S(1)}, bf16[2048,128]{1,0:T(8,128)(2,1)S(1)}, u32[]{:S(2)}, u32[]{:S(2)}) collective-permute-start(bf16[2048,128]{1,0:T(8,128)(2,1)S(1)} %get-tuple-element.27.own_ref), channel_id=1, source_target_pairs={{0,4},{1,5},{2,6},{3,7},{4,0},{5,1},{6,2},{7,3},{8,12},{9,13},{10,... | collective-permute-start | bytes 1572872 | tf_op jit(solution)/shard_map/ppermute | solution.py:364
  6.8 11.8 %collective-permute-start.3 = (bf16[2048,128]{1,0:T(8,128)(2,1)S(1)}, bf16[2048,128]{1,0:T(8,128)(2,1)S(1)}, u32[]{:S(2)}, u32[]{:S(2)}) collective-permute-start(bf16[2048,128]{1,0:T(8,128)(2,1)S(1)} %get-tuple-element.27.own_ref), channel_id=1, source_target_pairs={{0,1},{1,0},{2,3},{3,2},{4,8},{5,9},{6,10},{7,11},{8,4},{9,5},{10,... | collective-permute-start | bytes 1572872 | tf_op jit(solution)/shard_map/ppermute | solution.py:364
  18.6 8.7 %collective-permute-start.1 = (bf16[1024,128]{1,0:T(8,128)(2,1)S(1)}, bf16[1024,128]{1,0:T(8,128)(2,1)S(1)}, u32[]{:S(2)}, u32[]{:S(2)}) collective-permute-start(bf16[1024,128]{1,0:T(8,128)(2,1)S(1)} %get-tuple-element.43), channel_id=1, source_target_pairs={{0,4},{1,5},{2,6},{3,7},{4,0},{5,1},{6,2},{7,3},{8,12},{9,13},{10,... | collective-permute-start | bytes 786440 | tf_op jit(solution)/shard_map/ppermute | solution.py:364
  21.4 6.6 %collective-permute-start.4 = (bf16[1024,128]{1,0:T(8,128)(2,1)S(1)}, bf16[1024,128]{1,0:T(8,128)(2,1)S(1)}, u32[]{:S(2)}, u32[]{:S(2)}) collective-permute-start(bf16[1024,128]{1,0:T(8,128)(2,1)S(1)} %get-tuple-element.41), channel_id=1, source_target_pairs={{0,2},{1,3},{2,0},{3,1},{4,8},{5,9},{6,10},{7,11},{8,4},{9,5},{10,... | collective-permute-start | bytes 786440 | tf_op jit(solution)/shard_map/ppermute | solution.py:364
  21.9 6.0 %copy-start = (bf16[16,256,64]{1,2,0:T(8,128)(2,1)S(1)}, bf16[16,256,64]{1,2,0:T(8,128)(2,1)}, u32[]{:S(2)}) copy-start(bf16[16,256,64]{1,2,0:T(8,128)(2,1)} %param.15) | copy-start | bytes 1572868
  21.9 6.0 %copy-start.1 = (bf16[16,64,64]{2,1,0:T(8,128)(2,1)S(1)}, bf16[16,64,64]{2,1,0:T(8,128)(2,1)}, u32[]{:S(2)}) copy-start(bf16[16,64,64]{2,1,0:T(8,128)(2,1)} %up_one_ref.1) | copy-start | bytes 393220
  21.9 6.0 %copy-start.2 = (bf16[8,64,64]{2,1,0:T(8,128)(2,1)S(1)}, bf16[8,64,64]{2,1,0:T(8,128)(2,1)}, u32[]{:S(2)}) copy-start(bf16[8,64,64]{2,1,0:T(8,128)(2,1)} %up_two_ref.1) | copy-start | bytes 196612
  21.9 6.1 %copy-start.3 = (s32[16,16]{1,0:T(8,128)S(1)}, s32[16,16]{1,0:T(8,128)}, u32[]{:S(2)}) copy-start(s32[16,16]{1,0:T(8,128)} %zero_list.1) | copy-start | bytes 3076
  21.9 6.1 %copy-start.4 = (s32[8,16]{1,0:T(8,128)S(1)}, s32[8,16]{1,0:T(8,128)}, u32[]{:S(2)}) copy-start(s32[8,16]{1,0:T(8,128)} %one_list.1) | copy-start | bytes 1540
  21.9 6.1 %copy-start.5 = (s32[4,16]{1,0:T(4,128)S(1)}, s32[4,16]{1,0:T(4,128)}, u32[]{:S(2)}) copy-start(s32[4,16]{1,0:T(4,128)} %two_list.1) | copy-start | bytes 772
  22.0 6.0 %collective-permute-start.5 = (bf16[1024,128]{1,0:T(8,128)(2,1)S(1)}, bf16[1024,128]{1,0:T(8,128)(2,1)S(1)}, u32[]{:S(2)}, u32[]{:S(2)}) collective-permute-start(bf16[1024,128]{1,0:T(8,128)(2,1)S(1)} %get-tuple-element.42), channel_id=1, source_target_pairs={{0,1},{1,0},{2,3},{3,2},{4,6},{5,7},{6,4},{7,5},{8,10},{9,11},{10,... | collective-permute-start | bytes 786440 | tf_op jit(solution)/shard_map/ppermute | solution.py:364

commit v13 on v12

--- a/solution.py
+++ b/solution.py
@@ -10,7 +10,7 @@
 LEAF = 256
 REACH = 2
 SPAN = 2 * REACH + 1
-DEPTH = 4
+DEPTH = 3
 MIB = 1024 * 1024
 
 
@@ -79,15 +79,19 @@
 
 
 def near_kernel(
-    me_ref, list_hbm, x_hbm, blocks_hbm, out_ref, x_ref, list_ref, block_buf, sems, x_sems, list_sem,
+    me_ref, list_hbm, x_hbm, blocks_hbm, out_ref, edge_ref, x_ref,
+    list_ref, block_buf, sems, x_sems, list_sem,
 ):
     leaves, nears = list_ref.shape
     first = me_ref[0] * leaves
-
-    def copies(leaf, slot):
+    depth = block_buf.shape[0]
+
+    def copies(pair, slot):
+        both = pl.ds(2 * pair, 2)
         pairs = (
-            (blocks_hbm.at[leaf, pl.ds(0, 1)], block_buf.at[slot, pl.ds(0, 1)]),
-            (blocks_hbm.at[leaf, pl.ds(3, nears - 3)], block_buf.at[slot, pl.ds(1, nears - 3)]),
+            (blocks_hbm.at[both, pl.ds(0, 1)], block_buf.at[slot, :, pl.ds(0, 1)]),
+            (blocks_hbm.at[both, pl.ds(3, nears - 3)], block_buf.at[slot, :, pl.ds(1, nears - 3)]),
+            (blocks_hbm.at[both, pl.ds(1, 2)], edge_ref.at[both]),
         )
         return [
             pltpu.make_async_copy(src, dst, sems.at[slot, i]) for i, (src, dst) in enumerate(pairs)
@@ -103,33 +107,36 @@
         )
     for copy in x_copies:
         copy.start()
-    for leaf in range(DEPTH - 1):
-        for copy in copies(leaf, leaf):
+    for pair in range(depth - 1):
+        for copy in copies(pair, pair):
             copy.start()
     list_copy.wait()
     for copy in x_copies:
         copy.wait()
 
-    def step(leaf, carry):
-        slot = lax.rem(leaf, DEPTH)
-
-        @pl.when(leaf + DEPTH - 1 < leaves)
+    def step(pair, carry):
+        slot = lax.rem(pair, depth)
+
+        @pl.when(pair + depth - 1 < leaves // 2)
         def _():
-            for copy in copies(leaf + DEPTH - 1, lax.rem(leaf + DEPTH - 1, DEPTH)):
+            for copy in copies(pair + depth - 1, lax.rem(pair + depth - 1, depth)):
                 copy.start()
 
-        for copy in copies(leaf, slot):
+        for copy in copies(pair, slot):
             copy.wait()
-        rows = []
-        for k in (0, *range(3, nears)):
-            start = pl.multiple_of((list_ref[leaf, k] - first) * LEAF, LEAF)
-            rows.append(x_ref[pl.ds(start, LEAF), :])
-        blocks = [block_buf[slot, k] for k in range(nears - 2)]
-        here = pl.ds(pl.multiple_of(leaf * LEAF, LEAF), LEAF)
-        out_ref[here, :] = dot(jnp.concatenate(blocks, axis=1), jnp.concatenate(rows, axis=0))
+        totals = []
+        for side in range(2):
+            rows = []
+            for k in (0, *range(3, nears)):
+                start = (list_ref[2 * pair + side, k] - first) * LEAF
+                rows.append(x_ref[pl.ds(pl.multiple_of(start, LEAF), LEAF), :])
+            blocks = [block_buf[slot, side, k] for k in range(nears - 2)]
+            totals.append(dot(jnp.concatenate(blocks, axis=1), jnp.concatenate(rows, axis=0)))
+        here = pl.ds(pl.multiple_of(pair * 2 * LEAF, 2 * LEAF), 2 * LEAF)
+        out_ref[here, :] = jnp.concatenate(totals, axis=0)
         return carry
 
-    lax.fori_loop(0, leaves, step, 0)
+    lax.fori_loop(0, leaves // 2, step, 0)
 
 
 def add_edge(sum_ref, near_ref, edge_ref, side, rows):
@@ -150,10 +157,10 @@
 
 
 def prep_kernel(
-    me_ref, own_ref, pair_ref, first_ref, second_ref, near_ref,
-    blocks_hbm, zero_hbm, one_hbm, two_hbm,
-    sum_ref, edge_ref, zero_win, one_win, two_win, zero_wide, one_wide, two_wide,
-    zero_buf, one_buf, two_buf, sems, win_sems, edge_sems,
+    me_ref, own_ref, pair_ref, first_ref, second_ref, near_ref, edge_ref,
+    zero_hbm, one_hbm, two_hbm,
+    sum_ref, zero_win, one_win, two_win, zero_wide, one_wide, two_wide,
+    zero_buf, one_buf, two_buf, sems, win_sems,
 ):
     levels = (
         (two_hbm, two_buf, two_wide),
@@ -167,12 +174,6 @@
             copy = pltpu.make_async_copy(hbm.at[some], buf.at[some], sems.at[len(chunks)])
             copy.start()
             chunks.append((copy, buf, wide, first))
-    edges = []
-    for q in range(edge_ref.shape[0] // 4):
-        some = pl.ds(4 * q, 4)
-        src = blocks_hbm.at[some, pl.ds(1, 2)]
-        edges.append(pltpu.make_async_copy(src, edge_ref.at[some], edge_sems.at[q]))
-        edges[-1].start()
     me = me_ref[0]
     odd = lax.rem(me, 2)
     block = lax.rem(me // 2, 2)
@@ -191,14 +192,12 @@
     moves = window_copies(plans, win_sems)
     for move in moves:
         move.start()
+    add_edge(sum_ref, near_ref, edge_ref, odd, pair_ref[pl.ds(pair_ref.shape[0] - LEAF, LEAF), :])
     for copy, buf, wide, first in chunks:
         copy.wait()
         for node in range(first, first + 4):
             fars = buf.shape[1]
             wide[node] = jnp.concatenate([buf[node, k] for k in range(fars)], axis=1)
-    for copy in edges:
-        copy.wait()
-    add_edge(sum_ref, near_ref, edge_ref, odd, pair_ref[pl.ds(pair_ref.shape[0] - LEAF, LEAF), :])
     for move in moves:
         move.wait()
 
@@ -370,15 +369,19 @@
     turns = (lambda i: i + 2 - i // 2 % 2 * 4, lambda i: i - 2 + i // 2 % 2 * 4)
     first, second = [send(plain, turn) for turn in turns]
 
-    near, points = pl.pallas_call(
+    near, edge, points = pl.pallas_call(
         near_kernel,
         in_specs=[smem] + [hbm] * 3,
-        out_specs=[vmem] * 2,
-        out_shape=[pltpu.VMEM(vectors.shape, f32), pltpu.VMEM(vectors.shape, bf16)],
+        out_specs=[vmem] * 3,
+        out_shape=[
+            pltpu.VMEM(vectors.shape, f32),
+            pltpu.VMEM((leaves, 2, LEAF, LEAF), bf16),
+            pltpu.VMEM(vectors.shape, bf16),
+        ],
         scratch_shapes=[
             pltpu.SMEM(near_list.shape, jnp.int32),
-            pltpu.VMEM((DEPTH, nears - 2, LEAF, LEAF), bf16),
-            pltpu.SemaphoreType.DMA((DEPTH, 2)),
+            pltpu.VMEM((DEPTH, 2, nears - 2, LEAF, LEAF), bf16),
+            pltpu.SemaphoreType.DMA((DEPTH, 3)),
             pltpu.SemaphoreType.DMA((leaves // 4,)),
             pltpu.SemaphoreType.DMA,
         ],
@@ -406,13 +409,12 @@
     )
     got_third = send(upper, lambda i: partner(i) if has_second(i) else -1)
 
-    sums, edge, *rest = pl.pallas_call(
+    sums, *rest = pl.pallas_call(
         prep_kernel,
-        in_specs=[smem] + [vmem] * 5 + [hbm] * 4,
-        out_specs=[vmem] * 8,
+        in_specs=[smem] + [vmem] * 6 + [hbm] * 3,
+        out_specs=[vmem] * 7,
         out_shape=[
             pltpu.VMEM(vectors.shape, f32),
-            pltpu.VMEM((leaves, 2, LEAF, LEAF), bf16),
             *[pltpu.VMEM((SPAN * n * rank, columns), bf16) for n in counts],
             *[pltpu.VMEM((n, rank, fars * rank), bf16) for n in counts],
         ],
@@ -420,18 +422,17 @@
             *[pltpu.VMEM((n, fars, rank, rank), bf16) for n in counts],
             pltpu.SemaphoreType.DMA((sum(n // 4 for n in counts),)),
             pltpu.SemaphoreType.DMA((12,)),
-            pltpu.SemaphoreType.DMA((leaves // 4,)),
         ],
         compiler_params=pltpu.CompilerParams(vmem_limit_bytes=16 * MIB),
         cost_estimate=pl.CostEstimate(
             flops=4 * 10**9,
-            bytes_accessed=4 * nodes * fars * rank * rank + 4 * leaves * LEAF * LEAF,
+            bytes_accessed=4 * nodes * fars * rank * rank,
             transcendentals=0,
         ),
         name="prep",
     )(
-        me, plain, from_pair, first, second, near,
-        *in_hbm(near_blocks, couple_zero, couple_one, couple_two),
+        me, plain, from_pair, first, second, near, edge,
+        *in_hbm(couple_zero, couple_one, couple_two),
     )
     windows, wides = rest[:3], rest[3:]
 

time: 32.7 us -> 32.7 us (level)
  waiting for transfers between devices: 2.08 us -> 3.7 us
  Pallas kernels: 22.4 us -> 20.8 us
    pallas_call x1, Pallas kernels: 5.3 us -> 3.57 us  [body(): pl.pallas_call(prep_kernel, in_specs=[smem] + [vmem] * 6 + [hbm] * 3, out...]
    ppermute x6, waiting for transfers between devices: 2.08 us -> 3.7 us  [send(): return lax.ppermute(array, ('space', 'rhs'), pairs)]
  transfers between devices with their start and end apart: 6 -> 6, of which waited for: 2 -> 3; matrix products, arithmetic and copies ran while one was open for 0% -> 0% of each run, Pallas kernels for 48% -> 43%
where the time goes in v13:
time: 32.7 us; the launch traced here: 32.6 us
  Pallas kernels  20.8 us (64%)
  starting transfers between devices  7.89 us (24%)
  waiting for transfers between devices  3.7 us (11%)
    pallas_call x1, Pallas kernels, body(): pl.pallas_call(near_kernel, in_specs=[smem] + [hbm] * 3, out_specs=[vmem]...  10.5 us
    ppermute x6, starting transfers between devices, send(): return lax.ppermute(array, ('space', 'rhs'), pairs)  7.89 us
    pallas_call x1, Pallas kernels, body(): pl.pallas_call(functools.partial(far_kernel, size=size), in_specs=[smem]...  4.57 us
    ppermute x6, waiting for transfers between devices, send(): return lax.ppermute(array, ('space', 'rhs'), pairs)  3.7 us
    pallas_call x1, Pallas kernels, body(): pl.pallas_call(prep_kernel, in_specs=[smem] + [vmem] * 6 + [hbm] * 3, out...  3.57 us
    pallas_call x1, Pallas kernels, body(): pl.pallas_call(up_kernel, in_specs=[smem] + [hbm] * 4, out_specs=[vmem] *...  2.16 us
  transfers between devices with their start and end apart: 6, of which 3 were waited for; matrix products, arithmetic and copies ran while one was open for 0% of the time, Pallas kernels for 43%

profile of v13, /device:TPU:0, one launch (start us, length us, event | category | flops | bytes accessed | tf_op | source)
XLA Modules:
  0.0 32.6 jit_solution(15095037685061282693)
XLA Ops:
  0.0 2.2 %up_pass.1 = (bf16[2048,128]{1,0:T(8,128)(2,1)S(1)}, bf16[2048,128]{1,0:T(8,128)(2,1)S(1)}) custom-call(s32[1]{0:T(128)} %bitcast.me_ref, bf16[4096,128]{1,0:T(8,128)(2,1)} %x_hbm.3, bf16[16,64,256]{2,1,0:T(8,128)(2,1)} %bitcast.2, bf16[16,64,64]{2,1,0:T(8,128)(2,1)} %up_one_ref.1, bf16[8,64,64]{2,1,0:T(8,128)(2,1)} %up_two_ref.1), custom_call_target="tpu_custom_call" | custom-call | tf_op jit(solution)/shard_map/up_pass/pallas_call | solution.py:338
  2.2 3.0 %collective-permute-start = (bf16[2048,128]{1,0:T(8,128)(2,1)S(1)}, bf16[2048,128]{1,0:T(8,128)(2,1)S(1)}, u32[]{:S(2)}, u32[]{:S(2)}) collective-permute-start(bf16[2048,128]{1,0:T(8,128)(2,1)S(1)} %get-tuple-element.24), channel_id=1, source_target_pairs={{0,2},{1,3},{2,0},{3,1},{4,6},{5,7},{6,4},{7,5},{8,10},{9,11},{10,... | collective-permute-start | bytes 1572872 | tf_op jit(solution)/shard_map/ppermute | solution.py:363
  5.2 1.6 %collective-permute-start.2 = (bf16[2048,128]{1,0:T(8,128)(2,1)S(1)}, bf16[2048,128]{1,0:T(8,128)(2,1)S(1)}, u32[]{:S(2)}, u32[]{:S(2)}) collective-permute-start(bf16[2048,128]{1,0:T(8,128)(2,1)S(1)} %get-tuple-element.27.own_ref), channel_id=1, source_target_pairs={{0,4},{1,5},{2,6},{3,7},{4,0},{5,1},{6,2},{7,3},{8,12},{9,13},{10,... | collective-permute-start | bytes 1572872 | tf_op jit(solution)/shard_map/ppermute | solution.py:363
  6.8 0.0 collective-permute-start.3
  6.8 10.5 %near_own.1 = (f32[4096,128]{1,0:T(8,128)S(1)}, bf16[16,2,256,256]{3,2,1,0:T(8,128)(2,1)S(1)}, bf16[4096,128]{1,0:T(8,128)(2,1)S(1)}) custom-call(s32[1]{0:T(128)} %bitcast.me_ref, s32[16,12]{1,0:T(8,128)} %list_hbm.1, bf16[4096,128]{1,0:T(8,128)(2,1)} %x_hbm.3, bf16[16,12,256,256]{3,2,1,0:T(8,128)(2,1)} %blocks_hbm.1), custom_call_target="tpu_custom_call" | custom-call | flops 2684354560 | bytes 28311552 | tf_op jit(solution)/shard_map/near_own/pallas_call | solution.py:372
  17.3 0.0 collective-permute-done.pair_ref
  17.3 1.3 %collective-permute-done.2.first_ref = bf16[2048,128]{1,0:T(8,128)(2,1)S(1)} collective-permute-done((bf16[2048,128]{1,0:T(8,128)(2,1)S(1)}, bf16[2048,128]{1,0:T(8,128)(2,1)S(1)}, u32[]{:S(2)}, u32[]{:S(2)}) %collective-permute-start.2) | collective-permute-done | bytes 524320 | tf_op jit(solution)/shard_map/ppermute | solution.py:363
  18.6 0.0 collective-permute-done.3.second_ref
  18.6 0.1 broadcast_select_fusion
  18.6 2.8 %collective-permute-start.1 = (bf16[1024,128]{1,0:T(8,128)(2,1)S(1)}, bf16[1024,128]{1,0:T(8,128)(2,1)S(1)}, u32[]{:S(2)}, u32[]{:S(2)}) collective-permute-start(bf16[1024,128]{1,0:T(8,128)(2,1)S(1)} %get-tuple-element.43), channel_id=1, source_target_pairs={{0,4},{1,5},{2,6},{3,7},{4,0},{5,1},{6,2},{7,3},{8,12},{9,13},{10,... | collective-permute-start | bytes 786440 | tf_op jit(solution)/shard_map/ppermute | solution.py:363
  21.4 0.5 %collective-permute-start.4 = (bf16[1024,128]{1,0:T(8,128)(2,1)S(1)}, bf16[1024,128]{1,0:T(8,128)(2,1)S(1)}, u32[]{:S(2)}, u32[]{:S(2)}) collective-permute-start(bf16[1024,128]{1,0:T(8,128)(2,1)S(1)} %get-tuple-element.41), channel_id=1, source_target_pairs={{0,2},{1,3},{2,0},{3,1},{4,8},{5,9},{6,10},{7,11},{8,4},{9,5},{10,... | collective-permute-start | bytes 786440 | tf_op jit(solution)/shard_map/ppermute | solution.py:363
  21.9 0.0 collective-permute-start.5
  21.9 0.0 copy-start
  21.9 0.0 copy-start.1
  21.9 0.0 copy-start.2
  21.9 0.0 copy-start.3
  22.0 0.0 copy-start.4
  22.0 0.0 copy-start.5
  22.0 3.6 %prep.1 = (f32[4096,128]{1,0:T(8,128)S(1)}, bf16[5120,128]{1,0:T(8,128)(2,1)S(1)}, bf16[2560,128]{1,0:T(8,128)(2,1)S(1)}, bf16[1280,128]{1,0:T(8,128)(2,1)S(1)},...) custom-call(s32[1]{0:T(128)} %bitcast.me_ref, ...), custom_call_target="tpu_custom_call" | custom-call | flops 4000000000 | bytes 7340032 | tf_op jit(solution)/shard_map/prep/pallas_call | solution.py:412
  25.6 0.9 %collective-permute-done.1.got_first = bf16[1024,128]{1,0:T(8,128)(2,1)S(1)} collective-permute-done((bf16[1024,128]{1,0:T(8,128)(2,1)S(1)}, bf16[1024,128]{1,0:T(8,128)(2,1)S(1)}, u32[]{:S(2)}, u32[]{:S(2)}) %collective-permute-start.1) | collective-permute-done | bytes 262176 | tf_op jit(solution)/shard_map/ppermute | solution.py:363
  26.5 1.5 %collective-permute-done.4.got_second = bf16[1024,128]{1,0:T(8,128)(2,1)S(1)} collective-permute-done((bf16[1024,128]{1,0:T(8,128)(2,1)S(1)}, bf16[1024,128]{1,0:T(8,128)(2,1)S(1)}, u32[]{:S(2)}, u32[]{:S(2)}) %collective-permute-start.4) | collective-permute-done | bytes 262176 | tf_op jit(solution)/shard_map/ppermute | solution.py:363
  28.0 0.0 collective-permute-done.5.got_third
  28.0 0.0 copy-done
  28.0 0.0 copy-done.1
  28.0 0.0 copy-done.2
  28.0 0.0 copy-done.3
  28.0 0.0 copy-done.4
  28.0 0.0 copy-done.5
  28.0 4.6 %far_down.1 = (bf16[4096,128]{1,0:T(8,128)(2,1)}, bf16[5120,128]{1,0:T(8,128)(2,1)S(1)}, bf16[2560,128]{1,0:T(8,128)(2,1)S(1)}, bf16[1280,128]{1,0:T(8,128)(2,1)S(1)}) custom-call(s32[1]{0:T(128)} %bitcast.me_ref, s32[16,16]{1,0:T(8,128)S(1)} %copy-done.3, s32[8,16]{1,0:T(8,128)S(1)} %copy-done.4, ...), custom_call_target="tpu_custom_call", output_to_operand_aliasing={{1}: (16, {}), {2}: (17, {}), {3}: (18, {})} | custom-call | tf_op jit(solution)/shard_map/far_down/pallas_call | solution.py:439
Async XLA Ops:
  2.2 15.1 %collective-permute-start = (bf16[2048,128]{1,0:T(8,128)(2,1)S(1)}, bf16[2048,128]{1,0:T(8,128)(2,1)S(1)}, u32[]{:S(2)}, u32[]{:S(2)}) collective-permute-start(bf16[2048,128]{1,0:T(8,128)(2,1)S(1)} %get-tuple-element.24), channel_id=1, source_target_pairs={{0,2},{1,3},{2,0},{3,1},{4,6},{5,7},{6,4},{7,5},{8,10},{9,11},{10,... | collective-permute-start | bytes 1572872 | tf_op jit(solution)/shard_map/ppermute | solution.py:363
  5.2 13.4 %collective-permute-start.2 = (bf16[2048,128]{1,0:T(8,128)(2,1)S(1)}, bf16[2048,128]{1,0:T(8,128)(2,1)S(1)}, u32[]{:S(2)}, u32[]{:S(2)}) collective-permute-start(bf16[2048,128]{1,0:T(8,128)(2,1)S(1)} %get-tuple-element.27.own_ref), channel_id=1, source_target_pairs={{0,4},{1,5},{2,6},{3,7},{4,0},{5,1},{6,2},{7,3},{8,12},{9,13},{10,... | collective-permute-start | bytes 1572872 | tf_op jit(solution)/shard_map/ppermute | solution.py:363
  6.8 11.8 %collective-permute-start.3 = (bf16[2048,128]{1,0:T(8,128)(2,1)S(1)}, bf16[2048,128]{1,0:T(8,128)(2,1)S(1)}, u32[]{:S(2)}, u32[]{:S(2)}) collective-permute-start(bf16[2048,128]{1,0:T(8,128)(2,1)S(1)} %get-tuple-element.27.own_ref), channel_id=1, source_target_pairs={{0,1},{1,0},{2,3},{3,2},{4,8},{5,9},{6,10},{7,11},{8,4},{9,5},{10,... | collective-permute-start | bytes 1572872 | tf_op jit(solution)/shard_map/ppermute | solution.py:363
  18.6 7.9 %collective-permute-start.1 = (bf16[1024,128]{1,0:T(8,128)(2,1)S(1)}, bf16[1024,128]{1,0:T(8,128)(2,1)S(1)}, u32[]{:S(2)}, u32[]{:S(2)}) collective-permute-start(bf16[1024,128]{1,0:T(8,128)(2,1)S(1)} %get-tuple-element.43), channel_id=1, source_target_pairs={{0,4},{1,5},{2,6},{3,7},{4,0},{5,1},{6,2},{7,3},{8,12},{9,13},{10,... | collective-permute-start | bytes 786440 | tf_op jit(solution)/shard_map/ppermute | solution.py:363
  21.4 6.6 %collective-permute-start.4 = (bf16[1024,128]{1,0:T(8,128)(2,1)S(1)}, bf16[1024,128]{1,0:T(8,128)(2,1)S(1)}, u32[]{:S(2)}, u32[]{:S(2)}) collective-permute-start(bf16[1024,128]{1,0:T(8,128)(2,1)S(1)} %get-tuple-element.41), channel_id=1, source_target_pairs={{0,2},{1,3},{2,0},{3,1},{4,8},{5,9},{6,10},{7,11},{8,4},{9,5},{10,... | collective-permute-start | bytes 786440 | tf_op jit(solution)/shard_map/ppermute | solution.py:363
  21.9 6.0 %collective-permute-start.5 = (bf16[1024,128]{1,0:T(8,128)(2,1)S(1)}, bf16[1024,128]{1,0:T(8,128)(2,1)S(1)}, u32[]{:S(2)}, u32[]{:S(2)}) collective-permute-start(bf16[1024,128]{1,0:T(8,128)(2,1)S(1)} %get-tuple-element.42), channel_id=1, source_target_pairs={{0,1},{1,0},{2,3},{3,2},{4,6},{5,7},{6,4},{7,5},{8,10},{9,11},{10,... | collective-permute-start | bytes 786440 | tf_op jit(solution)/shard_map/ppermute | solution.py:363
  21.9 6.0 %copy-start = (bf16[16,256,64]{1,2,0:T(8,128)(2,1)S(1)}, bf16[16,256,64]{1,2,0:T(8,128)(2,1)}, u32[]{:S(2)}) copy-start(bf16[16,256,64]{1,2,0:T(8,128)(2,1)} %param.15) | copy-start | bytes 1572868
  21.9 6.0 %copy-start.1 = (bf16[16,64,64]{2,1,0:T(8,128)(2,1)S(1)}, bf16[16,64,64]{2,1,0:T(8,128)(2,1)}, u32[]{:S(2)}) copy-start(bf16[16,64,64]{2,1,0:T(8,128)(2,1)} %up_one_ref.1) | copy-start | bytes 393220
  21.9 6.0 %copy-start.2 = (bf16[8,64,64]{2,1,0:T(8,128)(2,1)S(1)}, bf16[8,64,64]{2,1,0:T(8,128)(2,1)}, u32[]{:S(2)}) copy-start(bf16[8,64,64]{2,1,0:T(8,128)(2,1)} %up_two_ref.1) | copy-start | bytes 196612
  21.9 6.0 %copy-start.3 = (s32[16,16]{1,0:T(8,128)S(1)}, s32[16,16]{1,0:T(8,128)}, u32[]{:S(2)}) copy-start(s32[16,16]{1,0:T(8,128)} %zero_list.1) | copy-start | bytes 3076
  22.0 6.0 %copy-start.4 = (s32[8,16]{1,0:T(8,128)S(1)}, s32[8,16]{1,0:T(8,128)}, u32[]{:S(2)}) copy-start(s32[8,16]{1,0:T(8,128)} %one_list.1) | copy-start | bytes 1540
  22.0 6.0 %copy-start.5 = (s32[4,16]{1,0:T(4,128)S(1)}, s32[4,16]{1,0:T(4,128)}, u32[]{:S(2)}) copy-start(s32[4,16]{1,0:T(4,128)} %two_list.1) | copy-start | bytes 772

commit v14 on v13

--- a/solution.py
+++ b/solution.py
@@ -399,10 +399,10 @@
 
     split = leaves * rank
     from_pair, near = lax.optimization_barrier((from_pair, near))
-    low = from_pair[:split]
+    low = lax.optimization_barrier(from_pair[:split])
     got_first = send(low, turns[0])
-    first, second, near = lax.optimization_barrier((first, second, near))
-    upper = jnp.where((me[0] // 2 + me[0]) % 2 == 0, first[split:], second[split:])
+    second, first, low = lax.optimization_barrier((second, first, low))
+    upper = jnp.where((me[0] // 2 + me[0]) % 2 == 1, second[split:], first[split:])
     at_end = (me[0] < 2) | (me[0] >= size - 2)
     got_second = send(
         jnp.where(at_end, upper, low), lambda i: turns[1](i) if has_second(i) else partner(i)

time: 32.7 us -> 31.5 us (0.963)
  starting transfers between devices: 7.89 us -> 7.18 us
  waiting for transfers between devices: 3.7 us -> 3.09 us
    ppermute x6, starting transfers between devices: 7.89 us -> 7.18 us  [send(): return lax.ppermute(array, ('space', 'rhs'), pairs)]
    ppermute x6, waiting for transfers between devices: 3.7 us -> 3.09 us  [send(): return lax.ppermute(array, ('space', 'rhs'), pairs)]
  transfers between devices with their start and end apart: 6 -> 6, of which waited for: 3 -> 2; matrix products, arithmetic and copies ran while one was open for 0% -> 0% of each run, Pallas kernels for 43% -> 45%
where the time goes in v14:
time: 31.5 us; the launch traced here: 31.3 us
  Pallas kernels  20.8 us (66%)
  starting transfers between devices  7.18 us (23%)
  waiting for transfers between devices  3.09 us (10%)
    pallas_call x1, Pallas kernels, body(): pl.pallas_call(near_kernel, in_specs=[smem] + [hbm] * 3, out_specs=[vmem]...  10.5 us
    ppermute x6, starting transfers between devices, send(): return lax.ppermute(array, ('space', 'rhs'), pairs)  7.18 us
    pallas_call x1, Pallas kernels, body(): pl.pallas_call(functools.partial(far_kernel, size=size), in_specs=[smem]...  4.57 us
    pallas_call x1, Pallas kernels, body(): pl.pallas_call(prep_kernel, in_specs=[smem] + [vmem] * 6 + [hbm] * 3, out...  3.57 us
    ppermute x6, waiting for transfers between devices, send(): return lax.ppermute(array, ('space', 'rhs'), pairs)  3.09 us
    pallas_call x1, Pallas kernels, body(): pl.pallas_call(up_kernel, in_specs=[smem] + [hbm] * 4, out_specs=[vmem] *...  2.16 us
  transfers between devices with their start and end apart: 6, of which 2 were waited for; matrix products, arithmetic and copies ran while one was open for 0% of the time, Pallas kernels for 45%

profile of v14, /device:TPU:0, one launch (start us, length us, event | category | flops | bytes accessed | tf_op | source)
XLA Modules:
  0.0 31.3 jit_solution(10305252483324956160)
XLA Ops:
  0.0 2.2 %up_pass.1 = (bf16[2048,128]{1,0:T(8,128)(2,1)S(1)}, bf16[2048,128]{1,0:T(8,128)(2,1)S(1)}) custom-call(s32[1]{0:T(128)} %bitcast.me_ref, bf16[4096,128]{1,0:T(8,128)(2,1)} %x_hbm.3, bf16[16,64,256]{2,1,0:T(8,128)(2,1)} %bitcast.2, bf16[16,64,64]{2,1,0:T(8,128)(2,1)} %up_one_ref.1, bf16[8,64,64]{2,1,0:T(8,128)(2,1)} %up_two_ref.1), custom_call_target="tpu_custom_call" | custom-call | tf_op jit(solution)/shard_map/up_pass/pallas_call | solution.py:338
  2.2 3.0 %collective-permute-start = (bf16[2048,128]{1,0:T(8,128)(2,1)S(1)}, bf16[2048,128]{1,0:T(8,128)(2,1)S(1)}, u32[]{:S(2)}, u32[]{:S(2)}) collective-permute-start(bf16[2048,128]{1,0:T(8,128)(2,1)S(1)} %get-tuple-element.24), channel_id=1, source_target_pairs={{0,2},{1,3},{2,0},{3,1},{4,6},{5,7},{6,4},{7,5},{8,10},{9,11},{10,... | collective-permute-start | bytes 1572872 | tf_op jit(solution)/shard_map/ppermute | solution.py:363
  5.2 0.0 collective-permute-start.2
  5.2 3.2 %collective-permute-start.3 = (bf16[2048,128]{1,0:T(8,128)(2,1)S(1)}, bf16[2048,128]{1,0:T(8,128)(2,1)S(1)}, u32[]{:S(2)}, u32[]{:S(2)}) collective-permute-start(bf16[2048,128]{1,0:T(8,128)(2,1)S(1)} %get-tuple-element.27.own_ref), channel_id=1, source_target_pairs={{0,4},{1,5},{2,6},{3,7},{4,0},{5,1},{6,2},{7,3},{8,12},{9,13},{10,... | collective-permute-start | bytes 1572872 | tf_op jit(solution)/shard_map/ppermute | solution.py:363
  8.3 10.5 %near_own.1 = (f32[4096,128]{1,0:T(8,128)S(1)}, bf16[16,2,256,256]{3,2,1,0:T(8,128)(2,1)S(1)}, bf16[4096,128]{1,0:T(8,128)(2,1)S(1)}) custom-call(s32[1]{0:T(128)} %bitcast.me_ref, s32[16,12]{1,0:T(8,128)} %list_hbm.1, bf16[4096,128]{1,0:T(8,128)(2,1)} %x_hbm.3, bf16[16,12,256,256]{3,2,1,0:T(8,128)(2,1)} %blocks_hbm.1), custom_call_target="tpu_custom_call" | custom-call | flops 2684354560 | bytes 28311552 | tf_op jit(solution)/shard_map/near_own/pallas_call | solution.py:372
  18.8 0.0 collective-permute-done.pair_ref
  18.9 0.1 collective-permute-start.1
  19.0 0.0 collective-permute-done.2.second_ref
  19.0 0.7 %collective-permute-done.3.first_ref = bf16[2048,128]{1,0:T(8,128)(2,1)S(1)} collective-permute-done((bf16[2048,128]{1,0:T(8,128)(2,1)S(1)}, bf16[2048,128]{1,0:T(8,128)(2,1)S(1)}, u32[]{:S(2)}, u32[]{:S(2)}) %collective-permute-start.3) | collective-permute-done | bytes 524320 | tf_op jit(solution)/shard_map/ppermute | solution.py:363
  19.7 0.1 broadcast_select_fusion
  19.8 0.9 %collective-permute-start.4 = (bf16[1024,128]{1,0:T(8,128)(2,1)S(1)}, bf16[1024,128]{1,0:T(8,128)(2,1)S(1)}, u32[]{:S(2)}, u32[]{:S(2)}) collective-permute-start(bf16[1024,128]{1,0:T(8,128)(2,1)S(1)} %get-tuple-element.41), channel_id=1, source_target_pairs={{0,2},{1,3},{2,0},{3,1},{4,8},{5,9},{6,10},{7,11},{8,4},{9,5},{10,... | collective-permute-start | bytes 786440 | tf_op jit(solution)/shard_map/ppermute | solution.py:363
  20.6 0.0 collective-permute-start.5
  20.6 0.0 copy-start
  20.7 0.0 copy-start.1
  20.7 0.0 copy-start.2
  20.7 0.0 copy-start.3
  20.7 0.0 copy-start.4
  20.7 0.0 copy-start.5
  20.7 3.6 %prep.1 = (f32[4096,128]{1,0:T(8,128)S(1)}, bf16[5120,128]{1,0:T(8,128)(2,1)S(1)}, bf16[2560,128]{1,0:T(8,128)(2,1)S(1)}, bf16[1280,128]{1,0:T(8,128)(2,1)S(1)},...) custom-call(s32[1]{0:T(128)} %bitcast.me_ref, ...), custom_call_target="tpu_custom_call" | custom-call | flops 4000000000 | bytes 7340032 | tf_op jit(solution)/shard_map/prep/pallas_call | solution.py:412
  24.3 2.4 %collective-permute-done.4.got_second = bf16[1024,128]{1,0:T(8,128)(2,1)S(1)} collective-permute-done((bf16[1024,128]{1,0:T(8,128)(2,1)S(1)}, bf16[1024,128]{1,0:T(8,128)(2,1)S(1)}, u32[]{:S(2)}, u32[]{:S(2)}) %collective-permute-start.4) | collective-permute-done | bytes 262176 | tf_op jit(solution)/shard_map/ppermute | solution.py:363
  26.7 0.0 collective-permute-done.5.got_third
  26.7 0.0 collective-permute-done.1.got_first
  26.7 0.0 copy-done
  26.7 0.0 copy-done.1
  26.7 0.0 copy-done.2
  26.7 0.0 copy-done.3
  26.7 0.0 copy-done.4
  26.7 0.0 copy-done.5
  26.7 4.6 %far_down.1 = (bf16[4096,128]{1,0:T(8,128)(2,1)}, bf16[5120,128]{1,0:T(8,128)(2,1)S(1)}, bf16[2560,128]{1,0:T(8,128)(2,1)S(1)}, bf16[1280,128]{1,0:T(8,128)(2,1)S(1)}) custom-call(s32[1]{0:T(128)} %bitcast.me_ref, s32[16,16]{1,0:T(8,128)S(1)} %copy-done.3, s32[8,16]{1,0:T(8,128)S(1)} %copy-done.4, ...), custom_call_target="tpu_custom_call", output_to_operand_aliasing={{1}: (16, {}), {2}: (17, {}), {3}: (18, {})} | custom-call | tf_op jit(solution)/shard_map/far_down/pallas_call | solution.py:439
  (1 shorter events, 0.0 us)
Async XLA Ops:
  2.2 16.7 %collective-permute-start = (bf16[2048,128]{1,0:T(8,128)(2,1)S(1)}, bf16[2048,128]{1,0:T(8,128)(2,1)S(1)}, u32[]{:S(2)}, u32[]{:S(2)}) collective-permute-start(bf16[2048,128]{1,0:T(8,128)(2,1)S(1)} %get-tuple-element.24), channel_id=1, source_target_pairs={{0,2},{1,3},{2,0},{3,1},{4,6},{5,7},{6,4},{7,5},{8,10},{9,11},{10,... | collective-permute-start | bytes 1572872 | tf_op jit(solution)/shard_map/ppermute | solution.py:363
  5.2 13.8 %collective-permute-start.2 = (bf16[2048,128]{1,0:T(8,128)(2,1)S(1)}, bf16[2048,128]{1,0:T(8,128)(2,1)S(1)}, u32[]{:S(2)}, u32[]{:S(2)}) collective-permute-start(bf16[2048,128]{1,0:T(8,128)(2,1)S(1)} %get-tuple-element.27.own_ref), channel_id=1, source_target_pairs={{0,1},{1,0},{2,3},{3,2},{4,8},{5,9},{6,10},{7,11},{8,4},{9,5},{10,... | collective-permute-start | bytes 1572872 | tf_op jit(solution)/shard_map/ppermute | solution.py:363
  5.2 14.5 %collective-permute-start.3 = (bf16[2048,128]{1,0:T(8,128)(2,1)S(1)}, bf16[2048,128]{1,0:T(8,128)(2,1)S(1)}, u32[]{:S(2)}, u32[]{:S(2)}) collective-permute-start(bf16[2048,128]{1,0:T(8,128)(2,1)S(1)} %get-tuple-element.27.own_ref), channel_id=1, source_target_pairs={{0,4},{1,5},{2,6},{3,7},{4,0},{5,1},{6,2},{7,3},{8,12},{9,13},{10,... | collective-permute-start | bytes 1572872 | tf_op jit(solution)/shard_map/ppermute | solution.py:363
  18.9 7.8 %collective-permute-start.1 = (bf16[1024,128]{1,0:T(8,128)(2,1)S(1)}, bf16[1024,128]{1,0:T(8,128)(2,1)S(1)}, u32[]{:S(2)}, u32[]{:S(2)}) collective-permute-start(bf16[1024,128]{1,0:T(8,128)(2,1)S(1)} %slice.9), channel_id=1, source_target_pairs={{0,4},{1,5},{2,6},{3,7},{4,0},{5,1},{6,2},{7,3},{8,12},{9,13},{10,... | collective-permute-start | bytes 786440 | tf_op jit(solution)/shard_map/ppermute | solution.py:363
  19.8 6.9 %collective-permute-start.4 = (bf16[1024,128]{1,0:T(8,128)(2,1)S(1)}, bf16[1024,128]{1,0:T(8,128)(2,1)S(1)}, u32[]{:S(2)}, u32[]{:S(2)}) collective-permute-start(bf16[1024,128]{1,0:T(8,128)(2,1)S(1)} %get-tuple-element.41), channel_id=1, source_target_pairs={{0,2},{1,3},{2,0},{3,1},{4,8},{5,9},{6,10},{7,11},{8,4},{9,5},{10,... | collective-permute-start | bytes 786440 | tf_op jit(solution)/shard_map/ppermute | solution.py:363
  20.6 6.0 %collective-permute-start.5 = (bf16[1024,128]{1,0:T(8,128)(2,1)S(1)}, bf16[1024,128]{1,0:T(8,128)(2,1)S(1)}, u32[]{:S(2)}, u32[]{:S(2)}) collective-permute-start(bf16[1024,128]{1,0:T(8,128)(2,1)S(1)} %get-tuple-element.42), channel_id=1, source_target_pairs={{0,1},{1,0},{2,3},{3,2},{4,6},{5,7},{6,4},{7,5},{8,10},{9,11},{10,... | collective-permute-start | bytes 786440 | tf_op jit(solution)/shard_map/ppermute | solution.py:363
  20.6 6.0 %copy-start = (bf16[16,256,64]{1,2,0:T(8,128)(2,1)S(1)}, bf16[16,256,64]{1,2,0:T(8,128)(2,1)}, u32[]{:S(2)}) copy-start(bf16[16,256,64]{1,2,0:T(8,128)(2,1)} %param.15) | copy-start | bytes 1572868
  20.7 6.0 %copy-start.1 = (bf16[16,64,64]{2,1,0:T(8,128)(2,1)S(1)}, bf16[16,64,64]{2,1,0:T(8,128)(2,1)}, u32[]{:S(2)}) copy-start(bf16[16,64,64]{2,1,0:T(8,128)(2,1)} %up_one_ref.1) | copy-start | bytes 393220
  20.7 6.1 %copy-start.2 = (bf16[8,64,64]{2,1,0:T(8,128)(2,1)S(1)}, bf16[8,64,64]{2,1,0:T(8,128)(2,1)}, u32[]{:S(2)}) copy-start(bf16[8,64,64]{2,1,0:T(8,128)(2,1)} %up_two_ref.1) | copy-start | bytes 196612
  20.7 6.1 %copy-start.3 = (s32[16,16]{1,0:T(8,128)S(1)}, s32[16,16]{1,0:T(8,128)}, u32[]{:S(2)}) copy-start(s32[16,16]{1,0:T(8,128)} %zero_list.1) | copy-start | bytes 3076
  20.7 6.1 %copy-start.4 = (s32[8,16]{1,0:T(8,128)S(1)}, s32[8,16]{1,0:T(8,128)}, u32[]{:S(2)}) copy-start(s32[8,16]{1,0:T(8,128)} %one_list.1) | copy-start | bytes 1540
  20.7 6.0 %copy-start.5 = (s32[4,16]{1,0:T(4,128)S(1)}, s32[4,16]{1,0:T(4,128)}, u32[]{:S(2)}) copy-start(s32[4,16]{1,0:T(4,128)} %two_list.1) | copy-start | bytes 772

commit v15 on v14

--- a/solution.py
+++ b/solution.py
@@ -78,12 +78,19 @@
     plain_ref[end, :] = x_ref[pl.ds(pl.multiple_of(odd * last, LEAF), LEAF), :]
 
 
+def last_place(me):
+    return REACH - 1 + 2 * lax.rem(me, 2)
+
+
 def near_kernel(
-    me_ref, list_hbm, x_hbm, blocks_hbm, out_ref, edge_ref, x_ref,
-    list_ref, block_buf, sems, x_sems, list_sem,
+    me_ref, near_hbm, zero_hbm, one_hbm, two_hbm, x_hbm, blocks_hbm,
+    out_ref, edge_ref, x_ref, starts_ref, turns_ref,
+    list_ref, zero_list, one_list, two_list, block_buf, sems, x_sems, list_sems,
 ):
     leaves, nears = list_ref.shape
-    first = me_ref[0] * leaves
+    ones, twos = one_list.shape[0], two_list.shape[0]
+    me = me_ref[0]
+    first = me * leaves
     depth = block_buf.shape[0]
 
     def copies(pair, slot):
@@ -97,8 +104,14 @@
             pltpu.make_async_copy(src, dst, sems.at[slot, i]) for i, (src, dst) in enumerate(pairs)
         ]
 
-    list_copy = pltpu.make_async_copy(list_hbm, list_ref, list_sem)
-    list_copy.start()
+    hbms = (near_hbm, zero_hbm, one_hbm, two_hbm)
+    lists = (list_ref, zero_list, one_list, two_list)
+    list_copies = [
+        pltpu.make_async_copy(src, dst, list_sems.at[i])
+        for i, (src, dst) in enumerate(zip(hbms, lists))
+    ]
+    for copy in list_copies:
+        copy.start()
     x_copies = []
     for q in range(leaves // 4):
         rows = pl.ds(q * 4 * LEAF, 4 * LEAF)
@@ -110,11 +123,32 @@
     for pair in range(depth - 1):
         for copy in copies(pair, pair):
             copy.start()
-    list_copy.wait()
+    for copy in list_copies:
+        copy.wait()
+
+    def order(where, node, row):
+        per, fars = where.shape
+        base = (me - REACH) * per
+        low = last_place(me) * per
+        count = jnp.int32(0)
+        for k in range(fars):
+            index = where[node, k] - base
+            late = (index >= low) & (index < low + per)
+            at = jnp.where(late, count, fars - 1 - k + count)
+            starts_ref[row, at] = index
+            turns_ref[row, at] = k
+            count = count + late.astype(jnp.int32)
+        return count
+
+    most = jnp.int32(0)
+    for p in range(ones):
+        most = jnp.maximum(most, order(one_list, p, leaves + p))
+    for q in range(twos):
+        most = jnp.maximum(most, order(two_list, q, leaves + ones + q))
     for copy in x_copies:
         copy.wait()
 
-    def step(pair, carry):
+    def step(pair, most):
         slot = lax.rem(pair, depth)
 
         @pl.when(pair + depth - 1 < leaves // 2)
@@ -134,9 +168,12 @@
             totals.append(dot(jnp.concatenate(blocks, axis=1), jnp.concatenate(rows, axis=0)))
         here = pl.ds(pl.multiple_of(pair * 2 * LEAF, 2 * LEAF), 2 * LEAF)
         out_ref[here, :] = jnp.concatenate(totals, axis=0)
-        return carry
-
-    lax.fori_loop(0, leaves // 2, step, 0)
+        for side in range(2):
+            leaf = 2 * pair + side
+            most = jnp.maximum(most, order(zero_list, leaf, leaf))
+        return most
+
+    starts_ref[leaves + ones + twos, 0] = lax.fori_loop(0, leaves // 2, step, most)
 
 
 def add_edge(sum_ref, near_ref, edge_ref, side, rows):
@@ -156,24 +193,35 @@
     return copies
 
 
+def field(wide, starts_ref, row, win, slots):
+    rank = wide.shape[0]
+    rows = []
+    for k in slots:
+        rows.append(win[pl.ds(pl.multiple_of(starts_ref[row, k] * rank, rank), rank), :])
+    some = wide[:, slots[0] * rank : (slots[-1] + 1) * rank]
+    return dot(some, jnp.concatenate(rows, axis=0))
+
+
 def prep_kernel(
-    me_ref, own_ref, pair_ref, first_ref, second_ref, near_ref, edge_ref,
+    me_ref, starts_ref, turns_ref, own_ref, pair_ref, first_ref, second_ref, near_ref, edge_ref,
     zero_hbm, one_hbm, two_hbm,
-    sum_ref, zero_win, one_win, two_win, zero_wide, one_wide, two_wide,
+    sum_ref, zero_win, one_win, two_win, zero_wide, one_wide, two_wide, part_ref,
     zero_buf, one_buf, two_buf, sems, win_sems,
 ):
+    leaves, fars, rank = zero_buf.shape[:3]
+    base = leaves + one_buf.shape[0]
     levels = (
-        (two_hbm, two_buf, two_wide),
-        (one_hbm, one_buf, one_wide),
-        (zero_hbm, zero_buf, zero_wide),
+        (two_hbm, two_buf, two_wide, two_win, base),
+        (one_hbm, one_buf, one_wide, one_win, leaves),
+        (zero_hbm, zero_buf, zero_wide, zero_win, 0),
     )
     chunks = []
-    for hbm, buf, wide in levels:
+    for hbm, buf, wide, _, row in levels:
         for first in range(0, buf.shape[0], 4):
             some = pl.ds(first, 4)
             copy = pltpu.make_async_copy(hbm.at[some], buf.at[some], sems.at[len(chunks)])
             copy.start()
-            chunks.append((copy, buf, wide, first))
+            chunks.append((copy, buf, wide, first, row))
     me = me_ref[0]
     odd = lax.rem(me, 2)
     block = lax.rem(me // 2, 2)
@@ -193,19 +241,23 @@
     for move in moves:
         move.start()
     add_edge(sum_ref, near_ref, edge_ref, odd, pair_ref[pl.ds(pair_ref.shape[0] - LEAF, LEAF), :])
-    for copy, buf, wide, first in chunks:
+    for copy, buf, wide, first, row in chunks:
         copy.wait()
         for node in range(first, first + 4):
-            fars = buf.shape[1]
-            wide[node] = jnp.concatenate([buf[node, k] for k in range(fars)], axis=1)
+            picked = [buf[node, turns_ref[row + node, k]] for k in range(fars)]
+            wide[node] = jnp.concatenate(picked, axis=1)
     for move in moves:
         move.wait()
+    for _, _, wide, win, row in levels:
+        for node in range(wide.shape[0]):
+            part = field(wide.at[node], starts_ref, row + node, win, range(fars // 2, fars))
+            part_ref[pl.ds((row + node) * rank, rank), :] = part
 
 
 def far_kernel(
-    me_ref, zero_list, one_list, two_list, x_ref, got_first, got_second, got_third, near_ref,
-    edge_ref, basis_ref, up_one_ref, up_two_ref, zero_wide, one_wide, two_wide, zero_in, one_in, two_in,
-    out_hbm, zero_win, one_win, two_win,
+    me_ref, starts_ref, x_ref, got_first, got_second, got_third, near_ref,
+    edge_ref, basis_ref, up_one_ref, up_two_ref, zero_wide, one_wide, two_wide, part_ref,
+    zero_in, one_in, two_in, out_hbm, zero_win, one_win, two_win,
     sum_buf, out_buf, rows_buf, field_buf, down_buf, win_sems, out_sems, *, size,
 ):
     del zero_in, one_in, two_in
@@ -214,7 +266,7 @@
     fars = deep // rank
     me = me_ref[0]
     odd = lax.rem(me, 2)
-    place = REACH - 1 + 2 * odd
+    place = last_place(me)
     sizes = [n * rank for n in (leaves, ones, twos)]
     at = [pl.multiple_of(place * n, n) for n in sizes]
 
@@ -262,19 +314,25 @@
         return pl.ds(row * rank, rank)
 
     base = leaves + ones
-    levels = (
-        (two_wide, two_list, two_win, base),
-        (one_wide, one_list, one_win, leaves),
-        (zero_wide, zero_list, zero_win, 0),
-    )
-    for wide, where, win, row in levels:
-        first = (me - REACH) * wide.shape[0]
+    half = fars // 2
+    levels = ((two_wide, two_win, base), (one_wide, one_win, leaves), (zero_wide, zero_win, 0))
+    for wide, win, row in levels:
         for node in range(wide.shape[0]):
-            picked = []
-            for k in range(fars):
-                start = pl.multiple_of((where[node, k] - first) * rank, rank)
-                picked.append(win[pl.ds(start, rank), :])
-            field_buf[node_rows(row + node), :] = dot(wide[node], jnp.concatenate(picked, axis=0))
+            part = field(wide.at[node], starts_ref, row + node, win, range(half))
+            rows = node_rows(row + node)
+            field_buf[rows, :] = part_ref[rows, :] + part
+
+    @pl.when(starts_ref[base + twos, 0] > half)
+    def _():
+        for wide, win, row in levels:
+
+            def again(node, carry):
+                part = field(wide.at[node], starts_ref, row + node, win, range(fars))
+                field_buf[pl.ds(pl.multiple_of((row + node) * rank, rank), rank), :] = part
+                return carry
+
+            lax.fori_loop(0, wide.shape[0], again, 0)
+
     for q in range(twos):
         down_buf[node_rows(base + q), :] = field_buf[node_rows(base + q), :].astype(jnp.bfloat16)
     for p in range(ones):
@@ -369,21 +427,23 @@
     turns = (lambda i: i + 2 - i // 2 % 2 * 4, lambda i: i - 2 + i // 2 % 2 * 4)
     first, second = [send(plain, turn) for turn in turns]
 
-    near, edge, points = pl.pallas_call(
+    near, edge, points, starts, turns_taken = pl.pallas_call(
         near_kernel,
-        in_specs=[smem] + [hbm] * 3,
-        out_specs=[vmem] * 3,
+        in_specs=[smem] + [hbm] * 6,
+        out_specs=[vmem] * 3 + [smem] * 2,
         out_shape=[
             pltpu.VMEM(vectors.shape, f32),
             pltpu.VMEM((leaves, 2, LEAF, LEAF), bf16),
             pltpu.VMEM(vectors.shape, bf16),
+            jax.ShapeDtypeStruct((nodes + 1, fars), jnp.int32),
+            jax.ShapeDtypeStruct((nodes + 1, fars), jnp.int32),
         ],
         scratch_shapes=[
-            pltpu.SMEM(near_list.shape, jnp.int32),
+            *[pltpu.SMEM(a.shape, jnp.int32) for a in (near_list, far_zero, far_one, far_two)],
             pltpu.VMEM((DEPTH, 2, nears - 2, LEAF, LEAF), bf16),
             pltpu.SemaphoreType.DMA((DEPTH, 3)),
             pltpu.SemaphoreType.DMA((leaves // 4,)),
-            pltpu.SemaphoreType.DMA,
+            pltpu.SemaphoreType.DMA((4,)),
         ],
         compiler_params=pltpu.CompilerParams(vmem_limit_bytes=16 * MIB),
         cost_estimate=pl.CostEstimate(
@@ -392,7 +452,7 @@
             transcendentals=0,
         ),
         name="near_own",
-    )(me, *in_hbm(near_list, vectors, near_blocks))
+    )(me, *in_hbm(near_list, far_zero, far_one, far_two, vectors, near_blocks))
 
     def has_second(i):
         return 0 <= turns[1](i) < size
@@ -409,14 +469,15 @@
     )
     got_third = send(upper, lambda i: partner(i) if has_second(i) else -1)
 
-    sums, *rest = pl.pallas_call(
+    sums, *rest, part = pl.pallas_call(
         prep_kernel,
-        in_specs=[smem] + [vmem] * 6 + [hbm] * 3,
-        out_specs=[vmem] * 7,
+        in_specs=[smem] * 3 + [vmem] * 6 + [hbm] * 3,
+        out_specs=[vmem] * 8,
         out_shape=[
             pltpu.VMEM(vectors.shape, f32),
             *[pltpu.VMEM((SPAN * n * rank, columns), bf16) for n in counts],
             *[pltpu.VMEM((n, rank, fars * rank), bf16) for n in counts],
+            pltpu.VMEM((nodes * rank, columns), f32),
         ],
         scratch_shapes=[
             *[pltpu.VMEM((n, fars, rank, rank), bf16) for n in counts],
@@ -431,20 +492,20 @@
         ),
         name="prep",
     )(
-        me, plain, from_pair, first, second, near, edge,
+        me, starts, turns_taken, plain, from_pair, first, second, near, edge,
         *in_hbm(couple_zero, couple_one, couple_two),
     )
     windows, wides = rest[:3], rest[3:]
 
     out, *_ = pl.pallas_call(
         functools.partial(far_kernel, size=size),
-        in_specs=[smem] * 4 + [vmem] * 15,
+        in_specs=[smem] * 2 + [vmem] * 16,
         out_specs=[hbm] + [vmem] * 3,
         out_shape=[
             jax.ShapeDtypeStruct(vectors.shape, bf16),
             *[pltpu.VMEM((SPAN * n * rank, columns), bf16) for n in counts],
         ],
-        input_output_aliases={16: 1, 17: 2, 18: 3},
+        input_output_aliases={15: 1, 16: 2, 17: 3},
         scratch_shapes=[
             pltpu.VMEM(vectors.shape, f32),
             pltpu.VMEM(vectors.shape, bf16),
@@ -457,8 +518,8 @@
         compiler_params=pltpu.CompilerParams(vmem_limit_bytes=16 * MIB),
         name="far_down",
     )(
-        me, far_zero, far_one, far_two, points, got_first, got_second, got_third, sums, edge,
-        basis_t, up_one, up_two, *wides, *windows,
+        me, starts, points, got_first, got_second, got_third, sums, edge,
+        basis_t, up_one, up_two, *wides, part, *windows,
     )
     return out
 

time: 31.5 us -> 31.6 us (level)
  Pallas kernels: 20.8 us -> 23.1 us
  waiting for transfers between devices: 3.09 us -> 1.34 us
    pallas_call x2, Pallas kernels: 14.1 us -> 16.7 us  [the longest x1 11.5 us: body(): pl.pallas_call(near_kernel, in_specs=[smem] + [hbm] * 6, out_specs=[vmem]...]
    ppermute x6, waiting for transfers between devices: 3.09 us -> 1.34 us  [send(): return lax.ppermute(array, ('space', 'rhs'), pairs)]
    pallas_call x1, Pallas kernels: 4.57 us -> 4.18 us  [body(): pl.pallas_call(functools.partial(far_kernel, size=size), in_specs=[smem]...]
  transfers between devices with their start and end apart: 6 -> 6, of which waited for: 2 -> 1; matrix products, arithmetic and copies ran while one was open for 0% -> 0% of each run, Pallas kernels for 45% -> 53%
where the time goes in v15:
time: 31.6 us; the launch traced here: 31.5 us
  Pallas kernels  23.1 us (73%)
  starting transfers between devices  6.87 us (22%)
  waiting for transfers between devices  1.34 us (4%)
    pallas_call x1, Pallas kernels, body(): pl.pallas_call(near_kernel, in_specs=[smem] + [hbm] * 6, out_specs=[vmem]...  11.5 us
    ppermute x6, starting transfers between devices, send(): return lax.ppermute(array, ('space', 'rhs'), pairs)  6.87 us
    pallas_call x1, Pallas kernels, body(): pl.pallas_call(prep_kernel, in_specs=[smem] * 3 + [vmem] * 6 + [hbm] * 3,...  5.27 us
    pallas_call x1, Pallas kernels, body(): pl.pallas_call(functools.partial(far_kernel, size=size), in_specs=[smem]...  4.18 us
    pallas_call x1, Pallas kernels, body(): pl.pallas_call(up_kernel, in_specs=[smem] + [hbm] * 4, out_specs=[vmem] *...  2.16 us
    ppermute x6, waiting for transfers between devices, send(): return lax.ppermute(array, ('space', 'rhs'), pairs)  1.34 us
  transfers between devices with their start and end apart: 6, of which 1 were waited for; matrix products, arithmetic and copies ran while one was open for 0% of the time, Pallas kernels for 53%

profile of v15, /device:TPU:0, one launch (start us, length us, event | category | flops | bytes accessed | tf_op | source)
XLA Modules:
  0.0 31.5 jit_solution(3947195927140012977)
XLA Ops:
  0.0 2.2 %up_pass.1 = (bf16[2048,128]{1,0:T(8,128)(2,1)S(1)}, bf16[2048,128]{1,0:T(8,128)(2,1)S(1)}) custom-call(s32[1]{0:T(128)} %bitcast.me_ref, bf16[4096,128]{1,0:T(8,128)(2,1)} %x_hbm.3, bf16[16,64,256]{2,1,0:T(8,128)(2,1)} %bitcast.2, bf16[16,64,64]{2,1,0:T(8,128)(2,1)} %up_one_ref.1, bf16[8,64,64]{2,1,0:T(8,128)(2,1)} %up_two_ref.1), custom_call_target="tpu_custom_call" | custom-call | tf_op jit(solution)/shard_map/up_pass/pallas_call | solution.py:396
  2.2 3.0 %collective-permute-start = (bf16[2048,128]{1,0:T(8,128)(2,1)S(1)}, bf16[2048,128]{1,0:T(8,128)(2,1)S(1)}, u32[]{:S(2)}, u32[]{:S(2)}) collective-permute-start(bf16[2048,128]{1,0:T(8,128)(2,1)S(1)} %get-tuple-element.28), channel_id=1, source_target_pairs={{0,2},{1,3},{2,0},{3,1},{4,6},{5,7},{6,4},{7,5},{8,10},{9,11},{10,... | collective-permute-start | bytes 1572872 | tf_op jit(solution)/shard_map/ppermute | solution.py:421
  5.2 0.0 collective-permute-start.2
  5.2 3.2 %collective-permute-start.3 = (bf16[2048,128]{1,0:T(8,128)(2,1)S(1)}, bf16[2048,128]{1,0:T(8,128)(2,1)S(1)}, u32[]{:S(2)}, u32[]{:S(2)}) collective-permute-start(bf16[2048,128]{1,0:T(8,128)(2,1)S(1)} %get-tuple-element.31.own_ref), channel_id=1, source_target_pairs={{0,4},{1,5},{2,6},{3,7},{4,0},{5,1},{6,2},{7,3},{8,12},{9,13},{10,... | collective-permute-start | bytes 1572872 | tf_op jit(solution)/shard_map/ppermute | solution.py:421
  8.3 11.5 %near_own.1 = (f32[4096,128]{1,0:T(8,128)S(1)}, bf16[16,2,256,256]{3,2,1,0:T(8,128)(2,1)S(1)}, bf16[4096,128]{1,0:T(8,128)(2,1)S(1)}, s32[29,16]{1,0:T(8,128)S(1)}, s32[29,16]{1,0:T(8,128)S(1)}) custom-call(s32[1]{0:T(128)} %bitcast.me_ref, s32[16,12]{1,0:T(8,128)} %near_hbm.1, s32[16,16]{1,0:T(8,128)} %zero_hbm.2, s32[8,16]{1,0:T(8,128)} %one_hbm.2, ...), custom_call_target="tpu_custom_call" | custom-call | flops 2684354560 | bytes 28311552 | tf_op jit(solution)/shard_map/near_own/pallas_call | solution.py:430
  19.8 0.0 collective-permute-done.pair_ref
  19.8 0.1 collective-permute-start.1
  19.9 0.0 collective-permute-done.2.second_ref
  19.9 0.0 collective-permute-done.3.first_ref
  19.9 0.1 broadcast_select_fusion
  20.0 0.6 %collective-permute-start.4 = (bf16[1024,128]{1,0:T(8,128)(2,1)S(1)}, bf16[1024,128]{1,0:T(8,128)(2,1)S(1)}, u32[]{:S(2)}, u32[]{:S(2)}) collective-permute-start(bf16[1024,128]{1,0:T(8,128)(2,1)S(1)} %get-tuple-element.47), channel_id=1, source_target_pairs={{0,2},{1,3},{2,0},{3,1},{4,8},{5,9},{6,10},{7,11},{8,4},{9,5},{10,... | collective-permute-start | bytes 786440 | tf_op jit(solution)/shard_map/ppermute | solution.py:421
  20.6 0.0 collective-permute-start.5
  20.6 0.0 copy-start
  20.7 0.0 copy-start.1
  20.7 0.0 copy-start.2
  20.7 5.3 %prep.1 = (f32[4096,128]{1,0:T(8,128)S(1)}, bf16[5120,128]{1,0:T(8,128)(2,1)S(1)}, bf16[2560,128]{1,0:T(8,128)(2,1)S(1)}, bf16[1280,128]{1,0:T(8,128)(2,1)S(1)},...) custom-call(s32[1]{0:T(128)} %bitcast.me_ref, ...), custom_call_target="tpu_custom_call" | custom-call | flops 4000000000 | bytes 7340032 | tf_op jit(solution)/shard_map/prep/pallas_call | solution.py:472
  25.9 1.3 %collective-permute-done.4.got_second = bf16[1024,128]{1,0:T(8,128)(2,1)S(1)} collective-permute-done((bf16[1024,128]{1,0:T(8,128)(2,1)S(1)}, bf16[1024,128]{1,0:T(8,128)(2,1)S(1)}, u32[]{:S(2)}, u32[]{:S(2)}) %collective-permute-start.4) | collective-permute-done | bytes 262176 | tf_op jit(solution)/shard_map/ppermute | solution.py:421
  27.3 0.0 collective-permute-done.5.got_third
  27.3 0.0 collective-permute-done.1.got_first
  27.3 0.0 copy-done
  27.3 0.0 copy-done.1
  27.3 0.0 copy-done.2
  27.3 4.2 %far_down.1 = (bf16[4096,128]{1,0:T(8,128)(2,1)}, bf16[5120,128]{1,0:T(8,128)(2,1)S(1)}, bf16[2560,128]{1,0:T(8,128)(2,1)S(1)}, bf16[1280,128]{1,0:T(8,128)(2,1)S(1)}) custom-call(s32[1]{0:T(128)} %bitcast.me_ref, s32[29,16]{1,0:T(8,128)S(1)} %get-tuple-element.26.starts_ref, ...), custom_call_target="tpu_custom_call", output_to_operand_aliasing={{1}: (15, {}), {2}: (16, {}), {3}: (17, {})} | custom-call | tf_op jit(solution)/shard_map/far_down/pallas_call | solution.py:500
  (1 shorter events, 0.0 us)
Async XLA Ops:
  2.2 17.6 %collective-permute-start = (bf16[2048,128]{1,0:T(8,128)(2,1)S(1)}, bf16[2048,128]{1,0:T(8,128)(2,1)S(1)}, u32[]{:S(2)}, u32[]{:S(2)}) collective-permute-start(bf16[2048,128]{1,0:T(8,128)(2,1)S(1)} %get-tuple-element.28), channel_id=1, source_target_pairs={{0,2},{1,3},{2,0},{3,1},{4,6},{5,7},{6,4},{7,5},{8,10},{9,11},{10,... | collective-permute-start | bytes 1572872 | tf_op jit(solution)/shard_map/ppermute | solution.py:421
  5.2 14.7 %collective-permute-start.2 = (bf16[2048,128]{1,0:T(8,128)(2,1)S(1)}, bf16[2048,128]{1,0:T(8,128)(2,1)S(1)}, u32[]{:S(2)}, u32[]{:S(2)}) collective-permute-start(bf16[2048,128]{1,0:T(8,128)(2,1)S(1)} %get-tuple-element.31.own_ref), channel_id=1, source_target_pairs={{0,1},{1,0},{2,3},{3,2},{4,8},{5,9},{6,10},{7,11},{8,4},{9,5},{10,... | collective-permute-start | bytes 1572872 | tf_op jit(solution)/shard_map/ppermute | solution.py:421
  5.2 14.7 %collective-permute-start.3 = (bf16[2048,128]{1,0:T(8,128)(2,1)S(1)}, bf16[2048,128]{1,0:T(8,128)(2,1)S(1)}, u32[]{:S(2)}, u32[]{:S(2)}) collective-permute-start(bf16[2048,128]{1,0:T(8,128)(2,1)S(1)} %get-tuple-element.31.own_ref), channel_id=1, source_target_pairs={{0,4},{1,5},{2,6},{3,7},{4,0},{5,1},{6,2},{7,3},{8,12},{9,13},{10,... | collective-permute-start | bytes 1572872 | tf_op jit(solution)/shard_map/ppermute | solution.py:421
  19.8 7.5 %collective-permute-start.1 = (bf16[1024,128]{1,0:T(8,128)(2,1)S(1)}, bf16[1024,128]{1,0:T(8,128)(2,1)S(1)}, u32[]{:S(2)}, u32[]{:S(2)}) collective-permute-start(bf16[1024,128]{1,0:T(8,128)(2,1)S(1)} %slice.9), channel_id=1, source_target_pairs={{0,4},{1,5},{2,6},{3,7},{4,0},{5,1},{6,2},{7,3},{8,12},{9,13},{10,... | collective-permute-start | bytes 786440 | tf_op jit(solution)/shard_map/ppermute | solution.py:421
  20.0 7.3 %collective-permute-start.4 = (bf16[1024,128]{1,0:T(8,128)(2,1)S(1)}, bf16[1024,128]{1,0:T(8,128)(2,1)S(1)}, u32[]{:S(2)}, u32[]{:S(2)}) collective-permute-start(bf16[1024,128]{1,0:T(8,128)(2,1)S(1)} %get-tuple-element.47), channel_id=1, source_target_pairs={{0,2},{1,3},{2,0},{3,1},{4,8},{5,9},{6,10},{7,11},{8,4},{9,5},{10,... | collective-permute-start | bytes 786440 | tf_op jit(solution)/shard_map/ppermute | solution.py:421
  20.6 6.6 %collective-permute-start.5 = (bf16[1024,128]{1,0:T(8,128)(2,1)S(1)}, bf16[1024,128]{1,0:T(8,128)(2,1)S(1)}, u32[]{:S(2)}, u32[]{:S(2)}) collective-permute-start(bf16[1024,128]{1,0:T(8,128)(2,1)S(1)} %get-tuple-element.48), channel_id=1, source_target_pairs={{0,1},{1,0},{2,3},{3,2},{4,6},{5,7},{6,4},{7,5},{8,10},{9,11},{10,... | collective-permute-start | bytes 786440 | tf_op jit(solution)/shard_map/ppermute | solution.py:421
  20.6 6.6 %copy-start = (bf16[16,256,64]{1,2,0:T(8,128)(2,1)S(1)}, bf16[16,256,64]{1,2,0:T(8,128)(2,1)}, u32[]{:S(2)}) copy-start(bf16[16,256,64]{1,2,0:T(8,128)(2,1)} %param.15) | copy-start | bytes 1572868
  20.7 6.6 %copy-start.1 = (bf16[16,64,64]{2,1,0:T(8,128)(2,1)S(1)}, bf16[16,64,64]{2,1,0:T(8,128)(2,1)}, u32[]{:S(2)}) copy-start(bf16[16,64,64]{2,1,0:T(8,128)(2,1)} %up_one_ref.1) | copy-start | bytes 393220
  20.7 6.6 %copy-start.2 = (bf16[8,64,64]{2,1,0:T(8,128)(2,1)S(1)}, bf16[8,64,64]{2,1,0:T(8,128)(2,1)}, u32[]{:S(2)}) copy-start(bf16[8,64,64]{2,1,0:T(8,128)(2,1)} %up_two_ref.1) | copy-start | bytes 196612

commit v16 on v15

--- a/solution.py
+++ b/solution.py
@@ -458,10 +458,9 @@
         return 0 <= turns[1](i) < size
 
     split = leaves * rank
-    from_pair, near = lax.optimization_barrier((from_pair, near))
-    low = lax.optimization_barrier(from_pair[:split])
+    second, first, from_pair, near = lax.optimization_barrier((second, first, from_pair, near))
+    low = from_pair[:split]
     got_first = send(low, turns[0])
-    second, first, low = lax.optimization_barrier((second, first, low))
     upper = jnp.where((me[0] // 2 + me[0]) % 2 == 1, second[split:], first[split:])
     at_end = (me[0] < 2) | (me[0] >= size - 2)
     got_second = send(

time: 31.6 us -> 31.6 us (level)
  starting transfers between devices: 6.87 us -> 8 us
  waiting for transfers between devices: 1.34 us -> 0.24 us
    ppermute x6, starting transfers between devices: 6.87 us -> 8 us  [send(): return lax.ppermute(array, ('space', 'rhs'), pairs)]
    ppermute x6, waiting for transfers between devices: 1.34 us -> 0.24 us  [send(): return lax.ppermute(array, ('space', 'rhs'), pairs)]
  transfers between devices with their start and end apart: 6 -> 6, of which waited for: 1 -> 2; matrix products, arithmetic and copies ran while one was open for 0% -> 0% of each run, Pallas kernels for 53% -> 53%
where the time goes in v16:
time: 31.6 us; the launch traced here: 31.4 us
  Pallas kernels  23 us (73%)
  starting transfers between devices  8 us (25%)
    pallas_call x1, Pallas kernels, body(): pl.pallas_call(near_kernel, in_specs=[smem] + [hbm] * 6, out_specs=[vmem]...  11.5 us
    ppermute x6, starting transfers between devices, send(): return lax.ppermute(array, ('space', 'rhs'), pairs)  8 us
    pallas_call x1, Pallas kernels, body(): pl.pallas_call(prep_kernel, in_specs=[smem] * 3 + [vmem] * 6 + [hbm] * 3,...  5.27 us
    pallas_call x1, Pallas kernels, body(): pl.pallas_call(functools.partial(far_kernel, size=size), in_specs=[smem]...  4.17 us
    pallas_call x1, Pallas kernels, body(): pl.pallas_call(up_kernel, in_specs=[smem] + [hbm] * 4, out_specs=[vmem] *...  2.16 us
  transfers between devices with their start and end apart: 6, of which 2 were waited for; matrix products, arithmetic and copies ran while one was open for 0% of the time, Pallas kernels for 53%

profile of v16, /device:TPU:0, one launch (start us, length us, event | category | flops | bytes accessed | tf_op | source)
XLA Modules:
  0.0 31.4 jit_solution(10761153714183151298)
XLA Ops:
  0.0 2.2 %up_pass.1 = (bf16[2048,128]{1,0:T(8,128)(2,1)S(1)}, bf16[2048,128]{1,0:T(8,128)(2,1)S(1)}) custom-call(s32[1]{0:T(128)} %bitcast.me_ref, bf16[4096,128]{1,0:T(8,128)(2,1)} %x_hbm.3, bf16[16,64,256]{2,1,0:T(8,128)(2,1)} %bitcast.2, bf16[16,64,64]{2,1,0:T(8,128)(2,1)} %up_one_ref.1, bf16[8,64,64]{2,1,0:T(8,128)(2,1)} %up_two_ref.1), custom_call_target="tpu_custom_call" | custom-call | tf_op jit(solution)/shard_map/up_pass/pallas_call | solution.py:396
  2.2 0.5 %collective-permute-start = (bf16[2048,128]{1,0:T(8,128)(2,1)S(1)}, bf16[2048,128]{1,0:T(8,128)(2,1)S(1)}, u32[]{:S(2)}, u32[]{:S(2)}) collective-permute-start(bf16[2048,128]{1,0:T(8,128)(2,1)S(1)} %get-tuple-element.27.own_ref), channel_id=1, source_target_pairs={{0,1},{1,0},{2,3},{3,2},{4,8},{5,9},{6,10},{7,11},{8,4},{9,5},{10,... | collective-permute-start | bytes 1572872 | tf_op jit(solution)/shard_map/ppermute | solution.py:421
  2.7 4.1 %collective-permute-start.1 = (bf16[2048,128]{1,0:T(8,128)(2,1)S(1)}, bf16[2048,128]{1,0:T(8,128)(2,1)S(1)}, u32[]{:S(2)}, u32[]{:S(2)}) collective-permute-start(bf16[2048,128]{1,0:T(8,128)(2,1)S(1)} %get-tuple-element.27.own_ref), channel_id=1, source_target_pairs={{0,4},{1,5},{2,6},{3,7},{4,0},{5,1},{6,2},{7,3},{8,12},{9,13},{10,... | collective-permute-start | bytes 1572872 | tf_op jit(solution)/shard_map/ppermute | solution.py:421
  6.8 1.5 %collective-permute-start.2 = (bf16[2048,128]{1,0:T(8,128)(2,1)S(1)}, bf16[2048,128]{1,0:T(8,128)(2,1)S(1)}, u32[]{:S(2)}, u32[]{:S(2)}) collective-permute-start(bf16[2048,128]{1,0:T(8,128)(2,1)S(1)} %get-tuple-element.28), channel_id=1, source_target_pairs={{0,2},{1,3},{2,0},{3,1},{4,6},{5,7},{6,4},{7,5},{8,10},{9,11},{10,... | collective-permute-start | bytes 1572872 | tf_op jit(solution)/shard_map/ppermute | solution.py:421
  8.3 11.5 %near_own.1 = (f32[4096,128]{1,0:T(8,128)S(1)}, bf16[16,2,256,256]{3,2,1,0:T(8,128)(2,1)S(1)}, bf16[4096,128]{1,0:T(8,128)(2,1)S(1)}, s32[29,16]{1,0:T(8,128)S(1)}, s32[29,16]{1,0:T(8,128)S(1)}) custom-call(s32[1]{0:T(128)} %bitcast.me_ref, s32[16,12]{1,0:T(8,128)} %near_hbm.1, s32[16,16]{1,0:T(8,128)} %zero_hbm.2, s32[8,16]{1,0:T(8,128)} %one_hbm.2, ...), custom_call_target="tpu_custom_call" | custom-call | flops 2684354560 | bytes 28311552 | tf_op jit(solution)/shard_map/near_own/pallas_call | solution.py:430
  19.8 0.0 collective-permute-done.second_ref
  19.8 0.0 collective-permute-done.1.first_ref
  19.8 0.1 collective-permute-done.2.pair_ref
  19.9 0.1 broadcast_select_fusion
  20.0 0.3 %collective-permute-start.3 = (bf16[1024,128]{1,0:T(8,128)(2,1)S(1)}, bf16[1024,128]{1,0:T(8,128)(2,1)S(1)}, u32[]{:S(2)}, u32[]{:S(2)}) collective-permute-start(bf16[1024,128]{1,0:T(8,128)(2,1)S(1)} %get-tuple-element.47), channel_id=1, source_target_pairs={{0,4},{1,5},{2,6},{3,7},{4,0},{5,1},{6,2},{7,3},{8,12},{9,13},{10,... | collective-permute-start | bytes 786440 | tf_op jit(solution)/shard_map/ppermute | solution.py:421
  20.3 1.5 %collective-permute-start.4 = (bf16[1024,128]{1,0:T(8,128)(2,1)S(1)}, bf16[1024,128]{1,0:T(8,128)(2,1)S(1)}, u32[]{:S(2)}, u32[]{:S(2)}) collective-permute-start(bf16[1024,128]{1,0:T(8,128)(2,1)S(1)} %get-tuple-element.45), channel_id=1, source_target_pairs={{0,2},{1,3},{2,0},{3,1},{4,8},{5,9},{6,10},{7,11},{8,4},{9,5},{10,... | collective-permute-start | bytes 786440 | tf_op jit(solution)/shard_map/ppermute | solution.py:421
  21.8 0.0 collective-permute-start.5
  21.8 0.0 copy-start
  21.8 0.0 copy-start.1
  21.8 0.0 copy-start.2
  21.9 5.3 %prep.1 = (f32[4096,128]{1,0:T(8,128)S(1)}, bf16[5120,128]{1,0:T(8,128)(2,1)S(1)}, bf16[2560,128]{1,0:T(8,128)(2,1)S(1)}, bf16[1280,128]{1,0:T(8,128)(2,1)S(1)},...) custom-call(s32[1]{0:T(128)} %bitcast.me_ref, ...), custom_call_target="tpu_custom_call" | custom-call | flops 4000000000 | bytes 7340032 | tf_op jit(solution)/shard_map/prep/pallas_call | solution.py:471
  27.1 0.0 collective-permute-done.3.got_first
  27.2 0.1 collective-permute-done.4.got_second
  27.2 0.0 collective-permute-done.5.got_third
  27.2 0.0 copy-done
  27.2 0.0 copy-done.1
  27.2 0.0 copy-done.2
  27.3 4.2 %far_down.1 = (bf16[4096,128]{1,0:T(8,128)(2,1)}, bf16[5120,128]{1,0:T(8,128)(2,1)S(1)}, bf16[2560,128]{1,0:T(8,128)(2,1)S(1)}, bf16[1280,128]{1,0:T(8,128)(2,1)S(1)}) custom-call(s32[1]{0:T(128)} %bitcast.me_ref, s32[29,16]{1,0:T(8,128)S(1)} %get-tuple-element.25.starts_ref, ...), custom_call_target="tpu_custom_call", output_to_operand_aliasing={{1}: (15, {}), {2}: (16, {}), {3}: (17, {})} | custom-call | tf_op jit(solution)/shard_map/far_down/pallas_call | solution.py:499
Async XLA Ops:
  2.2 17.6 %collective-permute-start = (bf16[2048,128]{1,0:T(8,128)(2,1)S(1)}, bf16[2048,128]{1,0:T(8,128)(2,1)S(1)}, u32[]{:S(2)}, u32[]{:S(2)}) collective-permute-start(bf16[2048,128]{1,0:T(8,128)(2,1)S(1)} %get-tuple-element.27.own_ref), channel_id=1, source_target_pairs={{0,1},{1,0},{2,3},{3,2},{4,8},{5,9},{6,10},{7,11},{8,4},{9,5},{10,... | collective-permute-start | bytes 1572872 | tf_op jit(solution)/shard_map/ppermute | solution.py:421
  2.7 17.1 %collective-permute-start.1 = (bf16[2048,128]{1,0:T(8,128)(2,1)S(1)}, bf16[2048,128]{1,0:T(8,128)(2,1)S(1)}, u32[]{:S(2)}, u32[]{:S(2)}) collective-permute-start(bf16[2048,128]{1,0:T(8,128)(2,1)S(1)} %get-tuple-element.27.own_ref), channel_id=1, source_target_pairs={{0,4},{1,5},{2,6},{3,7},{4,0},{5,1},{6,2},{7,3},{8,12},{9,13},{10,... | collective-permute-start | bytes 1572872 | tf_op jit(solution)/shard_map/ppermute | solution.py:421
  6.8 13.1 %collective-permute-start.2 = (bf16[2048,128]{1,0:T(8,128)(2,1)S(1)}, bf16[2048,128]{1,0:T(8,128)(2,1)S(1)}, u32[]{:S(2)}, u32[]{:S(2)}) collective-permute-start(bf16[2048,128]{1,0:T(8,128)(2,1)S(1)} %get-tuple-element.28), channel_id=1, source_target_pairs={{0,2},{1,3},{2,0},{3,1},{4,6},{5,7},{6,4},{7,5},{8,10},{9,11},{10,... | collective-permute-start | bytes 1572872 | tf_op jit(solution)/shard_map/ppermute | solution.py:421
  20.0 7.2 %collective-permute-start.3 = (bf16[1024,128]{1,0:T(8,128)(2,1)S(1)}, bf16[1024,128]{1,0:T(8,128)(2,1)S(1)}, u32[]{:S(2)}, u32[]{:S(2)}) collective-permute-start(bf16[1024,128]{1,0:T(8,128)(2,1)S(1)} %get-tuple-element.47), channel_id=1, source_target_pairs={{0,4},{1,5},{2,6},{3,7},{4,0},{5,1},{6,2},{7,3},{8,12},{9,13},{10,... | collective-permute-start | bytes 786440 | tf_op jit(solution)/shard_map/ppermute | solution.py:421
  20.3 6.9 %collective-permute-start.4 = (bf16[1024,128]{1,0:T(8,128)(2,1)S(1)}, bf16[1024,128]{1,0:T(8,128)(2,1)S(1)}, u32[]{:S(2)}, u32[]{:S(2)}) collective-permute-start(bf16[1024,128]{1,0:T(8,128)(2,1)S(1)} %get-tuple-element.45), channel_id=1, source_target_pairs={{0,2},{1,3},{2,0},{3,1},{4,8},{5,9},{6,10},{7,11},{8,4},{9,5},{10,... | collective-permute-start | bytes 786440 | tf_op jit(solution)/shard_map/ppermute | solution.py:421
  21.8 5.4 %collective-permute-start.5 = (bf16[1024,128]{1,0:T(8,128)(2,1)S(1)}, bf16[1024,128]{1,0:T(8,128)(2,1)S(1)}, u32[]{:S(2)}, u32[]{:S(2)}) collective-permute-start(bf16[1024,128]{1,0:T(8,128)(2,1)S(1)} %get-tuple-element.46), channel_id=1, source_target_pairs={{0,1},{1,0},{2,3},{3,2},{4,6},{5,7},{6,4},{7,5},{8,10},{9,11},{10,... | collective-permute-start | bytes 786440 | tf_op jit(solution)/shard_map/ppermute | solution.py:421
  21.8 5.4 %copy-start = (bf16[16,256,64]{1,2,0:T(8,128)(2,1)S(1)}, bf16[16,256,64]{1,2,0:T(8,128)(2,1)}, u32[]{:S(2)}) copy-start(bf16[16,256,64]{1,2,0:T(8,128)(2,1)} %param.15) | copy-start | bytes 1572868
  21.8 5.4 %copy-start.1 = (bf16[16,64,64]{2,1,0:T(8,128)(2,1)S(1)}, bf16[16,64,64]{2,1,0:T(8,128)(2,1)}, u32[]{:S(2)}) copy-start(bf16[16,64,64]{2,1,0:T(8,128)(2,1)} %up_one_ref.1) | copy-start | bytes 393220
  21.8 5.4 %copy-start.2 = (bf16[8,64,64]{2,1,0:T(8,128)(2,1)S(1)}, bf16[8,64,64]{2,1,0:T(8,128)(2,1)}, u32[]{:S(2)}) copy-start(bf16[8,64,64]{2,1,0:T(8,128)(2,1)} %up_two_ref.1) | copy-start | bytes 196612

commit v17 on v15

--- a/solution.py
+++ b/solution.py
@@ -176,21 +176,14 @@
     starts_ref[leaves + ones + twos, 0] = lax.fori_loop(0, leaves // 2, step, most)
 
 
-def add_edge(sum_ref, near_ref, edge_ref, side, rows):
-    for leaf in range(edge_ref.shape[0]):
+def add_edge(sum_ref, near_ref, edge_ref, side, rows, leaves):
+    for leaf in leaves:
         here = pl.ds(leaf * LEAF, LEAF)
         sum_ref[here, :] = near_ref[here, :] + dot(edge_ref[leaf, side], rows)
 
 
-def window_copies(plans, sems):
-    copies = []
-    for ref, start, win, at, size in plans:
-        copies.append(
-            pltpu.make_async_copy(
-                ref.at[pl.ds(start, size), :], win.at[pl.ds(at, size), :], sems.at[len(copies)]
-            )
-        )
-    return copies
+def place_piece(ref, start, win, at, size):
+    win[pl.ds(at, size), :] = ref[pl.ds(start, size), :]
 
 
 def field(wide, starts_ref, row, win, slots):
@@ -206,7 +199,7 @@
     me_ref, starts_ref, turns_ref, own_ref, pair_ref, first_ref, second_ref, near_ref, edge_ref,
     zero_hbm, one_hbm, two_hbm,
     sum_ref, zero_win, one_win, two_win, zero_wide, one_wide, two_wide, part_ref,
-    zero_buf, one_buf, two_buf, sems, win_sems,
+    zero_buf, one_buf, two_buf, sems,
 ):
     leaves, fars, rank = zero_buf.shape[:3]
     base = leaves + one_buf.shape[0]
@@ -231,23 +224,18 @@
         (second_ref, 0, block * (SPAN - 1)),
         (pair_ref, 0, REACH + 1 - 2 * odd),
     )
-    plans = []
     for ref, start, place in pieces:
         for win in (zero_win, one_win, two_win):
             size = win.shape[0] // SPAN
-            plans.append((ref, start, win, pl.multiple_of(place * size, size), size))
+            place_piece(ref, start, win, pl.multiple_of(place * size, size), size)
             start += size
-    moves = window_copies(plans, win_sems)
-    for move in moves:
-        move.start()
-    add_edge(sum_ref, near_ref, edge_ref, odd, pair_ref[pl.ds(pair_ref.shape[0] - LEAF, LEAF), :])
+    rows = pair_ref[pl.ds(pair_ref.shape[0] - LEAF, LEAF), :]
+    add_edge(sum_ref, near_ref, edge_ref, odd, rows, range(leaves))
     for copy, buf, wide, first, row in chunks:
         copy.wait()
         for node in range(first, first + 4):
             picked = [buf[node, turns_ref[row + node, k]] for k in range(fars)]
             wide[node] = jnp.concatenate(picked, axis=1)
-    for move in moves:
-        move.wait()
     for _, _, wide, win, row in levels:
         for node in range(wide.shape[0]):
             part = field(wide.at[node], starts_ref, row + node, win, range(fars // 2, fars))
@@ -255,12 +243,12 @@
 
 
 def far_kernel(
-    me_ref, starts_ref, x_ref, got_first, got_second, got_third, near_ref,
+    me_ref, starts_ref, x_ref, got_first, got_second, got_third, sum_in,
     edge_ref, basis_ref, up_one_ref, up_two_ref, zero_wide, one_wide, two_wide, part_ref,
-    zero_in, one_in, two_in, out_hbm, zero_win, one_win, two_win,
-    sum_buf, out_buf, rows_buf, field_buf, down_buf, win_sems, out_sems, *, size,
+    zero_in, one_in, two_in, out_hbm, sum_ref, zero_win, one_win, two_win,
+    out_buf, rows_buf, field_buf, down_buf, out_sems, *, size,
 ):
-    del zero_in, one_in, two_in
+    del sum_in, zero_in, one_in, two_in
     leaves, rank, deep = zero_wide.shape
     ones, twos = leaves // 2, leaves // 4
     fars = deep // rank
@@ -270,22 +258,15 @@
     sizes = [n * rank for n in (leaves, ones, twos)]
     at = [pl.multiple_of(place * n, n) for n in sizes]
 
-    def arrivals(low_ref, high_ref):
-        plans = (
-            (low_ref, 0, zero_win, at[0], sizes[0]),
-            (high_ref, 0, one_win, at[1], sizes[1]),
-            (high_ref, sizes[1], two_win, at[2], sizes[2]),
-        )
-        return window_copies(plans, win_sems)
-
     end = pl.ds(got_first.shape[0] - LEAF, LEAF)
     low_first = lax.rem(me + me // 2, 2) == 1
     at_end = (me < 2) | (me >= size - 2)
 
     def take(low_ref, high_ref):
         def _():
-            for move in arrivals(low_ref, high_ref):
-                move.start()
+            place_piece(low_ref, 0, zero_win, at[0], sizes[0])
+            place_piece(high_ref, 0, one_win, at[1], sizes[1])
+            place_piece(high_ref, sizes[1], two_win, at[2], sizes[2])
             rows_buf[...] = high_ref[end, :]
 
         return _
@@ -293,22 +274,15 @@
     pl.when(low_first & at_end)(take(got_first, got_second))
     pl.when(low_first & jnp.logical_not(at_end))(take(got_first, got_third))
     pl.when(jnp.logical_not(low_first))(take(got_second, got_third))
-    moves = arrivals(got_first, got_second)
 
     alone = (me == 0) | (me == size - 1)
 
     @pl.when(alone)
     def _():
+        rows_buf[...] = jnp.zeros_like(rows_buf)
         for leaf in range(leaves):
             here = pl.ds(leaf * LEAF, LEAF)
-            sum_buf[here, :] = near_ref[here, :] + dot(edge_ref[leaf, 1 - odd], x_ref[here, :])
-
-    @pl.when(jnp.logical_not(alone))
-    def _():
-        add_edge(sum_buf, near_ref, edge_ref, 1 - odd, rows_buf[...])
-
-    for move in moves:
-        move.wait()
+            sum_ref[here, :] += dot(edge_ref[leaf, 1 - odd], x_ref[here, :])
 
     def node_rows(row):
         return pl.ds(row * rank, rank)
@@ -333,12 +307,15 @@
 
             lax.fori_loop(0, wide.shape[0], again, 0)
 
+    rows = rows_buf[...]
+    add_edge(sum_ref, sum_ref, edge_ref, 1 - odd, rows, range(leaves // 2))
     for q in range(twos):
         down_buf[node_rows(base + q), :] = field_buf[node_rows(base + q), :].astype(jnp.bfloat16)
     for p in range(ones):
         total = dot(up_two_ref[p], down_buf[node_rows(base + p // 2), :])
         total = total + field_buf[node_rows(leaves + p), :]
         down_buf[node_rows(leaves + p), :] = total.astype(jnp.bfloat16)
+    add_edge(sum_ref, sum_ref, edge_ref, 1 - odd, rows, range(leaves // 2, leaves))
     for leaf in range(leaves):
         total = dot(up_one_ref[leaf], down_buf[node_rows(leaves + leaf // 2), :])
         total = total + field_buf[node_rows(leaf), :]
@@ -346,13 +323,13 @@
     outs = []
     for leaf in range(leaves):
         here = pl.ds(leaf * LEAF, LEAF)
-        total = sum_buf[here, :] + dot_t(basis_ref[leaf], down_buf[node_rows(leaf), :])
+        total = sum_ref[here, :] + dot_t(basis_ref[leaf], down_buf[node_rows(leaf), :])
         out_buf[here, :] = total.astype(jnp.bfloat16)
-        if leaf % 4 == 3:
-            some = pl.ds((leaf - 3) * LEAF, 4 * LEAF)
+        if leaf % 2 == 1:
+            some = pl.ds((leaf - 1) * LEAF, 2 * LEAF)
             outs.append(
                 pltpu.make_async_copy(
-                    out_buf.at[some, :], out_hbm.at[some, :], out_sems.at[leaf // 4]
+                    out_buf.at[some, :], out_hbm.at[some, :], out_sems.at[leaf // 2]
                 )
             )
             outs[-1].start()
@@ -461,7 +438,7 @@
     from_pair, near = lax.optimization_barrier((from_pair, near))
     low = lax.optimization_barrier(from_pair[:split])
     got_first = send(low, turns[0])
-    second, first, low = lax.optimization_barrier((second, first, low))
+    first, second, low = lax.optimization_barrier((first, second, low))
     upper = jnp.where((me[0] // 2 + me[0]) % 2 == 1, second[split:], first[split:])
     at_end = (me[0] < 2) | (me[0] >= size - 2)
     got_second = send(
@@ -482,7 +459,6 @@
         scratch_shapes=[
             *[pltpu.VMEM((n, fars, rank, rank), bf16) for n in counts],
             pltpu.SemaphoreType.DMA((sum(n // 4 for n in counts),)),
-            pltpu.SemaphoreType.DMA((12,)),
         ],
         compiler_params=pltpu.CompilerParams(vmem_limit_bytes=16 * MIB),
         cost_estimate=pl.CostEstimate(
@@ -500,20 +476,19 @@
     out, *_ = pl.pallas_call(
         functools.partial(far_kernel, size=size),
         in_specs=[smem] * 2 + [vmem] * 16,
-        out_specs=[hbm] + [vmem] * 3,
+        out_specs=[hbm] + [vmem] * 4,
         out_shape=[
             jax.ShapeDtypeStruct(vectors.shape, bf16),
+            pltpu.VMEM(vectors.shape, f32),
             *[pltpu.VMEM((SPAN * n * rank, columns), bf16) for n in counts],
         ],
-        input_output_aliases={15: 1, 16: 2, 17: 3},
+        input_output_aliases={6: 1, 15: 2, 16: 3, 17: 4},
         scratch_shapes=[
-            pltpu.VMEM(vectors.shape, f32),
             pltpu.VMEM(vectors.shape, bf16),
             pltpu.VMEM((LEAF, columns), bf16),
             pltpu.VMEM((nodes * rank, columns), f32),
             pltpu.VMEM((nodes * rank, columns), bf16),
-            pltpu.SemaphoreType.DMA((3,)),
-            pltpu.SemaphoreType.DMA((leaves // 4,)),
+            pltpu.SemaphoreType.DMA((leaves // 2,)),
         ],
         compiler_params=pltpu.CompilerParams(vmem_limit_bytes=16 * MIB),
         name="far_down",

time: 31.6 us -> 31.8 us (level)
  transfers between devices with their start and end apart: 6 -> 6, of which waited for: 1 -> 2; matrix products, arithmetic and copies ran while one was open for 0% -> 0% of each run, Pallas kernels for 53% -> 53%
where the time goes in v17:
time: 31.8 us; the launch traced here: 31.6 us
  Pallas kernels  23.2 us (73%)
  starting transfers between devices  6.87 us (22%)
  waiting for transfers between devices  1.38 us (4%)
    pallas_call x1, Pallas kernels, body(): pl.pallas_call(near_kernel, in_specs=[smem] + [hbm] * 6, out_specs=[vmem]...  11.5 us
    ppermute x6, starting transfers between devices, send(): return lax.ppermute(array, ('space', 'rhs'), pairs)  6.87 us
    pallas_call x1, Pallas kernels, body(): pl.pallas_call(prep_kernel, in_specs=[smem] * 3 + [vmem] * 6 + [hbm] * 3,...  5.23 us
    pallas_call x1, Pallas kernels, body(): pl.pallas_call(functools.partial(far_kernel, size=size), in_specs=[smem]...  4.34 us
    pallas_call x1, Pallas kernels, body(): pl.pallas_call(up_kernel, in_specs=[smem] + [hbm] * 4, out_specs=[vmem] *...  2.16 us
    ppermute x6, waiting for transfers between devices, send(): return lax.ppermute(array, ('space', 'rhs'), pairs)  1.38 us
  transfers between devices with their start and end apart: 6, of which 2 were waited for; matrix products, arithmetic and copies ran while one was open for 0% of the time, Pallas kernels for 53%

profile of v17, /device:TPU:0, one launch (start us, length us, event | category | flops | bytes accessed | tf_op | source)
XLA Modules:
  0.0 31.6 jit_solution(12409743579862635288)
XLA Ops:
  0.0 2.2 %up_pass.1 = (bf16[2048,128]{1,0:T(8,128)(2,1)S(1)}, bf16[2048,128]{1,0:T(8,128)(2,1)S(1)}) custom-call(s32[1]{0:T(128)} %bitcast.me_ref, bf16[4096,128]{1,0:T(8,128)(2,1)} %x_hbm.3, bf16[16,64,256]{2,1,0:T(8,128)(2,1)} %bitcast.2, bf16[16,64,64]{2,1,0:T(8,128)(2,1)} %up_one_ref.1, bf16[8,64,64]{2,1,0:T(8,128)(2,1)} %up_two_ref.1), custom_call_target="tpu_custom_call" | custom-call | tf_op jit(solution)/shard_map/up_pass/pallas_call | solution.py:373
  2.2 3.0 %collective-permute-start = (bf16[2048,128]{1,0:T(8,128)(2,1)S(1)}, bf16[2048,128]{1,0:T(8,128)(2,1)S(1)}, u32[]{:S(2)}, u32[]{:S(2)}) collective-permute-start(bf16[2048,128]{1,0:T(8,128)(2,1)S(1)} %get-tuple-element.28), channel_id=1, source_target_pairs={{0,2},{1,3},{2,0},{3,1},{4,6},{5,7},{6,4},{7,5},{8,10},{9,11},{10,... | collective-permute-start | bytes 1572872 | tf_op jit(solution)/shard_map/ppermute | solution.py:398
  5.2 0.0 collective-permute-start.3
  5.2 3.2 %collective-permute-start.2 = (bf16[2048,128]{1,0:T(8,128)(2,1)S(1)}, bf16[2048,128]{1,0:T(8,128)(2,1)S(1)}, u32[]{:S(2)}, u32[]{:S(2)}) collective-permute-start(bf16[2048,128]{1,0:T(8,128)(2,1)S(1)} %get-tuple-element.31.own_ref), channel_id=1, source_target_pairs={{0,4},{1,5},{2,6},{3,7},{4,0},{5,1},{6,2},{7,3},{8,12},{9,13},{10,... | collective-permute-start | bytes 1572872 | tf_op jit(solution)/shard_map/ppermute | solution.py:398
  8.3 11.5 %near_own.1 = (f32[4096,128]{1,0:T(8,128)S(1)}, bf16[16,2,256,256]{3,2,1,0:T(8,128)(2,1)S(1)}, bf16[4096,128]{1,0:T(8,128)(2,1)S(1)}, s32[29,16]{1,0:T(8,128)S(1)}, s32[29,16]{1,0:T(8,128)S(1)}) custom-call(s32[1]{0:T(128)} %bitcast.me_ref, s32[16,12]{1,0:T(8,128)} %near_hbm.1, s32[16,16]{1,0:T(8,128)} %zero_hbm.2, s32[8,16]{1,0:T(8,128)} %one_hbm.2, ...), custom_call_target="tpu_custom_call" | custom-call | flops 2684354560 | bytes 28311552 | tf_op jit(solution)/shard_map/near_own/pallas_call | solution.py:407
  19.8 0.0 collective-permute-done.pair_ref
  19.8 0.1 collective-permute-start.1
  19.9 0.0 collective-permute-done.3.second_ref
  19.9 0.0 collective-permute-done.2.first_ref
  19.9 0.1 broadcast_select_fusion
  20.0 0.6 %collective-permute-start.4 = (bf16[1024,128]{1,0:T(8,128)(2,1)S(1)}, bf16[1024,128]{1,0:T(8,128)(2,1)S(1)}, u32[]{:S(2)}, u32[]{:S(2)}) collective-permute-start(bf16[1024,128]{1,0:T(8,128)(2,1)S(1)} %get-tuple-element.47), channel_id=1, source_target_pairs={{0,2},{1,3},{2,0},{3,1},{4,8},{5,9},{6,10},{7,11},{8,4},{9,5},{10,... | collective-permute-start | bytes 786440 | tf_op jit(solution)/shard_map/ppermute | solution.py:398
  20.6 0.0 collective-permute-start.5
  20.6 0.0 copy-start
  20.7 0.0 copy-start.1
  20.7 0.0 copy-start.2
  20.7 5.2 %prep.1 = (f32[4096,128]{1,0:T(8,128)S(1)}, bf16[5120,128]{1,0:T(8,128)(2,1)S(1)}, bf16[2560,128]{1,0:T(8,128)(2,1)S(1)}, bf16[1280,128]{1,0:T(8,128)(2,1)S(1)},...) custom-call(s32[1]{0:T(128)} %bitcast.me_ref, ...), custom_call_target="tpu_custom_call" | custom-call | flops 4000000000 | bytes 7340032 | tf_op jit(solution)/shard_map/prep/pallas_call | solution.py:449
  25.9 1.2 %collective-permute-done.1.got_first = bf16[1024,128]{1,0:T(8,128)(2,1)S(1)} collective-permute-done((bf16[1024,128]{1,0:T(8,128)(2,1)S(1)}, bf16[1024,128]{1,0:T(8,128)(2,1)S(1)}, u32[]{:S(2)}, u32[]{:S(2)}) %collective-permute-start.1) | collective-permute-done | bytes 262176 | tf_op jit(solution)/shard_map/ppermute | solution.py:398
  27.1 0.2 collective-permute-done.4.got_second
  27.3 0.0 collective-permute-done.5.got_third
  27.3 0.0 copy-done
  27.3 0.0 copy-done.1
  27.3 0.0 copy-done.2
  27.3 4.3 %far_down.1 = (bf16[4096,128]{1,0:T(8,128)(2,1)}, f32[4096,128]{1,0:T(8,128)S(1)}, bf16[5120,128]{1,0:T(8,128)(2,1)S(1)}, bf16[2560,128]{1,0:T(8,128)(2,1)S(1)}, bf16[1280,128]{1,0:T(8,128)(2,1)S(1)}) custom-call(s32[1]{0:T(128)} %bitcast.me_ref, ...), custom_call_target="tpu_custom_call", output_to_operand_aliasing={{1}: (6, {}), {2}: (15, {}), {3}: (16, {}), {4}: (17, {})} | custom-call | tf_op jit(solution)/shard_map/far_down/pallas_call | solution.py:476
  (1 shorter events, 0.0 us)
Async XLA Ops:
  2.2 17.6 %collective-permute-start = (bf16[2048,128]{1,0:T(8,128)(2,1)S(1)}, bf16[2048,128]{1,0:T(8,128)(2,1)S(1)}, u32[]{:S(2)}, u32[]{:S(2)}) collective-permute-start(bf16[2048,128]{1,0:T(8,128)(2,1)S(1)} %get-tuple-element.28), channel_id=1, source_target_pairs={{0,2},{1,3},{2,0},{3,1},{4,6},{5,7},{6,4},{7,5},{8,10},{9,11},{10,... | collective-permute-start | bytes 1572872 | tf_op jit(solution)/shard_map/ppermute | solution.py:398
  5.2 14.7 %collective-permute-start.3 = (bf16[2048,128]{1,0:T(8,128)(2,1)S(1)}, bf16[2048,128]{1,0:T(8,128)(2,1)S(1)}, u32[]{:S(2)}, u32[]{:S(2)}) collective-permute-start(bf16[2048,128]{1,0:T(8,128)(2,1)S(1)} %get-tuple-element.31.own_ref), channel_id=1, source_target_pairs={{0,1},{1,0},{2,3},{3,2},{4,8},{5,9},{6,10},{7,11},{8,4},{9,5},{10,... | collective-permute-start | bytes 1572872 | tf_op jit(solution)/shard_map/ppermute | solution.py:398
  5.2 14.7 %collective-permute-start.2 = (bf16[2048,128]{1,0:T(8,128)(2,1)S(1)}, bf16[2048,128]{1,0:T(8,128)(2,1)S(1)}, u32[]{:S(2)}, u32[]{:S(2)}) collective-permute-start(bf16[2048,128]{1,0:T(8,128)(2,1)S(1)} %get-tuple-element.31.own_ref), channel_id=1, source_target_pairs={{0,4},{1,5},{2,6},{3,7},{4,0},{5,1},{6,2},{7,3},{8,12},{9,13},{10,... | collective-permute-start | bytes 1572872 | tf_op jit(solution)/shard_map/ppermute | solution.py:398
  19.8 7.3 %collective-permute-start.1 = (bf16[1024,128]{1,0:T(8,128)(2,1)S(1)}, bf16[1024,128]{1,0:T(8,128)(2,1)S(1)}, u32[]{:S(2)}, u32[]{:S(2)}) collective-permute-start(bf16[1024,128]{1,0:T(8,128)(2,1)S(1)} %slice.9), channel_id=1, source_target_pairs={{0,4},{1,5},{2,6},{3,7},{4,0},{5,1},{6,2},{7,3},{8,12},{9,13},{10,... | collective-permute-start | bytes 786440 | tf_op jit(solution)/shard_map/ppermute | solution.py:398
  20.0 7.3 %collective-permute-start.4 = (bf16[1024,128]{1,0:T(8,128)(2,1)S(1)}, bf16[1024,128]{1,0:T(8,128)(2,1)S(1)}, u32[]{:S(2)}, u32[]{:S(2)}) collective-permute-start(bf16[1024,128]{1,0:T(8,128)(2,1)S(1)} %get-tuple-element.47), channel_id=1, source_target_pairs={{0,2},{1,3},{2,0},{3,1},{4,8},{5,9},{6,10},{7,11},{8,4},{9,5},{10,... | collective-permute-start | bytes 786440 | tf_op jit(solution)/shard_map/ppermute | solution.py:398
  20.6 6.6 %collective-permute-start.5 = (bf16[1024,128]{1,0:T(8,128)(2,1)S(1)}, bf16[1024,128]{1,0:T(8,128)(2,1)S(1)}, u32[]{:S(2)}, u32[]{:S(2)}) collective-permute-start(bf16[1024,128]{1,0:T(8,128)(2,1)S(1)} %get-tuple-element.48), channel_id=1, source_target_pairs={{0,1},{1,0},{2,3},{3,2},{4,6},{5,7},{6,4},{7,5},{8,10},{9,11},{10,... | collective-permute-start | bytes 786440 | tf_op jit(solution)/shard_map/ppermute | solution.py:398
  20.6 6.6 %copy-start = (bf16[16,256,64]{1,2,0:T(8,128)(2,1)S(1)}, bf16[16,256,64]{1,2,0:T(8,128)(2,1)}, u32[]{:S(2)}) copy-start(bf16[16,256,64]{1,2,0:T(8,128)(2,1)} %param.15) | copy-start | bytes 1572868
  20.7 6.6 %copy-start.1 = (bf16[16,64,64]{2,1,0:T(8,128)(2,1)S(1)}, bf16[16,64,64]{2,1,0:T(8,128)(2,1)}, u32[]{:S(2)}) copy-start(bf16[16,64,64]{2,1,0:T(8,128)(2,1)} %up_one_ref.1) | copy-start | bytes 393220
  20.7 6.6 %copy-start.2 = (bf16[8,64,64]{2,1,0:T(8,128)(2,1)S(1)}, bf16[8,64,64]{2,1,0:T(8,128)(2,1)}, u32[]{:S(2)}) copy-start(bf16[8,64,64]{2,1,0:T(8,128)(2,1)} %up_two_ref.1) | copy-start | bytes 196612

commit v18 on v17

--- a/solution.py
+++ b/solution.py
@@ -277,12 +277,11 @@
 
     alone = (me == 0) | (me == size - 1)
 
-    @pl.when(alone)
-    def _():
-        rows_buf[...] = jnp.zeros_like(rows_buf)
-        for leaf in range(leaves):
+    def add_last(some):
+        for leaf in some:
             here = pl.ds(leaf * LEAF, LEAF)
-            sum_ref[here, :] += dot(edge_ref[leaf, 1 - odd], x_ref[here, :])
+            rows = jnp.where(alone, x_ref[here, :], rows_buf[...])
+            sum_ref[here, :] += dot(edge_ref[leaf, 1 - odd], rows)
 
     def node_rows(row):
         return pl.ds(row * rank, rank)
@@ -307,15 +306,14 @@
 
             lax.fori_loop(0, wide.shape[0], again, 0)
 
-    rows = rows_buf[...]
-    add_edge(sum_ref, sum_ref, edge_ref, 1 - odd, rows, range(leaves // 2))
+    add_last(range(leaves // 2))
     for q in range(twos):
         down_buf[node_rows(base + q), :] = field_buf[node_rows(base + q), :].astype(jnp.bfloat16)
     for p in range(ones):
         total = dot(up_two_ref[p], down_buf[node_rows(base + p // 2), :])
         total = total + field_buf[node_rows(leaves + p), :]
         down_buf[node_rows(leaves + p), :] = total.astype(jnp.bfloat16)
-    add_edge(sum_ref, sum_ref, edge_ref, 1 - odd, rows, range(leaves // 2, leaves))
+    add_last(range(leaves // 2, leaves))
     for leaf in range(leaves):
         total = dot(up_one_ref[leaf], down_buf[node_rows(leaves + leaf // 2), :])
         total = total + field_buf[node_rows(leaf), :]

time: 31.8 us -> 31 us (0.975)
  Pallas kernels: 23.2 us -> 22.5 us
    pallas_call x1, Pallas kernels: 4.34 us -> 3.61 us  [body(): pl.pallas_call(functools.partial(far_kernel, size=size), in_specs=[smem]...]
  transfers between devices with their start and end apart: 6 -> 6, of which waited for: 2 -> 2; matrix products, arithmetic and copies ran while one was open for 0% -> 0% of each run, Pallas kernels for 53% -> 54%
where the time goes in v18:
time: 31 us; the launch traced here: 30.9 us
  Pallas kernels  22.5 us (73%)
  starting transfers between devices  6.87 us (22%)
  waiting for transfers between devices  1.38 us (4%)
    pallas_call x1, Pallas kernels, body(): pl.pallas_call(near_kernel, in_specs=[smem] + [hbm] * 6, out_specs=[vmem]...  11.5 us
    ppermute x6, starting transfers between devices, send(): return lax.ppermute(array, ('space', 'rhs'), pairs)  6.87 us
    pallas_call x1, Pallas kernels, body(): pl.pallas_call(prep_kernel, in_specs=[smem] * 3 + [vmem] * 6 + [hbm] * 3,...  5.23 us
    pallas_call x1, Pallas kernels, body(): pl.pallas_call(functools.partial(far_kernel, size=size), in_specs=[smem]...  3.61 us
    pallas_call x1, Pallas kernels, body(): pl.pallas_call(up_kernel, in_specs=[smem] + [hbm] * 4, out_specs=[vmem] *...  2.16 us
    ppermute x6, waiting for transfers between devices, send(): return lax.ppermute(array, ('space', 'rhs'), pairs)  1.38 us
  transfers between devices with their start and end apart: 6, of which 2 were waited for; matrix products, arithmetic and copies ran while one was open for 0% of the time, Pallas kernels for 54%

profile of v18, /device:TPU:0, one launch (start us, length us, event | category | flops | bytes accessed | tf_op | source)
XLA Modules:
  0.0 30.9 jit_solution(11447512407648468957)
XLA Ops:
  0.0 2.2 %up_pass.1 = (bf16[2048,128]{1,0:T(8,128)(2,1)S(1)}, bf16[2048,128]{1,0:T(8,128)(2,1)S(1)}) custom-call(s32[1]{0:T(128)} %bitcast.me_ref, bf16[4096,128]{1,0:T(8,128)(2,1)} %x_hbm.3, bf16[16,64,256]{2,1,0:T(8,128)(2,1)} %bitcast.2, bf16[16,64,64]{2,1,0:T(8,128)(2,1)} %up_one_ref.1, bf16[8,64,64]{2,1,0:T(8,128)(2,1)} %up_two_ref.1), custom_call_target="tpu_custom_call" | custom-call | tf_op jit(solution)/shard_map/up_pass/pallas_call | solution.py:371
  2.2 3.0 %collective-permute-start = (bf16[2048,128]{1,0:T(8,128)(2,1)S(1)}, bf16[2048,128]{1,0:T(8,128)(2,1)S(1)}, u32[]{:S(2)}, u32[]{:S(2)}) collective-permute-start(bf16[2048,128]{1,0:T(8,128)(2,1)S(1)} %get-tuple-element.28), channel_id=1, source_target_pairs={{0,2},{1,3},{2,0},{3,1},{4,6},{5,7},{6,4},{7,5},{8,10},{9,11},{10,... | collective-permute-start | bytes 1572872 | tf_op jit(solution)/shard_map/ppermute | solution.py:396
  5.2 0.0 collective-permute-start.3
  5.2 3.2 %collective-permute-start.2 = (bf16[2048,128]{1,0:T(8,128)(2,1)S(1)}, bf16[2048,128]{1,0:T(8,128)(2,1)S(1)}, u32[]{:S(2)}, u32[]{:S(2)}) collective-permute-start(bf16[2048,128]{1,0:T(8,128)(2,1)S(1)} %get-tuple-element.31.own_ref), channel_id=1, source_target_pairs={{0,4},{1,5},{2,6},{3,7},{4,0},{5,1},{6,2},{7,3},{8,12},{9,13},{10,... | collective-permute-start | bytes 1572872 | tf_op jit(solution)/shard_map/ppermute | solution.py:396
  8.3 11.5 %near_own.1 = (f32[4096,128]{1,0:T(8,128)S(1)}, bf16[16,2,256,256]{3,2,1,0:T(8,128)(2,1)S(1)}, bf16[4096,128]{1,0:T(8,128)(2,1)S(1)}, s32[29,16]{1,0:T(8,128)S(1)}, s32[29,16]{1,0:T(8,128)S(1)}) custom-call(s32[1]{0:T(128)} %bitcast.me_ref, s32[16,12]{1,0:T(8,128)} %near_hbm.1, s32[16,16]{1,0:T(8,128)} %zero_hbm.2, s32[8,16]{1,0:T(8,128)} %one_hbm.2, ...), custom_call_target="tpu_custom_call" | custom-call | flops 2684354560 | bytes 28311552 | tf_op jit(solution)/shard_map/near_own/pallas_call | solution.py:405
  19.8 0.0 collective-permute-done.pair_ref
  19.8 0.1 collective-permute-start.1
  19.9 0.0 collective-permute-done.3.second_ref
  19.9 0.0 collective-permute-done.2.first_ref
  19.9 0.1 broadcast_select_fusion
  20.0 0.6 %collective-permute-start.4 = (bf16[1024,128]{1,0:T(8,128)(2,1)S(1)}, bf16[1024,128]{1,0:T(8,128)(2,1)S(1)}, u32[]{:S(2)}, u32[]{:S(2)}) collective-permute-start(bf16[1024,128]{1,0:T(8,128)(2,1)S(1)} %get-tuple-element.47), channel_id=1, source_target_pairs={{0,2},{1,3},{2,0},{3,1},{4,8},{5,9},{6,10},{7,11},{8,4},{9,5},{10,... | collective-permute-start | bytes 786440 | tf_op jit(solution)/shard_map/ppermute | solution.py:396
  20.6 0.0 collective-permute-start.5
  20.6 0.0 copy-start
  20.7 0.0 copy-start.1
  20.7 0.0 copy-start.2
  20.7 5.2 %prep.1 = (f32[4096,128]{1,0:T(8,128)S(1)}, bf16[5120,128]{1,0:T(8,128)(2,1)S(1)}, bf16[2560,128]{1,0:T(8,128)(2,1)S(1)}, bf16[1280,128]{1,0:T(8,128)(2,1)S(1)},...) custom-call(s32[1]{0:T(128)} %bitcast.me_ref, ...), custom_call_target="tpu_custom_call" | custom-call | flops 4000000000 | bytes 7340032 | tf_op jit(solution)/shard_map/prep/pallas_call | solution.py:447
  25.9 1.2 %collective-permute-done.1.got_first = bf16[1024,128]{1,0:T(8,128)(2,1)S(1)} collective-permute-done((bf16[1024,128]{1,0:T(8,128)(2,1)S(1)}, bf16[1024,128]{1,0:T(8,128)(2,1)S(1)}, u32[]{:S(2)}, u32[]{:S(2)}) %collective-permute-start.1) | collective-permute-done | bytes 262176 | tf_op jit(solution)/shard_map/ppermute | solution.py:396
  27.1 0.2 collective-permute-done.4.got_second
  27.3 0.0 collective-permute-done.5.got_third
  27.3 0.0 copy-done
  27.3 0.0 copy-done.1
  27.3 0.0 copy-done.2
  27.3 3.6 %far_down.1 = (bf16[4096,128]{1,0:T(8,128)(2,1)}, f32[4096,128]{1,0:T(8,128)S(1)}, bf16[5120,128]{1,0:T(8,128)(2,1)S(1)}, bf16[2560,128]{1,0:T(8,128)(2,1)S(1)}, bf16[1280,128]{1,0:T(8,128)(2,1)S(1)}) custom-call(s32[1]{0:T(128)} %bitcast.me_ref, ...), custom_call_target="tpu_custom_call", output_to_operand_aliasing={{1}: (6, {}), {2}: (15, {}), {3}: (16, {}), {4}: (17, {})} | custom-call | tf_op jit(solution)/shard_map/far_down/pallas_call | solution.py:474
  (1 shorter events, 0.0 us)
Async XLA Ops:
  2.2 17.6 %collective-permute-start = (bf16[2048,128]{1,0:T(8,128)(2,1)S(1)}, bf16[2048,128]{1,0:T(8,128)(2,1)S(1)}, u32[]{:S(2)}, u32[]{:S(2)}) collective-permute-start(bf16[2048,128]{1,0:T(8,128)(2,1)S(1)} %get-tuple-element.28), channel_id=1, source_target_pairs={{0,2},{1,3},{2,0},{3,1},{4,6},{5,7},{6,4},{7,5},{8,10},{9,11},{10,... | collective-permute-start | bytes 1572872 | tf_op jit(solution)/shard_map/ppermute | solution.py:396
  5.2 14.7 %collective-permute-start.3 = (bf16[2048,128]{1,0:T(8,128)(2,1)S(1)}, bf16[2048,128]{1,0:T(8,128)(2,1)S(1)}, u32[]{:S(2)}, u32[]{:S(2)}) collective-permute-start(bf16[2048,128]{1,0:T(8,128)(2,1)S(1)} %get-tuple-element.31.own_ref), channel_id=1, source_target_pairs={{0,1},{1,0},{2,3},{3,2},{4,8},{5,9},{6,10},{7,11},{8,4},{9,5},{10,... | collective-permute-start | bytes 1572872 | tf_op jit(solution)/shard_map/ppermute | solution.py:396
  5.2 14.7 %collective-permute-start.2 = (bf16[2048,128]{1,0:T(8,128)(2,1)S(1)}, bf16[2048,128]{1,0:T(8,128)(2,1)S(1)}, u32[]{:S(2)}, u32[]{:S(2)}) collective-permute-start(bf16[2048,128]{1,0:T(8,128)(2,1)S(1)} %get-tuple-element.31.own_ref), channel_id=1, source_target_pairs={{0,4},{1,5},{2,6},{3,7},{4,0},{5,1},{6,2},{7,3},{8,12},{9,13},{10,... | collective-permute-start | bytes 1572872 | tf_op jit(solution)/shard_map/ppermute | solution.py:396
  19.8 7.3 %collective-permute-start.1 = (bf16[1024,128]{1,0:T(8,128)(2,1)S(1)}, bf16[1024,128]{1,0:T(8,128)(2,1)S(1)}, u32[]{:S(2)}, u32[]{:S(2)}) collective-permute-start(bf16[1024,128]{1,0:T(8,128)(2,1)S(1)} %slice.9), channel_id=1, source_target_pairs={{0,4},{1,5},{2,6},{3,7},{4,0},{5,1},{6,2},{7,3},{8,12},{9,13},{10,... | collective-permute-start | bytes 786440 | tf_op jit(solution)/shard_map/ppermute | solution.py:396
  20.0 7.3 %collective-permute-start.4 = (bf16[1024,128]{1,0:T(8,128)(2,1)S(1)}, bf16[1024,128]{1,0:T(8,128)(2,1)S(1)}, u32[]{:S(2)}, u32[]{:S(2)}) collective-permute-start(bf16[1024,128]{1,0:T(8,128)(2,1)S(1)} %get-tuple-element.47), channel_id=1, source_target_pairs={{0,2},{1,3},{2,0},{3,1},{4,8},{5,9},{6,10},{7,11},{8,4},{9,5},{10,... | collective-permute-start | bytes 786440 | tf_op jit(solution)/shard_map/ppermute | solution.py:396
  20.6 6.6 %collective-permute-start.5 = (bf16[1024,128]{1,0:T(8,128)(2,1)S(1)}, bf16[1024,128]{1,0:T(8,128)(2,1)S(1)}, u32[]{:S(2)}, u32[]{:S(2)}) collective-permute-start(bf16[1024,128]{1,0:T(8,128)(2,1)S(1)} %get-tuple-element.48), channel_id=1, source_target_pairs={{0,1},{1,0},{2,3},{3,2},{4,6},{5,7},{6,4},{7,5},{8,10},{9,11},{10,... | collective-permute-start | bytes 786440 | tf_op jit(solution)/shard_map/ppermute | solution.py:396
  20.6 6.6 %copy-start = (bf16[16,256,64]{1,2,0:T(8,128)(2,1)S(1)}, bf16[16,256,64]{1,2,0:T(8,128)(2,1)}, u32[]{:S(2)}) copy-start(bf16[16,256,64]{1,2,0:T(8,128)(2,1)} %param.15) | copy-start | bytes 1572868
  20.7 6.6 %copy-start.1 = (bf16[16,64,64]{2,1,0:T(8,128)(2,1)S(1)}, bf16[16,64,64]{2,1,0:T(8,128)(2,1)}, u32[]{:S(2)}) copy-start(bf16[16,64,64]{2,1,0:T(8,128)(2,1)} %up_one_ref.1) | copy-start | bytes 393220
  20.7 6.6 %copy-start.2 = (bf16[8,64,64]{2,1,0:T(8,128)(2,1)S(1)}, bf16[8,64,64]{2,1,0:T(8,128)(2,1)}, u32[]{:S(2)}) copy-start(bf16[8,64,64]{2,1,0:T(8,128)(2,1)} %up_two_ref.1) | copy-start | bytes 196612
